TPU v7x, 512 devices: a whole 4x4x16 slice. The times are simulated.
512 devices in a mesh: gz: 8 (over y, core), row: 8 (over x, z_hi), col: 8 (over z_lo).
Axes of the slice: x: 4, y: 4, z: 16 (z_hi: 2, z_lo: 8; z = z_hi * 8 + z_lo), core: 2. Of those that a mesh axis runs over, the one named last changes fastest.
Arguments:
- contributions: bfloat16 [8, 8192, 8192], P('gz', 'row', 'col'), may hold values from -1.5 to 1.5
- block_pattern: int32 [32, 32], replicated, may hold values 0 or 1
- row_map: int32 [32], replicated, may hold values from 0 to 31, each once
- col_map: int32 [32], replicated, may hold values from 0 to 31, each once
- lower_inv: float32 [2, 256, 256], replicated, may hold values from -1 to 1, as said below
- upper_inv: float32 [2, 256, 256], replicated, may hold values from -2 to 2, as said below
Outputs:
- factored: bfloat16 [8192, 8192], P('row', ('col', 'gz'))
Inputs may be any that keep to these rules, and one draw needn't show every extreme that they name: `row_map`: each block index appears once. `col_map`: each block index appears once. `lower_inv`: zero above the diagonal, ones on it. `upper_inv`: zero below the diagonal, diagonal entries from 0.5 to 2.
All inputs are finite; a program needn't handle non-finite values.
Results may differ from a plain program's by a relative error of at most 0.0012.
Values sent between devices are 32-bit elements; how exact they have to be, the bound alone decides.
No kernel may reach another device: no remote copies, remote signals or barrier semaphores. Data moves between devices by JAX's collectives and lax.ppermute only.
A program may use at most 64 MiB of HBM per device.

v0:
```python
import jax
import jax.numpy as jnp
from jax import lax
from jax.sharding import PartitionSpec as P


def spread(block, axis, holder):
    block = jnp.where(lax.axis_index(axis) == holder, block, jnp.zeros_like(block))
    return lax.psum(block, axis)


def lookup(indices, table):
    iota = jnp.arange(table.shape[0], dtype=jnp.int32)
    return jnp.sum(jnp.where(indices[:, None] == iota[None, :], table[None, :], 0), axis=1)


def position_of(table, value):
    iota = jnp.arange(table.shape[0], dtype=jnp.int32)
    return jnp.sum(jnp.where(table == value, iota, 0))


def hot_rows(indices, block_count):
    iota = jnp.arange(block_count, dtype=jnp.int32)
    return (indices[:, None] == iota[None, :]).astype(jnp.float32)


def lower_reduce(partial_term):
    reduced = lax.psum(partial_term, ("gz", "col"))
    return reduced


def shards(contributions, block_pattern, row_map, col_map, lower_inv, upper_inv):
    highest = lax.Precision.HIGHEST
    block_size = upper_inv.shape[-1]
    layer_id = lax.axis_index("gz")
    row_id = lax.axis_index("row")
    col_id = lax.axis_index("col")
    local_sum = contributions[0].astype(jnp.float32)
    row_blocks = local_sum.shape[0] // block_size
    block_count = block_pattern.shape[0]
    merged = lax.psum_scatter(local_sum, "gz", scatter_dimension=1, tiled=True)
    col_width = merged.shape[1]
    col_first = col_id * local_sum.shape[1] + layer_id * col_width
    col_index = col_first + jnp.arange(col_width, dtype=jnp.int32)
    col_offset = col_index % block_size
    col_global = lookup(col_index // block_size, col_map)
    row_slots = row_id * row_blocks + jnp.arange(row_blocks, dtype=jnp.int32)
    row_global = lookup(row_slots, row_map)
    pattern_f = jnp.maximum(block_pattern, jnp.eye(block_count, dtype=jnp.int32)).astype(
        jnp.float32
    )
    pattern_local = jnp.dot(
        jnp.dot(hot_rows(row_global, block_count), pattern_f, precision=highest),
        hot_rows(col_global, block_count).T,
        precision=highest,
    )
    matrix = merged.reshape(row_blocks, block_size, col_width) * pattern_local[:, None, :]
    offsets = jnp.arange(block_size, dtype=jnp.int32)
    for pivot_step in range(2):
        pivot_row = position_of(row_map, pivot_step)
        chosen = col_global == pivot_step
        selector = jnp.where(
            (col_offset[None, :] == offsets[:, None]) & chosen[None, :], 1.0, 0.0
        ).astype(jnp.float32)
        gathered_inv = jnp.dot(selector.T, upper_inv[pivot_step], precision=highest)
        flat_rows = matrix.reshape(row_blocks * block_size, col_width)
        partial_term = jnp.dot(flat_rows, gathered_inv, precision=highest)
        low_panel = lower_reduce(partial_term)
        row_keep = row_global > pivot_step
        low_panel = (
            low_panel.reshape(row_blocks, block_size, block_size)
            * row_keep.astype(jnp.float32)[:, None, None]
        )
        pivot_rows = lax.dynamic_slice_in_dim(matrix, pivot_row % row_blocks, 1, 0)[0]
        col_keep = col_global > pivot_step
        candidate = (
            jnp.dot(lower_inv[pivot_step], pivot_rows, precision=highest)
            * col_keep.astype(jnp.float32)[None, :]
        )
        up_panel = spread(candidate, "row", pivot_row // row_blocks)
        low_flat = low_panel.reshape(row_blocks * block_size, block_size)
        update = jnp.dot(low_flat, up_panel, precision=highest).reshape(
            row_blocks, block_size, col_width
        )
        matrix = matrix - pattern_local[:, None, :] * update
        placed = jnp.dot(low_flat, selector, precision=highest).reshape(
            row_blocks, block_size, col_width
        )
        matrix = jnp.where(chosen[None, None, :] & row_keep[:, None, None], placed, matrix)
        matrix = jnp.where(
            (row_slots == pivot_row)[:, None, None] & col_keep[None, None, :],
            up_panel[None],
            matrix,
        )
    result = matrix.reshape(row_blocks * block_size, col_width)
    return result.astype(jnp.bfloat16)


def solution(mesh):
    in_specs = (P("gz", "row", "col"), P(), P(), P(), P(), P())
    out_specs = P("row", ("col", "gz"))
    return jax.shard_map(shards, mesh=mesh, in_specs=in_specs, out_specs=out_specs, check_vma=False)
```

profile of v0, /device:TPU:6, one launch (start us, length us, event | category | flops | bytes accessed | tf_op | source)
XLA Modules:
  0.0 2029.3 jit_solution(16704291419229361258)
XLA Ops:
  6.5 0.0 reduce-scatter.2.cloned.1.call-start
  6.6 4.1 bitcast_convert_fusion
  10.6 0.0 reduce-scatter.2.cloned.1.call-update
  10.7 0.0 all-reduce.5.cloned.1.call-start
  10.7 0.0 copy-done.4
  10.7 0.7 fusion.56
  14.2 0.2 select_reduce_fusion.1
  14.4 0.0 copy-done.5
  14.4 0.1 select_reduce_fusion
  14.5 0.0 copy-done.3
  14.5 0.2 fusion.51
  14.7 0.2 fusion.49
  14.9 0.0 copy-done.2
  14.9 0.4 fusion.12
  15.3 45.5 %reduce-scatter.2.cloned.1.call-done = f32[1024,128]{1,0:T(8,128)} async-done(((f32[1024,1024]{1,0:T(8,128)}), f32[1024,128]{1,0:T(8,128)}) %reduce-scatter.2.cloned.1.call-update) | async-done | bytes 524304 | tf_op jit(solution)/shard_map/reduce_scatter | solution.py:41
  60.8 1.1 broadcast_multiply_fusion.2
  61.9 0.0 copy-done.1
  61.9 1.1 fusion.8
  63.0 0.0 all-reduce.5.cloned.1.call-update
  63.0 0.0 all-reduce.7.cloned.1.call-start
  63.1 1.1 bitcast_multiply_fusion
  64.1 2.0 fusion.72
  66.1 0.0 all-reduce.7.cloned.1.call-update
  66.2 0.0 all-reduce.9.cloned.1.call-start
  68.8 0.1 broadcast_bitcast_fusion
  68.9 0.7 broadcast_compare_fusion.2
  69.5 0.1 broadcast_and_fusion.1
  69.6 0.3 fusion.9
  70.0 141.8 %all-reduce.5.cloned.1.call-done = f32[256,128]{0,1:T(8,128)} async-done(((f32[256,128]{0,1:T(8,128)}), f32[256,128]{0,1:T(8,128)}) %all-reduce.5.cloned.1.call-update) | async-done | bytes 131088 | tf_op jit(solution)/shard_map/psum | solution.py:9
  211.8 1.0 copy.11
  212.7 826.3 %all-reduce.7.cloned.1.call-done = f32[1024,256]{1,0:T(8,128)} async-done(((f32[1024,256]{1,0:T(8,128)}), f32[1024,256]{1,0:T(8,128)}) %all-reduce.7.cloned.1.call-update) | async-done | bytes 1048592 | tf_op jit(solution)/shard_map/psum | solution.py:28
  1039.1 1.4 broadcast_multiply_fusion.1
  1040.5 0.0 copy-done
  1040.5 1.9 fusion.2
  1042.4 1.0 fusion
  1043.4 1.1 fusion.6
  1044.5 0.0 all-reduce.9.cloned.1.call-update
  1044.5 0.0 all-reduce.11.cloned.1.call-start
  1044.6 2.0 fusion.73
  1046.6 0.0 all-reduce.11.cloned.1.call-update
  1046.6 0.6 broadcast_compare_fusion.7
  1047.2 0.1 broadcast_and_fusion
  1047.3 143.2 %all-reduce.9.cloned.1.call-done = f32[256,128]{0,1:T(8,128)} async-done(((f32[256,128]{0,1:T(8,128)}), f32[256,128]{0,1:T(8,128)}) %all-reduce.9.cloned.1.call-update) | async-done | bytes 131088 | tf_op jit(solution)/shard_map/psum | solution.py:9
  1190.5 1.0 copy.13
  1191.5 826.2 %all-reduce.11.cloned.1.call-done = f32[1024,256]{1,0:T(8,128)} async-done(((f32[1024,256]{1,0:T(8,128)}), f32[1024,256]{1,0:T(8,128)}) %all-reduce.11.cloned.1.call-update) | async-done | bytes 1048592 | tf_op jit(solution)/shard_map/psum | solution.py:28
  2017.8 1.4 broadcast_multiply_fusion
  2019.2 1.9 fusion.3
  2021.1 1.7 fusion.4
  (13 shorter events, 0.1 us)
Async XLA Ops:
  6.5 4.2 copy-start.4
  6.5 7.8 copy-start.5
  6.5 7.9 copy-start.3
  6.5 8.3 copy-start.2
  6.5 54.2 %reduce-scatter.2.cloned.1.call-start = ((), (), s32[]{:S(2)}) async-start(), calls=%async_computation.1 | async-start | bytes 4718592 | tf_op jit(solution)/shard_map/reduce_scatter | solution.py:41
  10.6 51.3 %copy-start.1 = (f32[2,256,256]{2,1,0:T(8,128)S(1)}, f32[2,256,256]{2,1,0:T(8,128)}, u32[]{:S(2)}) copy-start(f32[2,256,256]{2,1,0:T(8,128)} %param.10) | copy-start | bytes 1572868
  10.7 201.1 %all-reduce.5.cloned.1.call-start = ((), (), s32[]{:S(2)}) async-start(), calls=%async_computation.2 | async-start | bytes 262144 | tf_op jit(solution)/shard_map/psum | solution.py:9
  60.8 979.8 %copy-start = (f32[1024,128]{1,0:T(8,128)S(1)}, f32[1024,128]{1,0:T(8,128)}, u32[]{:S(2)}) copy-start(f32[1024,128]{1,0:T(8,128)} %reduce-scatter.2.cloned.1.call-done) | copy-start | bytes 1572868
  63.0 976.1 %all-reduce.7.cloned.1.call-start = ((), (), s32[]{:S(2)}) async-start(), calls=%async_computation.3 | async-start | bytes 2097152 | tf_op jit(solution)/shard_map/psum | solution.py:28
  66.2 1124.4 %all-reduce.9.cloned.1.call-start = ((), (), s32[]{:S(2)}) async-start(), calls=%async_computation.4 | async-start | bytes 262144 | tf_op jit(solution)/shard_map/psum | solution.py:9
  1044.5 973.3 %all-reduce.11.cloned.1.call-start = ((), (), s32[]{:S(2)}) async-start(), calls=%async_computation.5 | async-start | bytes 2097152 | tf_op jit(solution)/shard_map/psum | solution.py:28
Sparse Core Ops, SparseCore 0:
  10.8 49.9 reduce-scatter.1
  63.6 148.0 all-reduce.4
  214.9 824.1 all-reduce.6
  1044.6 145.8 all-reduce.8
  1193.5 824.1 all-reduce.10
where the time goes:
time: 2030 us
  waiting for transfers between devices  1980 us (98%)
    psum x2, waiting for transfers between devices, lower_reduce(): reduced = lax.psum(partial_term, ('gz', 'col'))  1650 us
    psum x2, waiting for transfers between devices, spread(): return lax.psum(block, axis)  285 us
    reduce_scatter x1, waiting for transfers between devices, shards(): merged = lax.psum_scatter(local_sum, 'gz', scatter_dimension=1, tiled=True)  45.5 us
  transfers between devices with their start and end apart: 5, of which 5 were waited for; matrix products, arithmetic and copies ran while one was open for 1% of the time, Pallas kernels for 0%

commit v1 on v0

v1 whole, which is shorter than its diff:
```python
import jax
import jax.numpy as jnp
from jax import lax
from jax.sharding import PartitionSpec as P

HIGHEST = lax.Precision.HIGHEST


def lookup(index, table):
    iota = jnp.arange(table.shape[0], dtype=jnp.int32)
    return jnp.sum(jnp.where(index == iota, table, 0))


def position_of(table, value):
    iota = jnp.arange(table.shape[0], dtype=jnp.int32)
    return jnp.sum(jnp.where(table == value, iota, 0)).astype(jnp.int32)


def mm(a, b):
    return jnp.dot(a, b, precision=HIGHEST)


def swap(x, axis, size, bit):
    return lax.ppermute(x, axis, [(i, i ^ bit) for i in range(size)])


def bit_of(index, bit):
    return (index // bit) % 2


def part(x, axis, which):
    half = x.shape[axis] // 2
    return lax.dynamic_slice_in_dim(x, which * half, half, axis)


def join(mine, other, axis, which):
    return jnp.where(
        which == 0,
        jnp.concatenate([mine, other], axis),
        jnp.concatenate([other, mine], axis),
    )


def choose(mine, other, me, sources, bit):
    same = [bit_of(me, bit) == bit_of(s, bit) for s in sources]
    return jnp.stack([jnp.where(same[k], mine[k], other[k]) for k in range(2)])


def spread(data, axis, size, me, sources, near, far, cross):
    for bit in (near, far):
        which = bit_of(me, bit)
        other = swap(part(data, 1, 1 - which), axis, size, bit)
        data = choose(part(data, 1, which), other, me, sources, bit)
    other = swap(data, axis, size, cross)
    data = choose(data, other, me, sources, cross)
    for bit in (far, near):
        which = bit_of(me, bit)
        data = join(data, swap(data, axis, size, bit), 1, which)
    return data


def shards(contributions, block_pattern, row_map, col_map, lower_inv, upper_inv):
    size = upper_inv.shape[-1]
    local = contributions[0]
    slots = local.shape[0] // size
    count = block_pattern.shape[0]
    n_gz, n_row, n_col = lax.axis_size("gz"), lax.axis_size("row"), lax.axis_size("col")
    gz, row, col = lax.axis_index("gz"), lax.axis_index("row"), lax.axis_index("col")
    y, core = gz // 2, gz % 2
    n_y = n_gz // 2
    thin = size // n_gz
    row_at = [position_of(row_map, k) for k in range(2)]
    col_at = [position_of(col_map, k) for k in range(2)]
    row_owner = [p // slots for p in row_at]
    col_owner = [p // slots for p in col_at]
    pattern = jnp.maximum(block_pattern, jnp.eye(count, dtype=jnp.int32)).astype(jnp.float32)

    merged = lax.psum_scatter(local.astype(jnp.float32), "gz", scatter_dimension=1, tiled=True)
    width = merged.shape[1]

    panel = jnp.stack(
        [
            lax.dynamic_slice_in_dim(local, (p % slots) * size, size, 1).astype(jnp.float32)
            for p in col_at
        ]
    )
    panel = panel.reshape(2, slots, n_y, 2, thin, size)
    keep = lax.dynamic_index_in_dim(panel, core, 3, keepdims=False)
    give = lax.dynamic_index_in_dim(panel, 1 - core, 3, keepdims=False)
    panel = keep + swap(give, "gz", n_gz, 1)
    total = lax.dynamic_index_in_dim(panel, y, 2, keepdims=False)
    for step in (1, 3, 2):
        chunk = lax.dynamic_index_in_dim(panel, (y + step) % n_y, 2, keepdims=False)
        total = total + lax.ppermute(
            chunk, "gz", [(2 * i + c, 2 * ((i + step) % n_y) + c) for i in range(n_y) for c in range(2)]
        )

    corner = jnp.stack(
        [
            lax.dynamic_index_in_dim(total[k], row_at[1 - k] % slots, 0, keepdims=False)
            for k in range(2)
        ]
    )
    for bit in (1, 2, 4):
        corner = choose(corner, swap(corner, "row", n_row, bit), row, row_owner[::-1], bit)
    for bit in (4, 2, 1):
        corner = choose(corner, swap(corner, "col", n_col, bit), col, col_owner, bit)

    panel = spread(total.reshape(2, slots * thin, size), "col", n_col, col, col_owner, 1, 2, 4)
    mine = jnp.concatenate([panel, corner], 1)
    both = lax.all_gather(mine, "gz", axis=0)
    both = both.reshape(n_gz, 2, slots + 1, thin, size).transpose(1, 2, 0, 3, 4)
    both = both.reshape(2, slots + 1, size, size)
    raw = both[:, :slots].reshape(2, slots * size, size)
    below, above = both[0, slots], both[1, slots]

    blocks = merged.reshape(slots, size, width)
    rows = jnp.stack(
        [lax.dynamic_index_in_dim(blocks, p % slots, 0, keepdims=False) for p in row_at]
    )
    rows = spread(rows, "row", n_row, row, row_owner, 2, 4, 1)

    col_first = col * local.shape[1] + gz * width
    offset = col_first % size
    col_global = lookup(col_first // size, col_map)
    row_global = jnp.stack([lookup(row * slots + s, row_map) for s in range(slots)])
    pattern_col = jnp.sum(
        jnp.where(jnp.arange(count) == col_global, pattern, 0.0), axis=1
    )
    hot = (row_global[:, None] == jnp.arange(count)).astype(jnp.float32)
    pattern_own = jnp.sum(hot * pattern_col, axis=1)
    keep = [
        (row_global > k).astype(jnp.float32) * jnp.sum(hot * pattern[:, k], axis=1)
        for k in range(2)
    ]
    keep = [jnp.repeat(k, size)[:, None] for k in keep]

    low0 = keep[0] * mm(raw[0], upper_inv[0])
    low0_at = pattern[1, 0] * mm(below, upper_inv[0])
    up0_at = pattern[0, 1] * mm(lower_inv[0], above)
    low1 = keep[1] * mm(raw[1] - mm(low0, up0_at), upper_inv[1])
    up0 = jnp.where(col_global > 0, pattern_col[0], 0.0) * mm(lower_inv[0], rows[0])
    up1 = jnp.where(col_global > 1, pattern_col[1], 0.0) * mm(
        lower_inv[1], rows[1] - mm(low0_at, up0)
    )
    update = (mm(low0, up0) + mm(low1, up1)).reshape(slots, size, width)
    matrix = pattern_own[:, None, None] * (blocks - update)
    lows = [
        lax.dynamic_slice_in_dim(low, offset, width, 1).reshape(slots, size, width)
        for low in (low0, low1)
    ]
    rg = row_global[:, None, None]
    matrix = jnp.where((col_global == 0) & (rg > 0), lows[0], matrix)
    matrix = jnp.where((col_global == 1) & (rg > 1), lows[1], matrix)
    matrix = jnp.where((rg == 0) & (col_global > 0), up0[None], matrix)
    matrix = jnp.where((rg == 1) & (col_global > 1), up1[None], matrix)
    return matrix.reshape(slots * size, width).astype(jnp.bfloat16)


def solution(mesh):
    in_specs = (P("gz", "row", "col"), P(), P(), P(), P(), P())
    out_specs = P("row", ("col", "gz"))
    return jax.shard_map(shards, mesh=mesh, in_specs=in_specs, out_specs=out_specs, check_vma=False)
```

time: 2030 us -> 254 us (0.13)
  waiting for transfers between devices: 1980 us -> 99.2 us
  starting transfers between devices: 0.2 us -> 87.6 us
    psum x4 -> x0, waiting for transfers between devices: 1940 us -> none  [the longest x2 1650 us: lower_reduce(): reduced = lax.psum(partial_term, ('gz', 'col'))]
    ppermute x0 -> x20, starting transfers between devices: none -> 87.6 us  [the longest x17 76 us: swap(): return lax.ppermute(x, axis, [(i, i ^ bit) for i in range(size)])]
    ppermute x0 -> x20, waiting for transfers between devices: none -> 35.1 us  [the longest x17 34 us: swap(): return lax.ppermute(x, axis, [(i, i ^ bit) for i in range(size)])]
  transfers between devices with their start and end apart: 5 -> 22, of which waited for: 5 -> 18; matrix products, arithmetic and copies ran while one was open for 1% -> 8% of each run, Pallas kernels for 0% -> 0%
where the time goes in v1:
time: 254 us; the launch traced here: 252 us
  waiting for transfers between devices  99.2 us (39%)
  starting transfers between devices  87.6 us (34%)
  between operations  28.9 us (11%)
  matrix products  15.9 us (6%)
  local copies, waits for them, and re-layouts  11.7 us (5%)
  other arithmetic  8.99 us (4%)
    ppermute x17, starting transfers between devices, swap(): return lax.ppermute(x, axis, [(i, i ^ bit) for i in range(size)])  76 us
    reduce_scatter x1, waiting for transfers between devices, shards(): lax.psum_scatter(local.astype(jnp.float32), 'gz', scatter_dimension=1, ti...  45.1 us
    ppermute x17, waiting for transfers between devices, swap(): return lax.ppermute(x, axis, [(i, i ^ bit) for i in range(size)])  34 us
    all_gather x1, waiting for transfers between devices, shards(): both = lax.all_gather(mine, 'gz', axis=0)  18.9 us
    dot_general x10, matrix products, mm(): return jnp.dot(a, b, precision=HIGHEST)  15.9 us
    ppermute x3, starting transfers between devices, shards(): lax.ppermute(chunk, 'gz', [(2 * i + c, 2 * ((i + step) % n_y) + c) for i...  11.6 us
  transfers between devices with their start and end apart: 22, of which 18 were waited for; matrix products, arithmetic and copies ran while one was open for 8% of the time, Pallas kernels for 0%

profile of v1, /device:TPU:6, one launch (start us, length us, event | category | flops | bytes accessed | tf_op | source)
XLA Modules:
  0.0 252.4 jit_solution(3279614777335671348)
XLA Ops:
  6.5 1.5 fusion.29
  11.9 1.3 constant_dynamic-slice_fusion.4
  13.5 1.1 copy.31
  14.5 1.9 collective-permute-start.5
  16.5 2.8 %collective-permute-done.5 = f32[2,4,4,32,256]{4,3,1,0,2:T(8,128)S(1)} collective-permute-done((f32[2,4,4,32,256]{4,3,1,0,2:T(8,128)}, f32[2,4,4,32,256]{4,3,1,0,2:T(8,128)S(1)}, u32[]{:S(2)}, u32[]{:S(2)}) %collective-permute-start.5) | collective-permute-done | bytes 1048608 | tf_op jit(solution)/shard_map/ppermute | solution.py:24
  19.5 3.5 %collective-permute-start.6 = (f32[2,4,32,256]{3,2,1,0:T(8,128)S(1)}, f32[2,4,32,256]{3,2,1,0:T(8,128)S(1)}, u32[]{:S(2)}, u32[]{:S(2)}) collective-permute-start(f32[2,4,32,256]{3,2,1,0:T(8,128)S(1)} %get-tuple-element.27), channel_id=1, source_target_pairs={{0,128},{64,192},{128,256},{192,320},{256,384},{320,448},{384,0},{... | collective-permute-start | bytes 786440 | tf_op jit(solution)/shard_map/ppermute | solution.py:94
  23.0 4.8 %collective-permute-start.8 = (f32[2,4,32,256]{3,2,1,0:T(8,128)S(1)}, f32[2,4,32,256]{3,2,1,0:T(8,128)S(1)}, u32[]{:S(2)}, u32[]{:S(2)}) collective-permute-start(f32[2,4,32,256]{3,2,1,0:T(8,128)S(1)} %get-tuple-element.28), channel_id=1, source_target_pairs={{0,256},{64,320},{128,384},{192,448},{256,0},{320,64},{384,128},{4... | collective-permute-start | bytes 786440 | tf_op jit(solution)/shard_map/ppermute | solution.py:94
  27.8 3.3 %collective-permute-start.7 = (f32[2,4,32,256]{3,2,1,0:T(8,128)S(1)}, f32[2,4,32,256]{3,2,1,0:T(8,128)S(1)}, u32[]{:S(2)}, u32[]{:S(2)}) collective-permute-start(f32[2,4,32,256]{3,2,1,0:T(8,128)S(1)} %get-tuple-element.29), channel_id=1, source_target_pairs={{0,384},{64,448},{128,0},{192,64},{256,128},{320,192},{384,256},{4... | collective-permute-start | bytes 786440 | tf_op jit(solution)/shard_map/ppermute | solution.py:94
  38.0 1.1 collective-permute-done.7
  39.3 15.9 %collective-permute-start.14 = (f32[2,32,256]{2,1,0:T(8,128)S(1)}, f32[2,32,256]{2,1,0:T(8,128)S(1)}, u32[]{:S(2)}, u32[]{:S(2)}) collective-permute-start(f32[2,32,256]{2,1,0:T(8,128)S(1)} %pad_maximum_fusion.4), channel_id=1, source_target_pairs={{0,8},{8,0},{16,24},{24,16},{32,40},{40,32},{48,56},{56,48},{1,9},... | collective-permute-start | bytes 196616 | tf_op jit(solution)/shard_map/ppermute | solution.py:24
  55.2 2.9 %collective-permute-start.9 = (f32[2,64,256]{2,1,0:T(8,128)S(1)}, f32[2,64,256]{2,1,0:T(8,128)S(1)}, u32[]{:S(2)}, u32[]{:S(2)}) collective-permute-start(f32[2,64,256]{2,1,0:T(8,128)S(1)} %constant_dynamic-slice_fusion), channel_id=1, source_target_pairs={{0,1},{1,0},{2,3},{3,2},{4,5},{5,4},{6,7},{7,6},{8,9},{9,8},{10,11... | collective-permute-start | bytes 393224 | tf_op jit(solution)/shard_map/ppermute | solution.py:24
  59.2 2.7 %collective-permute-start.15 = (f32[2,32,256]{2,1,0:T(8,128)S(1)}, f32[2,32,256]{2,1,0:T(8,128)S(1)}, u32[]{:S(2)}, u32[]{:S(2)}) collective-permute-start(f32[2,32,256]{2,1,0:T(8,128)S(1)} %pad_maximum_fusion.5), channel_id=1, source_target_pairs={{0,16},{8,24},{16,0},{24,8},{32,48},{40,56},{48,32},{56,40},{1,17}... | collective-permute-start | bytes 196616 | tf_op jit(solution)/shard_map/ppermute | solution.py:24
  61.9 3.0 %collective-permute-done.9 = f32[2,64,256]{2,1,0:T(8,128)S(1)} collective-permute-done((f32[2,64,256]{2,1,0:T(8,128)S(1)}, f32[2,64,256]{2,1,0:T(8,128)S(1)}, u32[]{:S(2)}, u32[]{:S(2)}) %collective-permute-start.9) | collective-permute-done | bytes 131104 | tf_op jit(solution)/shard_map/ppermute | solution.py:24
  64.9 2.2 collective-permute-start.10
  67.2 3.3 %collective-permute-start.16 = (f32[2,32,256]{2,1,0:T(8,128)S(1)}, f32[2,32,256]{2,1,0:T(8,128)S(1)}, u32[]{:S(2)}, u32[]{:S(2)}) collective-permute-start(f32[2,32,256]{2,1,0:T(8,128)S(1)} %pad_maximum_fusion.6), channel_id=1, source_target_pairs={{0,32},{8,40},{16,48},{24,56},{32,0},{40,8},{48,16},{56,24},{1,33}... | collective-permute-start | bytes 196616 | tf_op jit(solution)/shard_map/ppermute | solution.py:24
  70.5 1.6 collective-permute-done.10
  72.2 4.5 %collective-permute-start.11 = (f32[2,32,256]{2,1,0:T(8,128)S(1)}, f32[2,32,256]{2,1,0:T(8,128)S(1)}, u32[]{:S(2)}, u32[]{:S(2)}) collective-permute-start(f32[2,32,256]{2,1,0:T(8,128)S(1)} %pad_maximum_fusion.2), channel_id=1, source_target_pairs={{0,4},{1,5},{2,6},{3,7},{4,0},{5,1},{6,2},{7,3},{8,12},{9,13},{10,... | collective-permute-start | bytes 196616 | tf_op jit(solution)/shard_map/ppermute | solution.py:24
  76.8 5.2 %collective-permute-start.17 = (f32[2,32,256]{2,1,0:T(8,128)S(1)}, f32[2,32,256]{2,1,0:T(8,128)S(1)}, u32[]{:S(2)}, u32[]{:S(2)}) collective-permute-start(f32[2,32,256]{2,1,0:T(8,128)S(1)} %pad_maximum_fusion.7), channel_id=1, source_target_pairs={{0,4},{1,5},{2,6},{3,7},{4,0},{5,1},{6,2},{7,3},{8,12},{9,13},{10,... | collective-permute-start | bytes 196616 | tf_op jit(solution)/shard_map/ppermute | solution.py:24
  82.0 6.7 %collective-permute-done.11 = f32[2,32,256]{2,1,0:T(8,128)S(1)} collective-permute-done((f32[2,32,256]{2,1,0:T(8,128)S(1)}, f32[2,32,256]{2,1,0:T(8,128)S(1)}, u32[]{:S(2)}, u32[]{:S(2)}) %collective-permute-start.11) | collective-permute-done | bytes 65568 | tf_op jit(solution)/shard_map/ppermute | solution.py:24
  88.8 2.0 collective-permute-done.17
  90.7 1.9 collective-permute-start.18
  92.7 4.8 %collective-permute-start.12 = (f32[2,32,256]{2,1,0:T(8,128)S(1)}, f32[2,32,256]{2,1,0:T(8,128)S(1)}, u32[]{:S(2)}, u32[]{:S(2)}) collective-permute-start(f32[2,32,256]{2,1,0:T(8,128)S(1)} %pad_maximum_fusion.3), channel_id=1, source_target_pairs={{0,2},{1,3},{2,0},{3,1},{4,6},{5,7},{6,4},{7,5},{8,10},{9,11},{10,... | collective-permute-start | bytes 196616 | tf_op jit(solution)/shard_map/ppermute | solution.py:24
  98.0 1.9 collective-permute-start.19
  100.4 3.5 %collective-permute-start.13 = (f32[2,64,256]{2,1,0:T(8,128)S(1)}, f32[2,64,256]{2,1,0:T(8,128)S(1)}, u32[]{:S(2)}, u32[]{:S(2)}) collective-permute-start(f32[2,64,256]{2,1,0:T(8,128)S(1)} %maximum_select_fusion.3), channel_id=1, source_target_pairs={{0,1},{1,0},{2,3},{3,2},{4,5},{5,4},{6,7},{7,6},{8,9},{9,8},{10,11... | collective-permute-start | bytes 393224 | tf_op jit(solution)/shard_map/ppermute | solution.py:24
  104.4 2.9 %collective-permute-done.13 = f32[2,64,256]{2,1,0:T(8,128)S(1)} collective-permute-done((f32[2,64,256]{2,1,0:T(8,128)S(1)}, f32[2,64,256]{2,1,0:T(8,128)S(1)}, u32[]{:S(2)}, u32[]{:S(2)}) %collective-permute-start.13) | collective-permute-done | bytes 131104 | tf_op jit(solution)/shard_map/ppermute | solution.py:24
  108.1 2.4 bitcast_convert_fusion
  113.3 2.6 %compare_and_fusion.1 = (pred[4]{0:T(512)(128)(4,1)S(1)}, s32[4]{0:T(128)S(1)}) fusion(pred[]{:T(512)S(6)} %gt.26, s32[1]{0:T(128)} %bitcast.3, s32[1]{0:T(128)} %bitcast.2, s32[1]{0:T(128)} %bitcast.1, s32[1]{0:T(128)} %bitcast), kind=kLoop, calls=%fused_computation.126 | loop fusion | flops 20 | bytes 37 | tf_op jit(solution)/shard_map/and | solution.py:156
  120.8 18.9 %all-gather.3.cloned.1.call-done = f32[16,160,256]{2,1,0:T(8,128)} async-done(((f32[2,160,256]{2,1,0:T(8,128)}), f32[16,160,256]{2,1,0:T(8,128)}) %all-gather.3.cloned.1.call-update) | async-done | bytes 2621456 | tf_op jit(solution)/shard_map/all_gather | solution.py:111
  139.7 2.0 copy.23
  141.8 1.5 copy-done
  143.5 45.1 %reduce-scatter.2.cloned.1.call-done = f32[1024,128]{1,0:T(8,128)} async-done(((f32[1024,1024]{1,0:T(8,128)}), f32[1024,128]{1,0:T(8,128)}) %reduce-scatter.2.cloned.1.call-update) | async-done | bytes 524304 | tf_op jit(solution)/shard_map/reduce_scatter | solution.py:78
  188.6 1.0 constant_dynamic-slice_fusion.5
  189.7 2.7 %collective-permute-start = (f32[2,128,128]{2,1,0:T(8,128)S(1)}, f32[2,128,128]{2,1,0:T(8,128)S(1)}, u32[]{:S(2)}, u32[]{:S(2)}) collective-permute-start(f32[2,128,128]{2,1,0:T(8,128)S(1)} %get-tuple-element.37), channel_id=1, source_target_pairs={{0,16},{8,24},{16,0},{24,8},{32,48},{40,56},{48,32},{56,40},{1,17}... | collective-permute-start | bytes 393224 | tf_op jit(solution)/shard_map/ppermute | solution.py:24
  192.5 1.9 convolution_multiply_fusion.1
  194.4 2.2 collective-permute-done
  196.6 3.5 %collective-permute-start.1 = (f32[2,64,128]{2,1,0:T(8,128)S(1)}, f32[2,64,128]{2,1,0:T(8,128)S(1)}, u32[]{:S(2)}, u32[]{:S(2)}) collective-permute-start(f32[2,64,128]{2,1,0:T(8,128)S(1)} %get-tuple-element.43), channel_id=1, source_target_pairs={{0,32},{8,40},{16,48},{24,56},{32,0},{40,8},{48,16},{56,24},{1,33}... | collective-permute-start | bytes 196616 | tf_op jit(solution)/shard_map/ppermute | solution.py:24
  200.1 2.2 convolution_multiply_fusion.2
  202.3 2.1 collective-permute-done.1
  204.5 13.1 %collective-permute-start.2 = (f32[2,64,128]{2,1,0:T(8,128)S(1)}, f32[2,64,128]{2,1,0:T(8,128)S(1)}, u32[]{:S(2)}, u32[]{:S(2)}) collective-permute-start(f32[2,64,128]{2,1,0:T(8,128)S(1)} %pad_maximum_fusion), channel_id=1, source_target_pairs={{0,8},{8,0},{16,24},{24,16},{32,40},{40,32},{48,56},{56,48},{1,9},... | collective-permute-start | bytes 196616 | tf_op jit(solution)/shard_map/ppermute | solution.py:24
  218.6 2.8 %collective-permute-done.2 = f32[2,64,128]{2,1,0:T(8,128)S(1)} collective-permute-done((f32[2,64,128]{2,1,0:T(8,128)S(1)}, f32[2,64,128]{2,1,0:T(8,128)S(1)}, u32[]{:S(2)}, u32[]{:S(2)}) %collective-permute-start.2) | collective-permute-done | bytes 65568 | tf_op jit(solution)/shard_map/ppermute | solution.py:24
  221.4 3.1 %collective-permute-start.3 = (f32[2,64,128]{2,1,0:T(8,128)S(1)}, f32[2,64,128]{2,1,0:T(8,128)S(1)}, u32[]{:S(2)}, u32[]{:S(2)}) collective-permute-start(f32[2,64,128]{2,1,0:T(8,128)S(1)} %pad_maximum_fusion.1), channel_id=1, source_target_pairs={{0,32},{8,40},{16,48},{24,56},{32,0},{40,8},{48,16},{56,24},{1,33}... | collective-permute-start | bytes 196616 | tf_op jit(solution)/shard_map/ppermute | solution.py:24
  225.5 3.5 %collective-permute-done.3 = f32[2,64,128]{2,1,0:T(8,128)S(1)} collective-permute-done((f32[2,64,128]{2,1,0:T(8,128)S(1)}, f32[2,64,128]{2,1,0:T(8,128)S(1)}, u32[]{:S(2)}, u32[]{:S(2)}) %collective-permute-start.3) | collective-permute-done | bytes 65568 | tf_op jit(solution)/shard_map/ppermute | solution.py:24
  229.1 2.7 %collective-permute-start.4 = (f32[2,128,128]{2,1,0:T(8,128)S(1)}, f32[2,128,128]{2,1,0:T(8,128)S(1)}, u32[]{:S(2)}, u32[]{:S(2)}) collective-permute-start(f32[2,128,128]{2,1,0:T(8,128)S(1)} %maximum_select_fusion.2), channel_id=1, source_target_pairs={{0,16},{8,24},{16,0},{24,8},{32,48},{40,56},{48,32},{56,40},{1,17}... | collective-permute-start | bytes 393224 | tf_op jit(solution)/shard_map/ppermute | solution.py:24
  231.8 2.0 convolution_multiply_fusion.3
  233.8 2.1 collective-permute-done.4
  237.4 1.0 fusion.42
  239.1 1.3 convolution_multiply_fusion.4
  241.5 4.1 %fusion.6 = bf16[1024,128]{1,0:T(8,128)(2,1)} fusion(bf16[1024,128]{1,0:T(8,128)(2,1)S(1)} %bitcast.112, bf16[1024,128]{1,0:T(8,128)(2,1)S(1)} %bitcast.113, f32[1024,128]{1,0:T(8,128)} %reduce-scatter.2.cloned.1.call-done, f32[1024,128]{1,0:T(8,128)S(1)} %fusion.43, f32[1024,256]{1,0:T(8,128)S(1)} %convolution_multiply_fusion, ...), kind=kOutput, calls=%fused_computation.11 | convolution fusion | flops 403570688 | bytes 3809284 | tf_op jit(solution)/shard_map/dot_general | solution.py:20
  (94 shorter events, 13.1 us)
Async XLA Ops:
  6.5 133.2 %all-gather.3.cloned.1.call-start = ((), (), s32[]{:S(2)}) async-start(), calls=%async_computation.2 | async-start | bytes 2949120 | tf_op jit(solution)/shard_map/all_gather | solution.py:111
  14.5 4.8 %collective-permute-start.5 = (f32[2,4,4,32,256]{4,3,1,0,2:T(8,128)}, f32[2,4,4,32,256]{4,3,1,0,2:T(8,128)S(1)}, u32[]{:S(2)}, u32[]{:S(2)}) collective-permute-start(f32[2,4,4,32,256]{4,3,1,0,2:T(8,128)} %bitcast.98), channel_id=1, source_target_pairs={{0,64},{64,0},{128,192},{192,128},{256,320},{320,256},{384,448},{4... | collective-permute-start | bytes 3145736 | tf_op jit(solution)/shard_map/ppermute | solution.py:24
  19.5 18.5 %collective-permute-start.6 = (f32[2,4,32,256]{3,2,1,0:T(8,128)S(1)}, f32[2,4,32,256]{3,2,1,0:T(8,128)S(1)}, u32[]{:S(2)}, u32[]{:S(2)}) collective-permute-start(f32[2,4,32,256]{3,2,1,0:T(8,128)S(1)} %get-tuple-element.27), channel_id=1, source_target_pairs={{0,128},{64,192},{128,256},{192,320},{256,384},{320,448},{384,0},{... | collective-permute-start | bytes 786440 | tf_op jit(solution)/shard_map/ppermute | solution.py:94
  23.0 15.0 %collective-permute-start.8 = (f32[2,4,32,256]{3,2,1,0:T(8,128)S(1)}, f32[2,4,32,256]{3,2,1,0:T(8,128)S(1)}, u32[]{:S(2)}, u32[]{:S(2)}) collective-permute-start(f32[2,4,32,256]{3,2,1,0:T(8,128)S(1)} %get-tuple-element.28), channel_id=1, source_target_pairs={{0,256},{64,320},{128,384},{192,448},{256,0},{320,64},{384,128},{4... | collective-permute-start | bytes 786440 | tf_op jit(solution)/shard_map/ppermute | solution.py:94
  27.8 11.3 %collective-permute-start.7 = (f32[2,4,32,256]{3,2,1,0:T(8,128)S(1)}, f32[2,4,32,256]{3,2,1,0:T(8,128)S(1)}, u32[]{:S(2)}, u32[]{:S(2)}) collective-permute-start(f32[2,4,32,256]{3,2,1,0:T(8,128)S(1)} %get-tuple-element.29), channel_id=1, source_target_pairs={{0,384},{64,448},{128,0},{192,64},{256,128},{320,192},{384,256},{4... | collective-permute-start | bytes 786440 | tf_op jit(solution)/shard_map/ppermute | solution.py:94
  39.3 68.8 %copy-start.1 = (bf16[1,1024,1024]{2,1,0:T(8,128)(2,1)S(1)}, bf16[1,1024,1024]{2,1,0:T(8,128)(2,1)}, u32[]{:S(2)}) copy-start(bf16[1,1024,1024]{2,1,0:T(8,128)(2,1)} %param.6) | copy-start | bytes 6291460
  39.3 19.8 %collective-permute-start.14 = (f32[2,32,256]{2,1,0:T(8,128)S(1)}, f32[2,32,256]{2,1,0:T(8,128)S(1)}, u32[]{:S(2)}, u32[]{:S(2)}) collective-permute-start(f32[2,32,256]{2,1,0:T(8,128)S(1)} %pad_maximum_fusion.4), channel_id=1, source_target_pairs={{0,8},{8,0},{16,24},{24,16},{32,40},{40,32},{48,56},{56,48},{1,9},... | collective-permute-start | bytes 196616 | tf_op jit(solution)/shard_map/ppermute | solution.py:24
  55.2 9.7 %collective-permute-start.9 = (f32[2,64,256]{2,1,0:T(8,128)S(1)}, f32[2,64,256]{2,1,0:T(8,128)S(1)}, u32[]{:S(2)}, u32[]{:S(2)}) collective-permute-start(f32[2,64,256]{2,1,0:T(8,128)S(1)} %constant_dynamic-slice_fusion), channel_id=1, source_target_pairs={{0,1},{1,0},{2,3},{3,2},{4,5},{5,4},{6,7},{7,6},{8,9},{9,8},{10,11... | collective-permute-start | bytes 393224 | tf_op jit(solution)/shard_map/ppermute | solution.py:24
  59.2 8.0 %collective-permute-start.15 = (f32[2,32,256]{2,1,0:T(8,128)S(1)}, f32[2,32,256]{2,1,0:T(8,128)S(1)}, u32[]{:S(2)}, u32[]{:S(2)}) collective-permute-start(f32[2,32,256]{2,1,0:T(8,128)S(1)} %pad_maximum_fusion.5), channel_id=1, source_target_pairs={{0,16},{8,24},{16,0},{24,8},{32,48},{40,56},{48,32},{56,40},{1,17}... | collective-permute-start | bytes 196616 | tf_op jit(solution)/shard_map/ppermute | solution.py:24
  64.9 7.2 %collective-permute-start.10 = (f32[2,32,256]{2,1,0:T(8,128)S(1)}, f32[2,32,256]{2,1,0:T(8,128)S(1)}, u32[]{:S(2)}, u32[]{:S(2)}) collective-permute-start(f32[2,32,256]{2,1,0:T(8,128)S(1)} %get-tuple-element.47), channel_id=1, source_target_pairs={{0,2},{1,3},{2,0},{3,1},{4,6},{5,7},{6,4},{7,5},{8,10},{9,11},{10,... | collective-permute-start | bytes 196616 | tf_op jit(solution)/shard_map/ppermute | solution.py:24
  67.2 9.5 %collective-permute-start.16 = (f32[2,32,256]{2,1,0:T(8,128)S(1)}, f32[2,32,256]{2,1,0:T(8,128)S(1)}, u32[]{:S(2)}, u32[]{:S(2)}) collective-permute-start(f32[2,32,256]{2,1,0:T(8,128)S(1)} %pad_maximum_fusion.6), channel_id=1, source_target_pairs={{0,32},{8,40},{16,48},{24,56},{32,0},{40,8},{48,16},{56,24},{1,33}... | collective-permute-start | bytes 196616 | tf_op jit(solution)/shard_map/ppermute | solution.py:24
  72.2 16.5 %collective-permute-start.11 = (f32[2,32,256]{2,1,0:T(8,128)S(1)}, f32[2,32,256]{2,1,0:T(8,128)S(1)}, u32[]{:S(2)}, u32[]{:S(2)}) collective-permute-start(f32[2,32,256]{2,1,0:T(8,128)S(1)} %pad_maximum_fusion.2), channel_id=1, source_target_pairs={{0,4},{1,5},{2,6},{3,7},{4,0},{5,1},{6,2},{7,3},{8,12},{9,13},{10,... | collective-permute-start | bytes 196616 | tf_op jit(solution)/shard_map/ppermute | solution.py:24
  76.8 13.9 %collective-permute-start.17 = (f32[2,32,256]{2,1,0:T(8,128)S(1)}, f32[2,32,256]{2,1,0:T(8,128)S(1)}, u32[]{:S(2)}, u32[]{:S(2)}) collective-permute-start(f32[2,32,256]{2,1,0:T(8,128)S(1)} %pad_maximum_fusion.7), channel_id=1, source_target_pairs={{0,4},{1,5},{2,6},{3,7},{4,0},{5,1},{6,2},{7,3},{8,12},{9,13},{10,... | collective-permute-start | bytes 196616 | tf_op jit(solution)/shard_map/ppermute | solution.py:24
  90.7 7.2 %collective-permute-start.18 = (f32[2,32,256]{2,1,0:T(8,128)S(1)}, f32[2,32,256]{2,1,0:T(8,128)S(1)}, u32[]{:S(2)}, u32[]{:S(2)}) collective-permute-start(f32[2,32,256]{2,1,0:T(8,128)S(1)} %pad_maximum_fusion.8), channel_id=1, source_target_pairs={{0,2},{1,3},{2,0},{3,1},{4,6},{5,7},{6,4},{7,5},{8,10},{9,11},{10,... | collective-permute-start | bytes 196616 | tf_op jit(solution)/shard_map/ppermute | solution.py:24
  92.7 7.7 %collective-permute-start.12 = (f32[2,32,256]{2,1,0:T(8,128)S(1)}, f32[2,32,256]{2,1,0:T(8,128)S(1)}, u32[]{:S(2)}, u32[]{:S(2)}) collective-permute-start(f32[2,32,256]{2,1,0:T(8,128)S(1)} %pad_maximum_fusion.3), channel_id=1, source_target_pairs={{0,2},{1,3},{2,0},{3,1},{4,6},{5,7},{6,4},{7,5},{8,10},{9,11},{10,... | collective-permute-start | bytes 196616 | tf_op jit(solution)/shard_map/ppermute | solution.py:24
  98.0 6.4 %collective-permute-start.19 = (f32[2,32,256]{2,1,0:T(8,128)S(1)}, f32[2,32,256]{2,1,0:T(8,128)S(1)}, u32[]{:S(2)}, u32[]{:S(2)}) collective-permute-start(f32[2,32,256]{2,1,0:T(8,128)S(1)} %pad_maximum_fusion.9), channel_id=1, source_target_pairs={{0,1},{1,0},{2,3},{3,2},{4,5},{5,4},{6,7},{7,6},{8,9},{9,8},{10,11... | collective-permute-start | bytes 196616 | tf_op jit(solution)/shard_map/ppermute | solution.py:24
  100.4 6.9 %collective-permute-start.13 = (f32[2,64,256]{2,1,0:T(8,128)S(1)}, f32[2,64,256]{2,1,0:T(8,128)S(1)}, u32[]{:S(2)}, u32[]{:S(2)}) collective-permute-start(f32[2,64,256]{2,1,0:T(8,128)S(1)} %maximum_select_fusion.3), channel_id=1, source_target_pairs={{0,1},{1,0},{2,3},{3,2},{4,5},{5,4},{6,7},{7,6},{8,9},{9,8},{10,11... | collective-permute-start | bytes 393224 | tf_op jit(solution)/shard_map/ppermute | solution.py:24
  108.0 80.6 %reduce-scatter.2.cloned.1.call-start = ((), (), s32[]{:S(2)}) async-start(), calls=%async_computation.1 | async-start | bytes 4718592 | tf_op jit(solution)/shard_map/reduce_scatter | solution.py:78
  110.5 7.0 %copy-start.5 = (s32[32,32]{1,0:T(8,128)S(1)}, s32[32,32]{1,0:T(8,128)}, u32[]{:S(2)}) copy-start(s32[32,32]{1,0:T(8,128)} %param.7) | copy-start | bytes 12292
  141.8 1.5 copy-start
  188.6 11.5 %copy-start.3 = (f32[2,256,256]{2,1,0:T(8,128)S(1)}, f32[2,256,256]{2,1,0:T(8,128)}, u32[]{:S(2)}) copy-start(f32[2,256,256]{2,1,0:T(8,128)} %param.10) | copy-start | bytes 1572868
  189.7 6.9 %collective-permute-start = (f32[2,128,128]{2,1,0:T(8,128)S(1)}, f32[2,128,128]{2,1,0:T(8,128)S(1)}, u32[]{:S(2)}, u32[]{:S(2)}) collective-permute-start(f32[2,128,128]{2,1,0:T(8,128)S(1)} %get-tuple-element.37), channel_id=1, source_target_pairs={{0,16},{8,24},{16,0},{24,8},{32,48},{40,56},{48,32},{56,40},{1,17}... | collective-permute-start | bytes 393224 | tf_op jit(solution)/shard_map/ppermute | solution.py:24
  196.6 27.9 %copy-start.2 = (f32[2,256,256]{2,1,0:T(8,128)S(1)}, f32[2,256,256]{2,1,0:T(8,128)}, u32[]{:S(2)}) copy-start(f32[2,256,256]{2,1,0:T(8,128)} %param.11) | copy-start | bytes 1572868
  196.6 7.8 %collective-permute-start.1 = (f32[2,64,128]{2,1,0:T(8,128)S(1)}, f32[2,64,128]{2,1,0:T(8,128)S(1)}, u32[]{:S(2)}, u32[]{:S(2)}) collective-permute-start(f32[2,64,128]{2,1,0:T(8,128)S(1)} %get-tuple-element.43), channel_id=1, source_target_pairs={{0,32},{8,40},{16,48},{24,56},{32,0},{40,8},{48,16},{56,24},{1,33}... | collective-permute-start | bytes 196616 | tf_op jit(solution)/shard_map/ppermute | solution.py:24
  204.5 16.9 %collective-permute-start.2 = (f32[2,64,128]{2,1,0:T(8,128)S(1)}, f32[2,64,128]{2,1,0:T(8,128)S(1)}, u32[]{:S(2)}, u32[]{:S(2)}) collective-permute-start(f32[2,64,128]{2,1,0:T(8,128)S(1)} %pad_maximum_fusion), channel_id=1, source_target_pairs={{0,8},{8,0},{16,24},{24,16},{32,40},{40,32},{48,56},{56,48},{1,9},... | collective-permute-start | bytes 196616 | tf_op jit(solution)/shard_map/ppermute | solution.py:24
  221.4 7.7 %collective-permute-start.3 = (f32[2,64,128]{2,1,0:T(8,128)S(1)}, f32[2,64,128]{2,1,0:T(8,128)S(1)}, u32[]{:S(2)}, u32[]{:S(2)}) collective-permute-start(f32[2,64,128]{2,1,0:T(8,128)S(1)} %pad_maximum_fusion.1), channel_id=1, source_target_pairs={{0,32},{8,40},{16,48},{24,56},{32,0},{40,8},{48,16},{56,24},{1,33}... | collective-permute-start | bytes 196616 | tf_op jit(solution)/shard_map/ppermute | solution.py:24
  225.5 13.6 %copy-start.4 = (f32[2,256,256]{2,1,0:T(8,128)S(1)}, f32[2,256,256]{2,1,0:T(8,128)}, u32[]{:S(2)}) copy-start(f32[2,256,256]{2,1,0:T(8,128)} %param.10) | copy-start | bytes 1572868
  229.1 6.9 %collective-permute-start.4 = (f32[2,128,128]{2,1,0:T(8,128)S(1)}, f32[2,128,128]{2,1,0:T(8,128)S(1)}, u32[]{:S(2)}, u32[]{:S(2)}) collective-permute-start(f32[2,128,128]{2,1,0:T(8,128)S(1)} %maximum_select_fusion.2), channel_id=1, source_target_pairs={{0,16},{8,24},{16,0},{24,8},{32,48},{40,56},{48,32},{56,40},{1,17}... | collective-permute-start | bytes 393224 | tf_op jit(solution)/shard_map/ppermute | solution.py:24
Sparse Core Ops, SparseCore 0:
  108.1 31.5 all-gather.2
  142.6 46.0 reduce-scatter.1

commit v2 on v0

v2 whole, which is shorter than its diff:
```python
import functools

import jax
import jax.numpy as jnp
from jax import lax
from jax.experimental import pallas as pl
from jax.experimental.pallas import tpu as pltpu
from jax.sharding import PartitionSpec as P

VMEM = pl.BlockSpec(memory_space=pltpu.VMEM)
SMEM = pl.BlockSpec(memory_space=pltpu.SMEM)
PARAMS = pltpu.CompilerParams(vmem_limit_bytes=32 << 20)


def position_of(table, value):
    iota = jnp.arange(table.shape[0], dtype=jnp.uint32)
    return jnp.sum(jnp.where(table == value, iota, 0), dtype=jnp.uint32)


def halves(a):
    high = a.astype(jnp.bfloat16)
    return high, (a - high.astype(jnp.float32)).astype(jnp.bfloat16)


def mm_halves(a, b):
    dot = functools.partial(jnp.dot, preferred_element_type=jnp.float32)
    return dot(a[0], b[0]) + (dot(a[0], b[1]) + dot(a[1], b[0]))


def mm(a, b):
    return mm_halves(halves(a), halves(b))


def find(ref, value):
    place = jnp.int32(0)
    for i in range(ref.shape[0]):
        place = jnp.where(ref[i] == value, i, place)
    return place


def panel_kernel(col_map, local, keep, give, buffer, sems):
    n_y, _, slots, thin, size = keep.shape
    core = lax.axis_index("gz") & 1
    copies = []
    for k in range(2):
        first = pl.multiple_of((find(col_map, k) & (slots - 1)) * size, size)
        copies.append(
            pltpu.make_async_copy(local.at[:, pl.ds(first, size)], buffer.at[k], sems.at[k])
        )
        copies[k].start()
    for k in range(2):
        copies[k].wait()
        for p in range(slots):
            for y in range(n_y):
                for out, which in ((keep, core), (give, 1 - core)):
                    first = pl.multiple_of(p * size + y * 2 * thin + which * thin, thin)
                    out[y, k, p] = buffer[k, pl.ds(first, thin), :].astype(jnp.float32)


def cut_panels(col_map, local, slots, n_y, thin, size):
    shape = jax.ShapeDtypeStruct((n_y, 2, slots, thin, size), jnp.float32)
    return pl.pallas_call(
        panel_kernel,
        out_shape=[shape, shape],
        in_specs=[SMEM, pl.BlockSpec(memory_space=pl.ANY)],
        out_specs=[VMEM, VMEM],
        scratch_shapes=[
            pltpu.VMEM((2, local.shape[0], size), jnp.bfloat16),
            pltpu.SemaphoreType.DMA((2,)),
        ],
        compiler_params=PARAMS,
    )(col_map, local)


def give_kernel(where, local, out):
    out[0] = local[...].astype(jnp.float32)


def cut_give(where, local, n_y, width):
    rows = local.shape[0]
    return pl.pallas_call(
        give_kernel,
        out_shape=jax.ShapeDtypeStruct((n_y, rows, width), jnp.float32),
        grid_spec=pltpu.PrefetchScalarGridSpec(
            num_scalar_prefetch=1,
            grid=(n_y,),
            in_specs=[pl.BlockSpec((rows, width), lambda i, w: (0, 2 * i + 1 - w[1]))],
            out_specs=pl.BlockSpec((1, rows, width), lambda i, w: (i, 0, 0)),
        ),
        compiler_params=PARAMS,
    )(where, local)


def add_kernel(where, local, other, *outs):
    for step in range(len(outs)):

        @pl.when(pl.program_id(0) == step)
        def _(out=outs[step]):
            out[...] = local[...].astype(jnp.float32) + other[0]


def add_cores(where, local, other, n_y, width):
    rows = local.shape[0]
    shape = jax.ShapeDtypeStruct((rows, width), jnp.float32)
    return pl.pallas_call(
        add_kernel,
        out_shape=[shape] * n_y,
        grid_spec=pltpu.PrefetchScalarGridSpec(
            num_scalar_prefetch=1,
            grid=(n_y,),
            in_specs=[
                pl.BlockSpec((rows, width), lambda i, w: (0, 2 * ((w[0] + i) & (n_y - 1)) + w[1])),
                pl.BlockSpec((1, rows, width), lambda i, w: ((w[0] + i) & (n_y - 1), 0, 0)),
            ],
            out_specs=[pl.BlockSpec((rows, width), lambda i, w: (0, 0))] * n_y,
        ),
        compiler_params=PARAMS,
    )(where, local, other)


def mask_at(block_pattern, row, col):
    return jnp.where(row == col, 1, block_pattern[row, col]).astype(jnp.float32)


def column_of(col_map, n_y):
    return col_map[lax.axis_index("col") * n_y + (lax.axis_index("gz") >> 1)]


def first_kernel(n_y, block_pattern, col_map, lower_inv, upper_inv, rows, up_out, term_out):
    col = column_of(col_map, n_y)
    mask = jnp.where(col > 0, mask_at(block_pattern, 0, col), 0.0)
    up = mask * mm(lower_inv[0], rows[0])
    up_out[...] = up
    term_out[...] = mm(upper_inv[0], up)


def first_terms(n_y, block_pattern, col_map, lower_inv, upper_inv, rows):
    shape = jax.ShapeDtypeStruct(rows.shape[1:], jnp.float32)
    return pl.pallas_call(
        functools.partial(first_kernel, n_y),
        out_shape=[shape, shape],
        in_specs=[SMEM] * 2 + [VMEM] * 3,
        out_specs=[VMEM, VMEM],
        compiler_params=PARAMS,
    )(block_pattern, col_map, lower_inv, upper_inv, rows)


def last_kernel(n_y, block_pattern, row_map, col_map, lower_inv, upper_inv, rows, up0, term0,
                ring, across, merged, out, high, low):
    slots = high.shape[1] - 1
    size, width = up0.shape
    thin = size // (2 * n_y)
    y = lax.axis_index("gz") >> 1
    core = lax.axis_index("gz") & 1
    col = column_of(col_map, n_y)
    order = [slots] + list(range(slots))
    for p in order:
        for source, which in ((ring, core), (across, 1 - core)):
            for step in range(n_y):
                owner = 2 * ((y + n_y - step) & (n_y - 1)) + which
                first = pl.multiple_of(owner * thin, thin)
                for k in range(2):
                    a, b = halves(source[step, k, p * thin : (p + 1) * thin, :])
                    high[k, p, pl.ds(first, thin), :] = a
                    low[k, p, pl.ds(first, thin), :] = b

    def stored(k, p):
        return high[k, p], low[k, p]

    lower0, lower1 = halves(lower_inv[0]), halves(lower_inv[1])
    upper0, upper1 = halves(upper_inv[0]), halves(upper_inv[1])
    up0 = up0[...]
    low_at = mask_at(block_pattern, 1, 0) * mm_halves(stored(0, slots), upper0)
    up_at = mask_at(block_pattern, 0, 1) * mm_halves(lower0, stored(1, slots))
    mask = jnp.where(col > 1, mask_at(block_pattern, 1, col), 0.0)
    up1 = mask * mm_halves(lower1, halves(rows[1] - mm(low_at, up0)))
    term1 = mm_halves(upper1, halves(up1))

    def own_half(matrix):
        left, right = matrix[:, :width], matrix[:, width:]
        return jnp.where(core == 0, left, right)

    term0 = jnp.where(col == 0, -own_half(upper_inv[0]), term0[...])
    term1 = jnp.where(col == 1, -own_half(upper_inv[1]), term1)
    term2 = mm_halves(upper0, halves(mm(up_at, term1)))
    both = halves(jnp.concatenate([term0, term2], axis=1))
    term1 = halves(term1)
    for p in range(slots):
        row = row_map[lax.axis_index("row") * slots + p]
        own = mask_at(block_pattern, row, col)
        keep0 = jnp.where(row > 0, mask_at(block_pattern, row, 0), 0.0)
        keep1 = jnp.where(row > 1, mask_at(block_pattern, row, 1), 0.0)
        panel0 = (col == 0) & (row > 0)
        panel1 = (col == 1) & (row > 1)
        scale = jnp.where(panel0 | panel1, 0.0, own)
        scale0 = jnp.where(panel0, keep0, scale * keep0)
        scale1 = jnp.where(panel1, keep1, scale * keep1)
        two = mm_halves(stored(0, p), both)
        one = mm_halves(stored(1, p), term1)
        here = slice(p * size, (p + 1) * size)
        value = (
            scale * merged[here, :]
            - scale0 * two[:, :width]
            - scale1 * (one - keep0 * two[:, width:])
        )
        value = jnp.where((row == 0) & (col > 0), up0, value)
        value = jnp.where((row == 1) & (col > 1), up1, value)
        out[here, :] = value.astype(jnp.bfloat16)


def last_terms(n_y, slots, block_pattern, row_map, col_map, lower_inv, upper_inv, rows, up0, term0,
               ring, across, merged):
    size = lower_inv.shape[-1]
    return pl.pallas_call(
        functools.partial(last_kernel, n_y),
        out_shape=jax.ShapeDtypeStruct(merged.shape, jnp.bfloat16),
        in_specs=[SMEM] * 3 + [VMEM] * 8,
        out_specs=VMEM,
        scratch_shapes=[pltpu.VMEM((2, slots + 1, size, size), jnp.bfloat16)] * 2,
        compiler_params=PARAMS,
    )(block_pattern, row_map, col_map, lower_inv, upper_inv, rows, up0, term0, ring, across, merged)


def swap(x, axis, size, bit):
    return lax.ppermute(x, axis, [(i, i ^ bit) for i in range(size)])


def bit_of(index, bit):
    return (index & jnp.uint32(bit)) != 0


def part(x, axis, second):
    half = x.shape[axis] // 2
    return lax.dynamic_slice_in_dim(x, second.astype(jnp.uint32) * half, half, axis)


def join(mine, other, axis, second):
    return jnp.where(
        second,
        jnp.concatenate([other, mine], axis),
        jnp.concatenate([mine, other], axis),
    )


def choose(mine, other, me, sources, bit):
    same = [bit_of(me, bit) == bit_of(s, bit) for s in sources]
    return jnp.stack([jnp.where(same[k], mine[k], other[k]) for k in range(2)])


def pick(x, index, axis):
    return lax.dynamic_index_in_dim(x, index, axis, keepdims=False)


def shards(contributions, block_pattern, row_map, col_map, lower_inv, upper_inv):
    size = upper_inv.shape[-1]
    local = contributions[0]
    slots = local.shape[0] // size
    n_gz, n_row, n_col = lax.axis_size("gz"), lax.axis_size("row"), lax.axis_size("col")
    gz, row, col = [lax.axis_index(a).astype(jnp.uint32) for a in ("gz", "row", "col")]
    y, core = gz >> 1, gz & 1
    n_y = n_gz // 2
    thin = size // n_gz
    width = local.shape[1] // n_gz
    row_at = [position_of(row_map, k) for k in range(2)]
    col_at = [position_of(col_map, k) for k in range(2)]
    shift = slots.bit_length() - 1
    row_owner = [p >> shift for p in row_at]
    col_owner = [p >> shift for p in col_at]
    row_slot = [p & (slots - 1) for p in row_at]
    where = jnp.stack([y, core]).astype(jnp.int32)

    def around(step):
        return [(2 * i + c, 2 * ((i + step) % n_y) + c) for i in range(n_y) for c in range(2)]

    keep, give = cut_panels(col_map, local, slots, n_y, thin, size)
    parts = keep + swap(give, "gz", n_gz, 1)
    panel = pick(parts, y, 0)
    for step in (1, 3, 2):
        chunk = pick(parts, (y + step) & (n_y - 1), 0)
        panel = panel + lax.ppermute(chunk, "gz", around(step))

    other = swap(cut_give(where, local, n_y, width), "gz", n_gz, 1)
    parts = add_cores(where, local, other, n_y, width)
    arrived = [lax.ppermute(parts[step], "gz", around(step)) for step in (1, 3, 2)]

    corner = jnp.stack([pick(panel[k], row_slot[1 - k], 0) for k in range(2)])
    for bit in (2, 4):
        corner = choose(corner, swap(corner, "row", n_row, bit), row, row_owner[::-1], bit)
    mirror = [(r * n_col + c, (r ^ 1) * n_col + c ^ (n_col - 1)) for r in range(n_row) for c in range(n_col)]
    other = lax.ppermute(corner, ("row", "col"), mirror)
    same = [bit_of(row, 1) == bit_of(r, 1) for r in row_owner[::-1]]
    corner = jnp.stack([jnp.where(same[k], corner[k], other[k]) for k in range(2)])
    corner_owner = [jnp.where(same[k], col_owner[k], col_owner[k] ^ (n_col - 1)) for k in range(2)]

    data = panel.reshape(2, slots * thin, size)
    for bit in (1, 2):
        second = bit_of(col, bit)
        other = swap(part(data, 1, ~second), "col", n_col, bit)
        data = choose(part(data, 1, second), other, col, col_owner, bit)
    data, arrived = lax.optimization_barrier((data, arrived))
    merged = parts[0] + (arrived[0] + arrived[1] + arrived[2])
    both = jnp.concatenate([data, corner], 1)
    other = swap(both, "col", n_col, 4)
    thick = data.shape[1]
    data = choose(data, other[:, :thick], col, col_owner, 4)
    corner = choose(corner, other[:, thick:], col, corner_owner, 4)
    for bit in (2, 1):
        second = bit_of(col, bit)
        thick = data.shape[1]
        other = swap(jnp.concatenate([data, corner], 1), "col", n_col, bit)
        data = join(data, other[:, :thick], 1, second)
        corner = choose(corner, other[:, thick:], col, corner_owner, bit)

    mine = jnp.concatenate([data, corner], 1)
    ring = [mine] + [lax.ppermute(mine, "gz", around(step)) for step in (1, 2, 3)]
    ring = jnp.stack(ring)
    across = swap(ring, "gz", n_gz, 1)

    blocks = merged.reshape(slots, size, width)
    rows = jnp.stack([pick(blocks, p, 0) for p in row_slot])
    for bit in (2, 4):
        second = bit_of(row, bit)
        other = swap(part(rows, 1, ~second), "row", n_row, bit)
        rows = choose(part(rows, 1, second), other, row, row_owner, bit)
    rows = choose(rows, swap(rows, "row", n_row, 1), row, row_owner, 1)
    for bit in (4, 2):
        rows = join(rows, swap(rows, "row", n_row, bit), 1, bit_of(row, bit))

    up0, term0 = first_terms(n_y, block_pattern, col_map, lower_inv, upper_inv, rows)
    return last_terms(n_y, slots, block_pattern, row_map, col_map, lower_inv, upper_inv, rows,
                      up0, term0, ring, across, merged)


def solution(mesh):
    in_specs = (P("gz", "row", "col"), P(), P(), P(), P(), P())
    out_specs = P("row", ("col", "gz"))
    return jax.shard_map(shards, mesh=mesh, in_specs=in_specs, out_specs=out_specs, check_vma=False)
```

time: 2030 us -> 193 us (0.10)
  waiting for transfers between devices: 1980 us -> 69.7 us
  starting transfers between devices: 0.2 us -> 95.8 us
    psum x4 -> x0, waiting for transfers between devices: 1940 us -> none  [the longest x2 1650 us: lower_reduce(): reduced = lax.psum(partial_term, ('gz', 'col'))]
    ppermute x0 -> x25, starting transfers between devices: none -> 95.8 us  [the longest x15 52.4 us: swap(): return lax.ppermute(x, axis, [(i, i ^ bit) for i in range(size)])]
    ppermute x0 -> x25, waiting for transfers between devices: none -> 69.7 us  [the longest x15 42.4 us: swap(): return lax.ppermute(x, axis, [(i, i ^ bit) for i in range(size)])]
    reduce_scatter x1 -> x0, waiting for transfers between devices: 45.5 us -> none  [shards(): merged = lax.psum_scatter(local_sum, 'gz', scatter_dimension=1, tiled=True)]
  transfers between devices with their start and end apart: 5 -> 25, of which waited for: 5 -> 13; matrix products, arithmetic and copies ran while one was open for 1% -> 2% of each run, Pallas kernels for 0% -> 4%
where the time goes in v2:
time: 193 us; the launch traced here: 191 us
  starting transfers between devices  95.8 us (50%)
  waiting for transfers between devices  69.7 us (36%)
  Pallas kernels  12.5 us (6%)
  other arithmetic  4.87 us (3%)
  between operations  4.68 us (2%)
  local copies, waits for them, and re-layouts  3.44 us (2%)
    ppermute x15, starting transfers between devices, swap(): return lax.ppermute(x, axis, [(i, i ^ bit) for i in range(size)])  52.4 us
    ppermute x15, waiting for transfers between devices, swap(): return lax.ppermute(x, axis, [(i, i ^ bit) for i in range(size)])  42.4 us
    ppermute x3, waiting for transfers between devices, shards(): lax.ppermute(parts[step], 'gz', around(step))  18.5 us
    ppermute x3, starting transfers between devices, shards(): lax.ppermute(mine, 'gz', around(step))  13.4 us
    ppermute x3, starting transfers between devices, shards(): panel = panel + lax.ppermute(chunk, 'gz', around(step))  10.9 us
    ppermute x1, starting transfers between devices, shards(): other = lax.ppermute(corner, ('row', 'col'), mirror)  9.76 us
    ppermute x3, starting transfers between devices, shards(): lax.ppermute(parts[step], 'gz', around(step))  9.3 us
    ppermute x3, waiting for transfers between devices, shards(): lax.ppermute(mine, 'gz', around(step))  8.81 us
  transfers between devices with their start and end apart: 25, of which 13 were waited for; matrix products, arithmetic and copies ran while one was open for 2% of the time, Pallas kernels for 4%

profile of v2, /device:TPU:6, one launch (start us, length us, event | category | flops | bytes accessed | tf_op | source)
XLA Modules:
  0.0 191.0 jit_solution(12255691682569843595)
XLA Ops:
  0.0 1.6 copy-done
  2.2 0.9 shard_map.66
  3.2 1.9 %collective-permute-start.1 = (f32[4,2,4,32,256]{4,3,2,1,0:T(8,128)S(1)}, f32[4,2,4,32,256]{4,3,2,1,0:T(8,128)S(1)}, u32[]{:S(2)}, u32[]{:S(2)}) collective-permute-start(f32[4,2,4,32,256]{4,3,2,1,0:T(8,128)S(1)} %get-tuple-element.19), channel_id=1, source_target_pairs={{0,64},{64,0},{128,192},{192,128},{256,320},{320,256},{384,448},{4... | collective-permute-start | bytes 3145736 | tf_op jit(solution)/shard_map/ppermute | solution.py:225
  5.1 2.6 %collective-permute-done.1 = f32[4,2,4,32,256]{4,3,2,1,0:T(8,128)S(1)} collective-permute-done((f32[4,2,4,32,256]{4,3,2,1,0:T(8,128)S(1)}, f32[4,2,4,32,256]{4,3,2,1,0:T(8,128)S(1)}, u32[]{:S(2)}, u32[]{:S(2)}) %collective-permute-start.1) | collective-permute-done | bytes 1048608 | tf_op jit(solution)/shard_map/ppermute | solution.py:225
  7.7 1.0 copy-done.9
  8.7 1.6 add.30
  10.4 3.5 %collective-permute-start.2 = (f32[2,4,32,256]{3,2,1,0:T(8,128)S(1)}, f32[2,4,32,256]{3,2,1,0:T(8,128)S(1)}, u32[]{:S(2)}, u32[]{:S(2)}) collective-permute-start(f32[2,4,32,256]{3,2,1,0:T(8,128)S(1)} %get-tuple-element.33), channel_id=1, source_target_pairs={{0,128},{64,192},{128,256},{192,320},{256,384},{320,448},{384,0},{... | collective-permute-start | bytes 786440 | tf_op jit(solution)/shard_map/ppermute | solution.py:280
  13.9 3.6 %collective-permute-start.3 = (f32[2,4,32,256]{3,2,1,0:T(8,128)S(1)}, f32[2,4,32,256]{3,2,1,0:T(8,128)S(1)}, u32[]{:S(2)}, u32[]{:S(2)}) collective-permute-start(f32[2,4,32,256]{3,2,1,0:T(8,128)S(1)} %get-tuple-element.35), channel_id=1, source_target_pairs={{0,384},{64,448},{128,0},{192,64},{256,128},{320,192},{384,256},{4... | collective-permute-start | bytes 786440 | tf_op jit(solution)/shard_map/ppermute | solution.py:280
  17.5 3.9 %collective-permute-start.4 = (f32[2,4,32,256]{3,2,1,0:T(8,128)S(1)}, f32[2,4,32,256]{3,2,1,0:T(8,128)}, u32[]{:S(2)}, u32[]{:S(2)}) collective-permute-start(f32[2,4,32,256]{3,2,1,0:T(8,128)S(1)} %get-tuple-element.34), channel_id=1, source_target_pairs={{0,256},{64,320},{128,384},{192,448},{256,0},{320,64},{384,128},{4... | collective-permute-start | bytes 786440 | tf_op jit(solution)/shard_map/ppermute | solution.py:280
  21.5 2.6 %shard_map.64 = f32[4,1024,128]{2,1,0:T(8,128)} custom-call(s32[2]{0:T(128)S(1)} %add_convert_fusion.where, bf16[1024,1024]{1,0:T(8,128)(2,1)S(1)} %bitcast.27), custom_call_target="tpu_custom_call" | custom-call | tf_op jit(solution)/shard_map/pallas_call | solution.py:81
  24.1 1.9 collective-permute-start
  29.3 0.7 fusion.12
  31.4 1.1 fusion.1
  32.6 2.7 %collective-permute-start.15 = (f32[2,32,256]{2,1,0:T(8,128)S(1)}, f32[2,32,256]{2,1,0:T(8,128)S(1)}, u32[]{:S(2)}, u32[]{:S(2)}) collective-permute-start(f32[2,32,256]{2,1,0:T(8,128)S(1)} %pad_maximum_fusion.5), channel_id=1, source_target_pairs={{0,16},{8,24},{16,0},{24,8},{32,48},{40,56},{48,32},{56,40},{1,17}... | collective-permute-start | bytes 196616 | tf_op jit(solution)/shard_map/ppermute | solution.py:225
  35.3 3.8 %collective-permute-start.5 = (f32[2,64,256]{2,1,0:T(8,128)S(1)}, f32[2,64,256]{2,1,0:T(8,128)S(1)}, u32[]{:S(2)}, u32[]{:S(2)}) collective-permute-start(f32[2,64,256]{2,1,0:T(8,128)S(1)} %constant_dynamic-slice_fusion.2), channel_id=1, source_target_pairs={{0,1},{1,0},{2,3},{3,2},{4,5},{5,4},{6,7},{7,6},{8,9},{9,8},{10,11... | collective-permute-start | bytes 393224 | tf_op jit(solution)/shard_map/ppermute | solution.py:225
  39.2 5.3 %collective-permute-start.16 = (f32[2,32,256]{2,1,0:T(8,128)S(1)}, f32[2,32,256]{2,1,0:T(8,128)S(1)}, u32[]{:S(2)}, u32[]{:S(2)}) collective-permute-start(f32[2,32,256]{2,1,0:T(8,128)S(1)} %pad_maximum_fusion.6), channel_id=1, source_target_pairs={{0,32},{8,40},{16,48},{24,56},{32,0},{40,8},{48,16},{56,24},{1,33}... | collective-permute-start | bytes 196616 | tf_op jit(solution)/shard_map/ppermute | solution.py:225
  44.6 3.7 %collective-permute-start.6 = (f32[2,32,256]{2,1,0:T(8,128)S(1)}, f32[2,32,256]{2,1,0:T(8,128)S(1)}, u32[]{:S(2)}, u32[]{:S(2)}) collective-permute-start(f32[2,32,256]{2,1,0:T(8,128)S(1)} %get-tuple-element.63), channel_id=1, source_target_pairs={{0,2},{1,3},{2,0},{3,1},{4,6},{5,7},{6,4},{7,5},{8,10},{9,11},{10,... | collective-permute-start | bytes 196616 | tf_op jit(solution)/shard_map/ppermute | solution.py:225
  48.3 9.8 %collective-permute-start.17 = (f32[2,32,256]{2,1,0:T(8,128)S(1)}, f32[2,32,256]{2,1,0:T(8,128)S(1)}, u32[]{:S(2)}, u32[]{:S(2)}) collective-permute-start(f32[2,32,256]{2,1,0:T(8,128)S(1)} %pad_maximum_fusion.7), channel_id=1, source_target_pairs={{0,15},{1,14},{2,13},{3,12},{4,11},{5,10},{6,9},{7,8},{8,7},{9,6},... | collective-permute-start | bytes 196616 | tf_op jit(solution)/shard_map/ppermute | solution.py:290
  58.1 3.1 %shard_map.65 = (f32[1024,128]{1,0:T(8,128)S(1)}, f32[1024,128]{1,0:T(8,128)S(1)}, f32[1024,128]{1,0:T(8,128)S(1)}, f32[1024,128]{1,0:T(8,128)S(1)}) custom-call(s32[2]{0:T(128)S(1)} %add_convert_fusion.where, bf16[1024,1024]{1,0:T(8,128)(2,1)S(1)} %bitcast.28, f32[4,1024,128]{2,1,0:T(8,128)} %collective-permute-done.other), custom_call_target="tpu_custom_call" | custom-call | tf_op jit(solution)/shard_map/pallas_call | solution.py:105
  61.2 2.6 %collective-permute-start.7 = (f32[1024,128]{1,0:T(8,128)S(1)}, f32[1024,128]{1,0:T(8,128)S(1)}, u32[]{:S(2)}, u32[]{:S(2)}) collective-permute-start(f32[1024,128]{1,0:T(8,128)S(1)} %get-tuple-element.20), channel_id=1, source_target_pairs={{0,128},{64,192},{128,256},{192,320},{256,384},{320,448},{384,0},{... | collective-permute-start | bytes 1572872 | tf_op jit(solution)/shard_map/ppermute | solution.py:284
  63.8 4.5 %collective-permute-start.8 = (f32[1024,128]{1,0:T(8,128)S(1)}, f32[1024,128]{1,0:T(8,128)S(1)}, u32[]{:S(2)}, u32[]{:S(2)}) collective-permute-start(f32[1024,128]{1,0:T(8,128)S(1)} %get-tuple-element.21), channel_id=1, source_target_pairs={{0,384},{64,448},{128,0},{192,64},{256,128},{320,192},{384,256},{4... | collective-permute-start | bytes 1572872 | tf_op jit(solution)/shard_map/ppermute | solution.py:284
  68.3 2.2 %collective-permute-start.9 = (f32[1024,128]{1,0:T(8,128)S(1)}, f32[1024,128]{1,0:T(8,128)S(1)}, u32[]{:S(2)}, u32[]{:S(2)}) collective-permute-start(f32[1024,128]{1,0:T(8,128)S(1)} %get-tuple-element.22), channel_id=1, source_target_pairs={{0,256},{64,320},{128,384},{192,448},{256,0},{320,64},{384,128},{4... | collective-permute-start | bytes 1572872 | tf_op jit(solution)/shard_map/ppermute | solution.py:284
  70.6 17.2 %collective-permute-done.7 = f32[1024,128]{1,0:T(8,128)S(1)} collective-permute-done((f32[1024,128]{1,0:T(8,128)S(1)}, f32[1024,128]{1,0:T(8,128)S(1)}, u32[]{:S(2)}, u32[]{:S(2)}) %collective-permute-start.7) | collective-permute-done | bytes 524320 | tf_op jit(solution)/shard_map/ppermute | solution.py:284
  87.9 1.2 collective-permute-done.8
  89.1 8.2 %collective-permute-start.18 = (f32[2,64,256]{2,1,0:T(8,128)S(1)}, f32[2,64,256]{2,1,0:T(8,128)S(1)}, u32[]{:S(2)}, u32[]{:S(2)}) collective-permute-start(f32[2,64,256]{2,1,0:T(8,128)S(1)} %maximum_maximum_fusion.2), channel_id=1, source_target_pairs={{0,4},{1,5},{2,6},{3,7},{4,0},{5,1},{6,2},{7,3},{8,12},{9,13},{10,... | collective-permute-start | bytes 393224 | tf_op jit(solution)/shard_map/ppermute | solution.py:225
  97.4 7.7 %collective-permute-done.18 = f32[2,64,256]{2,1,0:T(8,128)S(1)} collective-permute-done((f32[2,64,256]{2,1,0:T(8,128)S(1)}, f32[2,64,256]{2,1,0:T(8,128)S(1)}, u32[]{:S(2)}, u32[]{:S(2)}) %collective-permute-start.18) | collective-permute-done | bytes 131104 | tf_op jit(solution)/shard_map/ppermute | solution.py:225
  105.0 1.9 %collective-permute-start.19 = (f32[2,64,256]{2,1,0:T(8,128)S(1)}, f32[2,64,256]{2,1,0:T(8,128)S(1)}, u32[]{:S(2)}, u32[]{:S(2)}) collective-permute-start(f32[2,64,256]{2,1,0:T(8,128)S(1)} %maximum_maximum_fusion.3), channel_id=1, source_target_pairs={{0,2},{1,3},{2,0},{3,1},{4,6},{5,7},{6,4},{7,5},{8,10},{9,11},{10,... | collective-permute-start | bytes 393224 | tf_op jit(solution)/shard_map/ppermute | solution.py:225
  107.1 5.7 %collective-permute-done.19 = f32[2,64,256]{2,1,0:T(8,128)S(1)} collective-permute-done((f32[2,64,256]{2,1,0:T(8,128)S(1)}, f32[2,64,256]{2,1,0:T(8,128)S(1)}, u32[]{:S(2)}, u32[]{:S(2)}) %collective-permute-start.19) | collective-permute-done | bytes 131104 | tf_op jit(solution)/shard_map/ppermute | solution.py:225
  112.9 1.9 %collective-permute-start.20 = (f32[2,96,256]{2,1,0:T(8,128)S(1)}, f32[2,96,256]{2,1,0:T(8,128)S(1)}, u32[]{:S(2)}, u32[]{:S(2)}) collective-permute-start(f32[2,96,256]{2,1,0:T(8,128)S(1)} %maximum_maximum_fusion.1), channel_id=1, source_target_pairs={{0,1},{1,0},{2,3},{3,2},{4,5},{5,4},{6,7},{7,6},{8,9},{9,8},{10,11... | collective-permute-start | bytes 589832 | tf_op jit(solution)/shard_map/ppermute | solution.py:225
  114.9 3.5 %collective-permute-start.10 = (f32[2,128,128]{2,1,0:T(8,128)S(1)}, f32[2,128,128]{2,1,0:T(8,128)S(1)}, u32[]{:S(2)}, u32[]{:S(2)}) collective-permute-start(f32[2,128,128]{2,1,0:T(8,128)S(1)} %get-tuple-element.47), channel_id=1, source_target_pairs={{0,16},{8,24},{16,0},{24,8},{32,48},{40,56},{48,32},{56,40},{1,17}... | collective-permute-start | bytes 393224 | tf_op jit(solution)/shard_map/ppermute | solution.py:225
  118.4 2.1 %collective-permute-done.20 = f32[2,96,256]{2,1,0:T(8,128)S(1)} collective-permute-done((f32[2,96,256]{2,1,0:T(8,128)S(1)}, f32[2,96,256]{2,1,0:T(8,128)S(1)}, u32[]{:S(2)}, u32[]{:S(2)}) %collective-permute-start.20) | collective-permute-done | bytes 196640 | tf_op jit(solution)/shard_map/ppermute | solution.py:225
  120.6 6.9 %collective-permute-start.21 = (f32[2,160,256]{2,1,0:T(8,128)S(1)}, f32[2,160,256]{2,1,0:T(8,128)S(1)}, u32[]{:S(2)}, u32[]{:S(2)}) collective-permute-start(f32[2,160,256]{2,1,0:T(8,128)S(1)} %get-tuple-element.41), channel_id=1, source_target_pairs={{0,128},{64,192},{128,256},{192,320},{256,384},{320,448},{384,0},{... | collective-permute-start | bytes 983048 | tf_op jit(solution)/shard_map/ppermute | solution.py:315
  127.5 2.6 %collective-permute-start.22 = (f32[2,160,256]{2,1,0:T(8,128)S(1)}, f32[2,160,256]{2,1,0:T(8,128)S(1)}, u32[]{:S(2)}, u32[]{:S(2)}) collective-permute-start(f32[2,160,256]{2,1,0:T(8,128)S(1)} %get-tuple-element.41), channel_id=1, source_target_pairs={{0,256},{64,320},{128,384},{192,448},{256,0},{320,64},{384,128},{4... | collective-permute-start | bytes 983048 | tf_op jit(solution)/shard_map/ppermute | solution.py:315
  130.1 3.9 %collective-permute-start.23 = (f32[2,160,256]{2,1,0:T(8,128)S(1)}, f32[2,160,256]{2,1,0:T(8,128)S(1)}, u32[]{:S(2)}, u32[]{:S(2)}) collective-permute-start(f32[2,160,256]{2,1,0:T(8,128)S(1)} %get-tuple-element.41), channel_id=1, source_target_pairs={{0,384},{64,448},{128,0},{192,64},{256,128},{320,192},{384,256},{4... | collective-permute-start | bytes 983048 | tf_op jit(solution)/shard_map/ppermute | solution.py:315
  134.1 1.6 collective-permute-done.21
  135.7 4.6 %collective-permute-done.22 = f32[2,160,256]{2,1,0:T(8,128)S(1)} collective-permute-done((f32[2,160,256]{2,1,0:T(8,128)S(1)}, f32[2,160,256]{2,1,0:T(8,128)S(1)}, u32[]{:S(2)}, u32[]{:S(2)}) %collective-permute-start.22) | collective-permute-done | bytes 327712 | tf_op jit(solution)/shard_map/ppermute | solution.py:315
  140.2 2.7 %collective-permute-done.23 = f32[2,160,256]{2,1,0:T(8,128)S(1)} collective-permute-done((f32[2,160,256]{2,1,0:T(8,128)S(1)}, f32[2,160,256]{2,1,0:T(8,128)S(1)}, u32[]{:S(2)}, u32[]{:S(2)}) %collective-permute-start.23) | collective-permute-done | bytes 327712 | tf_op jit(solution)/shard_map/ppermute | solution.py:315
  143.1 2.1 %collective-permute-start.24 = (f32[4,2,160,256]{3,2,1,0:T(8,128)S(1)}, f32[4,2,160,256]{3,2,1,0:T(8,128)S(1)}, u32[]{:S(2)}, u32[]{:S(2)}) collective-permute-start(f32[4,2,160,256]{3,2,1,0:T(8,128)S(1)} %pad_maximum_fusion.ring), channel_id=1, source_target_pairs={{0,64},{64,0},{128,192},{192,128},{256,320},{320,256},{384,448},{4... | collective-permute-start | bytes 3932168 | tf_op jit(solution)/shard_map/ppermute | solution.py:225
  145.1 3.8 %collective-permute-start.11 = (f32[2,64,128]{2,1,0:T(8,128)S(1)}, f32[2,64,128]{2,1,0:T(8,128)S(1)}, u32[]{:S(2)}, u32[]{:S(2)}) collective-permute-start(f32[2,64,128]{2,1,0:T(8,128)S(1)} %get-tuple-element.59), channel_id=1, source_target_pairs={{0,32},{8,40},{16,48},{24,56},{32,0},{40,8},{48,16},{56,24},{1,33}... | collective-permute-start | bytes 196616 | tf_op jit(solution)/shard_map/ppermute | solution.py:225
  148.9 4.1 %collective-permute-done.11 = f32[2,64,128]{2,1,0:T(8,128)S(1)} collective-permute-done((f32[2,64,128]{2,1,0:T(8,128)S(1)}, f32[2,64,128]{2,1,0:T(8,128)S(1)}, u32[]{:S(2)}, u32[]{:S(2)}) %collective-permute-start.11) | collective-permute-done | bytes 65568 | tf_op jit(solution)/shard_map/ppermute | solution.py:225
  153.1 5.4 %collective-permute-start.12 = (f32[2,64,128]{2,1,0:T(8,128)S(1)}, f32[2,64,128]{2,1,0:T(8,128)S(1)}, u32[]{:S(2)}, u32[]{:S(2)}) collective-permute-start(f32[2,64,128]{2,1,0:T(8,128)S(1)} %pad_maximum_fusion.3), channel_id=1, source_target_pairs={{0,8},{8,0},{16,24},{24,16},{32,40},{40,32},{48,56},{56,48},{1,9},... | collective-permute-start | bytes 196616 | tf_op jit(solution)/shard_map/ppermute | solution.py:225
  158.5 12.0 %collective-permute-done.12 = f32[2,64,128]{2,1,0:T(8,128)S(1)} collective-permute-done((f32[2,64,128]{2,1,0:T(8,128)S(1)}, f32[2,64,128]{2,1,0:T(8,128)S(1)}, u32[]{:S(2)}, u32[]{:S(2)}) %collective-permute-start.12) | collective-permute-done | bytes 65568 | tf_op jit(solution)/shard_map/ppermute | solution.py:225
  170.6 3.6 %collective-permute-start.13 = (f32[2,64,128]{2,1,0:T(8,128)S(1)}, f32[2,64,128]{2,1,0:T(8,128)S(1)}, u32[]{:S(2)}, u32[]{:S(2)}) collective-permute-start(f32[2,64,128]{2,1,0:T(8,128)S(1)} %pad_maximum_fusion.4), channel_id=1, source_target_pairs={{0,32},{8,40},{16,48},{24,56},{32,0},{40,8},{48,16},{56,24},{1,33}... | collective-permute-start | bytes 196616 | tf_op jit(solution)/shard_map/ppermute | solution.py:225
  174.1 4.1 %collective-permute-done.13 = f32[2,64,128]{2,1,0:T(8,128)S(1)} collective-permute-done((f32[2,64,128]{2,1,0:T(8,128)S(1)}, f32[2,64,128]{2,1,0:T(8,128)S(1)}, u32[]{:S(2)}, u32[]{:S(2)}) %collective-permute-start.13) | collective-permute-done | bytes 65568 | tf_op jit(solution)/shard_map/ppermute | solution.py:225
  178.2 2.8 %collective-permute-start.14 = (f32[2,128,128]{2,1,0:T(8,128)S(1)}, f32[2,128,128]{2,1,0:T(8,128)S(1)}, u32[]{:S(2)}, u32[]{:S(2)}) collective-permute-start(f32[2,128,128]{2,1,0:T(8,128)S(1)} %maximum_select_fusion.2), channel_id=1, source_target_pairs={{0,16},{8,24},{16,0},{24,8},{32,48},{40,56},{48,32},{56,40},{1,17}... | collective-permute-start | bytes 393224 | tf_op jit(solution)/shard_map/ppermute | solution.py:225
  181.0 4.1 %collective-permute-done.14 = f32[2,128,128]{2,1,0:T(8,128)S(1)} collective-permute-done((f32[2,128,128]{2,1,0:T(8,128)S(1)}, f32[2,128,128]{2,1,0:T(8,128)S(1)}, u32[]{:S(2)}, u32[]{:S(2)}) %collective-permute-start.14) | collective-permute-done | bytes 131104 | tf_op jit(solution)/shard_map/ppermute | solution.py:225
  185.2 1.4 shard_map.67
  186.5 4.4 %shard_map.68 = bf16[1024,128]{1,0:T(8,128)(2,1)} custom-call(s32[32,32]{1,0:T(8,128)S(1)} %copy-done.4, s32[32]{0:T(128)S(1)} %copy-done.7, s32[32]{0:T(128)S(1)} %copy-done.6, f32[2,256,256]{2,1,0:T(8,128)S(1)} %copy-done.2, f32[2,256,256]{2,1,0:T(8,128)S(1)} %copy-done.3, f32[2,256,128]{2,1,0:T(8,128)S(1)} %maximum_select_fusion.rows, ...), custom_call_target="tpu_custom_call" | custom-call | tf_op jit(solution)/shard_map/pallas_call | solution.py:214
  (69 shorter events, 2.3 us)
Async XLA Ops:
  0.0 1.6 copy-start
  1.6 0.7 copy-start.5
  3.2 4.6 %collective-permute-start.1 = (f32[4,2,4,32,256]{4,3,2,1,0:T(8,128)S(1)}, f32[4,2,4,32,256]{4,3,2,1,0:T(8,128)S(1)}, u32[]{:S(2)}, u32[]{:S(2)}) collective-permute-start(f32[4,2,4,32,256]{4,3,2,1,0:T(8,128)S(1)} %get-tuple-element.19), channel_id=1, source_target_pairs={{0,64},{64,0},{128,192},{192,128},{256,320},{320,256},{384,448},{4... | collective-permute-start | bytes 3145736 | tf_op jit(solution)/shard_map/ppermute | solution.py:225
  7.7 1.0 copy-start.9
  8.7 12.8 %copy-start.1 = (bf16[1,1024,1024]{2,1,0:T(8,128)(2,1)S(1)}, bf16[1,1024,1024]{2,1,0:T(8,128)(2,1)}, u32[]{:S(2)}) copy-start(bf16[1,1024,1024]{2,1,0:T(8,128)(2,1)} %param.6) | copy-start | bytes 6291460
  10.4 11.0 %copy-start.8 = (f32[4,2,4,32,256]{4,3,2,1,0:T(8,128)}, f32[4,2,4,32,256]{4,3,2,1,0:T(8,128)S(1)}, u32[]{:S(2)}) copy-start(f32[4,2,4,32,256]{4,3,2,1,0:T(8,128)S(1)} %add.30) | copy-start | bytes 3145732
  10.4 20.9 %collective-permute-start.2 = (f32[2,4,32,256]{3,2,1,0:T(8,128)S(1)}, f32[2,4,32,256]{3,2,1,0:T(8,128)S(1)}, u32[]{:S(2)}, u32[]{:S(2)}) collective-permute-start(f32[2,4,32,256]{3,2,1,0:T(8,128)S(1)} %get-tuple-element.33), channel_id=1, source_target_pairs={{0,128},{64,192},{128,256},{192,320},{256,384},{320,448},{384,0},{... | collective-permute-start | bytes 786440 | tf_op jit(solution)/shard_map/ppermute | solution.py:280
  13.9 17.4 %collective-permute-start.3 = (f32[2,4,32,256]{3,2,1,0:T(8,128)S(1)}, f32[2,4,32,256]{3,2,1,0:T(8,128)S(1)}, u32[]{:S(2)}, u32[]{:S(2)}) collective-permute-start(f32[2,4,32,256]{3,2,1,0:T(8,128)S(1)} %get-tuple-element.35), channel_id=1, source_target_pairs={{0,384},{64,448},{128,0},{192,64},{256,128},{320,192},{384,256},{4... | collective-permute-start | bytes 786440 | tf_op jit(solution)/shard_map/ppermute | solution.py:280
  17.5 13.9 %collective-permute-start.4 = (f32[2,4,32,256]{3,2,1,0:T(8,128)S(1)}, f32[2,4,32,256]{3,2,1,0:T(8,128)}, u32[]{:S(2)}, u32[]{:S(2)}) collective-permute-start(f32[2,4,32,256]{3,2,1,0:T(8,128)S(1)} %get-tuple-element.34), channel_id=1, source_target_pairs={{0,256},{64,320},{128,384},{192,448},{256,0},{320,64},{384,128},{4... | collective-permute-start | bytes 786440 | tf_op jit(solution)/shard_map/ppermute | solution.py:280
  21.5 4.6 %copy-start.7 = (s32[32]{0:T(128)S(1)}, s32[32]{0:T(128)}, u32[]{:S(2)}) copy-start(s32[32]{0:T(128)} %row_map.1) | copy-start | bytes 388
  21.5 7.8 %copy-start.6 = (s32[32]{0:T(128)S(1)}, s32[32]{0:T(128)}, u32[]{:S(2)}) copy-start(s32[32]{0:T(128)} %col_map.5) | copy-start | bytes 388
  24.1 33.9 %collective-permute-start = (f32[4,1024,128]{2,1,0:T(8,128)}, f32[4,1024,128]{2,1,0:T(8,128)}, u32[]{:S(2)}, u32[]{:S(2)}) collective-permute-start(f32[4,1024,128]{2,1,0:T(8,128)} %shard_map.64), channel_id=1, source_target_pairs={{0,64},{64,0},{128,192},{192,128},{256,320},{320,256},{384,448},{4... | collective-permute-start | bytes 6291464 | tf_op jit(solution)/shard_map/ppermute | solution.py:225
  32.6 6.6 %collective-permute-start.15 = (f32[2,32,256]{2,1,0:T(8,128)S(1)}, f32[2,32,256]{2,1,0:T(8,128)S(1)}, u32[]{:S(2)}, u32[]{:S(2)}) collective-permute-start(f32[2,32,256]{2,1,0:T(8,128)S(1)} %pad_maximum_fusion.5), channel_id=1, source_target_pairs={{0,16},{8,24},{16,0},{24,8},{32,48},{40,56},{48,32},{56,40},{1,17}... | collective-permute-start | bytes 196616 | tf_op jit(solution)/shard_map/ppermute | solution.py:225
  35.3 9.2 %collective-permute-start.5 = (f32[2,64,256]{2,1,0:T(8,128)S(1)}, f32[2,64,256]{2,1,0:T(8,128)S(1)}, u32[]{:S(2)}, u32[]{:S(2)}) collective-permute-start(f32[2,64,256]{2,1,0:T(8,128)S(1)} %constant_dynamic-slice_fusion.2), channel_id=1, source_target_pairs={{0,1},{1,0},{2,3},{3,2},{4,5},{5,4},{6,7},{7,6},{8,9},{9,8},{10,11... | collective-permute-start | bytes 393224 | tf_op jit(solution)/shard_map/ppermute | solution.py:225
  39.2 9.1 %collective-permute-start.16 = (f32[2,32,256]{2,1,0:T(8,128)S(1)}, f32[2,32,256]{2,1,0:T(8,128)S(1)}, u32[]{:S(2)}, u32[]{:S(2)}) collective-permute-start(f32[2,32,256]{2,1,0:T(8,128)S(1)} %pad_maximum_fusion.6), channel_id=1, source_target_pairs={{0,32},{8,40},{16,48},{24,56},{32,0},{40,8},{48,16},{56,24},{1,33}... | collective-permute-start | bytes 196616 | tf_op jit(solution)/shard_map/ppermute | solution.py:225
  44.6 26.0 %collective-permute-start.6 = (f32[2,32,256]{2,1,0:T(8,128)S(1)}, f32[2,32,256]{2,1,0:T(8,128)S(1)}, u32[]{:S(2)}, u32[]{:S(2)}) collective-permute-start(f32[2,32,256]{2,1,0:T(8,128)S(1)} %get-tuple-element.63), channel_id=1, source_target_pairs={{0,2},{1,3},{2,0},{3,1},{4,6},{5,7},{6,4},{7,5},{8,10},{9,11},{10,... | collective-permute-start | bytes 196616 | tf_op jit(solution)/shard_map/ppermute | solution.py:225
  48.3 22.3 %collective-permute-start.17 = (f32[2,32,256]{2,1,0:T(8,128)S(1)}, f32[2,32,256]{2,1,0:T(8,128)S(1)}, u32[]{:S(2)}, u32[]{:S(2)}) collective-permute-start(f32[2,32,256]{2,1,0:T(8,128)S(1)} %pad_maximum_fusion.7), channel_id=1, source_target_pairs={{0,15},{1,14},{2,13},{3,12},{4,11},{5,10},{6,9},{7,8},{8,7},{9,6},... | collective-permute-start | bytes 196616 | tf_op jit(solution)/shard_map/ppermute | solution.py:290
  61.2 26.6 %collective-permute-start.7 = (f32[1024,128]{1,0:T(8,128)S(1)}, f32[1024,128]{1,0:T(8,128)S(1)}, u32[]{:S(2)}, u32[]{:S(2)}) collective-permute-start(f32[1024,128]{1,0:T(8,128)S(1)} %get-tuple-element.20), channel_id=1, source_target_pairs={{0,128},{64,192},{128,256},{192,320},{256,384},{320,448},{384,0},{... | collective-permute-start | bytes 1572872 | tf_op jit(solution)/shard_map/ppermute | solution.py:284
  63.8 25.3 %collective-permute-start.8 = (f32[1024,128]{1,0:T(8,128)S(1)}, f32[1024,128]{1,0:T(8,128)S(1)}, u32[]{:S(2)}, u32[]{:S(2)}) collective-permute-start(f32[1024,128]{1,0:T(8,128)S(1)} %get-tuple-element.21), channel_id=1, source_target_pairs={{0,384},{64,448},{128,0},{192,64},{256,128},{320,192},{384,256},{4... | collective-permute-start | bytes 1572872 | tf_op jit(solution)/shard_map/ppermute | solution.py:284
  68.3 20.8 %collective-permute-start.9 = (f32[1024,128]{1,0:T(8,128)S(1)}, f32[1024,128]{1,0:T(8,128)S(1)}, u32[]{:S(2)}, u32[]{:S(2)}) collective-permute-start(f32[1024,128]{1,0:T(8,128)S(1)} %get-tuple-element.22), channel_id=1, source_target_pairs={{0,256},{64,320},{128,384},{192,448},{256,0},{320,64},{384,128},{4... | collective-permute-start | bytes 1572872 | tf_op jit(solution)/shard_map/ppermute | solution.py:284
  89.1 15.9 %collective-permute-start.18 = (f32[2,64,256]{2,1,0:T(8,128)S(1)}, f32[2,64,256]{2,1,0:T(8,128)S(1)}, u32[]{:S(2)}, u32[]{:S(2)}) collective-permute-start(f32[2,64,256]{2,1,0:T(8,128)S(1)} %maximum_maximum_fusion.2), channel_id=1, source_target_pairs={{0,4},{1,5},{2,6},{3,7},{4,0},{5,1},{6,2},{7,3},{8,12},{9,13},{10,... | collective-permute-start | bytes 393224 | tf_op jit(solution)/shard_map/ppermute | solution.py:225
  105.0 7.8 %collective-permute-start.19 = (f32[2,64,256]{2,1,0:T(8,128)S(1)}, f32[2,64,256]{2,1,0:T(8,128)S(1)}, u32[]{:S(2)}, u32[]{:S(2)}) collective-permute-start(f32[2,64,256]{2,1,0:T(8,128)S(1)} %maximum_maximum_fusion.3), channel_id=1, source_target_pairs={{0,2},{1,3},{2,0},{3,1},{4,6},{5,7},{6,4},{7,5},{8,10},{9,11},{10,... | collective-permute-start | bytes 393224 | tf_op jit(solution)/shard_map/ppermute | solution.py:225
  112.9 7.6 %collective-permute-start.20 = (f32[2,96,256]{2,1,0:T(8,128)S(1)}, f32[2,96,256]{2,1,0:T(8,128)S(1)}, u32[]{:S(2)}, u32[]{:S(2)}) collective-permute-start(f32[2,96,256]{2,1,0:T(8,128)S(1)} %maximum_maximum_fusion.1), channel_id=1, source_target_pairs={{0,1},{1,0},{2,3},{3,2},{4,5},{5,4},{6,7},{7,6},{8,9},{9,8},{10,11... | collective-permute-start | bytes 589832 | tf_op jit(solution)/shard_map/ppermute | solution.py:225
  114.9 19.2 %collective-permute-start.10 = (f32[2,128,128]{2,1,0:T(8,128)S(1)}, f32[2,128,128]{2,1,0:T(8,128)S(1)}, u32[]{:S(2)}, u32[]{:S(2)}) collective-permute-start(f32[2,128,128]{2,1,0:T(8,128)S(1)} %get-tuple-element.47), channel_id=1, source_target_pairs={{0,16},{8,24},{16,0},{24,8},{32,48},{40,56},{48,32},{56,40},{1,17}... | collective-permute-start | bytes 393224 | tf_op jit(solution)/shard_map/ppermute | solution.py:225
  120.6 15.1 %collective-permute-start.21 = (f32[2,160,256]{2,1,0:T(8,128)S(1)}, f32[2,160,256]{2,1,0:T(8,128)S(1)}, u32[]{:S(2)}, u32[]{:S(2)}) collective-permute-start(f32[2,160,256]{2,1,0:T(8,128)S(1)} %get-tuple-element.41), channel_id=1, source_target_pairs={{0,128},{64,192},{128,256},{192,320},{256,384},{320,448},{384,0},{... | collective-permute-start | bytes 983048 | tf_op jit(solution)/shard_map/ppermute | solution.py:315
  127.5 12.7 %collective-permute-start.22 = (f32[2,160,256]{2,1,0:T(8,128)S(1)}, f32[2,160,256]{2,1,0:T(8,128)S(1)}, u32[]{:S(2)}, u32[]{:S(2)}) collective-permute-start(f32[2,160,256]{2,1,0:T(8,128)S(1)} %get-tuple-element.41), channel_id=1, source_target_pairs={{0,256},{64,320},{128,384},{192,448},{256,0},{320,64},{384,128},{4... | collective-permute-start | bytes 983048 | tf_op jit(solution)/shard_map/ppermute | solution.py:315
  130.1 12.8 %collective-permute-start.23 = (f32[2,160,256]{2,1,0:T(8,128)S(1)}, f32[2,160,256]{2,1,0:T(8,128)S(1)}, u32[]{:S(2)}, u32[]{:S(2)}) collective-permute-start(f32[2,160,256]{2,1,0:T(8,128)S(1)} %get-tuple-element.41), channel_id=1, source_target_pairs={{0,384},{64,448},{128,0},{192,64},{256,128},{320,192},{384,256},{4... | collective-permute-start | bytes 983048 | tf_op jit(solution)/shard_map/ppermute | solution.py:315
  143.0 42.1 %copy-start.2 = (f32[2,256,256]{2,1,0:T(8,128)S(1)}, f32[2,256,256]{2,1,0:T(8,128)}, u32[]{:S(2)}) copy-start(f32[2,256,256]{2,1,0:T(8,128)} %lower_inv.3) | copy-start | bytes 1572868
  143.0 42.1 %copy-start.3 = (f32[2,256,256]{2,1,0:T(8,128)S(1)}, f32[2,256,256]{2,1,0:T(8,128)}, u32[]{:S(2)}) copy-start(f32[2,256,256]{2,1,0:T(8,128)} %upper_inv.3) | copy-start | bytes 1572868
  143.0 42.1 %copy-start.4 = (s32[32,32]{1,0:T(8,128)S(1)}, s32[32,32]{1,0:T(8,128)}, u32[]{:S(2)}) copy-start(s32[32,32]{1,0:T(8,128)} %block_pattern.3) | copy-start | bytes 12292
  143.1 43.5 %collective-permute-start.24 = (f32[4,2,160,256]{3,2,1,0:T(8,128)S(1)}, f32[4,2,160,256]{3,2,1,0:T(8,128)S(1)}, u32[]{:S(2)}, u32[]{:S(2)}) collective-permute-start(f32[4,2,160,256]{3,2,1,0:T(8,128)S(1)} %pad_maximum_fusion.ring), channel_id=1, source_target_pairs={{0,64},{64,0},{128,192},{192,128},{256,320},{320,256},{384,448},{4... | collective-permute-start | bytes 3932168 | tf_op jit(solution)/shard_map/ppermute | solution.py:225
  145.1 7.9 %collective-permute-start.11 = (f32[2,64,128]{2,1,0:T(8,128)S(1)}, f32[2,64,128]{2,1,0:T(8,128)S(1)}, u32[]{:S(2)}, u32[]{:S(2)}) collective-permute-start(f32[2,64,128]{2,1,0:T(8,128)S(1)} %get-tuple-element.59), channel_id=1, source_target_pairs={{0,32},{8,40},{16,48},{24,56},{32,0},{40,8},{48,16},{56,24},{1,33}... | collective-permute-start | bytes 196616 | tf_op jit(solution)/shard_map/ppermute | solution.py:225
  153.1 17.5 %collective-permute-start.12 = (f32[2,64,128]{2,1,0:T(8,128)S(1)}, f32[2,64,128]{2,1,0:T(8,128)S(1)}, u32[]{:S(2)}, u32[]{:S(2)}) collective-permute-start(f32[2,64,128]{2,1,0:T(8,128)S(1)} %pad_maximum_fusion.3), channel_id=1, source_target_pairs={{0,8},{8,0},{16,24},{24,16},{32,40},{40,32},{48,56},{56,48},{1,9},... | collective-permute-start | bytes 196616 | tf_op jit(solution)/shard_map/ppermute | solution.py:225
  170.6 7.7 %collective-permute-start.13 = (f32[2,64,128]{2,1,0:T(8,128)S(1)}, f32[2,64,128]{2,1,0:T(8,128)S(1)}, u32[]{:S(2)}, u32[]{:S(2)}) collective-permute-start(f32[2,64,128]{2,1,0:T(8,128)S(1)} %pad_maximum_fusion.4), channel_id=1, source_target_pairs={{0,32},{8,40},{16,48},{24,56},{32,0},{40,8},{48,16},{56,24},{1,33}... | collective-permute-start | bytes 196616 | tf_op jit(solution)/shard_map/ppermute | solution.py:225
  178.2 6.9 %collective-permute-start.14 = (f32[2,128,128]{2,1,0:T(8,128)S(1)}, f32[2,128,128]{2,1,0:T(8,128)S(1)}, u32[]{:S(2)}, u32[]{:S(2)}) collective-permute-start(f32[2,128,128]{2,1,0:T(8,128)S(1)} %maximum_select_fusion.2), channel_id=1, source_target_pairs={{0,16},{8,24},{16,0},{24,8},{32,48},{40,56},{48,32},{56,40},{1,17}... | collective-permute-start | bytes 393224 | tf_op jit(solution)/shard_map/ppermute | solution.py:225

commit v3 on v2

--- a/solution.py
+++ b/solution.py
@@ -70,52 +70,6 @@
         ],
         compiler_params=PARAMS,
     )(col_map, local)
-
-
-def give_kernel(where, local, out):
-    out[0] = local[...].astype(jnp.float32)
-
-
-def cut_give(where, local, n_y, width):
-    rows = local.shape[0]
-    return pl.pallas_call(
-        give_kernel,
-        out_shape=jax.ShapeDtypeStruct((n_y, rows, width), jnp.float32),
-        grid_spec=pltpu.PrefetchScalarGridSpec(
-            num_scalar_prefetch=1,
-            grid=(n_y,),
-            in_specs=[pl.BlockSpec((rows, width), lambda i, w: (0, 2 * i + 1 - w[1]))],
-            out_specs=pl.BlockSpec((1, rows, width), lambda i, w: (i, 0, 0)),
-        ),
-        compiler_params=PARAMS,
-    )(where, local)
-
-
-def add_kernel(where, local, other, *outs):
-    for step in range(len(outs)):
-
-        @pl.when(pl.program_id(0) == step)
-        def _(out=outs[step]):
-            out[...] = local[...].astype(jnp.float32) + other[0]
-
-
-def add_cores(where, local, other, n_y, width):
-    rows = local.shape[0]
-    shape = jax.ShapeDtypeStruct((rows, width), jnp.float32)
-    return pl.pallas_call(
-        add_kernel,
-        out_shape=[shape] * n_y,
-        grid_spec=pltpu.PrefetchScalarGridSpec(
-            num_scalar_prefetch=1,
-            grid=(n_y,),
-            in_specs=[
-                pl.BlockSpec((rows, width), lambda i, w: (0, 2 * ((w[0] + i) & (n_y - 1)) + w[1])),
-                pl.BlockSpec((1, rows, width), lambda i, w: ((w[0] + i) & (n_y - 1), 0, 0)),
-            ],
-            out_specs=[pl.BlockSpec((rows, width), lambda i, w: (0, 0))] * n_y,
-        ),
-        compiler_params=PARAMS,
-    )(where, local, other)
 
 
 def mask_at(block_pattern, row, col):
@@ -267,8 +221,6 @@
     row_owner = [p >> shift for p in row_at]
     col_owner = [p >> shift for p in col_at]
     row_slot = [p & (slots - 1) for p in row_at]
-    where = jnp.stack([y, core]).astype(jnp.int32)
-
     def around(step):
         return [(2 * i + c, 2 * ((i + step) % n_y) + c) for i in range(n_y) for c in range(2)]
 
@@ -279,9 +231,7 @@
         chunk = pick(parts, (y + step) & (n_y - 1), 0)
         panel = panel + lax.ppermute(chunk, "gz", around(step))
 
-    other = swap(cut_give(where, local, n_y, width), "gz", n_gz, 1)
-    parts = add_cores(where, local, other, n_y, width)
-    arrived = [lax.ppermute(parts[step], "gz", around(step)) for step in (1, 3, 2)]
+    merged = lax.psum_scatter(local.astype(jnp.float32), "gz", scatter_dimension=1, tiled=True)
 
     corner = jnp.stack([pick(panel[k], row_slot[1 - k], 0) for k in range(2)])
     for bit in (2, 4):
@@ -297,34 +247,43 @@
         second = bit_of(col, bit)
         other = swap(part(data, 1, ~second), "col", n_col, bit)
         data = choose(part(data, 1, second), other, col, col_owner, bit)
-    data, arrived = lax.optimization_barrier((data, arrived))
-    merged = parts[0] + (arrived[0] + arrived[1] + arrived[2])
-    both = jnp.concatenate([data, corner], 1)
-    other = swap(both, "col", n_col, 4)
-    thick = data.shape[1]
-    data = choose(data, other[:, :thick], col, col_owner, 4)
-    corner = choose(corner, other[:, thick:], col, corner_owner, 4)
-    for bit in (2, 1):
-        second = bit_of(col, bit)
+    data, merged = lax.optimization_barrier((data, merged))
+    blocks = merged.reshape(slots, size, width)
+    rows = jnp.stack([pick(blocks, p, 0) for p in row_slot])
+
+    def narrow(rows, bit):
+        second = bit_of(row, bit)
+        other = swap(part(rows, 1, ~second), "row", n_row, bit)
+        return choose(part(rows, 1, second), other, row, row_owner, bit)
+
+    def widen(rows, bit):
+        return join(rows, swap(rows, "row", n_row, bit), 1, bit_of(row, bit))
+
+    def send_both(data, corner, bit):
+        other = swap(jnp.concatenate([data, corner], 1), "col", n_col, bit)
         thick = data.shape[1]
-        other = swap(jnp.concatenate([data, corner], 1), "col", n_col, bit)
-        data = join(data, other[:, :thick], 1, second)
         corner = choose(corner, other[:, thick:], col, corner_owner, bit)
+        return other[:, :thick], corner
+
+    other, corner = send_both(data, corner, 4)
+    data = choose(data, other, col, col_owner, 4)
+    rows = narrow(rows, 2)
+    other, corner = send_both(data, corner, 2)
+    data = join(data, other, 1, bit_of(col, 2))
+    data, rows = lax.optimization_barrier((data, rows))
+    rows = narrow(rows, 4)
+    other, corner = send_both(data, corner, 1)
+    data = join(data, other, 1, bit_of(col, 1))
 
     mine = jnp.concatenate([data, corner], 1)
+    mine, rows = lax.optimization_barrier((mine, rows))
+    rows = choose(rows, swap(rows, "row", n_row, 1), row, row_owner, 1)
+    rows = widen(rows, 4)
     ring = [mine] + [lax.ppermute(mine, "gz", around(step)) for step in (1, 2, 3)]
     ring = jnp.stack(ring)
+    ring, rows = lax.optimization_barrier((ring, rows))
     across = swap(ring, "gz", n_gz, 1)
-
-    blocks = merged.reshape(slots, size, width)
-    rows = jnp.stack([pick(blocks, p, 0) for p in row_slot])
-    for bit in (2, 4):
-        second = bit_of(row, bit)
-        other = swap(part(rows, 1, ~second), "row", n_row, bit)
-        rows = choose(part(rows, 1, second), other, row, row_owner, bit)
-    rows = choose(rows, swap(rows, "row", n_row, 1), row, row_owner, 1)
-    for bit in (4, 2):
-        rows = join(rows, swap(rows, "row", n_row, bit), 1, bit_of(row, bit))
+    rows = widen(rows, 2)
 
     up0, term0 = first_terms(n_y, block_pattern, col_map, lower_inv, upper_inv, rows)
     return last_terms(n_y, slots, block_pattern, row_map, col_map, lower_inv, upper_inv, rows,

time: 193 us -> 166 us (0.86)
  waiting for transfers between devices: 69.7 us -> 44.4 us
  between operations: 4.68 us -> 18 us
  starting transfers between devices: 95.8 us -> 83.1 us
  Pallas kernels: 12.5 us -> 7.7 us
  other arithmetic: 4.87 us -> 7.27 us
    ppermute x3 -> x0, waiting for transfers between devices: 18.5 us -> none  [shards(): lax.ppermute(parts[step], 'gz', around(step))]
    ppermute x15 -> x14, waiting for transfers between devices: 42.4 us -> 29.8 us  [swap(): return lax.ppermute(x, axis, [(i, i ^ bit) for i in range(size)])]
    ppermute x3 -> x0, starting transfers between devices: 9.3 us -> none  [shards(): lax.ppermute(parts[step], 'gz', around(step))]
    pallas_call x2 -> x0, Pallas kernels: 5.79 us -> none  [the longest x1 3.15 us: add_cores(): pl.pallas_call(add_kernel, out_shape=[shape] * n_y, grid_spec=pltpu.Prefe...]
    ppermute x3, waiting for transfers between devices: 0.01 us -> 5.64 us  [shards(): panel = panel + lax.ppermute(chunk, 'gz', around(step))]
    ppermute x1, waiting for transfers between devices: 0.01 us -> 4.29 us  [shards(): other = lax.ppermute(corner, ('row', 'col'), mirror)]
    ppermute x3, waiting for transfers between devices: 8.81 us -> 4.65 us  [shards(): lax.ppermute(mine, 'gz', around(step))]
    convert_element_type x1, other arithmetic: 0.08 us -> 4.03 us  [shards(): local.astype(jnp.float32)]
  transfers between devices with their start and end apart: 25 -> 22, of which waited for: 13 -> 12; matrix products, arithmetic and copies ran while one was open for 2% -> 3% of each run, Pallas kernels for 4% -> 2%
where the time goes in v3:
time: 166 us; the launch traced here: 163 us
  starting transfers between devices  83.1 us (50%)
  waiting for transfers between devices  44.4 us (27%)
  between operations  18 us (11%)
  Pallas kernels  7.7 us (5%)
  other arithmetic  7.27 us (4%)
  local copies, waits for them, and re-layouts  2.74 us (2%)
    ppermute x14, starting transfers between devices, swap(): return lax.ppermute(x, axis, [(i, i ^ bit) for i in range(size)])  50.4 us
    ppermute x14, waiting for transfers between devices, swap(): return lax.ppermute(x, axis, [(i, i ^ bit) for i in range(size)])  29.8 us
    ppermute x1, starting transfers between devices, shards(): other = lax.ppermute(corner, ('row', 'col'), mirror)  11 us
    ppermute x3, starting transfers between devices, shards(): panel = panel + lax.ppermute(chunk, 'gz', around(step))  10.9 us
    ppermute x3, starting transfers between devices, shards(): lax.ppermute(mine, 'gz', around(step))  10.8 us
    ppermute x3, waiting for transfers between devices, shards(): panel = panel + lax.ppermute(chunk, 'gz', around(step))  5.64 us
    ppermute x3, waiting for transfers between devices, shards(): lax.ppermute(mine, 'gz', around(step))  4.65 us
    pallas_call x1, Pallas kernels, last_terms(): pl.pallas_call(functools.partial(last_kernel, n_y), out_shape=jax.ShapeDt...  4.44 us
  transfers between devices with their start and end apart: 22, of which 12 were waited for; matrix products, arithmetic and copies ran while one was open for 3% of the time, Pallas kernels for 2%

profile of v3, /device:TPU:6, one launch (start us, length us, event | category | flops | bytes accessed | tf_op | source)
XLA Modules:
  0.0 163.2 jit_solution(11822476727048813753)
XLA Ops:
  6.5 4.0 %bitcast_convert_fusion = f32[1024,1024]{1,0:T(8,128)} fusion(bf16[1,1024,1024]{2,1,0:T(8,128)(2,1)} %param.6), kind=kLoop, calls=%fused_computation.74 | loop fusion | flops 1048576 | bytes 6291456 | tf_op jit(solution)/shard_map/convert_element_type | solution.py:234
  10.6 0.0 reduce-scatter.2.cloned.1.call-update
  10.6 1.6 copy-done
  12.2 1.9 %shard_map.64 = (f32[4,2,4,32,256]{4,3,2,1,0:T(8,128)S(1)}, f32[4,2,4,32,256]{4,3,2,1,0:T(8,128)}) custom-call(s32[32]{0:T(128)S(1)} %copy-done.5, bf16[1024,1024]{1,0:T(8,128)(2,1)S(1)} %bitcast.24), custom_call_target="tpu_custom_call" | custom-call | tf_op jit(solution)/shard_map/pallas_call | solution.py:62
  14.1 1.9 %collective-permute-start = (f32[4,2,4,32,256]{4,3,2,1,0:T(8,128)}, f32[4,2,4,32,256]{4,3,2,1,0:T(8,128)}, u32[]{:S(2)}, u32[]{:S(2)}) collective-permute-start(f32[4,2,4,32,256]{4,3,2,1,0:T(8,128)} %get-tuple-element.18), channel_id=1, source_target_pairs={{0,64},{64,0},{128,192},{192,128},{256,320},{320,256},{384,448},{4... | collective-permute-start | bytes 3145736 | tf_op jit(solution)/shard_map/ppermute | solution.py:179
  16.0 3.0 %collective-permute-done = f32[4,2,4,32,256]{4,3,2,1,0:T(8,128)} collective-permute-done((f32[4,2,4,32,256]{4,3,2,1,0:T(8,128)}, f32[4,2,4,32,256]{4,3,2,1,0:T(8,128)}, u32[]{:S(2)}, u32[]{:S(2)}) %collective-permute-start) | collective-permute-done | bytes 1048608 | tf_op jit(solution)/shard_map/ppermute | solution.py:179
  19.0 1.4 add.23
  20.3 0.0 copy-start.6
  20.4 0.1 dynamic-slice_bitcast_fusion.2
  20.4 5.1 %collective-permute-start.3 = (f32[2,4,32,256]{3,2,1,0:T(8,128)S(1)}, f32[2,4,32,256]{3,2,1,0:T(8,128)S(1)}, u32[]{:S(2)}, u32[]{:S(2)}) collective-permute-start(f32[2,4,32,256]{3,2,1,0:T(8,128)S(1)} %get-tuple-element.34), channel_id=1, source_target_pairs={{0,256},{64,320},{128,384},{192,448},{256,0},{320,64},{384,128},{4... | collective-permute-start | bytes 786440 | tf_op jit(solution)/shard_map/ppermute | solution.py:232
  25.5 3.0 %collective-permute-start.2 = (f32[2,4,32,256]{3,2,1,0:T(8,128)S(1)}, f32[2,4,32,256]{3,2,1,0:T(8,128)S(1)}, u32[]{:S(2)}, u32[]{:S(2)}) collective-permute-start(f32[2,4,32,256]{3,2,1,0:T(8,128)S(1)} %get-tuple-element.35), channel_id=1, source_target_pairs={{0,384},{64,448},{128,0},{192,64},{256,128},{320,192},{384,256},{4... | collective-permute-start | bytes 786440 | tf_op jit(solution)/shard_map/ppermute | solution.py:232
  28.5 2.9 %collective-permute-start.1 = (f32[2,4,32,256]{3,2,1,0:T(8,128)S(1)}, f32[2,4,32,256]{3,2,1,0:T(8,128)S(1)}, u32[]{:S(2)}, u32[]{:S(2)}) collective-permute-start(f32[2,4,32,256]{3,2,1,0:T(8,128)S(1)} %get-tuple-element.33), channel_id=1, source_target_pairs={{0,128},{64,192},{128,256},{192,320},{256,384},{320,448},{384,0},{... | collective-permute-start | bytes 786440 | tf_op jit(solution)/shard_map/ppermute | solution.py:232
  31.4 0.7 fusion.10
  34.7 0.7 fusion.9
  36.7 4.0 %collective-permute-done.2 = f32[2,4,32,256]{3,2,1,0:T(8,128)S(1)} collective-permute-done((f32[2,4,32,256]{3,2,1,0:T(8,128)S(1)}, f32[2,4,32,256]{3,2,1,0:T(8,128)S(1)}, u32[]{:S(2)}, u32[]{:S(2)}) %collective-permute-start.2) | collective-permute-done | bytes 262176 | tf_op jit(solution)/shard_map/ppermute | solution.py:232
  40.7 1.6 %collective-permute-done.1 = f32[2,4,32,256]{3,2,1,0:T(8,128)S(1)} collective-permute-done((f32[2,4,32,256]{3,2,1,0:T(8,128)S(1)}, f32[2,4,32,256]{3,2,1,0:T(8,128)S(1)}, u32[]{:S(2)}, u32[]{:S(2)}) %collective-permute-start.1) | collective-permute-done | bytes 262176 | tf_op jit(solution)/shard_map/ppermute | solution.py:232
  42.4 0.1 fusion.1
  42.5 2.7 %collective-permute-start.6 = (f32[2,32,256]{2,1,0:T(8,128)S(1)}, f32[2,32,256]{2,1,0:T(8,128)S(1)}, u32[]{:S(2)}, u32[]{:S(2)}) collective-permute-start(f32[2,32,256]{2,1,0:T(8,128)S(1)} %pad_maximum_fusion.4), channel_id=1, source_target_pairs={{0,16},{8,24},{16,0},{24,8},{32,48},{40,56},{48,32},{56,40},{1,17}... | collective-permute-start | bytes 196616 | tf_op jit(solution)/shard_map/ppermute | solution.py:179
  45.3 4.1 %collective-permute-start.4 = (f32[2,64,256]{2,1,0:T(8,128)S(1)}, f32[2,64,256]{2,1,0:T(8,128)S(1)}, u32[]{:S(2)}, u32[]{:S(2)}) collective-permute-start(f32[2,64,256]{2,1,0:T(8,128)S(1)} %constant_dynamic-slice_fusion.3), channel_id=1, source_target_pairs={{0,1},{1,0},{2,3},{3,2},{4,5},{5,4},{6,7},{7,6},{8,9},{9,8},{10,11... | collective-permute-start | bytes 393224 | tf_op jit(solution)/shard_map/ppermute | solution.py:179
  49.4 5.2 %collective-permute-start.7 = (f32[2,32,256]{2,1,0:T(8,128)S(1)}, f32[2,32,256]{2,1,0:T(8,128)S(1)}, u32[]{:S(2)}, u32[]{:S(2)}) collective-permute-start(f32[2,32,256]{2,1,0:T(8,128)S(1)} %pad_maximum_fusion.5), channel_id=1, source_target_pairs={{0,32},{8,40},{16,48},{24,56},{32,0},{40,8},{48,16},{56,24},{1,33}... | collective-permute-start | bytes 196616 | tf_op jit(solution)/shard_map/ppermute | solution.py:179
  54.7 3.2 %collective-permute-start.5 = (f32[2,32,256]{2,1,0:T(8,128)S(1)}, f32[2,32,256]{2,1,0:T(8,128)S(1)}, u32[]{:S(2)}, u32[]{:S(2)}) collective-permute-start(f32[2,32,256]{2,1,0:T(8,128)S(1)} %get-tuple-element.61), channel_id=1, source_target_pairs={{0,2},{1,3},{2,0},{3,1},{4,6},{5,7},{6,4},{7,5},{8,10},{9,11},{10,... | collective-permute-start | bytes 196616 | tf_op jit(solution)/shard_map/ppermute | solution.py:179
  57.9 11.0 %collective-permute-start.8 = (f32[2,32,256]{2,1,0:T(8,128)S(1)}, f32[2,32,256]{2,1,0:T(8,128)S(1)}, u32[]{:S(2)}, u32[]{:S(2)}) collective-permute-start(f32[2,32,256]{2,1,0:T(8,128)S(1)} %pad_maximum_fusion.6), channel_id=1, source_target_pairs={{0,15},{1,14},{2,13},{3,12},{4,11},{5,10},{6,9},{7,8},{8,7},{9,6},... | collective-permute-start | bytes 196616 | tf_op jit(solution)/shard_map/ppermute | solution.py:240
  68.9 4.3 %collective-permute-done.8 = f32[2,32,256]{2,1,0:T(8,128)S(1)} collective-permute-done((f32[2,32,256]{2,1,0:T(8,128)S(1)}, f32[2,32,256]{2,1,0:T(8,128)S(1)}, u32[]{:S(2)}, u32[]{:S(2)}) %collective-permute-start.8) | collective-permute-done | bytes 65568 | tf_op jit(solution)/shard_map/ppermute | solution.py:240
  73.2 0.0 reduce-scatter.2.cloned.1.call-done.merged
  73.3 6.0 %collective-permute-start.9 = (f32[2,64,256]{2,1,0:T(8,128)S(1)}, f32[2,64,256]{2,1,0:T(8,128)S(1)}, u32[]{:S(2)}, u32[]{:S(2)}) collective-permute-start(f32[2,64,256]{2,1,0:T(8,128)S(1)} %maximum_maximum_fusion.2), channel_id=1, source_target_pairs={{0,4},{1,5},{2,6},{3,7},{4,0},{5,1},{6,2},{7,3},{8,12},{9,13},{10,... | collective-permute-start | bytes 393224 | tf_op jit(solution)/shard_map/ppermute | solution.py:179
  79.3 1.0 constant_dynamic-slice_fusion.1
  80.3 3.1 %collective-permute-start.11 = (f32[2,128,128]{2,1,0:T(8,128)S(1)}, f32[2,128,128]{2,1,0:T(8,128)S(1)}, u32[]{:S(2)}, u32[]{:S(2)}) collective-permute-start(f32[2,128,128]{2,1,0:T(8,128)S(1)} %get-tuple-element.43), channel_id=1, source_target_pairs={{0,16},{8,24},{16,0},{24,8},{32,48},{40,56},{48,32},{56,40},{1,17}... | collective-permute-start | bytes 393224 | tf_op jit(solution)/shard_map/ppermute | solution.py:179
  83.4 5.6 %collective-permute-done.9 = f32[2,64,256]{2,1,0:T(8,128)S(1)} collective-permute-done((f32[2,64,256]{2,1,0:T(8,128)S(1)}, f32[2,64,256]{2,1,0:T(8,128)S(1)}, u32[]{:S(2)}, u32[]{:S(2)}) %collective-permute-start.9) | collective-permute-done | bytes 131104 | tf_op jit(solution)/shard_map/ppermute | solution.py:179
  89.0 1.9 %collective-permute-start.10 = (f32[2,64,256]{2,1,0:T(8,128)S(1)}, f32[2,64,256]{2,1,0:T(8,128)S(1)}, u32[]{:S(2)}, u32[]{:S(2)}) collective-permute-start(f32[2,64,256]{2,1,0:T(8,128)S(1)} %maximum_maximum_fusion.3), channel_id=1, source_target_pairs={{0,2},{1,3},{2,0},{3,1},{4,6},{5,7},{6,4},{7,5},{8,10},{9,11},{10,... | collective-permute-start | bytes 393224 | tf_op jit(solution)/shard_map/ppermute | solution.py:179
  91.0 6.7 %collective-permute-done.10 = f32[2,64,256]{2,1,0:T(8,128)S(1)} collective-permute-done((f32[2,64,256]{2,1,0:T(8,128)S(1)}, f32[2,64,256]{2,1,0:T(8,128)S(1)}, u32[]{:S(2)}, u32[]{:S(2)}) %collective-permute-start.10) | collective-permute-done | bytes 131104 | tf_op jit(solution)/shard_map/ppermute | solution.py:179
  97.8 3.6 %collective-permute-start.13 = (f32[2,64,128]{2,1,0:T(8,128)S(1)}, f32[2,64,128]{2,1,0:T(8,128)S(1)}, u32[]{:S(2)}, u32[]{:S(2)}) collective-permute-start(f32[2,64,128]{2,1,0:T(8,128)S(1)} %constant_dynamic-slice_fusion), channel_id=1, source_target_pairs={{0,32},{8,40},{16,48},{24,56},{32,0},{40,8},{48,16},{56,24},{1,33}... | collective-permute-start | bytes 196616 | tf_op jit(solution)/shard_map/ppermute | solution.py:179
  101.4 1.9 %collective-permute-start.12 = (f32[2,96,256]{2,1,0:T(8,128)S(1)}, f32[2,96,256]{2,1,0:T(8,128)S(1)}, u32[]{:S(2)}, u32[]{:S(2)}) collective-permute-start(f32[2,96,256]{2,1,0:T(8,128)S(1)} %maximum_maximum_fusion.1), channel_id=1, source_target_pairs={{0,1},{1,0},{2,3},{3,2},{4,5},{5,4},{6,7},{7,6},{8,9},{9,8},{10,11... | collective-permute-start | bytes 589832 | tf_op jit(solution)/shard_map/ppermute | solution.py:179
  103.3 2.1 %collective-permute-done.13 = f32[2,64,128]{2,1,0:T(8,128)S(1)} collective-permute-done((f32[2,64,128]{2,1,0:T(8,128)S(1)}, f32[2,64,128]{2,1,0:T(8,128)S(1)}, u32[]{:S(2)}, u32[]{:S(2)}) %collective-permute-start.13) | collective-permute-done | bytes 65568 | tf_op jit(solution)/shard_map/ppermute | solution.py:179
  105.5 3.9 %collective-permute-done.12 = f32[2,96,256]{2,1,0:T(8,128)S(1)} collective-permute-done((f32[2,96,256]{2,1,0:T(8,128)S(1)}, f32[2,96,256]{2,1,0:T(8,128)S(1)}, u32[]{:S(2)}, u32[]{:S(2)}) %collective-permute-start.12) | collective-permute-done | bytes 196640 | tf_op jit(solution)/shard_map/ppermute | solution.py:179
  109.4 7.8 %collective-permute-start.17 = (f32[2,64,128]{2,1,0:T(8,128)S(1)}, f32[2,64,128]{2,1,0:T(8,128)S(1)}, u32[]{:S(2)}, u32[]{:S(2)}) collective-permute-start(f32[2,64,128]{2,1,0:T(8,128)S(1)} %pad_maximum_fusion.7), channel_id=1, source_target_pairs={{0,8},{8,0},{16,24},{24,16},{32,40},{40,32},{48,56},{56,48},{1,9},... | collective-permute-start | bytes 196616 | tf_op jit(solution)/shard_map/ppermute | solution.py:179
  117.3 6.1 %collective-permute-start.16 = (f32[2,160,256]{2,1,0:T(8,128)S(1)}, f32[2,160,256]{2,1,0:T(8,128)S(1)}, u32[]{:S(2)}, u32[]{:S(2)}) collective-permute-start(f32[2,160,256]{2,1,0:T(8,128)S(1)} %maximum_maximum_fusion), channel_id=1, source_target_pairs={{0,384},{64,448},{128,0},{192,64},{256,128},{320,192},{384,256},{4... | collective-permute-start | bytes 983048 | tf_op jit(solution)/shard_map/ppermute | solution.py:282
  123.4 1.9 %collective-permute-start.15 = (f32[2,160,256]{2,1,0:T(8,128)S(1)}, f32[2,160,256]{2,1,0:T(8,128)S(1)}, u32[]{:S(2)}, u32[]{:S(2)}) collective-permute-start(f32[2,160,256]{2,1,0:T(8,128)S(1)} %maximum_maximum_fusion), channel_id=1, source_target_pairs={{0,256},{64,320},{128,384},{192,448},{256,0},{320,64},{384,128},{4... | collective-permute-start | bytes 983048 | tf_op jit(solution)/shard_map/ppermute | solution.py:282
  125.3 2.8 %collective-permute-start.14 = (f32[2,160,256]{2,1,0:T(8,128)S(1)}, f32[2,160,256]{2,1,0:T(8,128)S(1)}, u32[]{:S(2)}, u32[]{:S(2)}) collective-permute-start(f32[2,160,256]{2,1,0:T(8,128)S(1)} %maximum_maximum_fusion), channel_id=1, source_target_pairs={{0,128},{64,192},{128,256},{192,320},{256,384},{320,448},{384,0},{... | collective-permute-start | bytes 983048 | tf_op jit(solution)/shard_map/ppermute | solution.py:282
  128.1 4.0 %collective-permute-start.18 = (f32[2,64,128]{2,1,0:T(8,128)S(1)}, f32[2,64,128]{2,1,0:T(8,128)S(1)}, u32[]{:S(2)}, u32[]{:S(2)}) collective-permute-start(f32[2,64,128]{2,1,0:T(8,128)S(1)} %pad_maximum_fusion.8), channel_id=1, source_target_pairs={{0,32},{8,40},{16,48},{24,56},{32,0},{40,8},{48,16},{56,24},{1,33}... | collective-permute-start | bytes 196616 | tf_op jit(solution)/shard_map/ppermute | solution.py:179
  132.2 3.6 %collective-permute-done.18 = f32[2,64,128]{2,1,0:T(8,128)S(1)} collective-permute-done((f32[2,64,128]{2,1,0:T(8,128)S(1)}, f32[2,64,128]{2,1,0:T(8,128)S(1)}, u32[]{:S(2)}, u32[]{:S(2)}) %collective-permute-start.18) | collective-permute-done | bytes 65568 | tf_op jit(solution)/shard_map/ppermute | solution.py:179
  135.8 1.2 collective-permute-done.15
  137.1 3.4 %collective-permute-done.14 = f32[2,160,256]{2,1,0:T(8,128)S(1)} collective-permute-done((f32[2,160,256]{2,1,0:T(8,128)S(1)}, f32[2,160,256]{2,1,0:T(8,128)S(1)}, u32[]{:S(2)}, u32[]{:S(2)}) %collective-permute-start.14) | collective-permute-done | bytes 327712 | tf_op jit(solution)/shard_map/ppermute | solution.py:282
  140.5 0.1 pad_maximum_fusion.ring
  140.6 2.1 %collective-permute-start.20 = (f32[4,2,160,256]{3,2,1,0:T(8,128)S(1)}, f32[4,2,160,256]{3,2,1,0:T(8,128)S(1)}, u32[]{:S(2)}, u32[]{:S(2)}) collective-permute-start(f32[4,2,160,256]{3,2,1,0:T(8,128)S(1)} %pad_maximum_fusion.ring), channel_id=1, source_target_pairs={{0,64},{64,0},{128,192},{192,128},{256,320},{320,256},{384,448},{4... | collective-permute-start | bytes 3932168 | tf_op jit(solution)/shard_map/ppermute | solution.py:179
  142.6 2.9 %collective-permute-start.19 = (f32[2,128,128]{2,1,0:T(8,128)S(1)}, f32[2,128,128]{2,1,0:T(8,128)S(1)}, u32[]{:S(2)}, u32[]{:S(2)}) collective-permute-start(f32[2,128,128]{2,1,0:T(8,128)S(1)} %maximum_select_fusion.2), channel_id=1, source_target_pairs={{0,16},{8,24},{16,0},{24,8},{32,48},{40,56},{48,32},{56,40},{1,17}... | collective-permute-start | bytes 393224 | tf_op jit(solution)/shard_map/ppermute | solution.py:179
  145.5 4.9 %collective-permute-done.19 = f32[2,128,128]{2,1,0:T(8,128)S(1)} collective-permute-done((f32[2,128,128]{2,1,0:T(8,128)S(1)}, f32[2,128,128]{2,1,0:T(8,128)S(1)}, u32[]{:S(2)}, u32[]{:S(2)}) %collective-permute-start.19) | collective-permute-done | bytes 131104 | tf_op jit(solution)/shard_map/ppermute | solution.py:179
  150.5 1.4 shard_map.65
  151.9 4.4 %shard_map.66 = bf16[1024,128]{1,0:T(8,128)(2,1)} custom-call(s32[32,32]{1,0:T(8,128)S(1)} %copy-done.4, s32[32]{0:T(128)S(1)} %copy-done.6, s32[32]{0:T(128)S(1)} %copy-done.5, f32[2,256,256]{2,1,0:T(8,128)S(1)} %copy-done.1, f32[2,256,256]{2,1,0:T(8,128)S(1)} %copy-done.2, f32[2,256,128]{2,1,0:T(8,128)S(1)} %maximum_select_fusion.1.rows, ...), custom_call_target="tpu_custom_call" | custom-call | tf_op jit(solution)/shard_map/pallas_call | solution.py:168
  (56 shorter events, 0.5 us)
Async XLA Ops:
  6.5 66.7 %reduce-scatter.2.cloned.1.call-start = ((), (), s32[]{:S(2)}) async-start(), calls=%async_computation.1 | async-start | bytes 4718592 | tf_op jit(solution)/shard_map/reduce_scatter | solution.py:234
  10.6 1.6 copy-start
  10.6 1.6 copy-start.5
  14.1 4.9 %collective-permute-start = (f32[4,2,4,32,256]{4,3,2,1,0:T(8,128)}, f32[4,2,4,32,256]{4,3,2,1,0:T(8,128)}, u32[]{:S(2)}, u32[]{:S(2)}) collective-permute-start(f32[4,2,4,32,256]{4,3,2,1,0:T(8,128)} %get-tuple-element.18), channel_id=1, source_target_pairs={{0,64},{64,0},{128,192},{192,128},{256,320},{320,256},{384,448},{4... | collective-permute-start | bytes 3145736 | tf_op jit(solution)/shard_map/ppermute | solution.py:179
  20.3 11.1 %copy-start.6 = (s32[32]{0:T(128)S(1)}, s32[32]{0:T(128)}, u32[]{:S(2)}) copy-start(s32[32]{0:T(128)} %row_map.1) | copy-start | bytes 388
  20.4 16.3 %collective-permute-start.3 = (f32[2,4,32,256]{3,2,1,0:T(8,128)S(1)}, f32[2,4,32,256]{3,2,1,0:T(8,128)S(1)}, u32[]{:S(2)}, u32[]{:S(2)}) collective-permute-start(f32[2,4,32,256]{3,2,1,0:T(8,128)S(1)} %get-tuple-element.34), channel_id=1, source_target_pairs={{0,256},{64,320},{128,384},{192,448},{256,0},{320,64},{384,128},{4... | collective-permute-start | bytes 786440 | tf_op jit(solution)/shard_map/ppermute | solution.py:232
  25.5 15.2 %collective-permute-start.2 = (f32[2,4,32,256]{3,2,1,0:T(8,128)S(1)}, f32[2,4,32,256]{3,2,1,0:T(8,128)S(1)}, u32[]{:S(2)}, u32[]{:S(2)}) collective-permute-start(f32[2,4,32,256]{3,2,1,0:T(8,128)S(1)} %get-tuple-element.35), channel_id=1, source_target_pairs={{0,384},{64,448},{128,0},{192,64},{256,128},{320,192},{384,256},{4... | collective-permute-start | bytes 786440 | tf_op jit(solution)/shard_map/ppermute | solution.py:232
  28.5 13.9 %collective-permute-start.1 = (f32[2,4,32,256]{3,2,1,0:T(8,128)S(1)}, f32[2,4,32,256]{3,2,1,0:T(8,128)S(1)}, u32[]{:S(2)}, u32[]{:S(2)}) collective-permute-start(f32[2,4,32,256]{3,2,1,0:T(8,128)S(1)} %get-tuple-element.33), channel_id=1, source_target_pairs={{0,128},{64,192},{128,256},{192,320},{256,384},{320,448},{384,0},{... | collective-permute-start | bytes 786440 | tf_op jit(solution)/shard_map/ppermute | solution.py:232
  42.5 6.8 %collective-permute-start.6 = (f32[2,32,256]{2,1,0:T(8,128)S(1)}, f32[2,32,256]{2,1,0:T(8,128)S(1)}, u32[]{:S(2)}, u32[]{:S(2)}) collective-permute-start(f32[2,32,256]{2,1,0:T(8,128)S(1)} %pad_maximum_fusion.4), channel_id=1, source_target_pairs={{0,16},{8,24},{16,0},{24,8},{32,48},{40,56},{48,32},{56,40},{1,17}... | collective-permute-start | bytes 196616 | tf_op jit(solution)/shard_map/ppermute | solution.py:179
  45.3 9.4 %collective-permute-start.4 = (f32[2,64,256]{2,1,0:T(8,128)S(1)}, f32[2,64,256]{2,1,0:T(8,128)S(1)}, u32[]{:S(2)}, u32[]{:S(2)}) collective-permute-start(f32[2,64,256]{2,1,0:T(8,128)S(1)} %constant_dynamic-slice_fusion.3), channel_id=1, source_target_pairs={{0,1},{1,0},{2,3},{3,2},{4,5},{5,4},{6,7},{7,6},{8,9},{9,8},{10,11... | collective-permute-start | bytes 393224 | tf_op jit(solution)/shard_map/ppermute | solution.py:179
  49.4 8.5 %collective-permute-start.7 = (f32[2,32,256]{2,1,0:T(8,128)S(1)}, f32[2,32,256]{2,1,0:T(8,128)S(1)}, u32[]{:S(2)}, u32[]{:S(2)}) collective-permute-start(f32[2,32,256]{2,1,0:T(8,128)S(1)} %pad_maximum_fusion.5), channel_id=1, source_target_pairs={{0,32},{8,40},{16,48},{24,56},{32,0},{40,8},{48,16},{56,24},{1,33}... | collective-permute-start | bytes 196616 | tf_op jit(solution)/shard_map/ppermute | solution.py:179
  54.7 14.2 %collective-permute-start.5 = (f32[2,32,256]{2,1,0:T(8,128)S(1)}, f32[2,32,256]{2,1,0:T(8,128)S(1)}, u32[]{:S(2)}, u32[]{:S(2)}) collective-permute-start(f32[2,32,256]{2,1,0:T(8,128)S(1)} %get-tuple-element.61), channel_id=1, source_target_pairs={{0,2},{1,3},{2,0},{3,1},{4,6},{5,7},{6,4},{7,5},{8,10},{9,11},{10,... | collective-permute-start | bytes 196616 | tf_op jit(solution)/shard_map/ppermute | solution.py:179
  57.9 15.3 %collective-permute-start.8 = (f32[2,32,256]{2,1,0:T(8,128)S(1)}, f32[2,32,256]{2,1,0:T(8,128)S(1)}, u32[]{:S(2)}, u32[]{:S(2)}) collective-permute-start(f32[2,32,256]{2,1,0:T(8,128)S(1)} %pad_maximum_fusion.6), channel_id=1, source_target_pairs={{0,15},{1,14},{2,13},{3,12},{4,11},{5,10},{6,9},{7,8},{8,7},{9,6},... | collective-permute-start | bytes 196616 | tf_op jit(solution)/shard_map/ppermute | solution.py:240
  73.3 15.7 %collective-permute-start.9 = (f32[2,64,256]{2,1,0:T(8,128)S(1)}, f32[2,64,256]{2,1,0:T(8,128)S(1)}, u32[]{:S(2)}, u32[]{:S(2)}) collective-permute-start(f32[2,64,256]{2,1,0:T(8,128)S(1)} %maximum_maximum_fusion.2), channel_id=1, source_target_pairs={{0,4},{1,5},{2,6},{3,7},{4,0},{5,1},{6,2},{7,3},{8,12},{9,13},{10,... | collective-permute-start | bytes 393224 | tf_op jit(solution)/shard_map/ppermute | solution.py:179
  80.3 10.6 %collective-permute-start.11 = (f32[2,128,128]{2,1,0:T(8,128)S(1)}, f32[2,128,128]{2,1,0:T(8,128)S(1)}, u32[]{:S(2)}, u32[]{:S(2)}) collective-permute-start(f32[2,128,128]{2,1,0:T(8,128)S(1)} %get-tuple-element.43), channel_id=1, source_target_pairs={{0,16},{8,24},{16,0},{24,8},{32,48},{40,56},{48,32},{56,40},{1,17}... | collective-permute-start | bytes 393224 | tf_op jit(solution)/shard_map/ppermute | solution.py:179
  89.0 8.7 %collective-permute-start.10 = (f32[2,64,256]{2,1,0:T(8,128)S(1)}, f32[2,64,256]{2,1,0:T(8,128)S(1)}, u32[]{:S(2)}, u32[]{:S(2)}) collective-permute-start(f32[2,64,256]{2,1,0:T(8,128)S(1)} %maximum_maximum_fusion.3), channel_id=1, source_target_pairs={{0,2},{1,3},{2,0},{3,1},{4,6},{5,7},{6,4},{7,5},{8,10},{9,11},{10,... | collective-permute-start | bytes 393224 | tf_op jit(solution)/shard_map/ppermute | solution.py:179
  97.8 7.7 %collective-permute-start.13 = (f32[2,64,128]{2,1,0:T(8,128)S(1)}, f32[2,64,128]{2,1,0:T(8,128)S(1)}, u32[]{:S(2)}, u32[]{:S(2)}) collective-permute-start(f32[2,64,128]{2,1,0:T(8,128)S(1)} %constant_dynamic-slice_fusion), channel_id=1, source_target_pairs={{0,32},{8,40},{16,48},{24,56},{32,0},{40,8},{48,16},{56,24},{1,33}... | collective-permute-start | bytes 196616 | tf_op jit(solution)/shard_map/ppermute | solution.py:179
  101.4 7.9 %collective-permute-start.12 = (f32[2,96,256]{2,1,0:T(8,128)S(1)}, f32[2,96,256]{2,1,0:T(8,128)S(1)}, u32[]{:S(2)}, u32[]{:S(2)}) collective-permute-start(f32[2,96,256]{2,1,0:T(8,128)S(1)} %maximum_maximum_fusion.1), channel_id=1, source_target_pairs={{0,1},{1,0},{2,3},{3,2},{4,5},{5,4},{6,7},{7,6},{8,9},{9,8},{10,11... | collective-permute-start | bytes 589832 | tf_op jit(solution)/shard_map/ppermute | solution.py:179
  109.4 18.7 %collective-permute-start.17 = (f32[2,64,128]{2,1,0:T(8,128)S(1)}, f32[2,64,128]{2,1,0:T(8,128)S(1)}, u32[]{:S(2)}, u32[]{:S(2)}) collective-permute-start(f32[2,64,128]{2,1,0:T(8,128)S(1)} %pad_maximum_fusion.7), channel_id=1, source_target_pairs={{0,8},{8,0},{16,24},{24,16},{32,40},{40,32},{48,56},{56,48},{1,9},... | collective-permute-start | bytes 196616 | tf_op jit(solution)/shard_map/ppermute | solution.py:179
  117.3 18.6 %collective-permute-start.16 = (f32[2,160,256]{2,1,0:T(8,128)S(1)}, f32[2,160,256]{2,1,0:T(8,128)S(1)}, u32[]{:S(2)}, u32[]{:S(2)}) collective-permute-start(f32[2,160,256]{2,1,0:T(8,128)S(1)} %maximum_maximum_fusion), channel_id=1, source_target_pairs={{0,384},{64,448},{128,0},{192,64},{256,128},{320,192},{384,256},{4... | collective-permute-start | bytes 983048 | tf_op jit(solution)/shard_map/ppermute | solution.py:282
  123.4 13.7 %collective-permute-start.15 = (f32[2,160,256]{2,1,0:T(8,128)S(1)}, f32[2,160,256]{2,1,0:T(8,128)S(1)}, u32[]{:S(2)}, u32[]{:S(2)}) collective-permute-start(f32[2,160,256]{2,1,0:T(8,128)S(1)} %maximum_maximum_fusion), channel_id=1, source_target_pairs={{0,256},{64,320},{128,384},{192,448},{256,0},{320,64},{384,128},{4... | collective-permute-start | bytes 983048 | tf_op jit(solution)/shard_map/ppermute | solution.py:282
  125.3 15.2 %collective-permute-start.14 = (f32[2,160,256]{2,1,0:T(8,128)S(1)}, f32[2,160,256]{2,1,0:T(8,128)S(1)}, u32[]{:S(2)}, u32[]{:S(2)}) collective-permute-start(f32[2,160,256]{2,1,0:T(8,128)S(1)} %maximum_maximum_fusion), channel_id=1, source_target_pairs={{0,128},{64,192},{128,256},{192,320},{256,384},{320,448},{384,0},{... | collective-permute-start | bytes 983048 | tf_op jit(solution)/shard_map/ppermute | solution.py:282
  128.1 7.7 %collective-permute-start.18 = (f32[2,64,128]{2,1,0:T(8,128)S(1)}, f32[2,64,128]{2,1,0:T(8,128)S(1)}, u32[]{:S(2)}, u32[]{:S(2)}) collective-permute-start(f32[2,64,128]{2,1,0:T(8,128)S(1)} %pad_maximum_fusion.8), channel_id=1, source_target_pairs={{0,32},{8,40},{16,48},{24,56},{32,0},{40,8},{48,16},{56,24},{1,33}... | collective-permute-start | bytes 196616 | tf_op jit(solution)/shard_map/ppermute | solution.py:179
  140.5 10.0 %copy-start.1 = (f32[2,256,256]{2,1,0:T(8,128)S(1)}, f32[2,256,256]{2,1,0:T(8,128)}, u32[]{:S(2)}) copy-start(f32[2,256,256]{2,1,0:T(8,128)} %lower_inv.3) | copy-start | bytes 1572868
  140.5 10.0 %copy-start.2 = (f32[2,256,256]{2,1,0:T(8,128)S(1)}, f32[2,256,256]{2,1,0:T(8,128)}, u32[]{:S(2)}) copy-start(f32[2,256,256]{2,1,0:T(8,128)} %upper_inv.3) | copy-start | bytes 1572868
  140.5 10.0 %copy-start.4 = (s32[32,32]{1,0:T(8,128)S(1)}, s32[32,32]{1,0:T(8,128)}, u32[]{:S(2)}) copy-start(s32[32,32]{1,0:T(8,128)} %block_pattern.3) | copy-start | bytes 12292
  140.6 11.3 %copy-start.3 = (f32[1024,128]{1,0:T(8,128)S(1)}, f32[1024,128]{1,0:T(8,128)}, u32[]{:S(2)}) copy-start(f32[1024,128]{1,0:T(8,128)} %reduce-scatter.2.cloned.1.call-done.merged) | copy-start | bytes 1572868
  140.6 11.3 %collective-permute-start.20 = (f32[4,2,160,256]{3,2,1,0:T(8,128)S(1)}, f32[4,2,160,256]{3,2,1,0:T(8,128)S(1)}, u32[]{:S(2)}, u32[]{:S(2)}) collective-permute-start(f32[4,2,160,256]{3,2,1,0:T(8,128)S(1)} %pad_maximum_fusion.ring), channel_id=1, source_target_pairs={{0,64},{64,0},{128,192},{192,128},{256,320},{320,256},{384,448},{4... | collective-permute-start | bytes 3932168 | tf_op jit(solution)/shard_map/ppermute | solution.py:179
  142.6 7.8 %collective-permute-start.19 = (f32[2,128,128]{2,1,0:T(8,128)S(1)}, f32[2,128,128]{2,1,0:T(8,128)S(1)}, u32[]{:S(2)}, u32[]{:S(2)}) collective-permute-start(f32[2,128,128]{2,1,0:T(8,128)S(1)} %maximum_select_fusion.2), channel_id=1, source_target_pairs={{0,16},{8,24},{16,0},{24,8},{32,48},{40,56},{48,32},{56,40},{1,17}... | collective-permute-start | bytes 393224 | tf_op jit(solution)/shard_map/ppermute | solution.py:179
Sparse Core Ops, SparseCore 0:
  10.7 54.3 reduce-scatter.1

commit v4 on v3

--- a/solution.py
+++ b/solution.py
@@ -62,7 +62,7 @@
     return pl.pallas_call(
         panel_kernel,
         out_shape=[shape, shape],
-        in_specs=[SMEM, pl.BlockSpec(memory_space=pl.ANY)],
+        in_specs=[SMEM, pl.BlockSpec(memory_space=pltpu.HBM)],
         out_specs=[VMEM, VMEM],
         scratch_shapes=[
             pltpu.VMEM((2, local.shape[0], size), jnp.bfloat16),
@@ -100,23 +100,30 @@
 
 
 def last_kernel(n_y, block_pattern, row_map, col_map, lower_inv, upper_inv, rows, up0, term0,
-                ring, across, merged, out, high, low):
+                panels, ring, across, merged, out, high, low):
     slots = high.shape[1] - 1
     size, width = up0.shape
     thin = size // (2 * n_y)
     y = lax.axis_index("gz") >> 1
     core = lax.axis_index("gz") & 1
     col = column_of(col_map, n_y)
-    order = [slots] + list(range(slots))
-    for p in order:
-        for source, which in ((ring, core), (across, 1 - core)):
-            for step in range(n_y):
-                owner = 2 * ((y + n_y - step) & (n_y - 1)) + which
-                first = pl.multiple_of(owner * thin, thin)
-                for k in range(2):
-                    a, b = halves(source[step, k, p * thin : (p + 1) * thin, :])
-                    high[k, p, pl.ds(first, thin), :] = a
-                    low[k, p, pl.ds(first, thin), :] = b
+    for source, which in ((ring, core), (across, 1 - core)):
+        for step in range(n_y):
+            owner = 2 * ((y + n_y - step) & (n_y - 1)) + which
+            here = pl.ds(pl.multiple_of(owner * thin, thin), thin)
+            for k in range(2):
+                for half in range(2):
+                    lanes = slice(half * width, (half + 1) * width)
+                    a, b = halves(source[step, k, half * thin : (half + 1) * thin, :])
+                    high[k, slots, here, lanes] = a
+                    low[k, slots, here, lanes] = b
+    for p in range(slots):
+        for owner in range(2 * n_y):
+            here = slice(owner * thin, (owner + 1) * thin)
+            for k in range(2):
+                a, b = halves(panels[owner, k, p * thin : (p + 1) * thin, :])
+                high[k, p, here, :] = a
+                low[k, p, here, :] = b
 
     def stored(k, p):
         return high[k, p], low[k, p]
@@ -163,16 +170,17 @@
 
 
 def last_terms(n_y, slots, block_pattern, row_map, col_map, lower_inv, upper_inv, rows, up0, term0,
-               ring, across, merged):
+               panels, ring, across, merged):
     size = lower_inv.shape[-1]
     return pl.pallas_call(
         functools.partial(last_kernel, n_y),
         out_shape=jax.ShapeDtypeStruct(merged.shape, jnp.bfloat16),
-        in_specs=[SMEM] * 3 + [VMEM] * 8,
+        in_specs=[SMEM] * 3 + [VMEM] * 9,
         out_specs=VMEM,
         scratch_shapes=[pltpu.VMEM((2, slots + 1, size, size), jnp.bfloat16)] * 2,
         compiler_params=PARAMS,
-    )(block_pattern, row_map, col_map, lower_inv, upper_inv, rows, up0, term0, ring, across, merged)
+    )(block_pattern, row_map, col_map, lower_inv, upper_inv, rows, up0, term0, panels, ring, across,
+      merged)
 
 
 def swap(x, axis, size, bit):
@@ -225,69 +233,64 @@
         return [(2 * i + c, 2 * ((i + step) % n_y) + c) for i in range(n_y) for c in range(2)]
 
     keep, give = cut_panels(col_map, local, slots, n_y, thin, size)
+
+    give, local = lax.optimization_barrier((give, local))
+    merged = lax.psum_scatter(local.astype(jnp.float32), "gz", scatter_dimension=1, tiled=True)
     parts = keep + swap(give, "gz", n_gz, 1)
     panel = pick(parts, y, 0)
     for step in (1, 3, 2):
         chunk = pick(parts, (y + step) & (n_y - 1), 0)
         panel = panel + lax.ppermute(chunk, "gz", around(step))
 
-    merged = lax.psum_scatter(local.astype(jnp.float32), "gz", scatter_dimension=1, tiled=True)
-
     corner = jnp.stack([pick(panel[k], row_slot[1 - k], 0) for k in range(2)])
-    for bit in (2, 4):
-        corner = choose(corner, swap(corner, "row", n_row, bit), row, row_owner[::-1], bit)
-    mirror = [(r * n_col + c, (r ^ 1) * n_col + c ^ (n_col - 1)) for r in range(n_row) for c in range(n_col)]
-    other = lax.ppermute(corner, ("row", "col"), mirror)
-    same = [bit_of(row, 1) == bit_of(r, 1) for r in row_owner[::-1]]
-    corner = jnp.stack([jnp.where(same[k], corner[k], other[k]) for k in range(2)])
-    corner_owner = [jnp.where(same[k], col_owner[k], col_owner[k] ^ (n_col - 1)) for k in range(2)]
-
     data = panel.reshape(2, slots * thin, size)
-    for bit in (1, 2):
-        second = bit_of(col, bit)
-        other = swap(part(data, 1, ~second), "col", n_col, bit)
-        data = choose(part(data, 1, second), other, col, col_owner, bit)
-    data, merged = lax.optimization_barrier((data, merged))
+
+    def send_both(data, extra, axis, length, bit):
+        other = swap(jnp.concatenate([data, extra], 1), axis, length, bit)
+        return other[:, : data.shape[1]], other[:, data.shape[1] :]
+
+    for bit in (1, 2, 4):
+        mine = data
+        if bit < 4:
+            second = bit_of(col, bit)
+            mine, data = part(data, 1, second), part(data, 1, ~second)
+        other, extra = send_both(data, corner, "col", n_col, bit)
+        data = choose(mine, other, col, col_owner, bit)
+        corner = choose(corner, extra, col, col_owner, bit)
+
     blocks = merged.reshape(slots, size, width)
     rows = jnp.stack([pick(blocks, p, 0) for p in row_slot])
-
-    def narrow(rows, bit):
+    corner_rows = row_owner[::-1]
+    corner = jnp.concatenate([corner[..., :width], corner[..., width:]], 1)
+
+    def narrow(rows, corner, bit):
         second = bit_of(row, bit)
-        other = swap(part(rows, 1, ~second), "row", n_row, bit)
-        return choose(part(rows, 1, second), other, row, row_owner, bit)
-
-    def widen(rows, bit):
-        return join(rows, swap(rows, "row", n_row, bit), 1, bit_of(row, bit))
-
-    def send_both(data, corner, bit):
-        other = swap(jnp.concatenate([data, corner], 1), "col", n_col, bit)
-        thick = data.shape[1]
-        corner = choose(corner, other[:, thick:], col, corner_owner, bit)
-        return other[:, :thick], corner
-
-    other, corner = send_both(data, corner, 4)
-    data = choose(data, other, col, col_owner, 4)
-    rows = narrow(rows, 2)
-    other, corner = send_both(data, corner, 2)
-    data = join(data, other, 1, bit_of(col, 2))
+        other, extra = send_both(part(rows, 1, ~second), corner, "row", n_row, bit)
+        rows = choose(part(rows, 1, second), other, row, row_owner, bit)
+        return rows, choose(corner, extra, row, corner_rows, bit)
+
+    def widen(x, axis, length, me, bit):
+        return join(x, swap(x, axis, length, bit), 1, bit_of(me, bit))
+
+    rows, corner = narrow(rows, corner, 2)
+    data = widen(data, "col", n_col, col, 2)
     data, rows = lax.optimization_barrier((data, rows))
-    rows = narrow(rows, 4)
-    other, corner = send_both(data, corner, 1)
-    data = join(data, other, 1, bit_of(col, 1))
-
-    mine = jnp.concatenate([data, corner], 1)
-    mine, rows = lax.optimization_barrier((mine, rows))
-    rows = choose(rows, swap(rows, "row", n_row, 1), row, row_owner, 1)
-    rows = widen(rows, 4)
-    ring = [mine] + [lax.ppermute(mine, "gz", around(step)) for step in (1, 2, 3)]
-    ring = jnp.stack(ring)
-    ring, rows = lax.optimization_barrier((ring, rows))
+    rows, corner = narrow(rows, corner, 4)
+    data = widen(data, "col", n_col, col, 1)
+    data, rows = lax.optimization_barrier((data, rows))
+    panels = lax.all_gather(data, "gz", axis=0)
+
+    other, extra = send_both(rows, corner, "row", n_row, 1)
+    rows = choose(rows, other, row, row_owner, 1)
+    corner = choose(corner, extra, row, corner_rows, 1)
+    ring = jnp.stack([corner] + [lax.ppermute(corner, "gz", around(step)) for step in (1, 2, 3)])
+    rows = widen(rows, "row", n_row, row, 4)
     across = swap(ring, "gz", n_gz, 1)
-    rows = widen(rows, 2)
+    rows = widen(rows, "row", n_row, row, 2)
 
     up0, term0 = first_terms(n_y, block_pattern, col_map, lower_inv, upper_inv, rows)
     return last_terms(n_y, slots, block_pattern, row_map, col_map, lower_inv, upper_inv, rows,
-                      up0, term0, ring, across, merged)
+                      up0, term0, panels, ring, across, merged)
 
 
 def solution(mesh):

time: 166 us -> 158 us (0.952)
  starting transfers between devices: 83.1 us -> 70.9 us
  waiting for transfers between devices: 44.4 us -> 51.1 us
  local copies, waits for them, and re-layouts: 2.74 us -> 5 us
  other arithmetic: 7.27 us -> 5.23 us
    ppermute x14 -> x12, waiting for transfers between devices: 29.8 us -> 44 us  [swap(): return lax.ppermute(x, axis, [(i, i ^ bit) for i in range(size)])]
    ppermute x4 -> x3, starting transfers between devices: 21.8 us -> 11.5 us  [shards(): lax.ppermute(corner, 'gz', around(step))]
    ppermute x4 -> x3, waiting for transfers between devices: 8.93 us -> 1.83 us  [shards(): lax.ppermute(corner, 'gz', around(step))]
    unnamed x14 -> x18, local copies, waits for them, and re-layouts: 1.59 us -> 3.86 us
    ppermute x14 -> x12, starting transfers between devices: 50.4 us -> 48.4 us  [swap(): return lax.ppermute(x, axis, [(i, i ^ bit) for i in range(size)])]
  transfers between devices with their start and end apart: 22 -> 20, of which waited for: 12 -> 13; matrix products, arithmetic and copies ran while one was open for 3% -> 1% of each run, Pallas kernels for 2% -> 1%
where the time goes in v4:
time: 158 us; the launch traced here: 157 us
  starting transfers between devices  70.9 us (45%)
  waiting for transfers between devices  51.1 us (32%)
  between operations  18 us (11%)
  Pallas kernels  6.55 us (4%)
  other arithmetic  5.23 us (3%)
  local copies, waits for them, and re-layouts  5 us (3%)
    ppermute x12, starting transfers between devices, swap(): return lax.ppermute(x, axis, [(i, i ^ bit) for i in range(size)])  48.4 us
    ppermute x12, waiting for transfers between devices, swap(): return lax.ppermute(x, axis, [(i, i ^ bit) for i in range(size)])  44 us
    ppermute x3, starting transfers between devices, shards(): lax.ppermute(corner, 'gz', around(step))  11.5 us
    ppermute x3, starting transfers between devices, shards(): panel = panel + lax.ppermute(chunk, 'gz', around(step))  10.9 us
    ppermute x3, waiting for transfers between devices, shards(): panel = panel + lax.ppermute(chunk, 'gz', around(step))  5.27 us
    pallas_call x1, Pallas kernels, last_terms(): pl.pallas_call(functools.partial(last_kernel, n_y), out_shape=jax.ShapeDt...  4.29 us
    unnamed x18, local copies, waits for them, and re-layouts  3.86 us
  transfers between devices with their start and end apart: 20, of which 13 were waited for; matrix products, arithmetic and copies ran while one was open for 1% of the time, Pallas kernels for 1%

profile of v4, /device:TPU:6, one launch (start us, length us, event | category | flops | bytes accessed | tf_op | source)
XLA Modules:
  0.0 156.8 jit_solution(8240123792459564062)
XLA Ops:
  6.5 1.6 %copy-done = bf16[1,1024,1024]{2,1,0:T(8,128)(2,1)S(1)} copy-done((bf16[1,1024,1024]{2,1,0:T(8,128)(2,1)S(1)}, bf16[1,1024,1024]{2,1,0:T(8,128)(2,1)}, u32[]{:S(2)}) %copy-start) | copy-done | bytes 2097176
  8.1 0.7 copy-done.6
  8.8 0.9 shard_map.64
  9.7 2.4 %convert_element_type.28 = f32[1024,1024]{1,0:T(8,128)} convert(bf16[1024,1024]{1,0:T(8,128)(2,1)S(1)} %bitcast.26) | non-fusion elementwise | flops 1048576 | bytes 6291456 | tf_op jit(solution)/shard_map/convert_element_type | solution.py:238
  12.2 0.0 all-gather.3.cloned.1.call-start
  12.2 1.9 %collective-permute-start = (f32[4,2,4,32,256]{4,3,2,1,0:T(8,128)S(1)}, f32[4,2,4,32,256]{4,3,2,1,0:T(8,128)S(1)}, u32[]{:S(2)}, u32[]{:S(2)}) collective-permute-start(f32[4,2,4,32,256]{4,3,2,1,0:T(8,128)S(1)} %get-tuple-element.17), channel_id=1, source_target_pairs={{0,64},{64,0},{128,192},{192,128},{256,320},{320,256},{384,448},{4... | collective-permute-start | bytes 3145736 | tf_op jit(solution)/shard_map/ppermute | solution.py:187
  14.2 2.6 %collective-permute-done = f32[4,2,4,32,256]{4,3,2,1,0:T(8,128)S(1)} collective-permute-done((f32[4,2,4,32,256]{4,3,2,1,0:T(8,128)S(1)}, f32[4,2,4,32,256]{4,3,2,1,0:T(8,128)S(1)}, u32[]{:S(2)}, u32[]{:S(2)}) %collective-permute-start) | collective-permute-done | bytes 1048608 | tf_op jit(solution)/shard_map/ppermute | solution.py:187
  16.8 0.2 add.23
  17.0 0.1 dynamic-slice_bitcast_fusion.2
  17.1 3.5 %collective-permute-start.1 = (f32[2,4,32,256]{3,2,1,0:T(8,128)S(1)}, f32[2,4,32,256]{3,2,1,0:T(8,128)S(1)}, u32[]{:S(2)}, u32[]{:S(2)}) collective-permute-start(f32[2,4,32,256]{3,2,1,0:T(8,128)S(1)} %get-tuple-element.29), channel_id=1, source_target_pairs={{0,128},{64,192},{128,256},{192,320},{256,384},{320,448},{384,0},{... | collective-permute-start | bytes 786440 | tf_op jit(solution)/shard_map/ppermute | solution.py:243
  20.5 3.6 %collective-permute-start.2 = (f32[2,4,32,256]{3,2,1,0:T(8,128)S(1)}, f32[2,4,32,256]{3,2,1,0:T(8,128)S(1)}, u32[]{:S(2)}, u32[]{:S(2)}) collective-permute-start(f32[2,4,32,256]{3,2,1,0:T(8,128)S(1)} %get-tuple-element.31), channel_id=1, source_target_pairs={{0,384},{64,448},{128,0},{192,64},{256,128},{320,192},{384,256},{4... | collective-permute-start | bytes 786440 | tf_op jit(solution)/shard_map/ppermute | solution.py:243
  24.1 3.9 %collective-permute-start.3 = (f32[2,4,32,256]{3,2,1,0:T(8,128)S(1)}, f32[2,4,32,256]{3,2,1,0:T(8,128)S(1)}, u32[]{:S(2)}, u32[]{:S(2)}) collective-permute-start(f32[2,4,32,256]{3,2,1,0:T(8,128)S(1)} %get-tuple-element.30), channel_id=1, source_target_pairs={{0,256},{64,320},{128,384},{192,448},{256,0},{320,64},{384,128},{4... | collective-permute-start | bytes 786440 | tf_op jit(solution)/shard_map/ppermute | solution.py:243
  28.0 0.7 fusion.11
  30.1 1.5 collective-permute-done.2
  31.6 3.7 %collective-permute-done.3 = f32[2,4,32,256]{3,2,1,0:T(8,128)S(1)} collective-permute-done((f32[2,4,32,256]{3,2,1,0:T(8,128)S(1)}, f32[2,4,32,256]{3,2,1,0:T(8,128)S(1)}, u32[]{:S(2)}, u32[]{:S(2)}) %collective-permute-start.3) | collective-permute-done | bytes 262176 | tf_op jit(solution)/shard_map/ppermute | solution.py:243
  35.4 0.1 fusion.1
  35.6 3.8 %collective-permute-start.4 = (f32[2,96,256]{2,1,0:T(8,128)S(1)}, f32[2,96,256]{2,1,0:T(8,128)S(1)}, u32[]{:S(2)}, u32[]{:S(2)}) collective-permute-start(f32[2,96,256]{2,1,0:T(8,128)S(1)} %maximum_maximum_fusion), channel_id=1, source_target_pairs={{0,1},{1,0},{2,3},{3,2},{4,5},{5,4},{6,7},{7,6},{8,9},{9,8},{10,11... | collective-permute-start | bytes 589832 | tf_op jit(solution)/shard_map/ppermute | solution.py:187
  39.4 0.7 fusion.10
  41.4 1.8 %collective-permute-done.4 = f32[2,96,256]{2,1,0:T(8,128)S(1)} collective-permute-done((f32[2,96,256]{2,1,0:T(8,128)S(1)}, f32[2,96,256]{2,1,0:T(8,128)S(1)}, u32[]{:S(2)}, u32[]{:S(2)}) %collective-permute-start.4) | collective-permute-done | bytes 196640 | tf_op jit(solution)/shard_map/ppermute | solution.py:187
  43.3 5.2 %collective-permute-start.5 = (f32[2,64,256]{2,1,0:T(8,128)S(1)}, f32[2,64,256]{2,1,0:T(8,128)S(1)}, u32[]{:S(2)}, u32[]{:S(2)}) collective-permute-start(f32[2,64,256]{2,1,0:T(8,128)S(1)} %maximum_maximum_fusion.1), channel_id=1, source_target_pairs={{0,2},{1,3},{2,0},{3,1},{4,6},{5,7},{6,4},{7,5},{8,10},{9,11},{10,... | collective-permute-start | bytes 393224 | tf_op jit(solution)/shard_map/ppermute | solution.py:187
  48.5 4.5 %collective-permute-done.5 = f32[2,64,256]{2,1,0:T(8,128)S(1)} collective-permute-done((f32[2,64,256]{2,1,0:T(8,128)S(1)}, f32[2,64,256]{2,1,0:T(8,128)S(1)}, u32[]{:S(2)}, u32[]{:S(2)}) %collective-permute-start.5) | collective-permute-done | bytes 131104 | tf_op jit(solution)/shard_map/ppermute | solution.py:187
  53.1 8.7 %collective-permute-start.6 = (f32[2,64,256]{2,1,0:T(8,128)S(1)}, f32[2,64,256]{2,1,0:T(8,128)S(1)}, u32[]{:S(2)}, u32[]{:S(2)}) collective-permute-start(f32[2,64,256]{2,1,0:T(8,128)S(1)} %maximum_maximum_fusion.2), channel_id=1, source_target_pairs={{0,4},{1,5},{2,6},{3,7},{4,0},{5,1},{6,2},{7,3},{8,12},{9,13},{10,... | collective-permute-start | bytes 393224 | tf_op jit(solution)/shard_map/ppermute | solution.py:187
  61.8 9.5 %collective-permute-done.6 = f32[2,64,256]{2,1,0:T(8,128)S(1)} collective-permute-done((f32[2,64,256]{2,1,0:T(8,128)S(1)}, f32[2,64,256]{2,1,0:T(8,128)S(1)}, u32[]{:S(2)}, u32[]{:S(2)}) %collective-permute-start.6) | collective-permute-done | bytes 131104 | tf_op jit(solution)/shard_map/ppermute | solution.py:187
  71.3 0.0 reduce-scatter.2.cloned.1.call-done.merged
  71.3 1.0 constant_dynamic-slice_fusion.1
  72.4 2.7 %collective-permute-start.8 = (f32[2,192,128]{2,1,0:T(8,128)S(1)}, f32[2,192,128]{2,1,0:T(8,128)S(1)}, u32[]{:S(2)}, u32[]{:S(2)}) collective-permute-start(f32[2,192,128]{2,1,0:T(8,128)S(1)} %pad_maximum_fusion.1), channel_id=1, source_target_pairs={{0,16},{8,24},{16,0},{24,8},{32,48},{40,56},{48,32},{56,40},{1,17}... | collective-permute-start | bytes 589832 | tf_op jit(solution)/shard_map/ppermute | solution.py:187
  75.1 1.9 %collective-permute-start.7 = (f32[2,32,256]{2,1,0:T(8,128)S(1)}, f32[2,32,256]{2,1,0:T(8,128)S(1)}, u32[]{:S(2)}, u32[]{:S(2)}) collective-permute-start(f32[2,32,256]{2,1,0:T(8,128)S(1)} %pad_maximum_fusion.3), channel_id=1, source_target_pairs={{0,2},{1,3},{2,0},{3,1},{4,6},{5,7},{6,4},{7,5},{8,10},{9,11},{10,... | collective-permute-start | bytes 196616 | tf_op jit(solution)/shard_map/ppermute | solution.py:187
  78.4 3.8 %collective-permute-done.7 = f32[2,32,256]{2,1,0:T(8,128)S(1)} collective-permute-done((f32[2,32,256]{2,1,0:T(8,128)S(1)}, f32[2,32,256]{2,1,0:T(8,128)S(1)}, u32[]{:S(2)}, u32[]{:S(2)}) %collective-permute-start.7) | collective-permute-done | bytes 65568 | tf_op jit(solution)/shard_map/ppermute | solution.py:187
  82.4 6.1 %collective-permute-start.10 = (f32[2,128,128]{2,1,0:T(8,128)S(1)}, f32[2,128,128]{2,1,0:T(8,128)S(1)}, u32[]{:S(2)}, u32[]{:S(2)}) collective-permute-start(f32[2,128,128]{2,1,0:T(8,128)S(1)} %maximum_maximum_fusion.3), channel_id=1, source_target_pairs={{0,32},{8,40},{16,48},{24,56},{32,0},{40,8},{48,16},{56,24},{1,33}... | collective-permute-start | bytes 393224 | tf_op jit(solution)/shard_map/ppermute | solution.py:187
  88.5 1.9 %collective-permute-start.9 = (f32[2,64,256]{2,1,0:T(8,128)S(1)}, f32[2,64,256]{2,1,0:T(8,128)S(1)}, u32[]{:S(2)}, u32[]{:S(2)}) collective-permute-start(f32[2,64,256]{2,1,0:T(8,128)S(1)} %maximum_select_fusion.2), channel_id=1, source_target_pairs={{0,1},{1,0},{2,3},{3,2},{4,5},{5,4},{6,7},{7,6},{8,9},{9,8},{10,11... | collective-permute-start | bytes 393224 | tf_op jit(solution)/shard_map/ppermute | solution.py:187
  90.4 1.0 collective-permute-done.10
  91.4 3.9 %collective-permute-done.9 = f32[2,64,256]{2,1,0:T(8,128)S(1)} collective-permute-done((f32[2,64,256]{2,1,0:T(8,128)S(1)}, f32[2,64,256]{2,1,0:T(8,128)S(1)}, u32[]{:S(2)}, u32[]{:S(2)}) %collective-permute-start.9) | collective-permute-done | bytes 131104 | tf_op jit(solution)/shard_map/ppermute | solution.py:187
  95.3 0.7 maximum_select_fusion
  96.1 10.4 %collective-permute-start.11 = (f32[2,128,128]{2,1,0:T(8,128)S(1)}, f32[2,128,128]{2,1,0:T(8,128)S(1)}, u32[]{:S(2)}, u32[]{:S(2)}) collective-permute-start(f32[2,128,128]{2,1,0:T(8,128)S(1)} %maximum_maximum_fusion.4), channel_id=1, source_target_pairs={{0,8},{8,0},{16,24},{24,16},{32,40},{40,32},{48,56},{56,48},{1,9},... | collective-permute-start | bytes 393224 | tf_op jit(solution)/shard_map/ppermute | solution.py:187
  106.5 10.0 %collective-permute-done.11 = f32[2,128,128]{2,1,0:T(8,128)S(1)} collective-permute-done((f32[2,128,128]{2,1,0:T(8,128)S(1)}, f32[2,128,128]{2,1,0:T(8,128)S(1)}, u32[]{:S(2)}, u32[]{:S(2)}) %collective-permute-start.11) | collective-permute-done | bytes 131104 | tf_op jit(solution)/shard_map/ppermute | solution.py:187
  116.6 5.0 %collective-permute-start.14 = (f32[2,64,128]{2,1,0:T(8,128)S(1)}, f32[2,64,128]{2,1,0:T(8,128)S(1)}, u32[]{:S(2)}, u32[]{:S(2)}) collective-permute-start(f32[2,64,128]{2,1,0:T(8,128)S(1)} %get-tuple-element.67), channel_id=1, source_target_pairs={{0,128},{64,192},{128,256},{192,320},{256,384},{320,448},{384,0},{... | collective-permute-start | bytes 196616 | tf_op jit(solution)/shard_map/ppermute | solution.py:286
  121.5 4.1 %collective-permute-start.15 = (f32[2,64,128]{2,1,0:T(8,128)S(1)}, f32[2,64,128]{2,1,0:T(8,128)S(1)}, u32[]{:S(2)}, u32[]{:S(2)}) collective-permute-start(f32[2,64,128]{2,1,0:T(8,128)S(1)} %get-tuple-element.67), channel_id=1, source_target_pairs={{0,256},{64,320},{128,384},{192,448},{256,0},{320,64},{384,128},{4... | collective-permute-start | bytes 196616 | tf_op jit(solution)/shard_map/ppermute | solution.py:286
  125.7 2.4 %collective-permute-start.16 = (f32[2,64,128]{2,1,0:T(8,128)S(1)}, f32[2,64,128]{2,1,0:T(8,128)S(1)}, u32[]{:S(2)}, u32[]{:S(2)}) collective-permute-start(f32[2,64,128]{2,1,0:T(8,128)S(1)} %get-tuple-element.67), channel_id=1, source_target_pairs={{0,384},{64,448},{128,0},{192,64},{256,128},{320,192},{384,256},{4... | collective-permute-start | bytes 196616 | tf_op jit(solution)/shard_map/ppermute | solution.py:286
  128.1 1.9 %collective-permute-start.12 = (f32[2,64,128]{2,1,0:T(8,128)S(1)}, f32[2,64,128]{2,1,0:T(8,128)S(1)}, u32[]{:S(2)}, u32[]{:S(2)}) collective-permute-start(f32[2,64,128]{2,1,0:T(8,128)S(1)} %pad_maximum_fusion.5), channel_id=1, source_target_pairs={{0,32},{8,40},{16,48},{24,56},{32,0},{40,8},{48,16},{56,24},{1,33}... | collective-permute-start | bytes 196616 | tf_op jit(solution)/shard_map/ppermute | solution.py:187
  130.0 1.8 %collective-permute-done.16 = f32[2,64,128]{2,1,0:T(8,128)S(1)} collective-permute-done((f32[2,64,128]{2,1,0:T(8,128)S(1)}, f32[2,64,128]{2,1,0:T(8,128)S(1)}, u32[]{:S(2)}, u32[]{:S(2)}) %collective-permute-start.16) | collective-permute-done | bytes 65568 | tf_op jit(solution)/shard_map/ppermute | solution.py:286
  131.9 1.9 %collective-permute-start.17 = (f32[4,2,64,128]{3,2,1,0:T(8,128)S(1)}, f32[4,2,64,128]{3,2,1,0:T(8,128)S(1)}, u32[]{:S(2)}, u32[]{:S(2)}) collective-permute-start(f32[4,2,64,128]{3,2,1,0:T(8,128)S(1)} %pad_maximum_fusion.ring), channel_id=1, source_target_pairs={{0,64},{64,0},{128,192},{192,128},{256,320},{320,256},{384,448},{4... | collective-permute-start | bytes 786440 | tf_op jit(solution)/shard_map/ppermute | solution.py:187
  133.8 1.9 %collective-permute-done.12 = f32[2,64,128]{2,1,0:T(8,128)S(1)} collective-permute-done((f32[2,64,128]{2,1,0:T(8,128)S(1)}, f32[2,64,128]{2,1,0:T(8,128)S(1)}, u32[]{:S(2)}, u32[]{:S(2)}) %collective-permute-start.12) | collective-permute-done | bytes 65568 | tf_op jit(solution)/shard_map/ppermute | solution.py:187
  135.7 1.9 %collective-permute-start.13 = (f32[2,128,128]{2,1,0:T(8,128)S(1)}, f32[2,128,128]{2,1,0:T(8,128)S(1)}, u32[]{:S(2)}, u32[]{:S(2)}) collective-permute-start(f32[2,128,128]{2,1,0:T(8,128)S(1)} %maximum_select_fusion.3), channel_id=1, source_target_pairs={{0,16},{8,24},{16,0},{24,8},{32,48},{40,56},{48,32},{56,40},{1,17}... | collective-permute-start | bytes 393224 | tf_op jit(solution)/shard_map/ppermute | solution.py:187
  137.7 4.9 %collective-permute-done.13 = f32[2,128,128]{2,1,0:T(8,128)S(1)} collective-permute-done((f32[2,128,128]{2,1,0:T(8,128)S(1)}, f32[2,128,128]{2,1,0:T(8,128)S(1)}, u32[]{:S(2)}, u32[]{:S(2)}) %collective-permute-start.13) | collective-permute-done | bytes 131104 | tf_op jit(solution)/shard_map/ppermute | solution.py:187
  142.7 1.4 shard_map.65
  144.0 0.0 all-gather.3.cloned.1.call-done
  144.1 1.6 %copy-done.1 = f32[16,128,256]{2,1,0:T(8,128)S(1)} copy-done((f32[16,128,256]{2,1,0:T(8,128)S(1)}, f32[16,128,256]{2,1,0:T(8,128)}, u32[]{:S(2)}) %copy-start.1) | copy-done | bytes 2097176
  145.7 4.3 %shard_map.66 = bf16[1024,128]{1,0:T(8,128)(2,1)} custom-call(s32[32,32]{1,0:T(8,128)S(1)} %copy-done.5, s32[32]{0:T(128)S(1)} %copy-done.8, s32[32]{0:T(128)S(1)} %copy-done.7, f32[2,256,256]{2,1,0:T(8,128)S(1)} %copy-done.2, f32[2,256,256]{2,1,0:T(8,128)S(1)} %copy-done.3, f32[2,256,128]{2,1,0:T(8,128)S(1)} %maximum_select_fusion.1.rows, ...), custom_call_target="tpu_custom_call" | custom-call | tf_op jit(solution)/shard_map/pallas_call | solution.py:175
  (53 shorter events, 0.5 us)
Async XLA Ops:
  6.5 64.8 %reduce-scatter.2.cloned.1.call-start = ((), (), s32[]{:S(2)}) async-start(), calls=%async_computation.1 | async-start | bytes 4718592 | tf_op jit(solution)/shard_map/reduce_scatter | solution.py:238
  6.5 1.6 %copy-start = (bf16[1,1024,1024]{2,1,0:T(8,128)(2,1)S(1)}, bf16[1,1024,1024]{2,1,0:T(8,128)(2,1)}, u32[]{:S(2)}) copy-start(bf16[1,1024,1024]{2,1,0:T(8,128)(2,1)} %param.6) | copy-start | bytes 6291460
  8.1 0.7 copy-start.6
  12.2 131.9 %all-gather.3.cloned.1.call-start = ((), (), s32[]{:S(2)}) async-start(), calls=%async_computation.2 | async-start | bytes 2359296 | tf_op jit(solution)/shard_map/all_gather | solution.py:281
  12.2 4.6 %collective-permute-start = (f32[4,2,4,32,256]{4,3,2,1,0:T(8,128)S(1)}, f32[4,2,4,32,256]{4,3,2,1,0:T(8,128)S(1)}, u32[]{:S(2)}, u32[]{:S(2)}) collective-permute-start(f32[4,2,4,32,256]{4,3,2,1,0:T(8,128)S(1)} %get-tuple-element.17), channel_id=1, source_target_pairs={{0,64},{64,0},{128,192},{192,128},{256,320},{320,256},{384,448},{4... | collective-permute-start | bytes 3145736 | tf_op jit(solution)/shard_map/ppermute | solution.py:187
  16.8 11.3 %copy-start.8 = (s32[32]{0:T(128)S(1)}, s32[32]{0:T(128)}, u32[]{:S(2)}) copy-start(s32[32]{0:T(128)} %row_map.1) | copy-start | bytes 388
  17.0 22.4 %copy-start.7 = (s32[32]{0:T(128)S(1)}, s32[32]{0:T(128)}, u32[]{:S(2)}) copy-start(s32[32]{0:T(128)} %col_map.5) | copy-start | bytes 388
  17.1 13.0 %collective-permute-start.1 = (f32[2,4,32,256]{3,2,1,0:T(8,128)S(1)}, f32[2,4,32,256]{3,2,1,0:T(8,128)S(1)}, u32[]{:S(2)}, u32[]{:S(2)}) collective-permute-start(f32[2,4,32,256]{3,2,1,0:T(8,128)S(1)} %get-tuple-element.29), channel_id=1, source_target_pairs={{0,128},{64,192},{128,256},{192,320},{256,384},{320,448},{384,0},{... | collective-permute-start | bytes 786440 | tf_op jit(solution)/shard_map/ppermute | solution.py:243
  20.5 11.1 %collective-permute-start.2 = (f32[2,4,32,256]{3,2,1,0:T(8,128)S(1)}, f32[2,4,32,256]{3,2,1,0:T(8,128)S(1)}, u32[]{:S(2)}, u32[]{:S(2)}) collective-permute-start(f32[2,4,32,256]{3,2,1,0:T(8,128)S(1)} %get-tuple-element.31), channel_id=1, source_target_pairs={{0,384},{64,448},{128,0},{192,64},{256,128},{320,192},{384,256},{4... | collective-permute-start | bytes 786440 | tf_op jit(solution)/shard_map/ppermute | solution.py:243
  24.1 11.3 %collective-permute-start.3 = (f32[2,4,32,256]{3,2,1,0:T(8,128)S(1)}, f32[2,4,32,256]{3,2,1,0:T(8,128)S(1)}, u32[]{:S(2)}, u32[]{:S(2)}) collective-permute-start(f32[2,4,32,256]{3,2,1,0:T(8,128)S(1)} %get-tuple-element.30), channel_id=1, source_target_pairs={{0,256},{64,320},{128,384},{192,448},{256,0},{320,64},{384,128},{4... | collective-permute-start | bytes 786440 | tf_op jit(solution)/shard_map/ppermute | solution.py:243
  35.6 7.6 %collective-permute-start.4 = (f32[2,96,256]{2,1,0:T(8,128)S(1)}, f32[2,96,256]{2,1,0:T(8,128)S(1)}, u32[]{:S(2)}, u32[]{:S(2)}) collective-permute-start(f32[2,96,256]{2,1,0:T(8,128)S(1)} %maximum_maximum_fusion), channel_id=1, source_target_pairs={{0,1},{1,0},{2,3},{3,2},{4,5},{5,4},{6,7},{7,6},{8,9},{9,8},{10,11... | collective-permute-start | bytes 589832 | tf_op jit(solution)/shard_map/ppermute | solution.py:187
  43.3 9.8 %collective-permute-start.5 = (f32[2,64,256]{2,1,0:T(8,128)S(1)}, f32[2,64,256]{2,1,0:T(8,128)S(1)}, u32[]{:S(2)}, u32[]{:S(2)}) collective-permute-start(f32[2,64,256]{2,1,0:T(8,128)S(1)} %maximum_maximum_fusion.1), channel_id=1, source_target_pairs={{0,2},{1,3},{2,0},{3,1},{4,6},{5,7},{6,4},{7,5},{8,10},{9,11},{10,... | collective-permute-start | bytes 393224 | tf_op jit(solution)/shard_map/ppermute | solution.py:187
  53.1 18.2 %collective-permute-start.6 = (f32[2,64,256]{2,1,0:T(8,128)S(1)}, f32[2,64,256]{2,1,0:T(8,128)S(1)}, u32[]{:S(2)}, u32[]{:S(2)}) collective-permute-start(f32[2,64,256]{2,1,0:T(8,128)S(1)} %maximum_maximum_fusion.2), channel_id=1, source_target_pairs={{0,4},{1,5},{2,6},{3,7},{4,0},{5,1},{6,2},{7,3},{8,12},{9,13},{10,... | collective-permute-start | bytes 393224 | tf_op jit(solution)/shard_map/ppermute | solution.py:187
  72.4 9.8 %collective-permute-start.8 = (f32[2,192,128]{2,1,0:T(8,128)S(1)}, f32[2,192,128]{2,1,0:T(8,128)S(1)}, u32[]{:S(2)}, u32[]{:S(2)}) collective-permute-start(f32[2,192,128]{2,1,0:T(8,128)S(1)} %pad_maximum_fusion.1), channel_id=1, source_target_pairs={{0,16},{8,24},{16,0},{24,8},{32,48},{40,56},{48,32},{56,40},{1,17}... | collective-permute-start | bytes 589832 | tf_op jit(solution)/shard_map/ppermute | solution.py:187
  75.1 7.1 %collective-permute-start.7 = (f32[2,32,256]{2,1,0:T(8,128)S(1)}, f32[2,32,256]{2,1,0:T(8,128)S(1)}, u32[]{:S(2)}, u32[]{:S(2)}) collective-permute-start(f32[2,32,256]{2,1,0:T(8,128)S(1)} %pad_maximum_fusion.3), channel_id=1, source_target_pairs={{0,2},{1,3},{2,0},{3,1},{4,6},{5,7},{6,4},{7,5},{8,10},{9,11},{10,... | collective-permute-start | bytes 196616 | tf_op jit(solution)/shard_map/ppermute | solution.py:187
  82.3 60.3 %copy-start.2 = (f32[2,256,256]{2,1,0:T(8,128)S(1)}, f32[2,256,256]{2,1,0:T(8,128)}, u32[]{:S(2)}) copy-start(f32[2,256,256]{2,1,0:T(8,128)} %lower_inv.3) | copy-start | bytes 1572868
  82.3 60.3 %copy-start.3 = (f32[2,256,256]{2,1,0:T(8,128)S(1)}, f32[2,256,256]{2,1,0:T(8,128)}, u32[]{:S(2)}) copy-start(f32[2,256,256]{2,1,0:T(8,128)} %upper_inv.3) | copy-start | bytes 1572868
  82.3 60.3 %copy-start.5 = (s32[32,32]{1,0:T(8,128)S(1)}, s32[32,32]{1,0:T(8,128)}, u32[]{:S(2)}) copy-start(s32[32,32]{1,0:T(8,128)} %block_pattern.3) | copy-start | bytes 12292
  82.4 9.0 %collective-permute-start.10 = (f32[2,128,128]{2,1,0:T(8,128)S(1)}, f32[2,128,128]{2,1,0:T(8,128)S(1)}, u32[]{:S(2)}, u32[]{:S(2)}) collective-permute-start(f32[2,128,128]{2,1,0:T(8,128)S(1)} %maximum_maximum_fusion.3), channel_id=1, source_target_pairs={{0,32},{8,40},{16,48},{24,56},{32,0},{40,8},{48,16},{56,24},{1,33}... | collective-permute-start | bytes 393224 | tf_op jit(solution)/shard_map/ppermute | solution.py:187
  88.5 6.9 %collective-permute-start.9 = (f32[2,64,256]{2,1,0:T(8,128)S(1)}, f32[2,64,256]{2,1,0:T(8,128)S(1)}, u32[]{:S(2)}, u32[]{:S(2)}) collective-permute-start(f32[2,64,256]{2,1,0:T(8,128)S(1)} %maximum_select_fusion.2), channel_id=1, source_target_pairs={{0,1},{1,0},{2,3},{3,2},{4,5},{5,4},{6,7},{7,6},{8,9},{9,8},{10,11... | collective-permute-start | bytes 393224 | tf_op jit(solution)/shard_map/ppermute | solution.py:187
  96.1 48.0 %copy-start.4 = (f32[1024,128]{1,0:T(8,128)S(1)}, f32[1024,128]{1,0:T(8,128)}, u32[]{:S(2)}) copy-start(f32[1024,128]{1,0:T(8,128)} %reduce-scatter.2.cloned.1.call-done.merged) | copy-start | bytes 1572868
  96.1 20.4 %collective-permute-start.11 = (f32[2,128,128]{2,1,0:T(8,128)S(1)}, f32[2,128,128]{2,1,0:T(8,128)S(1)}, u32[]{:S(2)}, u32[]{:S(2)}) collective-permute-start(f32[2,128,128]{2,1,0:T(8,128)S(1)} %maximum_maximum_fusion.4), channel_id=1, source_target_pairs={{0,8},{8,0},{16,24},{24,16},{32,40},{40,32},{48,56},{56,48},{1,9},... | collective-permute-start | bytes 393224 | tf_op jit(solution)/shard_map/ppermute | solution.py:187
  116.6 13.4 %collective-permute-start.14 = (f32[2,64,128]{2,1,0:T(8,128)S(1)}, f32[2,64,128]{2,1,0:T(8,128)S(1)}, u32[]{:S(2)}, u32[]{:S(2)}) collective-permute-start(f32[2,64,128]{2,1,0:T(8,128)S(1)} %get-tuple-element.67), channel_id=1, source_target_pairs={{0,128},{64,192},{128,256},{192,320},{256,384},{320,448},{384,0},{... | collective-permute-start | bytes 196616 | tf_op jit(solution)/shard_map/ppermute | solution.py:286
  121.5 8.5 %collective-permute-start.15 = (f32[2,64,128]{2,1,0:T(8,128)S(1)}, f32[2,64,128]{2,1,0:T(8,128)S(1)}, u32[]{:S(2)}, u32[]{:S(2)}) collective-permute-start(f32[2,64,128]{2,1,0:T(8,128)S(1)} %get-tuple-element.67), channel_id=1, source_target_pairs={{0,256},{64,320},{128,384},{192,448},{256,0},{320,64},{384,128},{4... | collective-permute-start | bytes 196616 | tf_op jit(solution)/shard_map/ppermute | solution.py:286
  125.7 6.2 %collective-permute-start.16 = (f32[2,64,128]{2,1,0:T(8,128)S(1)}, f32[2,64,128]{2,1,0:T(8,128)S(1)}, u32[]{:S(2)}, u32[]{:S(2)}) collective-permute-start(f32[2,64,128]{2,1,0:T(8,128)S(1)} %get-tuple-element.67), channel_id=1, source_target_pairs={{0,384},{64,448},{128,0},{192,64},{256,128},{320,192},{384,256},{4... | collective-permute-start | bytes 196616 | tf_op jit(solution)/shard_map/ppermute | solution.py:286
  128.1 7.7 %collective-permute-start.12 = (f32[2,64,128]{2,1,0:T(8,128)S(1)}, f32[2,64,128]{2,1,0:T(8,128)S(1)}, u32[]{:S(2)}, u32[]{:S(2)}) collective-permute-start(f32[2,64,128]{2,1,0:T(8,128)S(1)} %pad_maximum_fusion.5), channel_id=1, source_target_pairs={{0,32},{8,40},{16,48},{24,56},{32,0},{40,8},{48,16},{56,24},{1,33}... | collective-permute-start | bytes 196616 | tf_op jit(solution)/shard_map/ppermute | solution.py:187
  131.9 12.2 %collective-permute-start.17 = (f32[4,2,64,128]{3,2,1,0:T(8,128)S(1)}, f32[4,2,64,128]{3,2,1,0:T(8,128)S(1)}, u32[]{:S(2)}, u32[]{:S(2)}) collective-permute-start(f32[4,2,64,128]{3,2,1,0:T(8,128)S(1)} %pad_maximum_fusion.ring), channel_id=1, source_target_pairs={{0,64},{64,0},{128,192},{192,128},{256,320},{320,256},{384,448},{4... | collective-permute-start | bytes 786440 | tf_op jit(solution)/shard_map/ppermute | solution.py:187
  135.7 6.9 %collective-permute-start.13 = (f32[2,128,128]{2,1,0:T(8,128)S(1)}, f32[2,128,128]{2,1,0:T(8,128)S(1)}, u32[]{:S(2)}, u32[]{:S(2)}) collective-permute-start(f32[2,128,128]{2,1,0:T(8,128)S(1)} %maximum_select_fusion.3), channel_id=1, source_target_pairs={{0,16},{8,24},{16,0},{24,8},{32,48},{40,56},{48,32},{56,40},{1,17}... | collective-permute-start | bytes 393224 | tf_op jit(solution)/shard_map/ppermute | solution.py:187
  144.1 1.6 %copy-start.1 = (f32[16,128,256]{2,1,0:T(8,128)S(1)}, f32[16,128,256]{2,1,0:T(8,128)}, u32[]{:S(2)}) copy-start(f32[16,128,256]{2,1,0:T(8,128)} %all-gather.3.cloned.1.call-done) | copy-start | bytes 6291460
Sparse Core Ops, SparseCore 0:
  12.3 50.1 reduce-scatter.1
  96.2 33.7 all-gather.2

commit v5 on v3

--- a/solution.py
+++ b/solution.py
@@ -39,16 +39,20 @@
 
 
 def panel_kernel(col_map, local, keep, give, buffer, sems):
-    n_y, _, slots, thin, size = keep.shape
+    n_y, panels, slots, thin, size = keep.shape
     core = lax.axis_index("gz") & 1
+    places = [find(col_map, k) for k in range(2)]
+    if panels == 1:
+        own = lax.axis_index("col") == places[1] // slots
+        places = [jnp.where(own, places[1], places[0])]
     copies = []
-    for k in range(2):
-        first = pl.multiple_of((find(col_map, k) & (slots - 1)) * size, size)
+    for k in range(panels):
+        first = pl.multiple_of((places[k] & (slots - 1)) * size, size)
         copies.append(
             pltpu.make_async_copy(local.at[:, pl.ds(first, size)], buffer.at[k], sems.at[k])
         )
         copies[k].start()
-    for k in range(2):
+    for k in range(panels):
         copies[k].wait()
         for p in range(slots):
             for y in range(n_y):
@@ -57,16 +61,16 @@
                     out[y, k, p] = buffer[k, pl.ds(first, thin), :].astype(jnp.float32)
 
 
-def cut_panels(col_map, local, slots, n_y, thin, size):
-    shape = jax.ShapeDtypeStruct((n_y, 2, slots, thin, size), jnp.float32)
+def cut_panels(col_map, local, panels, slots, n_y, thin, size):
+    shape = jax.ShapeDtypeStruct((n_y, panels, slots, thin, size), jnp.float32)
     return pl.pallas_call(
         panel_kernel,
         out_shape=[shape, shape],
-        in_specs=[SMEM, pl.BlockSpec(memory_space=pl.ANY)],
+        in_specs=[SMEM, pl.BlockSpec(memory_space=pltpu.HBM)],
         out_specs=[VMEM, VMEM],
         scratch_shapes=[
-            pltpu.VMEM((2, local.shape[0], size), jnp.bfloat16),
-            pltpu.SemaphoreType.DMA((2,)),
+            pltpu.VMEM((panels, local.shape[0], size), jnp.bfloat16),
+            pltpu.SemaphoreType.DMA((panels,)),
         ],
         compiler_params=PARAMS,
     )(col_map, local)
@@ -100,23 +104,29 @@
 
 
 def last_kernel(n_y, block_pattern, row_map, col_map, lower_inv, upper_inv, rows, up0, term0,
-                ring, across, merged, out, high, low):
+                merged, panels, out, high, low, buffer, sems):
     slots = high.shape[1] - 1
     size, width = up0.shape
     thin = size // (2 * n_y)
-    y = lax.axis_index("gz") >> 1
     core = lax.axis_index("gz") & 1
     col = column_of(col_map, n_y)
-    order = [slots] + list(range(slots))
-    for p in order:
-        for source, which in ((ring, core), (across, 1 - core)):
-            for step in range(n_y):
-                owner = 2 * ((y + n_y - step) & (n_y - 1)) + which
-                first = pl.multiple_of(owner * thin, thin)
-                for k in range(2):
-                    a, b = halves(source[step, k, p * thin : (p + 1) * thin, :])
-                    high[k, p, pl.ds(first, thin), :] = a
-                    low[k, p, pl.ds(first, thin), :] = b
+    copies = [
+        pltpu.make_async_copy(panels.at[:, :, here, :], buffer.at[:, :, here, :], sems.at[i])
+        for i, here in enumerate((pl.ds(slots * thin, thin), pl.ds(0, slots * thin)))
+    ]
+    for copy in copies:
+        copy.start()
+
+    def settle(p):
+        for owner in range(2 * n_y):
+            here = slice(owner * thin, (owner + 1) * thin)
+            for k in range(2):
+                a, b = halves(buffer[owner, k, p * thin : (p + 1) * thin, :])
+                high[k, p, here, :] = a
+                low[k, p, here, :] = b
+
+    copies[0].wait()
+    settle(slots)
 
     def stored(k, p):
         return high[k, p], low[k, p]
@@ -139,7 +149,9 @@
     term2 = mm_halves(upper0, halves(mm(up_at, term1)))
     both = halves(jnp.concatenate([term0, term2], axis=1))
     term1 = halves(term1)
+    copies[1].wait()
     for p in range(slots):
+        settle(p)
         row = row_map[lax.axis_index("row") * slots + p]
         own = mask_at(block_pattern, row, col)
         keep0 = jnp.where(row > 0, mask_at(block_pattern, row, 0), 0.0)
@@ -163,16 +175,21 @@
 
 
 def last_terms(n_y, slots, block_pattern, row_map, col_map, lower_inv, upper_inv, rows, up0, term0,
-               ring, across, merged):
+               panels, merged):
     size = lower_inv.shape[-1]
     return pl.pallas_call(
         functools.partial(last_kernel, n_y),
         out_shape=jax.ShapeDtypeStruct(merged.shape, jnp.bfloat16),
-        in_specs=[SMEM] * 3 + [VMEM] * 8,
+        in_specs=[SMEM] * 3 + [VMEM] * 6 + [pl.BlockSpec(memory_space=pltpu.HBM)],
         out_specs=VMEM,
-        scratch_shapes=[pltpu.VMEM((2, slots + 1, size, size), jnp.bfloat16)] * 2,
+        scratch_shapes=[
+            pltpu.VMEM((2, slots + 1, size, size), jnp.bfloat16),
+            pltpu.VMEM((2, slots + 1, size, size), jnp.bfloat16),
+            pltpu.VMEM(panels.shape, jnp.float32),
+            pltpu.SemaphoreType.DMA((2,)),
+        ],
         compiler_params=PARAMS,
-    )(block_pattern, row_map, col_map, lower_inv, upper_inv, rows, up0, term0, ring, across, merged)
+    )(block_pattern, row_map, col_map, lower_inv, upper_inv, rows, up0, term0, merged, panels)
 
 
 def swap(x, axis, size, bit):
@@ -198,7 +215,7 @@
 
 def choose(mine, other, me, sources, bit):
     same = [bit_of(me, bit) == bit_of(s, bit) for s in sources]
-    return jnp.stack([jnp.where(same[k], mine[k], other[k]) for k in range(2)])
+    return jnp.stack([jnp.where(same[k], mine[k], other[k]) for k in range(len(sources))])
 
 
 def pick(x, index, axis):
@@ -224,30 +241,53 @@
     def around(step):
         return [(2 * i + c, 2 * ((i + step) % n_y) + c) for i in range(n_y) for c in range(2)]
 
-    keep, give = cut_panels(col_map, local, slots, n_y, thin, size)
-    parts = keep + swap(give, "gz", n_gz, 1)
-    panel = pick(parts, y, 0)
-    for step in (1, 3, 2):
-        chunk = pick(parts, (y + step) & (n_y - 1), 0)
-        panel = panel + lax.ppermute(chunk, "gz", around(step))
-
     merged = lax.psum_scatter(local.astype(jnp.float32), "gz", scatter_dimension=1, tiled=True)
 
-    corner = jnp.stack([pick(panel[k], row_slot[1 - k], 0) for k in range(2)])
-    for bit in (2, 4):
-        corner = choose(corner, swap(corner, "row", n_row, bit), row, row_owner[::-1], bit)
-    mirror = [(r * n_col + c, (r ^ 1) * n_col + c ^ (n_col - 1)) for r in range(n_row) for c in range(n_col)]
-    other = lax.ppermute(corner, ("row", "col"), mirror)
-    same = [bit_of(row, 1) == bit_of(r, 1) for r in row_owner[::-1]]
-    corner = jnp.stack([jnp.where(same[k], corner[k], other[k]) for k in range(2)])
-    corner_owner = [jnp.where(same[k], col_owner[k], col_owner[k] ^ (n_col - 1)) for k in range(2)]
-
-    data = panel.reshape(2, slots * thin, size)
-    for bit in (1, 2):
-        second = bit_of(col, bit)
-        other = swap(part(data, 1, ~second), "col", n_col, bit)
-        data = choose(part(data, 1, second), other, col, col_owner, bit)
-    data, merged = lax.optimization_barrier((data, merged))
+    mirror = [
+        (r * n_col + c, (r ^ 1) * n_col + c ^ (n_col - 1))
+        for r in range(n_row)
+        for c in range(n_col)
+    ]
+    corner_rows = row_owner[::-1]
+    same_half = [bit_of(row, 1) == bit_of(r, 1) for r in corner_rows]
+
+    def gather(panels):
+        keep, give = cut_panels(col_map, local, panels, slots, n_y, thin, size)
+        parts = keep + swap(give, "gz", n_gz, 1)
+        panel = pick(parts, y, 0)
+        for step in (1, 3, 2):
+            chunk = pick(parts, (y + step) & (n_y - 1), 0)
+            panel = panel + lax.ppermute(chunk, "gz", around(step))
+        if panels == 1:
+            second = col == col_owner[1]
+            sources = [jnp.where(second, corner_rows[1], corner_rows[0])]
+            at = [jnp.where(second, row_slot[0], row_slot[1])]
+        else:
+            sources, at = corner_rows, row_slot[::-1]
+        corner = jnp.stack([pick(panel[k], at[k], 0) for k in range(panels)])
+        for bit in (2, 4):
+            other = swap(corner, "row", n_row, bit)
+            corner = choose(corner, other, row, sources, bit)
+        other = lax.ppermute(corner, ("row", "col"), mirror)
+        corner = jnp.stack(
+            [jnp.where(same_half[k], corner[k % panels], other[k % panels]) for k in range(2)]
+        )
+        data = panel.reshape(panels, slots * thin, size)
+        if panels == 1:
+            data = jnp.concatenate([data, data])
+        for bit in (1, 2):
+            second = bit_of(col, bit)
+            other = swap(part(data, 1, ~second), "col", n_col, bit)
+            data = choose(part(data, 1, second), other, col, col_owner, bit)
+        return data, corner
+
+    data, corner = lax.cond(
+        col_owner[0] == col_owner[1], lambda: gather(2), lambda: gather(1)
+    )
+    corner_owner = [
+        jnp.where(same_half[k], col_owner[k], col_owner[k] ^ (n_col - 1)) for k in range(2)
+    ]
+
     blocks = merged.reshape(slots, size, width)
     rows = jnp.stack([pick(blocks, p, 0) for p in row_slot])
 
@@ -256,38 +296,32 @@
         other = swap(part(rows, 1, ~second), "row", n_row, bit)
         return choose(part(rows, 1, second), other, row, row_owner, bit)
 
-    def widen(rows, bit):
-        return join(rows, swap(rows, "row", n_row, bit), 1, bit_of(row, bit))
+    def widen(x, other, me, bit):
+        return join(x, other, 1, bit_of(me, bit))
 
     def send_both(data, corner, bit):
         other = swap(jnp.concatenate([data, corner], 1), "col", n_col, bit)
         thick = data.shape[1]
-        corner = choose(corner, other[:, thick:], col, corner_owner, bit)
-        return other[:, :thick], corner
+        return other[:, :thick], choose(corner, other[:, thick:], col, corner_owner, bit)
 
     other, corner = send_both(data, corner, 4)
     data = choose(data, other, col, col_owner, 4)
     rows = narrow(rows, 2)
     other, corner = send_both(data, corner, 2)
-    data = join(data, other, 1, bit_of(col, 2))
+    data = widen(data, other, col, 2)
     data, rows = lax.optimization_barrier((data, rows))
     rows = narrow(rows, 4)
     other, corner = send_both(data, corner, 1)
-    data = join(data, other, 1, bit_of(col, 1))
-
-    mine = jnp.concatenate([data, corner], 1)
-    mine, rows = lax.optimization_barrier((mine, rows))
+    data = jnp.concatenate([widen(data, other, col, 1), corner], 1)
+    data, rows = lax.optimization_barrier((data, rows))
+    panels = lax.all_gather(data, "gz", axis=0)
     rows = choose(rows, swap(rows, "row", n_row, 1), row, row_owner, 1)
-    rows = widen(rows, 4)
-    ring = [mine] + [lax.ppermute(mine, "gz", around(step)) for step in (1, 2, 3)]
-    ring = jnp.stack(ring)
-    ring, rows = lax.optimization_barrier((ring, rows))
-    across = swap(ring, "gz", n_gz, 1)
-    rows = widen(rows, 2)
+    for bit in (4, 2):
+        rows = widen(rows, swap(rows, "row", n_row, bit), row, bit)
 
     up0, term0 = first_terms(n_y, block_pattern, col_map, lower_inv, upper_inv, rows)
     return last_terms(n_y, slots, block_pattern, row_map, col_map, lower_inv, upper_inv, rows,
-                      up0, term0, ring, across, merged)
+                      up0, term0, panels, merged)
 
 
 def solution(mesh):

time: 166 us -> 163 us (0.982)
  starting transfers between devices: 83.1 us -> 72.5 us
  waiting for transfers between devices: 44.4 us -> 53 us
    ppermute x14 -> x13, waiting for transfers between devices: 29.8 us -> 47.1 us  [swap(): return lax.ppermute(x, axis, [(i, i ^ bit) for i in range(size)])]
    ppermute x7 -> x4, starting transfers between devices: 32.7 us -> 20.9 us  [the longest x3 10.9 us: gather(): panel = panel + lax.ppermute(chunk, 'gz', around(step))]
    ppermute x7 -> x4, waiting for transfers between devices: 14.6 us -> 5.75 us  [the longest x3 5.75 us: gather(): panel = panel + lax.ppermute(chunk, 'gz', around(step))]
    ppermute x14 -> x13, starting transfers between devices: 50.4 us -> 51.6 us  [swap(): return lax.ppermute(x, axis, [(i, i ^ bit) for i in range(size)])]
  transfers between devices with their start and end apart: 22 -> 19, of which waited for: 12 -> 14; matrix products, arithmetic and copies ran while one was open for 3% -> 2% of each run, Pallas kernels for 2% -> 1%
where the time goes in v5:
time: 163 us; the launch traced here: 161 us
  starting transfers between devices  72.5 us (44%)
  waiting for transfers between devices  53 us (33%)
  between operations  17.7 us (11%)
  other arithmetic  7.39 us (5%)
  Pallas kernels  6.5 us (4%)
  local copies, waits for them, and re-layouts  3.42 us (2%)
    ppermute x13, starting transfers between devices, swap(): return lax.ppermute(x, axis, [(i, i ^ bit) for i in range(size)])  51.6 us
    ppermute x13, waiting for transfers between devices, swap(): return lax.ppermute(x, axis, [(i, i ^ bit) for i in range(size)])  47.1 us
    ppermute x3, starting transfers between devices, gather(): panel = panel + lax.ppermute(chunk, 'gz', around(step))  10.9 us
    ppermute x1, starting transfers between devices, gather(): other = lax.ppermute(corner, ('row', 'col'), mirror)  9.94 us
    ppermute x3, waiting for transfers between devices, gather(): panel = panel + lax.ppermute(chunk, 'gz', around(step))  5.75 us
    pallas_call x1, Pallas kernels, last_terms(): pl.pallas_call(functools.partial(last_kernel, n_y), out_shape=jax.ShapeDt...  4.38 us
    convert_element_type x1, other arithmetic, shards(): local.astype(jnp.float32)  4.03 us
  transfers between devices with their start and end apart: 19, of which 14 were waited for; matrix products, arithmetic and copies ran while one was open for 2% of the time, Pallas kernels for 1%

profile of v5, /device:TPU:6, one launch (start us, length us, event | category | flops | bytes accessed | tf_op | source)
XLA Modules:
  0.0 160.7 jit_solution(5452902704950745414)
XLA Ops:
  6.5 4.0 %bitcast_convert_fusion = f32[1024,1024]{1,0:T(8,128)} fusion(bf16[1,1024,1024]{2,1,0:T(8,128)(2,1)} %param.8), kind=kLoop, calls=%fused_computation.103 | loop fusion | flops 1048576 | bytes 6291456 | tf_op jit(solution)/shard_map/convert_element_type | solution.py:244
  10.6 0.0 reduce-scatter.2.cloned.1.call-update
  10.6 0.0 all-gather.3.cloned.1.call-start
  10.7 0.6 copy-done.5
  11.2 0.7 fusion.14
  15.9 61.9 %conditional.1 = (f32[2,32,256]{2,1,0:T(8,128)S(1)}, f32[2,32,256]{2,1,0:T(8,128)S(1)}, f32[1,32,256]{2,1,0:T(8,128)}, f32[1,32,256]{2,1,0:T(8,128)}) conditional(s32[]{:T(128)} %convert_element_type.25, (u32[]{:T(128)}, u32[]{:T(128)}, s32[32]{0:T(128)S(1)}, bf16[1024,1024]{1,0:T(8,128)(2,1)S(1)}, u32[]{:T(128)}, /*index=5*/u32[]{:T(128)}, ...), branch_computations={%region_4.5_spmd, %region_5.6_spmd} | conditional | flops 671787 | bytes 26346356 | solution.py:284
  15.9 0.8 branch_0_fun.1
  16.6 1.9 %collective-permute-start = (f32[4,1,4,32,256]{4,3,2,1,0:T(8,128)S(1)}, f32[4,1,4,32,256]{4,3,2,1,0:T(8,128)S(1)}, u32[]{:S(2)}, u32[]{:S(2)}) collective-permute-start(f32[4,1,4,32,256]{4,3,2,1,0:T(8,128)S(1)} %get-tuple-element.64), channel_id=1, source_target_pairs={{0,64},{64,0},{128,192},{192,128},{256,320},{320,256},{384,448},{4... | collective-permute-start | bytes 1572872 | tf_op jit(solution)/shard_map/cond/branch_0_fun/ppermute | solution.py:196
  18.6 1.9 %collective-permute-done = f32[4,1,4,32,256]{4,3,2,1,0:T(8,128)S(1)} collective-permute-done((f32[4,1,4,32,256]{4,3,2,1,0:T(8,128)S(1)}, f32[4,1,4,32,256]{4,3,2,1,0:T(8,128)S(1)}, u32[]{:S(2)}, u32[]{:S(2)}) %collective-permute-start) | collective-permute-done | bytes 524320 | tf_op jit(solution)/shard_map/cond/branch_0_fun/ppermute | solution.py:196
  20.5 0.1 add.30
  20.6 3.5 %collective-permute-start.1 = (f32[1,4,32,256]{3,2,1,0:T(8,128)S(1)}, f32[1,4,32,256]{3,2,1,0:T(8,128)S(1)}, u32[]{:S(2)}, u32[]{:S(2)}) collective-permute-start(f32[1,4,32,256]{3,2,1,0:T(8,128)S(1)} %get-tuple-element.113), channel_id=1, source_target_pairs={{0,128},{64,192},{128,256},{192,320},{256,384},{320,448},{384,0},{... | collective-permute-start | bytes 393224 | tf_op jit(solution)/shard_map/cond/branch_0_fun/ppermute | solution.py:260
  24.1 3.6 %collective-permute-start.2 = (f32[1,4,32,256]{3,2,1,0:T(8,128)S(1)}, f32[1,4,32,256]{3,2,1,0:T(8,128)S(1)}, u32[]{:S(2)}, u32[]{:S(2)}) collective-permute-start(f32[1,4,32,256]{3,2,1,0:T(8,128)S(1)} %get-tuple-element.115), channel_id=1, source_target_pairs={{0,384},{64,448},{128,0},{192,64},{256,128},{320,192},{384,256},{4... | collective-permute-start | bytes 393224 | tf_op jit(solution)/shard_map/cond/branch_0_fun/ppermute | solution.py:260
  27.6 3.9 %collective-permute-start.3 = (f32[1,4,32,256]{3,2,1,0:T(8,128)S(1)}, f32[1,4,32,256]{3,2,1,0:T(8,128)S(1)}, u32[]{:S(2)}, u32[]{:S(2)}) collective-permute-start(f32[1,4,32,256]{3,2,1,0:T(8,128)S(1)} %get-tuple-element.114), channel_id=1, source_target_pairs={{0,256},{64,320},{128,384},{192,448},{256,0},{320,64},{384,128},{4... | collective-permute-start | bytes 393224 | tf_op jit(solution)/shard_map/cond/branch_0_fun/ppermute | solution.py:260
  31.6 5.7 %collective-permute-done.3 = f32[1,4,32,256]{3,2,1,0:T(8,128)S(1)} collective-permute-done((f32[1,4,32,256]{3,2,1,0:T(8,128)S(1)}, f32[1,4,32,256]{3,2,1,0:T(8,128)S(1)}, u32[]{:S(2)}, u32[]{:S(2)}) %collective-permute-start.3) | collective-permute-done | bytes 131104 | tf_op jit(solution)/shard_map/cond/branch_0_fun/ppermute | solution.py:260
  37.4 2.7 %collective-permute-start.6 = (f32[1,32,256]{2,1,0:T(8,128)S(1)}, f32[1,32,256]{2,1,0:T(8,128)S(1)}, u32[]{:S(2)}, u32[]{:S(2)}) collective-permute-start(f32[1,32,256]{2,1,0:T(8,128)S(1)} %dynamic-slice_bitcast_fusion.3), channel_id=1, source_target_pairs={{0,16},{8,24},{16,0},{24,8},{32,48},{40,56},{48,32},{56,40},{1,17}... | collective-permute-start | bytes 98312 | tf_op jit(solution)/shard_map/cond/branch_0_fun/ppermute | solution.py:196
  40.1 3.1 %collective-permute-done.6 = f32[1,32,256]{2,1,0:T(8,128)S(1)} collective-permute-done((f32[1,32,256]{2,1,0:T(8,128)S(1)}, f32[1,32,256]{2,1,0:T(8,128)S(1)}, u32[]{:S(2)}, u32[]{:S(2)}) %collective-permute-start.6) | collective-permute-done | bytes 32800 | tf_op jit(solution)/shard_map/cond/branch_0_fun/ppermute | solution.py:196
  43.2 7.1 %collective-permute-start.7 = (f32[1,32,256]{2,1,0:T(8,128)S(1)}, f32[1,32,256]{2,1,0:T(8,128)S(1)}, u32[]{:S(2)}, u32[]{:S(2)}) collective-permute-start(f32[1,32,256]{2,1,0:T(8,128)S(1)} %broadcast_select_fusion.1), channel_id=1, source_target_pairs={{0,32},{8,40},{16,48},{24,56},{32,0},{40,8},{48,16},{56,24},{1,33}... | collective-permute-start | bytes 98312 | tf_op jit(solution)/shard_map/cond/branch_0_fun/ppermute | solution.py:196
  50.3 1.8 %collective-permute-done.7 = f32[1,32,256]{2,1,0:T(8,128)S(1)} collective-permute-done((f32[1,32,256]{2,1,0:T(8,128)S(1)}, f32[1,32,256]{2,1,0:T(8,128)S(1)}, u32[]{:S(2)}, u32[]{:S(2)}) %collective-permute-start.7) | collective-permute-done | bytes 32800 | tf_op jit(solution)/shard_map/cond/branch_0_fun/ppermute | solution.py:196
  52.2 9.9 %collective-permute-start.8 = (f32[1,32,256]{2,1,0:T(8,128)S(1)}, f32[1,32,256]{2,1,0:T(8,128)S(1)}, u32[]{:S(2)}, u32[]{:S(2)}) collective-permute-start(f32[1,32,256]{2,1,0:T(8,128)S(1)} %broadcast_select_fusion.2), channel_id=1, source_target_pairs={{0,15},{1,14},{2,13},{3,12},{4,11},{5,10},{6,9},{7,8},{8,7},{9,6},... | collective-permute-start | bytes 98312 | tf_op jit(solution)/shard_map/cond/branch_0_fun/ppermute | solution.py:271
  62.2 3.5 %collective-permute-start.4 = (f32[2,64,256]{2,1,0:T(8,128)S(1)}, f32[2,64,256]{2,1,0:T(8,128)S(1)}, u32[]{:S(2)}, u32[]{:S(2)}) collective-permute-start(f32[2,64,256]{2,1,0:T(8,128)S(1)} %get-tuple-element.123), channel_id=1, source_target_pairs={{0,1},{1,0},{2,3},{3,2},{4,5},{5,4},{6,7},{7,6},{8,9},{9,8},{10,11... | collective-permute-start | bytes 393224 | tf_op jit(solution)/shard_map/cond/branch_0_fun/ppermute | solution.py:196
  65.6 3.7 %collective-permute-done.4 = f32[2,64,256]{2,1,0:T(8,128)S(1)} collective-permute-done((f32[2,64,256]{2,1,0:T(8,128)S(1)}, f32[2,64,256]{2,1,0:T(8,128)S(1)}, u32[]{:S(2)}, u32[]{:S(2)}) %collective-permute-start.4) | collective-permute-done | bytes 131104 | tf_op jit(solution)/shard_map/cond/branch_0_fun/ppermute | solution.py:196
  69.3 4.2 %collective-permute-start.5 = (f32[2,32,256]{2,1,0:T(8,128)S(1)}, f32[2,32,256]{2,1,0:T(8,128)S(1)}, u32[]{:S(2)}, u32[]{:S(2)}) collective-permute-start(f32[2,32,256]{2,1,0:T(8,128)S(1)} %get-tuple-element.121), channel_id=1, source_target_pairs={{0,2},{1,3},{2,0},{3,1},{4,6},{5,7},{6,4},{7,5},{8,10},{9,11},{10,... | collective-permute-start | bytes 196616 | tf_op jit(solution)/shard_map/cond/branch_0_fun/ppermute | solution.py:196
  73.6 2.8 %collective-permute-done.5 = f32[2,32,256]{2,1,0:T(8,128)S(1)} collective-permute-done((f32[2,32,256]{2,1,0:T(8,128)S(1)}, f32[2,32,256]{2,1,0:T(8,128)S(1)}, u32[]{:S(2)}, u32[]{:S(2)}) %collective-permute-start.5) | collective-permute-done | bytes 65568 | tf_op jit(solution)/shard_map/cond/branch_0_fun/ppermute | solution.py:196
  76.4 0.6 slice_select_fusion.3
  77.0 0.8 pad_maximum_fusion
  77.8 8.2 %collective-permute-start.18 = (f32[2,64,256]{2,1,0:T(8,128)S(1)}, f32[2,64,256]{2,1,0:T(8,128)S(1)}, u32[]{:S(2)}, u32[]{:S(2)}) collective-permute-start(f32[2,64,256]{2,1,0:T(8,128)S(1)} %pad_maximum_fusion.7), channel_id=1, source_target_pairs={{0,4},{1,5},{2,6},{3,7},{4,0},{5,1},{6,2},{7,3},{8,12},{9,13},{10,... | collective-permute-start | bytes 393224 | tf_op jit(solution)/shard_map/ppermute | solution.py:196
  86.2 7.2 %collective-permute-done.18 = f32[2,64,256]{2,1,0:T(8,128)S(1)} collective-permute-done((f32[2,64,256]{2,1,0:T(8,128)S(1)}, f32[2,64,256]{2,1,0:T(8,128)S(1)}, u32[]{:S(2)}, u32[]{:S(2)}) %collective-permute-start.18) | collective-permute-done | bytes 131104 | tf_op jit(solution)/shard_map/ppermute | solution.py:196
  93.5 1.9 %collective-permute-start.19 = (f32[2,64,256]{2,1,0:T(8,128)S(1)}, f32[2,64,256]{2,1,0:T(8,128)S(1)}, u32[]{:S(2)}, u32[]{:S(2)}) collective-permute-start(f32[2,64,256]{2,1,0:T(8,128)S(1)} %maximum_maximum_fusion.2), channel_id=1, source_target_pairs={{0,2},{1,3},{2,0},{3,1},{4,6},{5,7},{6,4},{7,5},{8,10},{9,11},{10,... | collective-permute-start | bytes 393224 | tf_op jit(solution)/shard_map/ppermute | solution.py:196
  95.4 0.0 reduce-scatter.2.cloned.1.call-done.merged
  95.4 1.0 constant_dynamic-slice_fusion.2
  96.5 2.9 %collective-permute-start.20 = (f32[2,128,128]{2,1,0:T(8,128)S(1)}, f32[2,128,128]{2,1,0:T(8,128)S(1)}, u32[]{:S(2)}, u32[]{:S(2)}) collective-permute-start(f32[2,128,128]{2,1,0:T(8,128)S(1)} %get-tuple-element.150), channel_id=1, source_target_pairs={{0,16},{8,24},{16,0},{24,8},{32,48},{40,56},{48,32},{56,40},{1,17}... | collective-permute-start | bytes 393224 | tf_op jit(solution)/shard_map/ppermute | solution.py:196
  99.4 2.2 %collective-permute-done.19 = f32[2,64,256]{2,1,0:T(8,128)S(1)} collective-permute-done((f32[2,64,256]{2,1,0:T(8,128)S(1)}, f32[2,64,256]{2,1,0:T(8,128)S(1)}, u32[]{:S(2)}, u32[]{:S(2)}) %collective-permute-start.19) | collective-permute-done | bytes 131104 | tf_op jit(solution)/shard_map/ppermute | solution.py:196
  101.7 1.8 %collective-permute-done.20 = f32[2,128,128]{2,1,0:T(8,128)S(1)} collective-permute-done((f32[2,128,128]{2,1,0:T(8,128)S(1)}, f32[2,128,128]{2,1,0:T(8,128)S(1)}, u32[]{:S(2)}, u32[]{:S(2)}) %collective-permute-start.20) | collective-permute-done | bytes 131104 | tf_op jit(solution)/shard_map/ppermute | solution.py:196
  103.5 4.0 %collective-permute-start.22 = (f32[2,64,128]{2,1,0:T(8,128)S(1)}, f32[2,64,128]{2,1,0:T(8,128)S(1)}, u32[]{:S(2)}, u32[]{:S(2)}) collective-permute-start(f32[2,64,128]{2,1,0:T(8,128)S(1)} %constant_dynamic-slice_fusion.1), channel_id=1, source_target_pairs={{0,32},{8,40},{16,48},{24,56},{32,0},{40,8},{48,16},{56,24},{1,33}... | collective-permute-start | bytes 196616 | tf_op jit(solution)/shard_map/ppermute | solution.py:196
  107.5 1.9 %collective-permute-start.21 = (f32[2,96,256]{2,1,0:T(8,128)S(1)}, f32[2,96,256]{2,1,0:T(8,128)S(1)}, u32[]{:S(2)}, u32[]{:S(2)}) collective-permute-start(f32[2,96,256]{2,1,0:T(8,128)S(1)} %maximum_maximum_fusion.1), channel_id=1, source_target_pairs={{0,1},{1,0},{2,3},{3,2},{4,5},{5,4},{6,7},{7,6},{8,9},{9,8},{10,11... | collective-permute-start | bytes 589832 | tf_op jit(solution)/shard_map/ppermute | solution.py:196
  109.5 1.9 %collective-permute-done.22 = f32[2,64,128]{2,1,0:T(8,128)S(1)} collective-permute-done((f32[2,64,128]{2,1,0:T(8,128)S(1)}, f32[2,64,128]{2,1,0:T(8,128)S(1)}, u32[]{:S(2)}, u32[]{:S(2)}) %collective-permute-start.22) | collective-permute-done | bytes 65568 | tf_op jit(solution)/shard_map/ppermute | solution.py:196
  111.4 3.7 %collective-permute-done.21 = f32[2,96,256]{2,1,0:T(8,128)S(1)} collective-permute-done((f32[2,96,256]{2,1,0:T(8,128)S(1)}, f32[2,96,256]{2,1,0:T(8,128)S(1)}, u32[]{:S(2)}, u32[]{:S(2)}) %collective-permute-start.21) | collective-permute-done | bytes 196640 | tf_op jit(solution)/shard_map/ppermute | solution.py:196
  115.2 0.8 maximum_maximum_fusion
  115.9 7.3 %collective-permute-start.23 = (f32[2,64,128]{2,1,0:T(8,128)S(1)}, f32[2,64,128]{2,1,0:T(8,128)S(1)}, u32[]{:S(2)}, u32[]{:S(2)}) collective-permute-start(f32[2,64,128]{2,1,0:T(8,128)S(1)} %pad_maximum_fusion.10), channel_id=1, source_target_pairs={{0,8},{8,0},{16,24},{24,16},{32,40},{40,32},{48,56},{56,48},{1,9},... | collective-permute-start | bytes 196616 | tf_op jit(solution)/shard_map/ppermute | solution.py:196
  123.3 8.5 %collective-permute-done.23 = f32[2,64,128]{2,1,0:T(8,128)S(1)} collective-permute-done((f32[2,64,128]{2,1,0:T(8,128)S(1)}, f32[2,64,128]{2,1,0:T(8,128)S(1)}, u32[]{:S(2)}, u32[]{:S(2)}) %collective-permute-start.23) | collective-permute-done | bytes 65568 | tf_op jit(solution)/shard_map/ppermute | solution.py:196
  131.8 4.0 %collective-permute-start.24 = (f32[2,64,128]{2,1,0:T(8,128)S(1)}, f32[2,64,128]{2,1,0:T(8,128)S(1)}, u32[]{:S(2)}, u32[]{:S(2)}) collective-permute-start(f32[2,64,128]{2,1,0:T(8,128)S(1)} %pad_maximum_fusion.11), channel_id=1, source_target_pairs={{0,32},{8,40},{16,48},{24,56},{32,0},{40,8},{48,16},{56,24},{1,33}... | collective-permute-start | bytes 196616 | tf_op jit(solution)/shard_map/ppermute | solution.py:196
  135.7 3.7 %collective-permute-done.24 = f32[2,64,128]{2,1,0:T(8,128)S(1)} collective-permute-done((f32[2,64,128]{2,1,0:T(8,128)S(1)}, f32[2,64,128]{2,1,0:T(8,128)S(1)}, u32[]{:S(2)}, u32[]{:S(2)}) %collective-permute-start.24) | collective-permute-done | bytes 65568 | tf_op jit(solution)/shard_map/ppermute | solution.py:196
  139.4 1.9 %collective-permute-start.25 = (f32[2,128,128]{2,1,0:T(8,128)S(1)}, f32[2,128,128]{2,1,0:T(8,128)S(1)}, u32[]{:S(2)}, u32[]{:S(2)}) collective-permute-start(f32[2,128,128]{2,1,0:T(8,128)S(1)} %maximum_select_fusion.2), channel_id=1, source_target_pairs={{0,16},{8,24},{16,0},{24,8},{32,48},{40,56},{48,32},{56,40},{1,17}... | collective-permute-start | bytes 393224 | tf_op jit(solution)/shard_map/ppermute | solution.py:196
  141.4 4.9 %collective-permute-done.25 = f32[2,128,128]{2,1,0:T(8,128)S(1)} collective-permute-done((f32[2,128,128]{2,1,0:T(8,128)S(1)}, f32[2,128,128]{2,1,0:T(8,128)S(1)}, u32[]{:S(2)}, u32[]{:S(2)}) %collective-permute-start.25) | collective-permute-done | bytes 131104 | tf_op jit(solution)/shard_map/ppermute | solution.py:196
  146.3 1.4 shard_map.64
  147.7 0.0 all-gather.3.cloned.1.call-done
  147.8 1.7 %copy-done = f32[16,160,256]{2,1,0:T(8,128)S(1)} copy-done((f32[16,160,256]{2,1,0:T(8,128)S(1)}, f32[16,160,256]{2,1,0:T(8,128)}, u32[]{:S(2)}) %copy-start) | copy-done | bytes 2621464
  149.5 4.4 %shard_map.65 = bf16[1024,128]{1,0:T(8,128)(2,1)} custom-call(s32[32,32]{1,0:T(8,128)S(1)} %copy-done.4, s32[32]{0:T(128)S(1)} %copy-done.5, s32[32]{0:T(128)S(1)} %copy-done.8, f32[2,256,256]{2,1,0:T(8,128)S(1)} %copy-done.1, f32[2,256,256]{2,1,0:T(8,128)S(1)} %copy-done.2, f32[2,256,128]{2,1,0:T(8,128)S(1)} %maximum_select_fusion.1.rows, ...), custom_call_target="tpu_custom_call" | custom-call | tf_op jit(solution)/shard_map/pallas_call | solution.py:180
  (49 shorter events, 0.5 us)
Async XLA Ops:
  6.5 88.9 %reduce-scatter.2.cloned.1.call-start = ((), (), s32[]{:S(2)}) async-start(), calls=%async_computation.1 | async-start | bytes 4718592 | tf_op jit(solution)/shard_map/reduce_scatter | solution.py:244
  10.6 0.7 copy-start.5
  10.6 0.7 copy-start.8
  10.6 5.3 %copy-start.6 = (bf16[1,1024,1024]{2,1,0:T(8,128)(2,1)S(1)}, bf16[1,1024,1024]{2,1,0:T(8,128)(2,1)}, u32[]{:S(2)}) copy-start(bf16[1,1024,1024]{2,1,0:T(8,128)(2,1)} %param.8) | copy-start | bytes 6291460
  10.6 137.1 %all-gather.3.cloned.1.call-start = ((), (), s32[]{:S(2)}) async-start(), calls=%async_computation.2 | async-start | bytes 2949120 | tf_op jit(solution)/shard_map/all_gather | solution.py:317
  16.6 3.8 %collective-permute-start = (f32[4,1,4,32,256]{4,3,2,1,0:T(8,128)S(1)}, f32[4,1,4,32,256]{4,3,2,1,0:T(8,128)S(1)}, u32[]{:S(2)}, u32[]{:S(2)}) collective-permute-start(f32[4,1,4,32,256]{4,3,2,1,0:T(8,128)S(1)} %get-tuple-element.64), channel_id=1, source_target_pairs={{0,64},{64,0},{128,192},{192,128},{256,320},{320,256},{384,448},{4... | collective-permute-start | bytes 1572872 | tf_op jit(solution)/shard_map/cond/branch_0_fun/ppermute | solution.py:196
  20.6 11.0 %collective-permute-start.1 = (f32[1,4,32,256]{3,2,1,0:T(8,128)S(1)}, f32[1,4,32,256]{3,2,1,0:T(8,128)S(1)}, u32[]{:S(2)}, u32[]{:S(2)}) collective-permute-start(f32[1,4,32,256]{3,2,1,0:T(8,128)S(1)} %get-tuple-element.113), channel_id=1, source_target_pairs={{0,128},{64,192},{128,256},{192,320},{256,384},{320,448},{384,0},{... | collective-permute-start | bytes 393224 | tf_op jit(solution)/shard_map/cond/branch_0_fun/ppermute | solution.py:260
  24.1 7.5 %collective-permute-start.2 = (f32[1,4,32,256]{3,2,1,0:T(8,128)S(1)}, f32[1,4,32,256]{3,2,1,0:T(8,128)S(1)}, u32[]{:S(2)}, u32[]{:S(2)}) collective-permute-start(f32[1,4,32,256]{3,2,1,0:T(8,128)S(1)} %get-tuple-element.115), channel_id=1, source_target_pairs={{0,384},{64,448},{128,0},{192,64},{256,128},{320,192},{384,256},{4... | collective-permute-start | bytes 393224 | tf_op jit(solution)/shard_map/cond/branch_0_fun/ppermute | solution.py:260
  27.6 9.7 %collective-permute-start.3 = (f32[1,4,32,256]{3,2,1,0:T(8,128)S(1)}, f32[1,4,32,256]{3,2,1,0:T(8,128)S(1)}, u32[]{:S(2)}, u32[]{:S(2)}) collective-permute-start(f32[1,4,32,256]{3,2,1,0:T(8,128)S(1)} %get-tuple-element.114), channel_id=1, source_target_pairs={{0,256},{64,320},{128,384},{192,448},{256,0},{320,64},{384,128},{4... | collective-permute-start | bytes 393224 | tf_op jit(solution)/shard_map/cond/branch_0_fun/ppermute | solution.py:260
  37.4 5.8 %collective-permute-start.6 = (f32[1,32,256]{2,1,0:T(8,128)S(1)}, f32[1,32,256]{2,1,0:T(8,128)S(1)}, u32[]{:S(2)}, u32[]{:S(2)}) collective-permute-start(f32[1,32,256]{2,1,0:T(8,128)S(1)} %dynamic-slice_bitcast_fusion.3), channel_id=1, source_target_pairs={{0,16},{8,24},{16,0},{24,8},{32,48},{40,56},{48,32},{56,40},{1,17}... | collective-permute-start | bytes 98312 | tf_op jit(solution)/shard_map/cond/branch_0_fun/ppermute | solution.py:196
  43.2 9.0 %collective-permute-start.7 = (f32[1,32,256]{2,1,0:T(8,128)S(1)}, f32[1,32,256]{2,1,0:T(8,128)S(1)}, u32[]{:S(2)}, u32[]{:S(2)}) collective-permute-start(f32[1,32,256]{2,1,0:T(8,128)S(1)} %broadcast_select_fusion.1), channel_id=1, source_target_pairs={{0,32},{8,40},{16,48},{24,56},{32,0},{40,8},{48,16},{56,24},{1,33}... | collective-permute-start | bytes 98312 | tf_op jit(solution)/shard_map/cond/branch_0_fun/ppermute | solution.py:196
  52.2 13.4 %collective-permute-start.8 = (f32[1,32,256]{2,1,0:T(8,128)S(1)}, f32[1,32,256]{2,1,0:T(8,128)S(1)}, u32[]{:S(2)}, u32[]{:S(2)}) collective-permute-start(f32[1,32,256]{2,1,0:T(8,128)S(1)} %broadcast_select_fusion.2), channel_id=1, source_target_pairs={{0,15},{1,14},{2,13},{3,12},{4,11},{5,10},{6,9},{7,8},{8,7},{9,6},... | collective-permute-start | bytes 98312 | tf_op jit(solution)/shard_map/cond/branch_0_fun/ppermute | solution.py:271
  62.2 7.1 %collective-permute-start.4 = (f32[2,64,256]{2,1,0:T(8,128)S(1)}, f32[2,64,256]{2,1,0:T(8,128)S(1)}, u32[]{:S(2)}, u32[]{:S(2)}) collective-permute-start(f32[2,64,256]{2,1,0:T(8,128)S(1)} %get-tuple-element.123), channel_id=1, source_target_pairs={{0,1},{1,0},{2,3},{3,2},{4,5},{5,4},{6,7},{7,6},{8,9},{9,8},{10,11... | collective-permute-start | bytes 393224 | tf_op jit(solution)/shard_map/cond/branch_0_fun/ppermute | solution.py:196
  69.3 7.1 %collective-permute-start.5 = (f32[2,32,256]{2,1,0:T(8,128)S(1)}, f32[2,32,256]{2,1,0:T(8,128)S(1)}, u32[]{:S(2)}, u32[]{:S(2)}) collective-permute-start(f32[2,32,256]{2,1,0:T(8,128)S(1)} %get-tuple-element.121), channel_id=1, source_target_pairs={{0,2},{1,3},{2,0},{3,1},{4,6},{5,7},{6,4},{7,5},{8,10},{9,11},{10,... | collective-permute-start | bytes 196616 | tf_op jit(solution)/shard_map/cond/branch_0_fun/ppermute | solution.py:196
  77.8 15.6 %collective-permute-start.18 = (f32[2,64,256]{2,1,0:T(8,128)S(1)}, f32[2,64,256]{2,1,0:T(8,128)S(1)}, u32[]{:S(2)}, u32[]{:S(2)}) collective-permute-start(f32[2,64,256]{2,1,0:T(8,128)S(1)} %pad_maximum_fusion.7), channel_id=1, source_target_pairs={{0,4},{1,5},{2,6},{3,7},{4,0},{5,1},{6,2},{7,3},{8,12},{9,13},{10,... | collective-permute-start | bytes 393224 | tf_op jit(solution)/shard_map/ppermute | solution.py:196
  93.5 8.2 %collective-permute-start.19 = (f32[2,64,256]{2,1,0:T(8,128)S(1)}, f32[2,64,256]{2,1,0:T(8,128)S(1)}, u32[]{:S(2)}, u32[]{:S(2)}) collective-permute-start(f32[2,64,256]{2,1,0:T(8,128)S(1)} %maximum_maximum_fusion.2), channel_id=1, source_target_pairs={{0,2},{1,3},{2,0},{3,1},{4,6},{5,7},{6,4},{7,5},{8,10},{9,11},{10,... | collective-permute-start | bytes 393224 | tf_op jit(solution)/shard_map/ppermute | solution.py:196
  96.4 49.9 %copy-start.1 = (f32[2,256,256]{2,1,0:T(8,128)S(1)}, f32[2,256,256]{2,1,0:T(8,128)}, u32[]{:S(2)}) copy-start(f32[2,256,256]{2,1,0:T(8,128)} %lower_inv.3) | copy-start | bytes 1572868
  96.5 49.9 %copy-start.2 = (f32[2,256,256]{2,1,0:T(8,128)S(1)}, f32[2,256,256]{2,1,0:T(8,128)}, u32[]{:S(2)}) copy-start(f32[2,256,256]{2,1,0:T(8,128)} %upper_inv.3) | copy-start | bytes 1572868
  96.5 49.9 %copy-start.4 = (s32[32,32]{1,0:T(8,128)S(1)}, s32[32,32]{1,0:T(8,128)}, u32[]{:S(2)}) copy-start(s32[32,32]{1,0:T(8,128)} %block_pattern.3) | copy-start | bytes 12292
  96.5 7.0 %collective-permute-start.20 = (f32[2,128,128]{2,1,0:T(8,128)S(1)}, f32[2,128,128]{2,1,0:T(8,128)S(1)}, u32[]{:S(2)}, u32[]{:S(2)}) collective-permute-start(f32[2,128,128]{2,1,0:T(8,128)S(1)} %get-tuple-element.150), channel_id=1, source_target_pairs={{0,16},{8,24},{16,0},{24,8},{32,48},{40,56},{48,32},{56,40},{1,17}... | collective-permute-start | bytes 393224 | tf_op jit(solution)/shard_map/ppermute | solution.py:196
  103.5 44.2 %copy-start.3 = (f32[1024,128]{1,0:T(8,128)S(1)}, f32[1024,128]{1,0:T(8,128)}, u32[]{:S(2)}) copy-start(f32[1024,128]{1,0:T(8,128)} %reduce-scatter.2.cloned.1.call-done.merged) | copy-start | bytes 1572868
  103.5 7.8 %collective-permute-start.22 = (f32[2,64,128]{2,1,0:T(8,128)S(1)}, f32[2,64,128]{2,1,0:T(8,128)S(1)}, u32[]{:S(2)}, u32[]{:S(2)}) collective-permute-start(f32[2,64,128]{2,1,0:T(8,128)S(1)} %constant_dynamic-slice_fusion.1), channel_id=1, source_target_pairs={{0,32},{8,40},{16,48},{24,56},{32,0},{40,8},{48,16},{56,24},{1,33}... | collective-permute-start | bytes 196616 | tf_op jit(solution)/shard_map/ppermute | solution.py:196
  107.5 7.6 %collective-permute-start.21 = (f32[2,96,256]{2,1,0:T(8,128)S(1)}, f32[2,96,256]{2,1,0:T(8,128)S(1)}, u32[]{:S(2)}, u32[]{:S(2)}) collective-permute-start(f32[2,96,256]{2,1,0:T(8,128)S(1)} %maximum_maximum_fusion.1), channel_id=1, source_target_pairs={{0,1},{1,0},{2,3},{3,2},{4,5},{5,4},{6,7},{7,6},{8,9},{9,8},{10,11... | collective-permute-start | bytes 589832 | tf_op jit(solution)/shard_map/ppermute | solution.py:196
  115.9 15.8 %collective-permute-start.23 = (f32[2,64,128]{2,1,0:T(8,128)S(1)}, f32[2,64,128]{2,1,0:T(8,128)S(1)}, u32[]{:S(2)}, u32[]{:S(2)}) collective-permute-start(f32[2,64,128]{2,1,0:T(8,128)S(1)} %pad_maximum_fusion.10), channel_id=1, source_target_pairs={{0,8},{8,0},{16,24},{24,16},{32,40},{40,32},{48,56},{56,48},{1,9},... | collective-permute-start | bytes 196616 | tf_op jit(solution)/shard_map/ppermute | solution.py:196
  131.8 7.7 %collective-permute-start.24 = (f32[2,64,128]{2,1,0:T(8,128)S(1)}, f32[2,64,128]{2,1,0:T(8,128)S(1)}, u32[]{:S(2)}, u32[]{:S(2)}) collective-permute-start(f32[2,64,128]{2,1,0:T(8,128)S(1)} %pad_maximum_fusion.11), channel_id=1, source_target_pairs={{0,32},{8,40},{16,48},{24,56},{32,0},{40,8},{48,16},{56,24},{1,33}... | collective-permute-start | bytes 196616 | tf_op jit(solution)/shard_map/ppermute | solution.py:196
  139.4 6.9 %collective-permute-start.25 = (f32[2,128,128]{2,1,0:T(8,128)S(1)}, f32[2,128,128]{2,1,0:T(8,128)S(1)}, u32[]{:S(2)}, u32[]{:S(2)}) collective-permute-start(f32[2,128,128]{2,1,0:T(8,128)S(1)} %maximum_select_fusion.2), channel_id=1, source_target_pairs={{0,16},{8,24},{16,0},{24,8},{32,48},{40,56},{48,32},{56,40},{1,17}... | collective-permute-start | bytes 393224 | tf_op jit(solution)/shard_map/ppermute | solution.py:196
  147.8 1.7 %copy-start = (f32[16,160,256]{2,1,0:T(8,128)S(1)}, f32[16,160,256]{2,1,0:T(8,128)}, u32[]{:S(2)}) copy-start(f32[16,160,256]{2,1,0:T(8,128)} %all-gather.3.cloned.1.call-done) | copy-start | bytes 7864324
Sparse Core Ops, SparseCore 0:
  10.7 51.6 reduce-scatter.1
  116.1 31.4 all-gather.2

commit v6 on v5

--- a/solution.py
+++ b/solution.py
@@ -10,6 +10,7 @@
 VMEM = pl.BlockSpec(memory_space=pltpu.VMEM)
 SMEM = pl.BlockSpec(memory_space=pltpu.SMEM)
 PARAMS = pltpu.CompilerParams(vmem_limit_bytes=32 << 20)
+LARGE = pltpu.CompilerParams(vmem_limit_bytes=60 << 20)
 
 
 def position_of(table, value):
@@ -39,20 +40,16 @@
 
 
 def panel_kernel(col_map, local, keep, give, buffer, sems):
-    n_y, panels, slots, thin, size = keep.shape
+    n_y, _, slots, thin, size = keep.shape
     core = lax.axis_index("gz") & 1
-    places = [find(col_map, k) for k in range(2)]
-    if panels == 1:
-        own = lax.axis_index("col") == places[1] // slots
-        places = [jnp.where(own, places[1], places[0])]
     copies = []
-    for k in range(panels):
-        first = pl.multiple_of((places[k] & (slots - 1)) * size, size)
+    for k in range(2):
+        first = pl.multiple_of((find(col_map, k) & (slots - 1)) * size, size)
         copies.append(
             pltpu.make_async_copy(local.at[:, pl.ds(first, size)], buffer.at[k], sems.at[k])
         )
         copies[k].start()
-    for k in range(panels):
+    for k in range(2):
         copies[k].wait()
         for p in range(slots):
             for y in range(n_y):
@@ -61,18 +58,18 @@
                     out[y, k, p] = buffer[k, pl.ds(first, thin), :].astype(jnp.float32)
 
 
-def cut_panels(col_map, local, panels, slots, n_y, thin, size):
-    shape = jax.ShapeDtypeStruct((n_y, panels, slots, thin, size), jnp.float32)
+def cut_panels(col_map, local, slots, n_y, thin, size):
+    shape = jax.ShapeDtypeStruct((n_y, 2, slots, thin, size), jnp.float32)
     return pl.pallas_call(
         panel_kernel,
         out_shape=[shape, shape],
         in_specs=[SMEM, pl.BlockSpec(memory_space=pltpu.HBM)],
         out_specs=[VMEM, VMEM],
         scratch_shapes=[
-            pltpu.VMEM((panels, local.shape[0], size), jnp.bfloat16),
-            pltpu.SemaphoreType.DMA((panels,)),
+            pltpu.VMEM((2, local.shape[0], size), jnp.bfloat16),
+            pltpu.SemaphoreType.DMA((2,)),
         ],
-        compiler_params=PARAMS,
+        compiler_params=LARGE,
     )(col_map, local)
 
 
@@ -188,7 +185,7 @@
             pltpu.VMEM(panels.shape, jnp.float32),
             pltpu.SemaphoreType.DMA((2,)),
         ],
-        compiler_params=PARAMS,
+        compiler_params=LARGE,
     )(block_pattern, row_map, col_map, lower_inv, upper_inv, rows, up0, term0, merged, panels)
 
 
@@ -241,52 +238,41 @@
     def around(step):
         return [(2 * i + c, 2 * ((i + step) % n_y) + c) for i in range(n_y) for c in range(2)]
 
+    keep, give = cut_panels(col_map, local, slots, n_y, thin, size)
+    other = swap(give, "gz", n_gz, 1)
+    other, local = lax.optimization_barrier((other, local))
+    parts = keep + other
+    panel = pick(parts, y, 0)
+    for step in (1, 3, 2):
+        chunk = pick(parts, (y + step) & (n_y - 1), 0)
+        panel = panel + lax.ppermute(chunk, "gz", around(step))
+
     merged = lax.psum_scatter(local.astype(jnp.float32), "gz", scatter_dimension=1, tiled=True)
 
+    corner_rows = row_owner[::-1]
+    corner = jnp.stack([pick(panel[k], row_slot[1 - k], 0) for k in range(2)])
+    for bit in (2, 4):
+        corner = choose(corner, swap(corner, "row", n_row, bit), row, corner_rows, bit)
     mirror = [
         (r * n_col + c, (r ^ 1) * n_col + c ^ (n_col - 1))
         for r in range(n_row)
         for c in range(n_col)
     ]
-    corner_rows = row_owner[::-1]
-    same_half = [bit_of(row, 1) == bit_of(r, 1) for r in corner_rows]
-
-    def gather(panels):
-        keep, give = cut_panels(col_map, local, panels, slots, n_y, thin, size)
-        parts = keep + swap(give, "gz", n_gz, 1)
-        panel = pick(parts, y, 0)
-        for step in (1, 3, 2):
-            chunk = pick(parts, (y + step) & (n_y - 1), 0)
-            panel = panel + lax.ppermute(chunk, "gz", around(step))
-        if panels == 1:
-            second = col == col_owner[1]
-            sources = [jnp.where(second, corner_rows[1], corner_rows[0])]
-            at = [jnp.where(second, row_slot[0], row_slot[1])]
-        else:
-            sources, at = corner_rows, row_slot[::-1]
-        corner = jnp.stack([pick(panel[k], at[k], 0) for k in range(panels)])
-        for bit in (2, 4):
-            other = swap(corner, "row", n_row, bit)
-            corner = choose(corner, other, row, sources, bit)
-        other = lax.ppermute(corner, ("row", "col"), mirror)
-        corner = jnp.stack(
-            [jnp.where(same_half[k], corner[k % panels], other[k % panels]) for k in range(2)]
-        )
-        data = panel.reshape(panels, slots * thin, size)
-        if panels == 1:
-            data = jnp.concatenate([data, data])
-        for bit in (1, 2):
+    corner_other = lax.ppermute(corner, ("row", "col"), mirror)
+    corner = choose(corner, corner_other, row, corner_rows, 1)
+    corner_owner = [
+        jnp.where(bit_of(row, 1) == bit_of(corner_rows[k], 1), c, c ^ (n_col - 1))
+        for k, c in enumerate(col_owner)
+    ]
+
+    data = panel.reshape(2, slots * thin, size)
+    for bit in (1, 2, 4):
+        mine = data
+        if bit < 4:
             second = bit_of(col, bit)
-            other = swap(part(data, 1, ~second), "col", n_col, bit)
-            data = choose(part(data, 1, second), other, col, col_owner, bit)
-        return data, corner
-
-    data, corner = lax.cond(
-        col_owner[0] == col_owner[1], lambda: gather(2), lambda: gather(1)
-    )
-    corner_owner = [
-        jnp.where(same_half[k], col_owner[k], col_owner[k] ^ (n_col - 1)) for k in range(2)
-    ]
+            mine, data = part(data, 1, second), part(data, 1, ~second)
+        data = choose(mine, swap(data, "col", n_col, bit), col, col_owner, bit)
+    corner = choose(corner, swap(corner, "col", n_col, 4), col, corner_owner, 4)
 
     blocks = merged.reshape(slots, size, width)
     rows = jnp.stack([pick(blocks, p, 0) for p in row_slot])
@@ -304,8 +290,6 @@
         thick = data.shape[1]
         return other[:, :thick], choose(corner, other[:, thick:], col, corner_owner, bit)
 
-    other, corner = send_both(data, corner, 4)
-    data = choose(data, other, col, col_owner, 4)
     rows = narrow(rows, 2)
     other, corner = send_both(data, corner, 2)
     data = widen(data, other, col, 2)

time: 163 us -> 152 us (0.933)
  waiting for transfers between devices: 53 us -> 36.7 us
  Pallas kernels: 6.5 us -> 10.8 us
  starting transfers between devices: 72.5 us -> 76 us
  other arithmetic: 7.39 us -> 5.03 us
    ppermute x13 -> x14, waiting for transfers between devices: 47.1 us -> 33.7 us  [swap(): return lax.ppermute(x, axis, [(i, i ^ bit) for i in range(size)])]
    ppermute x4, waiting for transfers between devices: 5.75 us -> 2.98 us  [the longest x3 2.98 us: shards(): panel = panel + lax.ppermute(chunk, 'gz', around(step))]
    pallas_call x1, Pallas kernels: 0.75 us -> 3.5 us  [cut_panels(): pl.pallas_call(panel_kernel, out_shape=[shape, shape], in_specs=[SMEM, pl...]
    ppermute x4, starting transfers between devices: 20.9 us -> 22.8 us  [the longest x1 11.9 us: shards(): corner_other = lax.ppermute(corner, ('row', 'col'), mirror)]
    ppermute x13 -> x14, starting transfers between devices: 51.6 us -> 53.2 us  [swap(): return lax.ppermute(x, axis, [(i, i ^ bit) for i in range(size)])]
  transfers between devices with their start and end apart: 19 -> 20, of which waited for: 14 -> 12; matrix products, arithmetic and copies ran while one was open for 2% -> 2% of each run, Pallas kernels for 1% -> 1%
where the time goes in v6:
time: 152 us; the launch traced here: 150 us
  starting transfers between devices  76 us (50%)
  waiting for transfers between devices  36.7 us (24%)
  between operations  17.7 us (12%)
  Pallas kernels  10.8 us (7%)
  other arithmetic  5.03 us (3%)
  local copies, waits for them, and re-layouts  3.6 us (2%)
    ppermute x14, starting transfers between devices, swap(): return lax.ppermute(x, axis, [(i, i ^ bit) for i in range(size)])  53.2 us
    ppermute x14, waiting for transfers between devices, swap(): return lax.ppermute(x, axis, [(i, i ^ bit) for i in range(size)])  33.7 us
    ppermute x1, starting transfers between devices, shards(): corner_other = lax.ppermute(corner, ('row', 'col'), mirror)  11.9 us
    ppermute x3, starting transfers between devices, shards(): panel = panel + lax.ppermute(chunk, 'gz', around(step))  10.9 us
    pallas_call x1, Pallas kernels, last_terms(): pl.pallas_call(functools.partial(last_kernel, n_y), out_shape=jax.ShapeDt...  5.94 us
    pallas_call x1, Pallas kernels, cut_panels(): pl.pallas_call(panel_kernel, out_shape=[shape, shape], in_specs=[SMEM, pl...  3.5 us
  transfers between devices with their start and end apart: 20, of which 12 were waited for; matrix products, arithmetic and copies ran while one was open for 2% of the time, Pallas kernels for 1%

profile of v6, /device:TPU:6, one launch (start us, length us, event | category | flops | bytes accessed | tf_op | source)
XLA Modules:
  0.0 149.9 jit_solution(13967715775041953771)
XLA Ops:
  6.5 3.5 %shard_map.64 = (f32[4,2,4,32,256]{4,3,2,1,0:T(8,128)}, f32[4,2,4,32,256]{4,3,2,1,0:T(8,128)}) custom-call(s32[32]{0:T(128)} %col_map.5, bf16[1024,1024]{1,0:T(8,128)(2,1)} %bitcast.20), custom_call_target="tpu_custom_call" | custom-call | tf_op jit(solution)/shard_map/pallas_call | solution.py:63
  10.0 1.9 %collective-permute-start = (f32[4,2,4,32,256]{4,3,2,1,0:T(8,128)}, f32[4,2,4,32,256]{4,3,2,1,0:T(8,128)S(1)}, u32[]{:S(2)}, u32[]{:S(2)}) collective-permute-start(f32[4,2,4,32,256]{4,3,2,1,0:T(8,128)} %get-tuple-element.16), channel_id=1, source_target_pairs={{0,64},{64,0},{128,192},{192,128},{256,320},{320,256},{384,448},{4... | collective-permute-start | bytes 3145736 | tf_op jit(solution)/shard_map/ppermute | solution.py:193
  12.0 2.8 %collective-permute-done = f32[4,2,4,32,256]{4,3,2,1,0:T(8,128)S(1)} collective-permute-done((f32[4,2,4,32,256]{4,3,2,1,0:T(8,128)}, f32[4,2,4,32,256]{4,3,2,1,0:T(8,128)S(1)}, u32[]{:S(2)}, u32[]{:S(2)}) %collective-permute-start) | collective-permute-done | bytes 1048608 | tf_op jit(solution)/shard_map/ppermute | solution.py:193
  14.8 2.4 %convert_element_type.28 = f32[1024,1024]{1,0:T(8,128)} convert(bf16[1024,1024]{1,0:T(8,128)(2,1)S(1)} %bitcast.21) | non-fusion elementwise | flops 1048576 | bytes 6291456 | tf_op jit(solution)/shard_map/convert_element_type | solution.py:250
  17.3 0.0 reduce-scatter.2.cloned.1.call-update
  17.3 0.0 all-gather.3.cloned.1.call-start
  17.4 1.1 copy-done.8
  18.5 0.1 add.23
  18.6 0.1 dynamic-slice_bitcast_fusion.2
  18.7 5.1 %collective-permute-start.3 = (f32[2,4,32,256]{3,2,1,0:T(8,128)S(1)}, f32[2,4,32,256]{3,2,1,0:T(8,128)S(1)}, u32[]{:S(2)}, u32[]{:S(2)}) collective-permute-start(f32[2,4,32,256]{3,2,1,0:T(8,128)S(1)} %get-tuple-element.30), channel_id=1, source_target_pairs={{0,256},{64,320},{128,384},{192,448},{256,0},{320,64},{384,128},{4... | collective-permute-start | bytes 786440 | tf_op jit(solution)/shard_map/ppermute | solution.py:248
  23.8 3.0 %collective-permute-start.2 = (f32[2,4,32,256]{3,2,1,0:T(8,128)S(1)}, f32[2,4,32,256]{3,2,1,0:T(8,128)S(1)}, u32[]{:S(2)}, u32[]{:S(2)}) collective-permute-start(f32[2,4,32,256]{3,2,1,0:T(8,128)S(1)} %get-tuple-element.31), channel_id=1, source_target_pairs={{0,384},{64,448},{128,0},{192,64},{256,128},{320,192},{384,256},{4... | collective-permute-start | bytes 786440 | tf_op jit(solution)/shard_map/ppermute | solution.py:248
  26.8 2.9 %collective-permute-start.1 = (f32[2,4,32,256]{3,2,1,0:T(8,128)S(1)}, f32[2,4,32,256]{3,2,1,0:T(8,128)S(1)}, u32[]{:S(2)}, u32[]{:S(2)}) collective-permute-start(f32[2,4,32,256]{3,2,1,0:T(8,128)S(1)} %get-tuple-element.29), channel_id=1, source_target_pairs={{0,128},{64,192},{128,256},{192,320},{256,384},{320,448},{384,0},{... | collective-permute-start | bytes 786440 | tf_op jit(solution)/shard_map/ppermute | solution.py:248
  29.7 0.6 fusion.11
  32.7 0.6 fusion.9
  34.7 1.7 %collective-permute-done.2 = f32[2,4,32,256]{3,2,1,0:T(8,128)S(1)} collective-permute-done((f32[2,4,32,256]{3,2,1,0:T(8,128)S(1)}, f32[2,4,32,256]{3,2,1,0:T(8,128)S(1)}, u32[]{:S(2)}, u32[]{:S(2)}) %collective-permute-start.2) | collective-permute-done | bytes 262176 | tf_op jit(solution)/shard_map/ppermute | solution.py:248
  36.4 1.2 collective-permute-done.1
  37.7 0.1 fusion.1
  37.8 2.7 %collective-permute-start.7 = (f32[2,32,256]{2,1,0:T(8,128)S(1)}, f32[2,32,256]{2,1,0:T(8,128)S(1)}, u32[]{:S(2)}, u32[]{:S(2)}) collective-permute-start(f32[2,32,256]{2,1,0:T(8,128)S(1)} %pad_maximum_fusion.3), channel_id=1, source_target_pairs={{0,16},{8,24},{16,0},{24,8},{32,48},{40,56},{48,32},{56,40},{1,17}... | collective-permute-start | bytes 196616 | tf_op jit(solution)/shard_map/ppermute | solution.py:193
  40.6 3.8 %collective-permute-start.4 = (f32[2,64,256]{2,1,0:T(8,128)S(1)}, f32[2,64,256]{2,1,0:T(8,128)S(1)}, u32[]{:S(2)}, u32[]{:S(2)}) collective-permute-start(f32[2,64,256]{2,1,0:T(8,128)S(1)} %constant_dynamic-slice_fusion.3), channel_id=1, source_target_pairs={{0,1},{1,0},{2,3},{3,2},{4,5},{5,4},{6,7},{7,6},{8,9},{9,8},{10,11... | collective-permute-start | bytes 393224 | tf_op jit(solution)/shard_map/ppermute | solution.py:193
  44.5 5.2 %collective-permute-start.8 = (f32[2,32,256]{2,1,0:T(8,128)S(1)}, f32[2,32,256]{2,1,0:T(8,128)S(1)}, u32[]{:S(2)}, u32[]{:S(2)}) collective-permute-start(f32[2,32,256]{2,1,0:T(8,128)S(1)} %pad_maximum_fusion.4), channel_id=1, source_target_pairs={{0,32},{8,40},{16,48},{24,56},{32,0},{40,8},{48,16},{56,24},{1,33}... | collective-permute-start | bytes 196616 | tf_op jit(solution)/shard_map/ppermute | solution.py:193
  49.7 3.0 %collective-permute-start.5 = (f32[2,32,256]{2,1,0:T(8,128)S(1)}, f32[2,32,256]{2,1,0:T(8,128)S(1)}, u32[]{:S(2)}, u32[]{:S(2)}) collective-permute-start(f32[2,32,256]{2,1,0:T(8,128)S(1)} %get-tuple-element.53), channel_id=1, source_target_pairs={{0,2},{1,3},{2,0},{3,1},{4,6},{5,7},{6,4},{7,5},{8,10},{9,11},{10,... | collective-permute-start | bytes 196616 | tf_op jit(solution)/shard_map/ppermute | solution.py:193
  52.8 11.9 %collective-permute-start.9 = (f32[2,32,256]{2,1,0:T(8,128)S(1)}, f32[2,32,256]{2,1,0:T(8,128)S(1)}, u32[]{:S(2)}, u32[]{:S(2)}) collective-permute-start(f32[2,32,256]{2,1,0:T(8,128)S(1)} %pad_maximum_fusion.5), channel_id=1, source_target_pairs={{0,15},{1,14},{2,13},{3,12},{4,11},{5,10},{6,9},{7,8},{8,7},{9,6},... | collective-permute-start | bytes 196616 | tf_op jit(solution)/shard_map/ppermute | solution.py:261
  64.7 6.9 %collective-permute-start.6 = (f32[2,32,256]{2,1,0:T(8,128)S(1)}, f32[2,32,256]{2,1,0:T(8,128)S(1)}, u32[]{:S(2)}, u32[]{:S(2)}) collective-permute-start(f32[2,32,256]{2,1,0:T(8,128)S(1)} %pad_maximum_fusion.2), channel_id=1, source_target_pairs={{0,4},{1,5},{2,6},{3,7},{4,0},{5,1},{6,2},{7,3},{8,12},{9,13},{10,... | collective-permute-start | bytes 196616 | tf_op jit(solution)/shard_map/ppermute | solution.py:193
  71.7 3.2 %collective-permute-start.10 = (f32[2,32,256]{2,1,0:T(8,128)S(1)}, f32[2,32,256]{2,1,0:T(8,128)S(1)}, u32[]{:S(2)}, u32[]{:S(2)}) collective-permute-start(f32[2,32,256]{2,1,0:T(8,128)S(1)} %pad_maximum_fusion.6), channel_id=1, source_target_pairs={{0,4},{1,5},{2,6},{3,7},{4,0},{5,1},{6,2},{7,3},{8,12},{9,13},{10,... | collective-permute-start | bytes 196616 | tf_op jit(solution)/shard_map/ppermute | solution.py:193
  74.9 4.1 %collective-permute-done.6 = f32[2,32,256]{2,1,0:T(8,128)S(1)} collective-permute-done((f32[2,32,256]{2,1,0:T(8,128)S(1)}, f32[2,32,256]{2,1,0:T(8,128)S(1)}, u32[]{:S(2)}, u32[]{:S(2)}) %collective-permute-start.6) | collective-permute-done | bytes 65568 | tf_op jit(solution)/shard_map/ppermute | solution.py:193
  79.1 3.5 %collective-permute-done.10 = f32[2,32,256]{2,1,0:T(8,128)S(1)} collective-permute-done((f32[2,32,256]{2,1,0:T(8,128)S(1)}, f32[2,32,256]{2,1,0:T(8,128)S(1)}, u32[]{:S(2)}, u32[]{:S(2)}) %collective-permute-start.10) | collective-permute-done | bytes 65568 | tf_op jit(solution)/shard_map/ppermute | solution.py:193
  82.6 1.9 %collective-permute-start.11 = (f32[2,64,256]{2,1,0:T(8,128)S(1)}, f32[2,64,256]{2,1,0:T(8,128)S(1)}, u32[]{:S(2)}, u32[]{:S(2)}) collective-permute-start(f32[2,64,256]{2,1,0:T(8,128)S(1)} %maximum_maximum_fusion.2), channel_id=1, source_target_pairs={{0,2},{1,3},{2,0},{3,1},{4,6},{5,7},{6,4},{7,5},{8,10},{9,11},{10,... | collective-permute-start | bytes 393224 | tf_op jit(solution)/shard_map/ppermute | solution.py:193
  84.5 0.0 reduce-scatter.2.cloned.1.call-done.merged
  84.6 1.0 constant_dynamic-slice_fusion.1
  85.6 3.1 %collective-permute-start.12 = (f32[2,128,128]{2,1,0:T(8,128)S(1)}, f32[2,128,128]{2,1,0:T(8,128)S(1)}, u32[]{:S(2)}, u32[]{:S(2)}) collective-permute-start(f32[2,128,128]{2,1,0:T(8,128)S(1)} %get-tuple-element.39), channel_id=1, source_target_pairs={{0,16},{8,24},{16,0},{24,8},{32,48},{40,56},{48,32},{56,40},{1,17}... | collective-permute-start | bytes 393224 | tf_op jit(solution)/shard_map/ppermute | solution.py:193
  88.8 2.3 %collective-permute-done.11 = f32[2,64,256]{2,1,0:T(8,128)S(1)} collective-permute-done((f32[2,64,256]{2,1,0:T(8,128)S(1)}, f32[2,64,256]{2,1,0:T(8,128)S(1)}, u32[]{:S(2)}, u32[]{:S(2)}) %collective-permute-start.11) | collective-permute-done | bytes 131104 | tf_op jit(solution)/shard_map/ppermute | solution.py:193
  91.1 1.5 %collective-permute-done.12 = f32[2,128,128]{2,1,0:T(8,128)S(1)} collective-permute-done((f32[2,128,128]{2,1,0:T(8,128)S(1)}, f32[2,128,128]{2,1,0:T(8,128)S(1)}, u32[]{:S(2)}, u32[]{:S(2)}) %collective-permute-start.12) | collective-permute-done | bytes 131104 | tf_op jit(solution)/shard_map/ppermute | solution.py:193
  92.7 3.8 %collective-permute-start.14 = (f32[2,64,128]{2,1,0:T(8,128)S(1)}, f32[2,64,128]{2,1,0:T(8,128)S(1)}, u32[]{:S(2)}, u32[]{:S(2)}) collective-permute-start(f32[2,64,128]{2,1,0:T(8,128)S(1)} %constant_dynamic-slice_fusion), channel_id=1, source_target_pairs={{0,32},{8,40},{16,48},{24,56},{32,0},{40,8},{48,16},{56,24},{1,33}... | collective-permute-start | bytes 196616 | tf_op jit(solution)/shard_map/ppermute | solution.py:193
  96.5 1.9 %collective-permute-start.13 = (f32[2,96,256]{2,1,0:T(8,128)S(1)}, f32[2,96,256]{2,1,0:T(8,128)S(1)}, u32[]{:S(2)}, u32[]{:S(2)}) collective-permute-start(f32[2,96,256]{2,1,0:T(8,128)S(1)} %maximum_maximum_fusion.1), channel_id=1, source_target_pairs={{0,1},{1,0},{2,3},{3,2},{4,5},{5,4},{6,7},{7,6},{8,9},{9,8},{10,11... | collective-permute-start | bytes 589832 | tf_op jit(solution)/shard_map/ppermute | solution.py:193
  98.5 1.9 %collective-permute-done.14 = f32[2,64,128]{2,1,0:T(8,128)S(1)} collective-permute-done((f32[2,64,128]{2,1,0:T(8,128)S(1)}, f32[2,64,128]{2,1,0:T(8,128)S(1)}, u32[]{:S(2)}, u32[]{:S(2)}) %collective-permute-start.14) | collective-permute-done | bytes 65568 | tf_op jit(solution)/shard_map/ppermute | solution.py:193
  100.4 3.7 %collective-permute-done.13 = f32[2,96,256]{2,1,0:T(8,128)S(1)} collective-permute-done((f32[2,96,256]{2,1,0:T(8,128)S(1)}, f32[2,96,256]{2,1,0:T(8,128)S(1)}, u32[]{:S(2)}, u32[]{:S(2)}) %collective-permute-start.13) | collective-permute-done | bytes 196640 | tf_op jit(solution)/shard_map/ppermute | solution.py:193
  104.2 0.7 maximum_maximum_fusion
  104.9 0.0 all-gather.3.cloned.1.call-update
  104.9 9.4 %collective-permute-start.15 = (f32[2,64,128]{2,1,0:T(8,128)S(1)}, f32[2,64,128]{2,1,0:T(8,128)S(1)}, u32[]{:S(2)}, u32[]{:S(2)}) collective-permute-start(f32[2,64,128]{2,1,0:T(8,128)S(1)} %pad_maximum_fusion.7), channel_id=1, source_target_pairs={{0,8},{8,0},{16,24},{24,16},{32,40},{40,32},{48,56},{56,48},{1,9},... | collective-permute-start | bytes 196616 | tf_op jit(solution)/shard_map/ppermute | solution.py:193
  114.4 5.4 %collective-permute-done.15 = f32[2,64,128]{2,1,0:T(8,128)S(1)} collective-permute-done((f32[2,64,128]{2,1,0:T(8,128)S(1)}, f32[2,64,128]{2,1,0:T(8,128)S(1)}, u32[]{:S(2)}, u32[]{:S(2)}) %collective-permute-start.15) | collective-permute-done | bytes 65568 | tf_op jit(solution)/shard_map/ppermute | solution.py:193
  119.9 3.5 %collective-permute-start.16 = (f32[2,64,128]{2,1,0:T(8,128)S(1)}, f32[2,64,128]{2,1,0:T(8,128)S(1)}, u32[]{:S(2)}, u32[]{:S(2)}) collective-permute-start(f32[2,64,128]{2,1,0:T(8,128)S(1)} %pad_maximum_fusion.8), channel_id=1, source_target_pairs={{0,32},{8,40},{16,48},{24,56},{32,0},{40,8},{48,16},{56,24},{1,33}... | collective-permute-start | bytes 196616 | tf_op jit(solution)/shard_map/ppermute | solution.py:193
  123.4 4.1 %collective-permute-done.16 = f32[2,64,128]{2,1,0:T(8,128)S(1)} collective-permute-done((f32[2,64,128]{2,1,0:T(8,128)S(1)}, f32[2,64,128]{2,1,0:T(8,128)S(1)}, u32[]{:S(2)}, u32[]{:S(2)}) %collective-permute-start.16) | collective-permute-done | bytes 65568 | tf_op jit(solution)/shard_map/ppermute | solution.py:193
  127.5 2.6 %collective-permute-start.17 = (f32[2,128,128]{2,1,0:T(8,128)S(1)}, f32[2,128,128]{2,1,0:T(8,128)S(1)}, u32[]{:S(2)}, u32[]{:S(2)}) collective-permute-start(f32[2,128,128]{2,1,0:T(8,128)S(1)} %maximum_select_fusion.2), channel_id=1, source_target_pairs={{0,16},{8,24},{16,0},{24,8},{32,48},{40,56},{48,32},{56,40},{1,17}... | collective-permute-start | bytes 393224 | tf_op jit(solution)/shard_map/ppermute | solution.py:193
  130.1 4.3 %collective-permute-done.17 = f32[2,128,128]{2,1,0:T(8,128)S(1)} collective-permute-done((f32[2,128,128]{2,1,0:T(8,128)S(1)}, f32[2,128,128]{2,1,0:T(8,128)S(1)}, u32[]{:S(2)}, u32[]{:S(2)}) %collective-permute-start.17) | collective-permute-done | bytes 131104 | tf_op jit(solution)/shard_map/ppermute | solution.py:193
  134.5 1.4 shard_map.65
  135.8 0.6 copy-done.3
  136.5 0.7 copy-done.4
  137.1 5.9 %shard_map.66 = bf16[1024,128]{1,0:T(8,128)(2,1)} custom-call(s32[32,32]{1,0:T(8,128)} %block_pattern.3, s32[32]{0:T(128)} %row_map.1, s32[32]{0:T(128)} %col_map.5, f32[2,256,256]{2,1,0:T(8,128)} %lower_inv.3, f32[2,256,256]{2,1,0:T(8,128)} %upper_inv.3, f32[2,256,128]{2,1,0:T(8,128)} %copy-done, f32[256,128]{1,0:T(8,128)} %copy-done.3, ...), custom_call_target="tpu_custom_call" | custom-call | tf_op jit(solution)/shard_map/pallas_call | solution.py:177
  (59 shorter events, 0.5 us)
Async XLA Ops:
  6.5 8.3 %copy-start.7 = (bf16[1,1024,1024]{2,1,0:T(8,128)(2,1)S(1)}, bf16[1,1024,1024]{2,1,0:T(8,128)(2,1)}, u32[]{:S(2)}) copy-start(bf16[1,1024,1024]{2,1,0:T(8,128)(2,1)} %param.6) | copy-start | bytes 6291460
  6.5 78.0 %reduce-scatter.2.cloned.1.call-start = ((), (), s32[]{:S(2)}) async-start(), calls=%async_computation.1 | async-start | bytes 4718592 | tf_op jit(solution)/shard_map/reduce_scatter | solution.py:250
  10.0 4.8 %collective-permute-start = (f32[4,2,4,32,256]{4,3,2,1,0:T(8,128)}, f32[4,2,4,32,256]{4,3,2,1,0:T(8,128)S(1)}, u32[]{:S(2)}, u32[]{:S(2)}) collective-permute-start(f32[4,2,4,32,256]{4,3,2,1,0:T(8,128)} %get-tuple-element.16), channel_id=1, source_target_pairs={{0,64},{64,0},{128,192},{192,128},{256,320},{320,256},{384,448},{4... | collective-permute-start | bytes 3145736 | tf_op jit(solution)/shard_map/ppermute | solution.py:193
  17.2 1.2 copy-start.8
  17.3 12.4 %copy-start.9 = (s32[32]{0:T(128)S(1)}, s32[32]{0:T(128)}, u32[]{:S(2)}) copy-start(s32[32]{0:T(128)} %row_map.1) | copy-start | bytes 388
  17.3 15.4 %copy-start.6 = (s32[32]{0:T(128)S(1)}, s32[32]{0:T(128)}, u32[]{:S(2)}) copy-start(s32[32]{0:T(128)} %col_map.5) | copy-start | bytes 388
  17.3 119.8 %all-gather.3.cloned.1.call-start = ((), (), s32[]{:S(2)}) async-start(), calls=%async_computation.2 | async-start | bytes 2949120 | tf_op jit(solution)/shard_map/all_gather | solution.py:301
  18.7 16.0 %collective-permute-start.3 = (f32[2,4,32,256]{3,2,1,0:T(8,128)S(1)}, f32[2,4,32,256]{3,2,1,0:T(8,128)S(1)}, u32[]{:S(2)}, u32[]{:S(2)}) collective-permute-start(f32[2,4,32,256]{3,2,1,0:T(8,128)S(1)} %get-tuple-element.30), channel_id=1, source_target_pairs={{0,256},{64,320},{128,384},{192,448},{256,0},{320,64},{384,128},{4... | collective-permute-start | bytes 786440 | tf_op jit(solution)/shard_map/ppermute | solution.py:248
  23.8 12.6 %collective-permute-start.2 = (f32[2,4,32,256]{3,2,1,0:T(8,128)S(1)}, f32[2,4,32,256]{3,2,1,0:T(8,128)S(1)}, u32[]{:S(2)}, u32[]{:S(2)}) collective-permute-start(f32[2,4,32,256]{3,2,1,0:T(8,128)S(1)} %get-tuple-element.31), channel_id=1, source_target_pairs={{0,384},{64,448},{128,0},{192,64},{256,128},{320,192},{384,256},{4... | collective-permute-start | bytes 786440 | tf_op jit(solution)/shard_map/ppermute | solution.py:248
  26.8 10.9 %collective-permute-start.1 = (f32[2,4,32,256]{3,2,1,0:T(8,128)S(1)}, f32[2,4,32,256]{3,2,1,0:T(8,128)S(1)}, u32[]{:S(2)}, u32[]{:S(2)}) collective-permute-start(f32[2,4,32,256]{3,2,1,0:T(8,128)S(1)} %get-tuple-element.29), channel_id=1, source_target_pairs={{0,128},{64,192},{128,256},{192,320},{256,384},{320,448},{384,0},{... | collective-permute-start | bytes 786440 | tf_op jit(solution)/shard_map/ppermute | solution.py:248
  37.8 6.6 %collective-permute-start.7 = (f32[2,32,256]{2,1,0:T(8,128)S(1)}, f32[2,32,256]{2,1,0:T(8,128)S(1)}, u32[]{:S(2)}, u32[]{:S(2)}) collective-permute-start(f32[2,32,256]{2,1,0:T(8,128)S(1)} %pad_maximum_fusion.3), channel_id=1, source_target_pairs={{0,16},{8,24},{16,0},{24,8},{32,48},{40,56},{48,32},{56,40},{1,17}... | collective-permute-start | bytes 196616 | tf_op jit(solution)/shard_map/ppermute | solution.py:193
  40.6 9.1 %collective-permute-start.4 = (f32[2,64,256]{2,1,0:T(8,128)S(1)}, f32[2,64,256]{2,1,0:T(8,128)S(1)}, u32[]{:S(2)}, u32[]{:S(2)}) collective-permute-start(f32[2,64,256]{2,1,0:T(8,128)S(1)} %constant_dynamic-slice_fusion.3), channel_id=1, source_target_pairs={{0,1},{1,0},{2,3},{3,2},{4,5},{5,4},{6,7},{7,6},{8,9},{9,8},{10,11... | collective-permute-start | bytes 393224 | tf_op jit(solution)/shard_map/ppermute | solution.py:193
  44.5 8.3 %collective-permute-start.8 = (f32[2,32,256]{2,1,0:T(8,128)S(1)}, f32[2,32,256]{2,1,0:T(8,128)S(1)}, u32[]{:S(2)}, u32[]{:S(2)}) collective-permute-start(f32[2,32,256]{2,1,0:T(8,128)S(1)} %pad_maximum_fusion.4), channel_id=1, source_target_pairs={{0,32},{8,40},{16,48},{24,56},{32,0},{40,8},{48,16},{56,24},{1,33}... | collective-permute-start | bytes 196616 | tf_op jit(solution)/shard_map/ppermute | solution.py:193
  49.7 15.0 %collective-permute-start.5 = (f32[2,32,256]{2,1,0:T(8,128)S(1)}, f32[2,32,256]{2,1,0:T(8,128)S(1)}, u32[]{:S(2)}, u32[]{:S(2)}) collective-permute-start(f32[2,32,256]{2,1,0:T(8,128)S(1)} %get-tuple-element.53), channel_id=1, source_target_pairs={{0,2},{1,3},{2,0},{3,1},{4,6},{5,7},{6,4},{7,5},{8,10},{9,11},{10,... | collective-permute-start | bytes 196616 | tf_op jit(solution)/shard_map/ppermute | solution.py:193
  52.8 18.9 %collective-permute-start.9 = (f32[2,32,256]{2,1,0:T(8,128)S(1)}, f32[2,32,256]{2,1,0:T(8,128)S(1)}, u32[]{:S(2)}, u32[]{:S(2)}) collective-permute-start(f32[2,32,256]{2,1,0:T(8,128)S(1)} %pad_maximum_fusion.5), channel_id=1, source_target_pairs={{0,15},{1,14},{2,13},{3,12},{4,11},{5,10},{6,9},{7,8},{8,7},{9,6},... | collective-permute-start | bytes 196616 | tf_op jit(solution)/shard_map/ppermute | solution.py:261
  64.7 14.3 %collective-permute-start.6 = (f32[2,32,256]{2,1,0:T(8,128)S(1)}, f32[2,32,256]{2,1,0:T(8,128)S(1)}, u32[]{:S(2)}, u32[]{:S(2)}) collective-permute-start(f32[2,32,256]{2,1,0:T(8,128)S(1)} %pad_maximum_fusion.2), channel_id=1, source_target_pairs={{0,4},{1,5},{2,6},{3,7},{4,0},{5,1},{6,2},{7,3},{8,12},{9,13},{10,... | collective-permute-start | bytes 196616 | tf_op jit(solution)/shard_map/ppermute | solution.py:193
  71.7 10.9 %collective-permute-start.10 = (f32[2,32,256]{2,1,0:T(8,128)S(1)}, f32[2,32,256]{2,1,0:T(8,128)S(1)}, u32[]{:S(2)}, u32[]{:S(2)}) collective-permute-start(f32[2,32,256]{2,1,0:T(8,128)S(1)} %pad_maximum_fusion.6), channel_id=1, source_target_pairs={{0,4},{1,5},{2,6},{3,7},{4,0},{5,1},{6,2},{7,3},{8,12},{9,13},{10,... | collective-permute-start | bytes 196616 | tf_op jit(solution)/shard_map/ppermute | solution.py:193
  82.6 8.5 %collective-permute-start.11 = (f32[2,64,256]{2,1,0:T(8,128)S(1)}, f32[2,64,256]{2,1,0:T(8,128)S(1)}, u32[]{:S(2)}, u32[]{:S(2)}) collective-permute-start(f32[2,64,256]{2,1,0:T(8,128)S(1)} %maximum_maximum_fusion.2), channel_id=1, source_target_pairs={{0,2},{1,3},{2,0},{3,1},{4,6},{5,7},{6,4},{7,5},{8,10},{9,11},{10,... | collective-permute-start | bytes 393224 | tf_op jit(solution)/shard_map/ppermute | solution.py:193
  85.6 48.8 %copy-start.1 = (f32[2,256,256]{2,1,0:T(8,128)S(1)}, f32[2,256,256]{2,1,0:T(8,128)}, u32[]{:S(2)}) copy-start(f32[2,256,256]{2,1,0:T(8,128)} %lower_inv.3) | copy-start | bytes 1572868
  85.6 48.8 %copy-start.2 = (f32[2,256,256]{2,1,0:T(8,128)S(1)}, f32[2,256,256]{2,1,0:T(8,128)}, u32[]{:S(2)}) copy-start(f32[2,256,256]{2,1,0:T(8,128)} %upper_inv.3) | copy-start | bytes 1572868
  85.6 48.8 %copy-start.5 = (s32[32,32]{1,0:T(8,128)S(1)}, s32[32,32]{1,0:T(8,128)}, u32[]{:S(2)}) copy-start(s32[32,32]{1,0:T(8,128)} %block_pattern.3) | copy-start | bytes 12292
  85.6 7.0 %collective-permute-start.12 = (f32[2,128,128]{2,1,0:T(8,128)S(1)}, f32[2,128,128]{2,1,0:T(8,128)S(1)}, u32[]{:S(2)}, u32[]{:S(2)}) collective-permute-start(f32[2,128,128]{2,1,0:T(8,128)S(1)} %get-tuple-element.39), channel_id=1, source_target_pairs={{0,16},{8,24},{16,0},{24,8},{32,48},{40,56},{48,32},{56,40},{1,17}... | collective-permute-start | bytes 393224 | tf_op jit(solution)/shard_map/ppermute | solution.py:193
  92.7 7.7 %collective-permute-start.14 = (f32[2,64,128]{2,1,0:T(8,128)S(1)}, f32[2,64,128]{2,1,0:T(8,128)S(1)}, u32[]{:S(2)}, u32[]{:S(2)}) collective-permute-start(f32[2,64,128]{2,1,0:T(8,128)S(1)} %constant_dynamic-slice_fusion), channel_id=1, source_target_pairs={{0,32},{8,40},{16,48},{24,56},{32,0},{40,8},{48,16},{56,24},{1,33}... | collective-permute-start | bytes 196616 | tf_op jit(solution)/shard_map/ppermute | solution.py:193
  96.5 7.6 %collective-permute-start.13 = (f32[2,96,256]{2,1,0:T(8,128)S(1)}, f32[2,96,256]{2,1,0:T(8,128)S(1)}, u32[]{:S(2)}, u32[]{:S(2)}) collective-permute-start(f32[2,96,256]{2,1,0:T(8,128)S(1)} %maximum_maximum_fusion.1), channel_id=1, source_target_pairs={{0,1},{1,0},{2,3},{3,2},{4,5},{5,4},{6,7},{7,6},{8,9},{9,8},{10,11... | collective-permute-start | bytes 589832 | tf_op jit(solution)/shard_map/ppermute | solution.py:193
  104.9 14.9 %collective-permute-start.15 = (f32[2,64,128]{2,1,0:T(8,128)S(1)}, f32[2,64,128]{2,1,0:T(8,128)S(1)}, u32[]{:S(2)}, u32[]{:S(2)}) collective-permute-start(f32[2,64,128]{2,1,0:T(8,128)S(1)} %pad_maximum_fusion.7), channel_id=1, source_target_pairs={{0,8},{8,0},{16,24},{24,16},{32,40},{40,32},{48,56},{56,48},{1,9},... | collective-permute-start | bytes 196616 | tf_op jit(solution)/shard_map/ppermute | solution.py:193
  119.9 7.7 %collective-permute-start.16 = (f32[2,64,128]{2,1,0:T(8,128)S(1)}, f32[2,64,128]{2,1,0:T(8,128)S(1)}, u32[]{:S(2)}, u32[]{:S(2)}) collective-permute-start(f32[2,64,128]{2,1,0:T(8,128)S(1)} %pad_maximum_fusion.8), channel_id=1, source_target_pairs={{0,32},{8,40},{16,48},{24,56},{32,0},{40,8},{48,16},{56,24},{1,33}... | collective-permute-start | bytes 196616 | tf_op jit(solution)/shard_map/ppermute | solution.py:193
  127.5 6.9 %collective-permute-start.17 = (f32[2,128,128]{2,1,0:T(8,128)S(1)}, f32[2,128,128]{2,1,0:T(8,128)S(1)}, u32[]{:S(2)}, u32[]{:S(2)}) collective-permute-start(f32[2,128,128]{2,1,0:T(8,128)S(1)} %maximum_select_fusion.2), channel_id=1, source_target_pairs={{0,16},{8,24},{16,0},{24,8},{32,48},{40,56},{48,32},{56,40},{1,17}... | collective-permute-start | bytes 393224 | tf_op jit(solution)/shard_map/ppermute | solution.py:193
  134.5 2.7 %copy-start = (f32[2,256,128]{2,1,0:T(8,128)}, f32[2,256,128]{2,1,0:T(8,128)S(1)}, u32[]{:S(2)}) copy-start(f32[2,256,128]{2,1,0:T(8,128)S(1)} %maximum_select_fusion.1.rows) | copy-start | bytes 786436
  135.8 0.6 copy-start.3
  136.5 0.7 copy-start.4
Sparse Core Ops, SparseCore 0:
  17.4 49.9 reduce-scatter.1
  105.1 30.4 all-gather.2

commit v7 on v6

--- a/solution.py
+++ b/solution.py
@@ -69,7 +69,7 @@
             pltpu.VMEM((2, local.shape[0], size), jnp.bfloat16),
             pltpu.SemaphoreType.DMA((2,)),
         ],
-        compiler_params=LARGE,
+        compiler_params=PARAMS,
     )(col_map, local)
 
 
@@ -242,66 +242,62 @@
     other = swap(give, "gz", n_gz, 1)
     other, local = lax.optimization_barrier((other, local))
     parts = keep + other
-    panel = pick(parts, y, 0)
-    for step in (1, 3, 2):
-        chunk = pick(parts, (y + step) & (n_y - 1), 0)
-        panel = panel + lax.ppermute(chunk, "gz", around(step))
+    arrived = [
+        lax.ppermute(pick(parts, (y + step) & (n_y - 1), 0), "gz", around(step))
+        for step in (1, 3, 2)
+    ]
+    panel = pick(parts, y, 0) + (arrived[0] + arrived[1] + arrived[2])
 
     merged = lax.psum_scatter(local.astype(jnp.float32), "gz", scatter_dimension=1, tiled=True)
 
+    corner = jnp.stack([pick(panel[k], row_slot[1 - k], 0) for k in range(2)])
+    data = panel.reshape(2, slots * thin, size)
+
+    def send_both(data, extra, axis, length, bit):
+        other = swap(jnp.concatenate([data, extra], 1), axis, length, bit)
+        return other[:, : data.shape[1]], other[:, data.shape[1] :]
+
+    for bit in (1, 2, 4):
+        mine = data
+        if bit < 4:
+            second = bit_of(col, bit)
+            mine, data = part(data, 1, second), part(data, 1, ~second)
+        other, extra = send_both(data, corner, "col", n_col, bit)
+        data = choose(mine, other, col, col_owner, bit)
+        corner = choose(corner, extra, col, col_owner, bit)
+
     corner_rows = row_owner[::-1]
-    corner = jnp.stack([pick(panel[k], row_slot[1 - k], 0) for k in range(2)])
-    for bit in (2, 4):
-        corner = choose(corner, swap(corner, "row", n_row, bit), row, corner_rows, bit)
     mirror = [
         (r * n_col + c, (r ^ 1) * n_col + c ^ (n_col - 1))
         for r in range(n_row)
         for c in range(n_col)
     ]
-    corner_other = lax.ppermute(corner, ("row", "col"), mirror)
-    corner = choose(corner, corner_other, row, corner_rows, 1)
-    corner_owner = [
-        jnp.where(bit_of(row, 1) == bit_of(corner_rows[k], 1), c, c ^ (n_col - 1))
-        for k, c in enumerate(col_owner)
-    ]
-
-    data = panel.reshape(2, slots * thin, size)
-    for bit in (1, 2, 4):
-        mine = data
-        if bit < 4:
-            second = bit_of(col, bit)
-            mine, data = part(data, 1, second), part(data, 1, ~second)
-        data = choose(mine, swap(data, "col", n_col, bit), col, col_owner, bit)
-    corner = choose(corner, swap(corner, "col", n_col, 4), col, corner_owner, 4)
+    corner = choose(corner, lax.ppermute(corner, ("row", "col"), mirror), row, corner_rows, 1)
 
     blocks = merged.reshape(slots, size, width)
     rows = jnp.stack([pick(blocks, p, 0) for p in row_slot])
-
-    def narrow(rows, bit):
+    corner = jnp.concatenate([corner[..., :width], corner[..., width:]], 1)
+
+    def narrow(rows, corner, bit):
         second = bit_of(row, bit)
-        other = swap(part(rows, 1, ~second), "row", n_row, bit)
-        return choose(part(rows, 1, second), other, row, row_owner, bit)
-
-    def widen(x, other, me, bit):
-        return join(x, other, 1, bit_of(me, bit))
-
-    def send_both(data, corner, bit):
-        other = swap(jnp.concatenate([data, corner], 1), "col", n_col, bit)
-        thick = data.shape[1]
-        return other[:, :thick], choose(corner, other[:, thick:], col, corner_owner, bit)
-
-    rows = narrow(rows, 2)
-    other, corner = send_both(data, corner, 2)
-    data = widen(data, other, col, 2)
-    data, rows = lax.optimization_barrier((data, rows))
-    rows = narrow(rows, 4)
-    other, corner = send_both(data, corner, 1)
-    data = jnp.concatenate([widen(data, other, col, 1), corner], 1)
-    data, rows = lax.optimization_barrier((data, rows))
+        other, extra = send_both(part(rows, 1, ~second), corner, "row", n_row, bit)
+        rows = choose(part(rows, 1, second), other, row, row_owner, bit)
+        return rows, choose(corner, extra, row, corner_rows, bit)
+
+    def widen(x, axis, length, me, bit):
+        return join(x, swap(x, axis, length, bit), 1, bit_of(me, bit))
+
+    data = widen(data, "col", n_col, col, 2)
+    data, corner = lax.optimization_barrier((data, corner))
+    rows, corner = narrow(rows, corner, 2)
+    data = widen(data, "col", n_col, col, 1)
+    rows, corner = narrow(rows, corner, 4)
+    corner = jnp.concatenate([corner[:, :thin], corner[:, thin:]], 2)
+    data = jnp.concatenate([data, corner], 1)
     panels = lax.all_gather(data, "gz", axis=0)
     rows = choose(rows, swap(rows, "row", n_row, 1), row, row_owner, 1)
     for bit in (4, 2):
-        rows = widen(rows, swap(rows, "row", n_row, bit), row, bit)
+        rows = widen(rows, "row", n_row, row, bit)
 
     up0, term0 = first_terms(n_y, block_pattern, col_map, lower_inv, upper_inv, rows)
     return last_terms(n_y, slots, block_pattern, row_map, col_map, lower_inv, upper_inv, rows,

time: 152 us -> 155 us (1.020)
  waiting for transfers between devices: 36.7 us -> 55.1 us
  starting transfers between devices: 76 us -> 61.5 us
  Pallas kernels: 10.8 us -> 8.19 us
    ppermute x14 -> x11, waiting for transfers between devices: 33.7 us -> 49.8 us  [swap(): return lax.ppermute(x, axis, [(i, i ^ bit) for i in range(size)])]
    ppermute x14 -> x11, starting transfers between devices: 53.2 us -> 42 us  [swap(): return lax.ppermute(x, axis, [(i, i ^ bit) for i in range(size)])]
    ppermute x4, starting transfers between devices: 22.8 us -> 19.5 us  [the longest x3 12.2 us: shards(): lax.ppermute(pick(parts, y + step & n_y - 1, 0), 'gz', around(step))]
    pallas_call x1, Pallas kernels: 3.5 us -> 0.9 us  [cut_panels(): pl.pallas_call(panel_kernel, out_shape=[shape, shape], in_specs=[SMEM, pl...]
    ppermute x4, waiting for transfers between devices: 2.98 us -> 5.27 us  [the longest x3 3.58 us: shards(): lax.ppermute(pick(parts, y + step & n_y - 1, 0), 'gz', around(step))]
  transfers between devices with their start and end apart: 20 -> 17, of which waited for: 12 -> 13; matrix products, arithmetic and copies ran while one was open for 2% -> 1% of each run, Pallas kernels for 1% -> 1%
where the time goes in v7:
time: 155 us; the launch traced here: 153 us
  starting transfers between devices  61.5 us (40%)
  waiting for transfers between devices  55.1 us (36%)
  between operations  17.9 us (12%)
  Pallas kernels  8.19 us (5%)
  other arithmetic  5.16 us (3%)
  local copies, waits for them, and re-layouts  4.67 us (3%)
    ppermute x11, waiting for transfers between devices, swap(): return lax.ppermute(x, axis, [(i, i ^ bit) for i in range(size)])  49.8 us
    ppermute x11, starting transfers between devices, swap(): return lax.ppermute(x, axis, [(i, i ^ bit) for i in range(size)])  42 us
    ppermute x3, starting transfers between devices, shards(): lax.ppermute(pick(parts, y + step & n_y - 1, 0), 'gz', around(step))  12.2 us
    ppermute x1, starting transfers between devices, shards(): lax.ppermute(corner, ('row', 'col'), mirror)  7.35 us
    pallas_call x1, Pallas kernels, last_terms(): pl.pallas_call(functools.partial(last_kernel, n_y), out_shape=jax.ShapeDt...  5.93 us
    ppermute x3, waiting for transfers between devices, shards(): lax.ppermute(pick(parts, y + step & n_y - 1, 0), 'gz', around(step))  3.58 us
    unnamed x20, local copies, waits for them, and re-layouts  3.56 us
  transfers between devices with their start and end apart: 17, of which 13 were waited for; matrix products, arithmetic and copies ran while one was open for 1% of the time, Pallas kernels for 1%

profile of v7, /device:TPU:6, one launch (start us, length us, event | category | flops | bytes accessed | tf_op | source)
XLA Modules:
  0.0 152.5 jit_solution(5703470805472829755)
XLA Ops:
  6.5 1.6 %copy-done = bf16[1,1024,1024]{2,1,0:T(8,128)(2,1)S(1)} copy-done((bf16[1,1024,1024]{2,1,0:T(8,128)(2,1)S(1)}, bf16[1,1024,1024]{2,1,0:T(8,128)(2,1)}, u32[]{:S(2)}) %copy-start) | copy-done | bytes 2097176
  8.1 0.7 copy-done.7
  8.8 0.9 shard_map.64
  9.7 1.9 %collective-permute-start = (f32[4,2,4,32,256]{4,3,2,1,0:T(8,128)S(1)}, f32[4,2,4,32,256]{4,3,2,1,0:T(8,128)S(1)}, u32[]{:S(2)}, u32[]{:S(2)}) collective-permute-start(f32[4,2,4,32,256]{4,3,2,1,0:T(8,128)S(1)} %get-tuple-element.13), channel_id=1, source_target_pairs={{0,64},{64,0},{128,192},{192,128},{256,320},{320,256},{384,448},{4... | collective-permute-start | bytes 3145736 | tf_op jit(solution)/shard_map/ppermute | solution.py:193
  11.6 2.6 %collective-permute-done = f32[4,2,4,32,256]{4,3,2,1,0:T(8,128)S(1)} collective-permute-done((f32[4,2,4,32,256]{4,3,2,1,0:T(8,128)S(1)}, f32[4,2,4,32,256]{4,3,2,1,0:T(8,128)S(1)}, u32[]{:S(2)}, u32[]{:S(2)}) %collective-permute-start) | collective-permute-done | bytes 1048608 | tf_op jit(solution)/shard_map/ppermute | solution.py:193
  14.2 2.4 %convert_element_type.26 = f32[1024,1024]{1,0:T(8,128)} convert(bf16[1024,1024]{1,0:T(8,128)(2,1)S(1)} %bitcast.17) | non-fusion elementwise | flops 1048576 | bytes 6291456 | tf_op jit(solution)/shard_map/convert_element_type | solution.py:251
  16.7 0.0 reduce-scatter.2.cloned.1.call-update
  16.7 0.0 copy-start.9
  16.7 0.0 all-gather.3.cloned.1.call-start
  16.8 0.2 add.23
  17.0 0.1 dynamic-slice_bitcast_fusion.1
  17.0 5.1 %collective-permute-start.3 = (f32[2,4,32,256]{3,2,1,0:T(8,128)S(1)}, f32[2,4,32,256]{3,2,1,0:T(8,128)S(1)}, u32[]{:S(2)}, u32[]{:S(2)}) collective-permute-start(f32[2,4,32,256]{3,2,1,0:T(8,128)S(1)} %get-tuple-element.26), channel_id=1, source_target_pairs={{0,256},{64,320},{128,384},{192,448},{256,0},{320,64},{384,128},{4... | collective-permute-start | bytes 786440 | tf_op jit(solution)/shard_map/ppermute | solution.py:246
  22.1 2.6 %collective-permute-start.1 = (f32[2,4,32,256]{3,2,1,0:T(8,128)S(1)}, f32[2,4,32,256]{3,2,1,0:T(8,128)S(1)}, u32[]{:S(2)}, u32[]{:S(2)}) collective-permute-start(f32[2,4,32,256]{3,2,1,0:T(8,128)S(1)} %get-tuple-element.27), channel_id=1, source_target_pairs={{0,128},{64,192},{128,256},{192,320},{256,384},{320,448},{384,0},{... | collective-permute-start | bytes 786440 | tf_op jit(solution)/shard_map/ppermute | solution.py:246
  24.7 4.5 %collective-permute-start.2 = (f32[2,4,32,256]{3,2,1,0:T(8,128)S(1)}, f32[2,4,32,256]{3,2,1,0:T(8,128)S(1)}, u32[]{:S(2)}, u32[]{:S(2)}) collective-permute-start(f32[2,4,32,256]{3,2,1,0:T(8,128)S(1)} %get-tuple-element.25), channel_id=1, source_target_pairs={{0,384},{64,448},{128,0},{192,64},{256,128},{320,192},{384,256},{4... | collective-permute-start | bytes 786440 | tf_op jit(solution)/shard_map/ppermute | solution.py:246
  29.2 0.6 fusion.12
  31.1 3.2 %collective-permute-done.1 = f32[2,4,32,256]{3,2,1,0:T(8,128)S(1)} collective-permute-done((f32[2,4,32,256]{3,2,1,0:T(8,128)S(1)}, f32[2,4,32,256]{3,2,1,0:T(8,128)S(1)}, u32[]{:S(2)}, u32[]{:S(2)}) %collective-permute-start.1) | collective-permute-done | bytes 262176 | tf_op jit(solution)/shard_map/ppermute | solution.py:246
  34.4 0.3 collective-permute-done.2
  34.7 0.1 bitcast_add_fusion
  34.9 3.8 %collective-permute-start.4 = (f32[2,96,256]{2,1,0:T(8,128)S(1)}, f32[2,96,256]{2,1,0:T(8,128)S(1)}, u32[]{:S(2)}, u32[]{:S(2)}) collective-permute-start(f32[2,96,256]{2,1,0:T(8,128)S(1)} %maximum_maximum_fusion), channel_id=1, source_target_pairs={{0,1},{1,0},{2,3},{3,2},{4,5},{5,4},{6,7},{7,6},{8,9},{9,8},{10,11... | collective-permute-start | bytes 589832 | tf_op jit(solution)/shard_map/ppermute | solution.py:193
  38.8 0.7 fusion.13
  40.8 2.4 %collective-permute-done.4 = f32[2,96,256]{2,1,0:T(8,128)S(1)} collective-permute-done((f32[2,96,256]{2,1,0:T(8,128)S(1)}, f32[2,96,256]{2,1,0:T(8,128)S(1)}, u32[]{:S(2)}, u32[]{:S(2)}) %collective-permute-start.4) | collective-permute-done | bytes 196640 | tf_op jit(solution)/shard_map/ppermute | solution.py:193
  43.2 5.2 %collective-permute-start.5 = (f32[2,64,256]{2,1,0:T(8,128)S(1)}, f32[2,64,256]{2,1,0:T(8,128)S(1)}, u32[]{:S(2)}, u32[]{:S(2)}) collective-permute-start(f32[2,64,256]{2,1,0:T(8,128)S(1)} %maximum_maximum_fusion.1), channel_id=1, source_target_pairs={{0,2},{1,3},{2,0},{3,1},{4,6},{5,7},{6,4},{7,5},{8,10},{9,11},{10,... | collective-permute-start | bytes 393224 | tf_op jit(solution)/shard_map/ppermute | solution.py:193
  48.4 5.2 %collective-permute-done.5 = f32[2,64,256]{2,1,0:T(8,128)S(1)} collective-permute-done((f32[2,64,256]{2,1,0:T(8,128)S(1)}, f32[2,64,256]{2,1,0:T(8,128)S(1)}, u32[]{:S(2)}, u32[]{:S(2)}) %collective-permute-start.5) | collective-permute-done | bytes 131104 | tf_op jit(solution)/shard_map/ppermute | solution.py:193
  53.6 9.1 %collective-permute-start.6 = (f32[2,64,256]{2,1,0:T(8,128)S(1)}, f32[2,64,256]{2,1,0:T(8,128)S(1)}, u32[]{:S(2)}, u32[]{:S(2)}) collective-permute-start(f32[2,64,256]{2,1,0:T(8,128)S(1)} %maximum_maximum_fusion.2), channel_id=1, source_target_pairs={{0,4},{1,5},{2,6},{3,7},{4,0},{5,1},{6,2},{7,3},{8,12},{9,13},{10,... | collective-permute-start | bytes 393224 | tf_op jit(solution)/shard_map/ppermute | solution.py:193
  64.0 8.4 %collective-permute-done.6 = f32[2,64,256]{2,1,0:T(8,128)S(1)} collective-permute-done((f32[2,64,256]{2,1,0:T(8,128)S(1)}, f32[2,64,256]{2,1,0:T(8,128)S(1)}, u32[]{:S(2)}, u32[]{:S(2)}) %collective-permute-start.6) | collective-permute-done | bytes 131104 | tf_op jit(solution)/shard_map/ppermute | solution.py:193
  72.5 7.3 %collective-permute-start.8 = (f32[2,32,256]{2,1,0:T(8,128)S(1)}, f32[2,32,256]{2,1,0:T(8,128)S(1)}, u32[]{:S(2)}, u32[]{:S(2)}) collective-permute-start(f32[2,32,256]{2,1,0:T(8,128)S(1)} %pad_maximum_fusion.3), channel_id=1, source_target_pairs={{0,15},{1,14},{2,13},{3,12},{4,11},{5,10},{6,9},{7,8},{8,7},{9,6},... | collective-permute-start | bytes 196616 | tf_op jit(solution)/shard_map/ppermute | solution.py:275
  79.9 1.9 %collective-permute-start.7 = (f32[2,32,256]{2,1,0:T(8,128)S(1)}, f32[2,32,256]{2,1,0:T(8,128)S(1)}, u32[]{:S(2)}, u32[]{:S(2)}) collective-permute-start(f32[2,32,256]{2,1,0:T(8,128)S(1)} %pad_maximum_fusion.2), channel_id=1, source_target_pairs={{0,2},{1,3},{2,0},{3,1},{4,6},{5,7},{6,4},{7,5},{8,10},{9,11},{10,... | collective-permute-start | bytes 196616 | tf_op jit(solution)/shard_map/ppermute | solution.py:193
  81.8 1.7 %collective-permute-done.8 = f32[2,32,256]{2,1,0:T(8,128)S(1)} collective-permute-done((f32[2,32,256]{2,1,0:T(8,128)S(1)}, f32[2,32,256]{2,1,0:T(8,128)S(1)}, u32[]{:S(2)}, u32[]{:S(2)}) %collective-permute-start.8) | collective-permute-done | bytes 65568 | tf_op jit(solution)/shard_map/ppermute | solution.py:275
  83.5 3.7 %collective-permute-done.7 = f32[2,32,256]{2,1,0:T(8,128)S(1)} collective-permute-done((f32[2,32,256]{2,1,0:T(8,128)S(1)}, f32[2,32,256]{2,1,0:T(8,128)S(1)}, u32[]{:S(2)}, u32[]{:S(2)}) %collective-permute-start.7) | collective-permute-done | bytes 65568 | tf_op jit(solution)/shard_map/ppermute | solution.py:193
  87.3 0.0 reduce-scatter.2.cloned.1.call-done.merged
  87.3 1.0 constant_dynamic-slice_fusion.1
  88.4 2.9 %collective-permute-start.9 = (f32[2,192,128]{2,1,0:T(8,128)S(1)}, f32[2,192,128]{2,1,0:T(8,128)S(1)}, u32[]{:S(2)}, u32[]{:S(2)}) collective-permute-start(f32[2,192,128]{2,1,0:T(8,128)S(1)} %pad_maximum_fusion), channel_id=1, source_target_pairs={{0,16},{8,24},{16,0},{24,8},{32,48},{40,56},{48,32},{56,40},{1,17}... | collective-permute-start | bytes 589832 | tf_op jit(solution)/shard_map/ppermute | solution.py:193
  91.3 1.9 %collective-permute-start.14 = (f32[2,64,256]{2,1,0:T(8,128)S(1)}, f32[2,64,256]{2,1,0:T(8,128)S(1)}, u32[]{:S(2)}, u32[]{:S(2)}) collective-permute-start(f32[2,64,256]{2,1,0:T(8,128)S(1)} %maximum_select_fusion.2), channel_id=1, source_target_pairs={{0,1},{1,0},{2,3},{3,2},{4,5},{5,4},{6,7},{7,6},{8,9},{9,8},{10,11... | collective-permute-start | bytes 393224 | tf_op jit(solution)/shard_map/ppermute | solution.py:193
  93.2 3.7 %collective-permute-done.9 = f32[2,192,128]{2,1,0:T(8,128)S(1)} collective-permute-done((f32[2,192,128]{2,1,0:T(8,128)S(1)}, f32[2,192,128]{2,1,0:T(8,128)S(1)}, u32[]{:S(2)}, u32[]{:S(2)}) %collective-permute-start.9) | collective-permute-done | bytes 196640 | tf_op jit(solution)/shard_map/ppermute | solution.py:193
  97.0 3.3 %collective-permute-start.10 = (f32[2,128,128]{2,1,0:T(8,128)S(1)}, f32[2,128,128]{2,1,0:T(8,128)S(1)}, u32[]{:S(2)}, u32[]{:S(2)}) collective-permute-start(f32[2,128,128]{2,1,0:T(8,128)S(1)} %maximum_maximum_fusion.3), channel_id=1, source_target_pairs={{0,32},{8,40},{16,48},{24,56},{32,0},{40,8},{48,16},{56,24},{1,33}... | collective-permute-start | bytes 393224 | tf_op jit(solution)/shard_map/ppermute | solution.py:193
  100.4 5.0 %collective-permute-done.10 = f32[2,128,128]{2,1,0:T(8,128)S(1)} collective-permute-done((f32[2,128,128]{2,1,0:T(8,128)S(1)}, f32[2,128,128]{2,1,0:T(8,128)S(1)}, u32[]{:S(2)}, u32[]{:S(2)}) %collective-permute-start.10) | collective-permute-done | bytes 131104 | tf_op jit(solution)/shard_map/ppermute | solution.py:193
  105.4 0.8 fusion.1
  106.2 0.0 all-gather.3.cloned.1.call-update
  106.2 6.0 %collective-permute-start.11 = (f32[2,64,128]{2,1,0:T(8,128)S(1)}, f32[2,64,128]{2,1,0:T(8,128)S(1)}, u32[]{:S(2)}, u32[]{:S(2)}) collective-permute-start(f32[2,64,128]{2,1,0:T(8,128)S(1)} %pad_maximum_fusion.4), channel_id=1, source_target_pairs={{0,8},{8,0},{16,24},{24,16},{32,40},{40,32},{48,56},{56,48},{1,9},... | collective-permute-start | bytes 196616 | tf_op jit(solution)/shard_map/ppermute | solution.py:193
  112.2 9.8 %collective-permute-done.11 = f32[2,64,128]{2,1,0:T(8,128)S(1)} collective-permute-done((f32[2,64,128]{2,1,0:T(8,128)S(1)}, f32[2,64,128]{2,1,0:T(8,128)S(1)}, u32[]{:S(2)}, u32[]{:S(2)}) %collective-permute-start.11) | collective-permute-done | bytes 65568 | tf_op jit(solution)/shard_map/ppermute | solution.py:193
  122.0 4.0 %collective-permute-start.12 = (f32[2,64,128]{2,1,0:T(8,128)S(1)}, f32[2,64,128]{2,1,0:T(8,128)S(1)}, u32[]{:S(2)}, u32[]{:S(2)}) collective-permute-start(f32[2,64,128]{2,1,0:T(8,128)S(1)} %pad_maximum_fusion.5), channel_id=1, source_target_pairs={{0,32},{8,40},{16,48},{24,56},{32,0},{40,8},{48,16},{56,24},{1,33}... | collective-permute-start | bytes 196616 | tf_op jit(solution)/shard_map/ppermute | solution.py:193
  126.0 4.1 %collective-permute-done.12 = f32[2,64,128]{2,1,0:T(8,128)S(1)} collective-permute-done((f32[2,64,128]{2,1,0:T(8,128)S(1)}, f32[2,64,128]{2,1,0:T(8,128)S(1)}, u32[]{:S(2)}, u32[]{:S(2)}) %collective-permute-start.12) | collective-permute-done | bytes 65568 | tf_op jit(solution)/shard_map/ppermute | solution.py:193
  130.2 1.9 %collective-permute-start.13 = (f32[2,128,128]{2,1,0:T(8,128)S(1)}, f32[2,128,128]{2,1,0:T(8,128)S(1)}, u32[]{:S(2)}, u32[]{:S(2)}) collective-permute-start(f32[2,128,128]{2,1,0:T(8,128)S(1)} %maximum_select_fusion.3), channel_id=1, source_target_pairs={{0,16},{8,24},{16,0},{24,8},{32,48},{40,56},{48,32},{56,40},{1,17}... | collective-permute-start | bytes 393224 | tf_op jit(solution)/shard_map/ppermute | solution.py:193
  132.1 4.9 %collective-permute-done.13 = f32[2,128,128]{2,1,0:T(8,128)S(1)} collective-permute-done((f32[2,128,128]{2,1,0:T(8,128)S(1)}, f32[2,128,128]{2,1,0:T(8,128)S(1)}, u32[]{:S(2)}, u32[]{:S(2)}) %collective-permute-start.13) | collective-permute-done | bytes 131104 | tf_op jit(solution)/shard_map/ppermute | solution.py:193
  137.1 1.4 shard_map.65
  138.5 0.6 copy-done.4
  139.1 0.6 copy-done.5
  139.7 5.9 %shard_map.66 = bf16[1024,128]{1,0:T(8,128)(2,1)} custom-call(s32[32,32]{1,0:T(8,128)} %block_pattern.3, s32[32]{0:T(128)} %row_map.1, s32[32]{0:T(128)} %col_map.5, f32[2,256,256]{2,1,0:T(8,128)} %lower_inv.3, f32[2,256,256]{2,1,0:T(8,128)} %upper_inv.3, f32[2,256,128]{2,1,0:T(8,128)} %copy-done.1, f32[256,128]{1,0:T(8,128)} %copy-done.4, ...), custom_call_target="tpu_custom_call" | custom-call | tf_op jit(solution)/shard_map/pallas_call | solution.py:177
  (50 shorter events, 0.5 us)
Async XLA Ops:
  6.5 80.8 %reduce-scatter.2.cloned.1.call-start = ((), (), s32[]{:S(2)}) async-start(), calls=%async_computation.1 | async-start | bytes 4718592 | tf_op jit(solution)/shard_map/reduce_scatter | solution.py:251
  6.5 1.6 %copy-start = (bf16[1,1024,1024]{2,1,0:T(8,128)(2,1)S(1)}, bf16[1,1024,1024]{2,1,0:T(8,128)(2,1)}, u32[]{:S(2)}) copy-start(bf16[1,1024,1024]{2,1,0:T(8,128)(2,1)} %param.6) | copy-start | bytes 6291460
  8.1 0.7 copy-start.7
  9.7 4.6 %collective-permute-start = (f32[4,2,4,32,256]{4,3,2,1,0:T(8,128)S(1)}, f32[4,2,4,32,256]{4,3,2,1,0:T(8,128)S(1)}, u32[]{:S(2)}, u32[]{:S(2)}) collective-permute-start(f32[4,2,4,32,256]{4,3,2,1,0:T(8,128)S(1)} %get-tuple-element.13), channel_id=1, source_target_pairs={{0,64},{64,0},{128,192},{192,128},{256,320},{320,256},{384,448},{4... | collective-permute-start | bytes 3145736 | tf_op jit(solution)/shard_map/ppermute | solution.py:193
  16.7 12.5 %copy-start.9 = (s32[32]{0:T(128)S(1)}, s32[32]{0:T(128)}, u32[]{:S(2)}) copy-start(s32[32]{0:T(128)} %row_map.1) | copy-start | bytes 388
  16.7 123.0 %all-gather.3.cloned.1.call-start = ((), (), s32[]{:S(2)}) async-start(), calls=%async_computation.2 | async-start | bytes 2949120 | tf_op jit(solution)/shard_map/all_gather | solution.py:297
  16.9 21.8 %copy-start.8 = (s32[32]{0:T(128)S(1)}, s32[32]{0:T(128)}, u32[]{:S(2)}) copy-start(s32[32]{0:T(128)} %col_map.5) | copy-start | bytes 388
  17.0 14.1 %collective-permute-start.3 = (f32[2,4,32,256]{3,2,1,0:T(8,128)S(1)}, f32[2,4,32,256]{3,2,1,0:T(8,128)S(1)}, u32[]{:S(2)}, u32[]{:S(2)}) collective-permute-start(f32[2,4,32,256]{3,2,1,0:T(8,128)S(1)} %get-tuple-element.26), channel_id=1, source_target_pairs={{0,256},{64,320},{128,384},{192,448},{256,0},{320,64},{384,128},{4... | collective-permute-start | bytes 786440 | tf_op jit(solution)/shard_map/ppermute | solution.py:246
  22.1 12.3 %collective-permute-start.1 = (f32[2,4,32,256]{3,2,1,0:T(8,128)S(1)}, f32[2,4,32,256]{3,2,1,0:T(8,128)S(1)}, u32[]{:S(2)}, u32[]{:S(2)}) collective-permute-start(f32[2,4,32,256]{3,2,1,0:T(8,128)S(1)} %get-tuple-element.27), channel_id=1, source_target_pairs={{0,128},{64,192},{128,256},{192,320},{256,384},{320,448},{384,0},{... | collective-permute-start | bytes 786440 | tf_op jit(solution)/shard_map/ppermute | solution.py:246
  24.7 10.0 %collective-permute-start.2 = (f32[2,4,32,256]{3,2,1,0:T(8,128)S(1)}, f32[2,4,32,256]{3,2,1,0:T(8,128)S(1)}, u32[]{:S(2)}, u32[]{:S(2)}) collective-permute-start(f32[2,4,32,256]{3,2,1,0:T(8,128)S(1)} %get-tuple-element.25), channel_id=1, source_target_pairs={{0,384},{64,448},{128,0},{192,64},{256,128},{320,192},{384,256},{4... | collective-permute-start | bytes 786440 | tf_op jit(solution)/shard_map/ppermute | solution.py:246
  34.9 8.2 %collective-permute-start.4 = (f32[2,96,256]{2,1,0:T(8,128)S(1)}, f32[2,96,256]{2,1,0:T(8,128)S(1)}, u32[]{:S(2)}, u32[]{:S(2)}) collective-permute-start(f32[2,96,256]{2,1,0:T(8,128)S(1)} %maximum_maximum_fusion), channel_id=1, source_target_pairs={{0,1},{1,0},{2,3},{3,2},{4,5},{5,4},{6,7},{7,6},{8,9},{9,8},{10,11... | collective-permute-start | bytes 589832 | tf_op jit(solution)/shard_map/ppermute | solution.py:193
  43.2 10.4 %collective-permute-start.5 = (f32[2,64,256]{2,1,0:T(8,128)S(1)}, f32[2,64,256]{2,1,0:T(8,128)S(1)}, u32[]{:S(2)}, u32[]{:S(2)}) collective-permute-start(f32[2,64,256]{2,1,0:T(8,128)S(1)} %maximum_maximum_fusion.1), channel_id=1, source_target_pairs={{0,2},{1,3},{2,0},{3,1},{4,6},{5,7},{6,4},{7,5},{8,10},{9,11},{10,... | collective-permute-start | bytes 393224 | tf_op jit(solution)/shard_map/ppermute | solution.py:193
  53.6 18.8 %collective-permute-start.6 = (f32[2,64,256]{2,1,0:T(8,128)S(1)}, f32[2,64,256]{2,1,0:T(8,128)S(1)}, u32[]{:S(2)}, u32[]{:S(2)}) collective-permute-start(f32[2,64,256]{2,1,0:T(8,128)S(1)} %maximum_maximum_fusion.2), channel_id=1, source_target_pairs={{0,4},{1,5},{2,6},{3,7},{4,0},{5,1},{6,2},{7,3},{8,12},{9,13},{10,... | collective-permute-start | bytes 393224 | tf_op jit(solution)/shard_map/ppermute | solution.py:193
  72.5 11.0 %collective-permute-start.8 = (f32[2,32,256]{2,1,0:T(8,128)S(1)}, f32[2,32,256]{2,1,0:T(8,128)S(1)}, u32[]{:S(2)}, u32[]{:S(2)}) collective-permute-start(f32[2,32,256]{2,1,0:T(8,128)S(1)} %pad_maximum_fusion.3), channel_id=1, source_target_pairs={{0,15},{1,14},{2,13},{3,12},{4,11},{5,10},{6,9},{7,8},{8,7},{9,6},... | collective-permute-start | bytes 196616 | tf_op jit(solution)/shard_map/ppermute | solution.py:275
  79.9 7.4 %collective-permute-start.7 = (f32[2,32,256]{2,1,0:T(8,128)S(1)}, f32[2,32,256]{2,1,0:T(8,128)S(1)}, u32[]{:S(2)}, u32[]{:S(2)}) collective-permute-start(f32[2,32,256]{2,1,0:T(8,128)S(1)} %pad_maximum_fusion.2), channel_id=1, source_target_pairs={{0,2},{1,3},{2,0},{3,1},{4,6},{5,7},{6,4},{7,5},{8,10},{9,11},{10,... | collective-permute-start | bytes 196616 | tf_op jit(solution)/shard_map/ppermute | solution.py:193
  88.3 48.7 %copy-start.2 = (f32[2,256,256]{2,1,0:T(8,128)S(1)}, f32[2,256,256]{2,1,0:T(8,128)}, u32[]{:S(2)}) copy-start(f32[2,256,256]{2,1,0:T(8,128)} %lower_inv.3) | copy-start | bytes 1572868
  88.3 48.7 %copy-start.3 = (f32[2,256,256]{2,1,0:T(8,128)S(1)}, f32[2,256,256]{2,1,0:T(8,128)}, u32[]{:S(2)}) copy-start(f32[2,256,256]{2,1,0:T(8,128)} %upper_inv.3) | copy-start | bytes 1572868
  88.3 48.7 %copy-start.6 = (s32[32,32]{1,0:T(8,128)S(1)}, s32[32,32]{1,0:T(8,128)}, u32[]{:S(2)}) copy-start(s32[32,32]{1,0:T(8,128)} %block_pattern.3) | copy-start | bytes 12292
  88.4 8.5 %collective-permute-start.9 = (f32[2,192,128]{2,1,0:T(8,128)S(1)}, f32[2,192,128]{2,1,0:T(8,128)S(1)}, u32[]{:S(2)}, u32[]{:S(2)}) collective-permute-start(f32[2,192,128]{2,1,0:T(8,128)S(1)} %pad_maximum_fusion), channel_id=1, source_target_pairs={{0,16},{8,24},{16,0},{24,8},{32,48},{40,56},{48,32},{56,40},{1,17}... | collective-permute-start | bytes 589832 | tf_op jit(solution)/shard_map/ppermute | solution.py:193
  91.3 9.0 %collective-permute-start.14 = (f32[2,64,256]{2,1,0:T(8,128)S(1)}, f32[2,64,256]{2,1,0:T(8,128)S(1)}, u32[]{:S(2)}, u32[]{:S(2)}) collective-permute-start(f32[2,64,256]{2,1,0:T(8,128)S(1)} %maximum_select_fusion.2), channel_id=1, source_target_pairs={{0,1},{1,0},{2,3},{3,2},{4,5},{5,4},{6,7},{7,6},{8,9},{9,8},{10,11... | collective-permute-start | bytes 393224 | tf_op jit(solution)/shard_map/ppermute | solution.py:193
  97.0 8.4 %collective-permute-start.10 = (f32[2,128,128]{2,1,0:T(8,128)S(1)}, f32[2,128,128]{2,1,0:T(8,128)S(1)}, u32[]{:S(2)}, u32[]{:S(2)}) collective-permute-start(f32[2,128,128]{2,1,0:T(8,128)S(1)} %maximum_maximum_fusion.3), channel_id=1, source_target_pairs={{0,32},{8,40},{16,48},{24,56},{32,0},{40,8},{48,16},{56,24},{1,33}... | collective-permute-start | bytes 393224 | tf_op jit(solution)/shard_map/ppermute | solution.py:193
  106.2 15.8 %collective-permute-start.11 = (f32[2,64,128]{2,1,0:T(8,128)S(1)}, f32[2,64,128]{2,1,0:T(8,128)S(1)}, u32[]{:S(2)}, u32[]{:S(2)}) collective-permute-start(f32[2,64,128]{2,1,0:T(8,128)S(1)} %pad_maximum_fusion.4), channel_id=1, source_target_pairs={{0,8},{8,0},{16,24},{24,16},{32,40},{40,32},{48,56},{56,48},{1,9},... | collective-permute-start | bytes 196616 | tf_op jit(solution)/shard_map/ppermute | solution.py:193
  122.0 8.2 %collective-permute-start.12 = (f32[2,64,128]{2,1,0:T(8,128)S(1)}, f32[2,64,128]{2,1,0:T(8,128)S(1)}, u32[]{:S(2)}, u32[]{:S(2)}) collective-permute-start(f32[2,64,128]{2,1,0:T(8,128)S(1)} %pad_maximum_fusion.5), channel_id=1, source_target_pairs={{0,32},{8,40},{16,48},{24,56},{32,0},{40,8},{48,16},{56,24},{1,33}... | collective-permute-start | bytes 196616 | tf_op jit(solution)/shard_map/ppermute | solution.py:193
  130.2 6.9 %collective-permute-start.13 = (f32[2,128,128]{2,1,0:T(8,128)S(1)}, f32[2,128,128]{2,1,0:T(8,128)S(1)}, u32[]{:S(2)}, u32[]{:S(2)}) collective-permute-start(f32[2,128,128]{2,1,0:T(8,128)S(1)} %maximum_select_fusion.3), channel_id=1, source_target_pairs={{0,16},{8,24},{16,0},{24,8},{32,48},{40,56},{48,32},{56,40},{1,17}... | collective-permute-start | bytes 393224 | tf_op jit(solution)/shard_map/ppermute | solution.py:193
  137.1 2.7 %copy-start.1 = (f32[2,256,128]{2,1,0:T(8,128)}, f32[2,256,128]{2,1,0:T(8,128)S(1)}, u32[]{:S(2)}) copy-start(f32[2,256,128]{2,1,0:T(8,128)S(1)} %maximum_select_fusion.rows) | copy-start | bytes 786436
  138.4 0.6 copy-start.4
  139.1 0.6 copy-start.5
Sparse Core Ops, SparseCore 0:
  16.8 49.9 reduce-scatter.1
  106.3 31.1 all-gather.2

commit v8 on v7

--- a/solution.py
+++ b/solution.py
@@ -197,22 +197,20 @@
     return (index & jnp.uint32(bit)) != 0
 
 
-def part(x, axis, second):
-    half = x.shape[axis] // 2
-    return lax.dynamic_slice_in_dim(x, second.astype(jnp.uint32) * half, half, axis)
-
-
-def join(mine, other, axis, second):
-    return jnp.where(
-        second,
-        jnp.concatenate([other, mine], axis),
-        jnp.concatenate([mine, other], axis),
-    )
+def select(index, values):
+    out = values[0]
+    for i in range(1, len(values)):
+        out = jnp.where(index == i, values[i], out)
+    return out
 
 
 def choose(mine, other, me, sources, bit):
     same = [bit_of(me, bit) == bit_of(s, bit) for s in sources]
-    return jnp.stack([jnp.where(same[k], mine[k], other[k]) for k in range(len(sources))])
+    return jnp.stack([jnp.where(same[k], mine[k], other[k]) for k in range(2)])
+
+
+def choose_of_four(values, me, sources):
+    return jnp.stack([select(me ^ s, [v[k] for v in values]) for k, s in enumerate(sources)])
 
 
 def pick(x, index, axis):
@@ -253,18 +251,29 @@
     corner = jnp.stack([pick(panel[k], row_slot[1 - k], 0) for k in range(2)])
     data = panel.reshape(2, slots * thin, size)
 
-    def send_both(data, extra, axis, length, bit):
-        other = swap(jnp.concatenate([data, extra], 1), axis, length, bit)
-        return other[:, : data.shape[1]], other[:, data.shape[1] :]
-
-    for bit in (1, 2, 4):
-        mine = data
-        if bit < 4:
-            second = bit_of(col, bit)
-            mine, data = part(data, 1, second), part(data, 1, ~second)
-        other, extra = send_both(data, corner, "col", n_col, bit)
-        data = choose(mine, other, col, col_owner, bit)
-        corner = choose(corner, extra, col, col_owner, bit)
+    def split_four(data, extra, me, sources, axis, length, unit, extra_sources=None):
+        quarter = data.shape[1] // 4
+        kept, extras = [], []
+        for d in range(4):
+            chunk = lax.dynamic_slice_in_dim(data, (me ^ d) * quarter, quarter, 1)
+            both = jnp.concatenate([chunk, extra], 1)
+            if d:
+                both = swap(both, axis, length, d * unit)
+            kept.append(both[:, :quarter])
+            extras.append(both[:, quarter:])
+        return choose_of_four(kept, me, sources), choose_of_four(extras, me, extra_sources or sources)
+
+    def join_four(data, me, axis, length, unit):
+        parts = [data] + [swap(data, axis, length, d * unit) for d in range(1, 4)]
+        return jnp.concatenate([select(me ^ i, parts) for i in range(4)], 1)
+
+    col_member, row_member = col & 3, row >> 1
+    col_sources = [c & 3 for c in col_owner]
+    data, corner = split_four(data, corner, col_member, col_sources, "col", n_col, 1)
+    thick = data.shape[1]
+    both = jnp.concatenate([data, corner], 1)
+    both = choose(both, swap(both, "col", n_col, 4), col, col_owner, 4)
+    data, corner = both[:, :thick], both[:, thick:]
 
     corner_rows = row_owner[::-1]
     mirror = [
@@ -278,26 +287,16 @@
     rows = jnp.stack([pick(blocks, p, 0) for p in row_slot])
     corner = jnp.concatenate([corner[..., :width], corner[..., width:]], 1)
 
-    def narrow(rows, corner, bit):
-        second = bit_of(row, bit)
-        other, extra = send_both(part(rows, 1, ~second), corner, "row", n_row, bit)
-        rows = choose(part(rows, 1, second), other, row, row_owner, bit)
-        return rows, choose(corner, extra, row, corner_rows, bit)
-
-    def widen(x, axis, length, me, bit):
-        return join(x, swap(x, axis, length, bit), 1, bit_of(me, bit))
-
-    data = widen(data, "col", n_col, col, 2)
-    data, corner = lax.optimization_barrier((data, corner))
-    rows, corner = narrow(rows, corner, 2)
-    data = widen(data, "col", n_col, col, 1)
-    rows, corner = narrow(rows, corner, 4)
+    data = join_four(data, col_member, "col", n_col, 1)
+    rows, corner = split_four(
+        rows, corner, row_member, [r >> 1 for r in row_owner], "row", n_row, 2,
+        [r >> 1 for r in corner_rows],
+    )
     corner = jnp.concatenate([corner[:, :thin], corner[:, thin:]], 2)
     data = jnp.concatenate([data, corner], 1)
     panels = lax.all_gather(data, "gz", axis=0)
     rows = choose(rows, swap(rows, "row", n_row, 1), row, row_owner, 1)
-    for bit in (4, 2):
-        rows = widen(rows, "row", n_row, row, bit)
+    rows = join_four(rows, row_member, "row", n_row, 2)
 
     up0, term0 = first_terms(n_y, block_pattern, col_map, lower_inv, upper_inv, rows)
     return last_terms(n_y, slots, block_pattern, row_map, col_map, lower_inv, upper_inv, rows,

time: 155 us -> 159 us (1.026)
  the two profiles are of different devices: /device:TPU:6 before, /device:TPU:10 now
where the time goes in v8:
time: 159 us
  starting transfers between devices  76.1 us (48%)
  waiting for transfers between devices  46.2 us (29%)
  between operations  18 us (11%)
  Pallas kernels  8.2 us (5%)
  local copies, waits for them, and re-layouts  5.48 us (3%)
  other arithmetic  4.49 us (3%)
    ppermute x15, starting transfers between devices, swap(): return lax.ppermute(x, axis, [(i, i ^ bit) for i in range(size)])  57.7 us
    ppermute x15, waiting for transfers between devices, swap(): return lax.ppermute(x, axis, [(i, i ^ bit) for i in range(size)])  38.5 us
    ppermute x3, starting transfers between devices, shards(): lax.ppermute(pick(parts, y + step & n_y - 1, 0), 'gz', around(step))  10 us
    ppermute x1, starting transfers between devices, shards(): lax.ppermute(corner, ('row', 'col'), mirror)  8.36 us
    ppermute x3, waiting for transfers between devices, shards(): lax.ppermute(pick(parts, y + step & n_y - 1, 0), 'gz', around(step))  7.67 us
    pallas_call x1, Pallas kernels, last_terms(): pl.pallas_call(functools.partial(last_kernel, n_y), out_shape=jax.ShapeDt...  5.94 us
    unnamed x22, local copies, waits for them, and re-layouts  4.29 us
  transfers between devices with their start and end apart: 21, of which 12 were waited for; matrix products, arithmetic and copies ran while one was open for 1% of the time, Pallas kernels for 1%

profile of v8, /device:TPU:10, one launch (start us, length us, event | category | flops | bytes accessed | tf_op | source)
XLA Modules:
  0.0 158.6 jit_solution(13872903760579924627)
XLA Ops:
  6.5 1.6 %copy-done = bf16[1,1024,1024]{2,1,0:T(8,128)(2,1)S(1)} copy-done((bf16[1,1024,1024]{2,1,0:T(8,128)(2,1)S(1)}, bf16[1,1024,1024]{2,1,0:T(8,128)(2,1)}, u32[]{:S(2)}) %copy-start) | copy-done | bytes 2097176
  8.1 0.7 copy-done.7
  8.8 0.9 shard_map.64
  9.7 1.9 %collective-permute-start = (f32[4,2,4,32,256]{4,3,2,1,0:T(8,128)S(1)}, f32[4,2,4,32,256]{4,3,2,1,0:T(8,128)S(1)}, u32[]{:S(2)}, u32[]{:S(2)}) collective-permute-start(f32[4,2,4,32,256]{4,3,2,1,0:T(8,128)S(1)} %get-tuple-element.11), channel_id=1, source_target_pairs={{0,64},{64,0},{128,192},{192,128},{256,320},{320,256},{384,448},{4... | collective-permute-start | bytes 3145736 | tf_op jit(solution)/shard_map/ppermute | solution.py:193
  11.6 2.6 %collective-permute-done = f32[4,2,4,32,256]{4,3,2,1,0:T(8,128)S(1)} collective-permute-done((f32[4,2,4,32,256]{4,3,2,1,0:T(8,128)S(1)}, f32[4,2,4,32,256]{4,3,2,1,0:T(8,128)S(1)}, u32[]{:S(2)}, u32[]{:S(2)}) %collective-permute-start) | collective-permute-done | bytes 1048608 | tf_op jit(solution)/shard_map/ppermute | solution.py:193
  14.2 2.5 %convert_element_type.18 = f32[1024,1024]{1,0:T(8,128)} convert(bf16[1024,1024]{1,0:T(8,128)(2,1)S(1)} %bitcast.17) | non-fusion elementwise | flops 1048576 | bytes 6291456 | tf_op jit(solution)/shard_map/convert_element_type | solution.py:249
  16.7 0.0 all-gather.3.cloned.1.call-start
  16.8 0.2 add.23
  17.0 0.1 dynamic-slice_bitcast_fusion.1
  17.0 3.5 %collective-permute-start.1 = (f32[2,4,32,256]{3,2,1,0:T(8,128)S(1)}, f32[2,4,32,256]{3,2,1,0:T(8,128)S(1)}, u32[]{:S(2)}, u32[]{:S(2)}) collective-permute-start(f32[2,4,32,256]{3,2,1,0:T(8,128)S(1)} %get-tuple-element.23), channel_id=1, source_target_pairs={{0,128},{64,192},{128,256},{192,320},{256,384},{320,448},{384,0},{... | collective-permute-start | bytes 786440 | tf_op jit(solution)/shard_map/ppermute | solution.py:244
  20.5 2.4 %collective-permute-start.2 = (f32[2,4,32,256]{3,2,1,0:T(8,128)S(1)}, f32[2,4,32,256]{3,2,1,0:T(8,128)S(1)}, u32[]{:S(2)}, u32[]{:S(2)}) collective-permute-start(f32[2,4,32,256]{3,2,1,0:T(8,128)S(1)} %get-tuple-element.21), channel_id=1, source_target_pairs={{0,384},{64,448},{128,0},{192,64},{256,128},{320,192},{384,256},{4... | collective-permute-start | bytes 786440 | tf_op jit(solution)/shard_map/ppermute | solution.py:244
  22.9 4.2 %collective-permute-start.3 = (f32[2,4,32,256]{3,2,1,0:T(8,128)S(1)}, f32[2,4,32,256]{3,2,1,0:T(8,128)S(1)}, u32[]{:S(2)}, u32[]{:S(2)}) collective-permute-start(f32[2,4,32,256]{3,2,1,0:T(8,128)S(1)} %get-tuple-element.22), channel_id=1, source_target_pairs={{0,256},{64,320},{128,384},{192,448},{256,0},{320,64},{384,128},{4... | collective-permute-start | bytes 786440 | tf_op jit(solution)/shard_map/ppermute | solution.py:244
  27.1 0.7 fusion.32
  29.2 1.7 %collective-permute-done.2 = f32[2,4,32,256]{3,2,1,0:T(8,128)S(1)} collective-permute-done((f32[2,4,32,256]{3,2,1,0:T(8,128)S(1)}, f32[2,4,32,256]{3,2,1,0:T(8,128)S(1)}, u32[]{:S(2)}, u32[]{:S(2)}) %collective-permute-start.2) | collective-permute-done | bytes 262176 | tf_op jit(solution)/shard_map/ppermute | solution.py:244
  30.9 5.9 %collective-permute-done.3 = f32[2,4,32,256]{3,2,1,0:T(8,128)S(1)} collective-permute-done((f32[2,4,32,256]{3,2,1,0:T(8,128)S(1)}, f32[2,4,32,256]{3,2,1,0:T(8,128)S(1)}, u32[]{:S(2)}, u32[]{:S(2)}) %collective-permute-start.3) | collective-permute-done | bytes 262176 | tf_op jit(solution)/shard_map/ppermute | solution.py:244
  36.8 0.1 bitcast_add_fusion
  37.0 6.5 %collective-permute-start.4 = (f32[2,64,256]{2,1,0:T(8,128)S(1)}, f32[2,64,256]{2,1,0:T(8,128)S(1)}, u32[]{:S(2)}, u32[]{:S(2)}) collective-permute-start(f32[2,64,256]{2,1,0:T(8,128)S(1)} %get-tuple-element.58), channel_id=1, source_target_pairs={{0,3},{1,2},{2,1},{3,0},{4,7},{5,6},{6,5},{7,4},{8,11},{9,10},{10,... | collective-permute-start | bytes 393224 | tf_op jit(solution)/shard_map/ppermute | solution.py:193
  43.6 1.9 %collective-permute-start.5 = (f32[2,64,256]{2,1,0:T(8,128)S(1)}, f32[2,64,256]{2,1,0:T(8,128)S(1)}, u32[]{:S(2)}, u32[]{:S(2)}) collective-permute-start(f32[2,64,256]{2,1,0:T(8,128)S(1)} %get-tuple-element.59), channel_id=1, source_target_pairs={{0,2},{1,3},{2,0},{3,1},{4,6},{5,7},{6,4},{7,5},{8,10},{9,11},{10,... | collective-permute-start | bytes 393224 | tf_op jit(solution)/shard_map/ppermute | solution.py:193
  45.5 2.5 %collective-permute-start.6 = (f32[2,64,256]{2,1,0:T(8,128)S(1)}, f32[2,64,256]{2,1,0:T(8,128)S(1)}, u32[]{:S(2)}, u32[]{:S(2)}) collective-permute-start(f32[2,64,256]{2,1,0:T(8,128)S(1)} %get-tuple-element.60), channel_id=1, source_target_pairs={{0,1},{1,0},{2,3},{3,2},{4,5},{5,4},{6,7},{7,6},{8,9},{9,8},{10,11... | collective-permute-start | bytes 393224 | tf_op jit(solution)/shard_map/ppermute | solution.py:193
  48.0 0.7 fusion.33
  50.0 3.4 %collective-permute-done.5 = f32[2,64,256]{2,1,0:T(8,128)S(1)} collective-permute-done((f32[2,64,256]{2,1,0:T(8,128)S(1)}, f32[2,64,256]{2,1,0:T(8,128)S(1)}, u32[]{:S(2)}, u32[]{:S(2)}) %collective-permute-start.5) | collective-permute-done | bytes 131104 | tf_op jit(solution)/shard_map/ppermute | solution.py:193
  53.4 1.0 collective-permute-done.6
  54.5 9.1 %collective-permute-start.7 = (f32[2,64,256]{2,1,0:T(8,128)S(1)}, f32[2,64,256]{2,1,0:T(8,128)S(1)}, u32[]{:S(2)}, u32[]{:S(2)}) collective-permute-start(f32[2,64,256]{2,1,0:T(8,128)S(1)} %maximum_maximum_fusion), channel_id=1, source_target_pairs={{0,4},{1,5},{2,6},{3,7},{4,0},{5,1},{6,2},{7,3},{8,12},{9,13},{10,... | collective-permute-start | bytes 393224 | tf_op jit(solution)/shard_map/ppermute | solution.py:193
  63.6 9.9 %collective-permute-done.7 = f32[2,64,256]{2,1,0:T(8,128)S(1)} collective-permute-done((f32[2,64,256]{2,1,0:T(8,128)S(1)}, f32[2,64,256]{2,1,0:T(8,128)S(1)}, u32[]{:S(2)}, u32[]{:S(2)}) %collective-permute-start.7) | collective-permute-done | bytes 131104 | tf_op jit(solution)/shard_map/ppermute | solution.py:193
  73.6 8.4 %collective-permute-start.8 = (f32[2,32,256]{2,1,0:T(8,128)S(1)}, f32[2,32,256]{2,1,0:T(8,128)S(1)}, u32[]{:S(2)}, u32[]{:S(2)}) collective-permute-start(f32[2,32,256]{2,1,0:T(8,128)S(1)} %get-tuple-element.48), channel_id=1, source_target_pairs={{0,15},{1,14},{2,13},{3,12},{4,11},{5,10},{6,9},{7,8},{8,7},{9,6},... | collective-permute-start | bytes 196616 | tf_op jit(solution)/shard_map/ppermute | solution.py:284
  83.3 3.3 %collective-permute-start.16 = (f32[2,32,256]{2,1,0:T(8,128)S(1)}, f32[2,32,256]{2,1,0:T(8,128)S(1)}, u32[]{:S(2)}, u32[]{:S(2)}) collective-permute-start(f32[2,32,256]{2,1,0:T(8,128)S(1)} %get-tuple-element.47), channel_id=1, source_target_pairs={{0,3},{1,2},{2,1},{3,0},{4,7},{5,6},{6,5},{7,4},{8,11},{9,10},{10,... | collective-permute-start | bytes 196616 | tf_op jit(solution)/shard_map/ppermute | solution.py:193
  86.6 1.9 %collective-permute-start.17 = (f32[2,32,256]{2,1,0:T(8,128)S(1)}, f32[2,32,256]{2,1,0:T(8,128)S(1)}, u32[]{:S(2)}, u32[]{:S(2)}) collective-permute-start(f32[2,32,256]{2,1,0:T(8,128)S(1)} %get-tuple-element.47), channel_id=1, source_target_pairs={{0,2},{1,3},{2,0},{3,1},{4,6},{5,7},{6,4},{7,5},{8,10},{9,11},{10,... | collective-permute-start | bytes 196616 | tf_op jit(solution)/shard_map/ppermute | solution.py:193
  88.5 4.9 %collective-permute-start.18 = (f32[2,32,256]{2,1,0:T(8,128)S(1)}, f32[2,32,256]{2,1,0:T(8,128)S(1)}, u32[]{:S(2)}, u32[]{:S(2)}) collective-permute-start(f32[2,32,256]{2,1,0:T(8,128)S(1)} %get-tuple-element.47), channel_id=1, source_target_pairs={{0,1},{1,0},{2,3},{3,2},{4,5},{5,4},{6,7},{7,6},{8,9},{9,8},{10,11... | collective-permute-start | bytes 196616 | tf_op jit(solution)/shard_map/ppermute | solution.py:193
  93.5 0.7 collective-permute-done.17
  94.2 1.5 collective-permute-done.18
  95.8 1.1 constant_dynamic-slice_fusion.3
  97.0 4.1 %collective-permute-start.10 = (f32[2,128,128]{2,1,0:T(8,128)S(1)}, f32[2,128,128]{2,1,0:T(8,128)S(1)}, u32[]{:S(2)}, u32[]{:S(2)}) collective-permute-start(f32[2,128,128]{2,1,0:T(8,128)S(1)} %get-tuple-element.52), channel_id=1, source_target_pairs={{0,32},{8,40},{16,48},{24,56},{32,0},{40,8},{48,16},{56,24},{1,33}... | collective-permute-start | bytes 393224 | tf_op jit(solution)/shard_map/ppermute | solution.py:193
  101.0 3.3 %collective-permute-start.11 = (f32[2,128,128]{2,1,0:T(8,128)S(1)}, f32[2,128,128]{2,1,0:T(8,128)S(1)}, u32[]{:S(2)}, u32[]{:S(2)}) collective-permute-start(f32[2,128,128]{2,1,0:T(8,128)S(1)} %get-tuple-element.53), channel_id=1, source_target_pairs={{0,16},{8,24},{16,0},{24,8},{32,48},{40,56},{48,32},{56,40},{1,17}... | collective-permute-start | bytes 393224 | tf_op jit(solution)/shard_map/ppermute | solution.py:193
  104.4 2.4 %collective-permute-start.9 = (f32[2,128,128]{2,1,0:T(8,128)S(1)}, f32[2,128,128]{2,1,0:T(8,128)S(1)}, u32[]{:S(2)}, u32[]{:S(2)}) collective-permute-start(f32[2,128,128]{2,1,0:T(8,128)S(1)} %get-tuple-element.51), channel_id=1, source_target_pairs={{0,48},{8,56},{16,32},{24,40},{32,16},{40,24},{48,0},{56,8},{1,49}... | collective-permute-start | bytes 393224 | tf_op jit(solution)/shard_map/ppermute | solution.py:193
  106.8 1.3 collective-permute-done.11
  108.2 3.0 %collective-permute-done.9 = f32[2,128,128]{2,1,0:T(8,128)S(1)} collective-permute-done((f32[2,128,128]{2,1,0:T(8,128)S(1)}, f32[2,128,128]{2,1,0:T(8,128)S(1)}, u32[]{:S(2)}, u32[]{:S(2)}) %collective-permute-start.9) | collective-permute-done | bytes 131104 | tf_op jit(solution)/shard_map/ppermute | solution.py:193
  111.3 0.7 copy-done.9
  112.1 6.0 %collective-permute-start.12 = (f32[2,64,128]{2,1,0:T(8,128)S(1)}, f32[2,64,128]{2,1,0:T(8,128)S(1)}, u32[]{:S(2)}, u32[]{:S(2)}) collective-permute-start(f32[2,64,128]{2,1,0:T(8,128)S(1)} %pad_maximum_fusion.10), channel_id=1, source_target_pairs={{0,8},{8,0},{16,24},{24,16},{32,40},{40,32},{48,56},{56,48},{1,9},... | collective-permute-start | bytes 196616 | tf_op jit(solution)/shard_map/ppermute | solution.py:193
  118.1 11.0 %collective-permute-done.12 = f32[2,64,128]{2,1,0:T(8,128)S(1)} collective-permute-done((f32[2,64,128]{2,1,0:T(8,128)S(1)}, f32[2,64,128]{2,1,0:T(8,128)S(1)}, u32[]{:S(2)}, u32[]{:S(2)}) %collective-permute-start.12) | collective-permute-done | bytes 65568 | tf_op jit(solution)/shard_map/ppermute | solution.py:193
  129.1 1.9 %collective-permute-start.13 = (f32[2,64,128]{2,1,0:T(8,128)S(1)}, f32[2,64,128]{2,1,0:T(8,128)S(1)}, u32[]{:S(2)}, u32[]{:S(2)}) collective-permute-start(f32[2,64,128]{2,1,0:T(8,128)S(1)} %pad_maximum_fusion.11), channel_id=1, source_target_pairs={{0,48},{8,56},{16,32},{24,40},{32,16},{40,24},{48,0},{56,8},{1,49}... | collective-permute-start | bytes 196616 | tf_op jit(solution)/shard_map/ppermute | solution.py:193
  131.0 5.8 %collective-permute-start.14 = (f32[2,64,128]{2,1,0:T(8,128)S(1)}, f32[2,64,128]{2,1,0:T(8,128)S(1)}, u32[]{:S(2)}, u32[]{:S(2)}) collective-permute-start(f32[2,64,128]{2,1,0:T(8,128)S(1)} %pad_maximum_fusion.11), channel_id=1, source_target_pairs={{0,32},{8,40},{16,48},{24,56},{32,0},{40,8},{48,16},{56,24},{1,33}... | collective-permute-start | bytes 196616 | tf_op jit(solution)/shard_map/ppermute | solution.py:193
  136.8 2.1 %collective-permute-start.15 = (f32[2,64,128]{2,1,0:T(8,128)S(1)}, f32[2,64,128]{2,1,0:T(8,128)S(1)}, u32[]{:S(2)}, u32[]{:S(2)}) collective-permute-start(f32[2,64,128]{2,1,0:T(8,128)S(1)} %pad_maximum_fusion.11), channel_id=1, source_target_pairs={{0,16},{8,24},{16,0},{24,8},{32,48},{40,56},{48,32},{56,40},{1,17}... | collective-permute-start | bytes 196616 | tf_op jit(solution)/shard_map/ppermute | solution.py:193
  139.0 0.1 collective-permute-done.14
  139.1 3.9 %collective-permute-done.15 = f32[2,64,128]{2,1,0:T(8,128)S(1)} collective-permute-done((f32[2,64,128]{2,1,0:T(8,128)S(1)}, f32[2,64,128]{2,1,0:T(8,128)S(1)}, u32[]{:S(2)}, u32[]{:S(2)}) %collective-permute-start.15) | collective-permute-done | bytes 65568 | tf_op jit(solution)/shard_map/ppermute | solution.py:193
  143.1 1.4 shard_map.65
  144.5 0.6 copy-done.4
  145.1 0.7 copy-done.5
  145.8 5.9 %shard_map.66 = bf16[1024,128]{1,0:T(8,128)(2,1)} custom-call(s32[32,32]{1,0:T(8,128)} %block_pattern.3, s32[32]{0:T(128)} %row_map.1, s32[32]{0:T(128)} %col_map.5, f32[2,256,256]{2,1,0:T(8,128)} %lower_inv.3, f32[2,256,256]{2,1,0:T(8,128)} %upper_inv.3, f32[2,256,128]{2,1,0:T(8,128)} %copy-done.1, f32[256,128]{1,0:T(8,128)} %copy-done.4, ...), custom_call_target="tpu_custom_call" | custom-call | tf_op jit(solution)/shard_map/pallas_call | solution.py:177
  (55 shorter events, 0.6 us)
Async XLA Ops:
  6.5 89.3 %reduce-scatter.2.cloned.1.call-start = ((), (), s32[]{:S(2)}) async-start(), calls=%async_computation.1 | async-start | bytes 4718592 | tf_op jit(solution)/shard_map/reduce_scatter | solution.py:249
  6.5 1.6 %copy-start = (bf16[1,1024,1024]{2,1,0:T(8,128)(2,1)S(1)}, bf16[1,1024,1024]{2,1,0:T(8,128)(2,1)}, u32[]{:S(2)}) copy-start(bf16[1,1024,1024]{2,1,0:T(8,128)(2,1)} %param.6) | copy-start | bytes 6291460
  8.1 0.7 copy-start.7
  9.7 4.6 %collective-permute-start = (f32[4,2,4,32,256]{4,3,2,1,0:T(8,128)S(1)}, f32[4,2,4,32,256]{4,3,2,1,0:T(8,128)S(1)}, u32[]{:S(2)}, u32[]{:S(2)}) collective-permute-start(f32[4,2,4,32,256]{4,3,2,1,0:T(8,128)S(1)} %get-tuple-element.11), channel_id=1, source_target_pairs={{0,64},{64,0},{128,192},{192,128},{256,320},{320,256},{384,448},{4... | collective-permute-start | bytes 3145736 | tf_op jit(solution)/shard_map/ppermute | solution.py:193
  16.7 10.4 %copy-start.10 = (s32[32]{0:T(128)S(1)}, s32[32]{0:T(128)}, u32[]{:S(2)}) copy-start(s32[32]{0:T(128)} %row_map.1) | copy-start | bytes 388
  16.7 129.1 %all-gather.3.cloned.1.call-start = ((), (), s32[]{:S(2)}) async-start(), calls=%async_computation.2 | async-start | bytes 2949120 | tf_op jit(solution)/shard_map/all_gather | solution.py:297
  17.0 31.0 %copy-start.8 = (s32[32]{0:T(128)S(1)}, s32[32]{0:T(128)}, u32[]{:S(2)}) copy-start(s32[32]{0:T(128)} %col_map.5) | copy-start | bytes 388
  17.0 12.1 %collective-permute-start.1 = (f32[2,4,32,256]{3,2,1,0:T(8,128)S(1)}, f32[2,4,32,256]{3,2,1,0:T(8,128)S(1)}, u32[]{:S(2)}, u32[]{:S(2)}) collective-permute-start(f32[2,4,32,256]{3,2,1,0:T(8,128)S(1)} %get-tuple-element.23), channel_id=1, source_target_pairs={{0,128},{64,192},{128,256},{192,320},{256,384},{320,448},{384,0},{... | collective-permute-start | bytes 786440 | tf_op jit(solution)/shard_map/ppermute | solution.py:244
  20.5 10.4 %collective-permute-start.2 = (f32[2,4,32,256]{3,2,1,0:T(8,128)S(1)}, f32[2,4,32,256]{3,2,1,0:T(8,128)S(1)}, u32[]{:S(2)}, u32[]{:S(2)}) collective-permute-start(f32[2,4,32,256]{3,2,1,0:T(8,128)S(1)} %get-tuple-element.21), channel_id=1, source_target_pairs={{0,384},{64,448},{128,0},{192,64},{256,128},{320,192},{384,256},{4... | collective-permute-start | bytes 786440 | tf_op jit(solution)/shard_map/ppermute | solution.py:244
  22.9 13.9 %collective-permute-start.3 = (f32[2,4,32,256]{3,2,1,0:T(8,128)S(1)}, f32[2,4,32,256]{3,2,1,0:T(8,128)S(1)}, u32[]{:S(2)}, u32[]{:S(2)}) collective-permute-start(f32[2,4,32,256]{3,2,1,0:T(8,128)S(1)} %get-tuple-element.22), channel_id=1, source_target_pairs={{0,256},{64,320},{128,384},{192,448},{256,0},{320,64},{384,128},{4... | collective-permute-start | bytes 786440 | tf_op jit(solution)/shard_map/ppermute | solution.py:244
  37.0 13.0 %collective-permute-start.4 = (f32[2,64,256]{2,1,0:T(8,128)S(1)}, f32[2,64,256]{2,1,0:T(8,128)S(1)}, u32[]{:S(2)}, u32[]{:S(2)}) collective-permute-start(f32[2,64,256]{2,1,0:T(8,128)S(1)} %get-tuple-element.58), channel_id=1, source_target_pairs={{0,3},{1,2},{2,1},{3,0},{4,7},{5,6},{6,5},{7,4},{8,11},{9,10},{10,... | collective-permute-start | bytes 393224 | tf_op jit(solution)/shard_map/ppermute | solution.py:193
  43.6 9.8 %collective-permute-start.5 = (f32[2,64,256]{2,1,0:T(8,128)S(1)}, f32[2,64,256]{2,1,0:T(8,128)S(1)}, u32[]{:S(2)}, u32[]{:S(2)}) collective-permute-start(f32[2,64,256]{2,1,0:T(8,128)S(1)} %get-tuple-element.59), channel_id=1, source_target_pairs={{0,2},{1,3},{2,0},{3,1},{4,6},{5,7},{6,4},{7,5},{8,10},{9,11},{10,... | collective-permute-start | bytes 393224 | tf_op jit(solution)/shard_map/ppermute | solution.py:193
  45.5 8.9 %collective-permute-start.6 = (f32[2,64,256]{2,1,0:T(8,128)S(1)}, f32[2,64,256]{2,1,0:T(8,128)S(1)}, u32[]{:S(2)}, u32[]{:S(2)}) collective-permute-start(f32[2,64,256]{2,1,0:T(8,128)S(1)} %get-tuple-element.60), channel_id=1, source_target_pairs={{0,1},{1,0},{2,3},{3,2},{4,5},{5,4},{6,7},{7,6},{8,9},{9,8},{10,11... | collective-permute-start | bytes 393224 | tf_op jit(solution)/shard_map/ppermute | solution.py:193
  54.5 19.1 %collective-permute-start.7 = (f32[2,64,256]{2,1,0:T(8,128)S(1)}, f32[2,64,256]{2,1,0:T(8,128)S(1)}, u32[]{:S(2)}, u32[]{:S(2)}) collective-permute-start(f32[2,64,256]{2,1,0:T(8,128)S(1)} %maximum_maximum_fusion), channel_id=1, source_target_pairs={{0,4},{1,5},{2,6},{3,7},{4,0},{5,1},{6,2},{7,3},{8,12},{9,13},{10,... | collective-permute-start | bytes 393224 | tf_op jit(solution)/shard_map/ppermute | solution.py:193
  73.6 19.9 %collective-permute-start.8 = (f32[2,32,256]{2,1,0:T(8,128)S(1)}, f32[2,32,256]{2,1,0:T(8,128)S(1)}, u32[]{:S(2)}, u32[]{:S(2)}) collective-permute-start(f32[2,32,256]{2,1,0:T(8,128)S(1)} %get-tuple-element.48), channel_id=1, source_target_pairs={{0,15},{1,14},{2,13},{3,12},{4,11},{5,10},{6,9},{7,8},{8,7},{9,6},... | collective-permute-start | bytes 196616 | tf_op jit(solution)/shard_map/ppermute | solution.py:284
  83.3 10.2 %collective-permute-start.16 = (f32[2,32,256]{2,1,0:T(8,128)S(1)}, f32[2,32,256]{2,1,0:T(8,128)S(1)}, u32[]{:S(2)}, u32[]{:S(2)}) collective-permute-start(f32[2,32,256]{2,1,0:T(8,128)S(1)} %get-tuple-element.47), channel_id=1, source_target_pairs={{0,3},{1,2},{2,1},{3,0},{4,7},{5,6},{6,5},{7,4},{8,11},{9,10},{10,... | collective-permute-start | bytes 196616 | tf_op jit(solution)/shard_map/ppermute | solution.py:193
  86.6 7.6 %collective-permute-start.17 = (f32[2,32,256]{2,1,0:T(8,128)S(1)}, f32[2,32,256]{2,1,0:T(8,128)S(1)}, u32[]{:S(2)}, u32[]{:S(2)}) collective-permute-start(f32[2,32,256]{2,1,0:T(8,128)S(1)} %get-tuple-element.47), channel_id=1, source_target_pairs={{0,2},{1,3},{2,0},{3,1},{4,6},{5,7},{6,4},{7,5},{8,10},{9,11},{10,... | collective-permute-start | bytes 196616 | tf_op jit(solution)/shard_map/ppermute | solution.py:193
  88.5 7.1 %collective-permute-start.18 = (f32[2,32,256]{2,1,0:T(8,128)S(1)}, f32[2,32,256]{2,1,0:T(8,128)S(1)}, u32[]{:S(2)}, u32[]{:S(2)}) collective-permute-start(f32[2,32,256]{2,1,0:T(8,128)S(1)} %get-tuple-element.47), channel_id=1, source_target_pairs={{0,1},{1,0},{2,3},{3,2},{4,5},{5,4},{6,7},{7,6},{8,9},{9,8},{10,11... | collective-permute-start | bytes 196616 | tf_op jit(solution)/shard_map/ppermute | solution.py:193
  95.8 47.3 %copy-start.2 = (f32[2,256,256]{2,1,0:T(8,128)S(1)}, f32[2,256,256]{2,1,0:T(8,128)}, u32[]{:S(2)}) copy-start(f32[2,256,256]{2,1,0:T(8,128)} %lower_inv.3) | copy-start | bytes 1572868
  95.8 47.3 %copy-start.3 = (f32[2,256,256]{2,1,0:T(8,128)S(1)}, f32[2,256,256]{2,1,0:T(8,128)}, u32[]{:S(2)}) copy-start(f32[2,256,256]{2,1,0:T(8,128)} %upper_inv.3) | copy-start | bytes 1572868
  95.8 47.3 %copy-start.6 = (s32[32,32]{1,0:T(8,128)S(1)}, s32[32,32]{1,0:T(8,128)}, u32[]{:S(2)}) copy-start(s32[32,32]{1,0:T(8,128)} %block_pattern.3) | copy-start | bytes 12292
  97.0 9.9 %collective-permute-start.10 = (f32[2,128,128]{2,1,0:T(8,128)S(1)}, f32[2,128,128]{2,1,0:T(8,128)S(1)}, u32[]{:S(2)}, u32[]{:S(2)}) collective-permute-start(f32[2,128,128]{2,1,0:T(8,128)S(1)} %get-tuple-element.52), channel_id=1, source_target_pairs={{0,32},{8,40},{16,48},{24,56},{32,0},{40,8},{48,16},{56,24},{1,33}... | collective-permute-start | bytes 393224 | tf_op jit(solution)/shard_map/ppermute | solution.py:193
  101.0 7.2 %collective-permute-start.11 = (f32[2,128,128]{2,1,0:T(8,128)S(1)}, f32[2,128,128]{2,1,0:T(8,128)S(1)}, u32[]{:S(2)}, u32[]{:S(2)}) collective-permute-start(f32[2,128,128]{2,1,0:T(8,128)S(1)} %get-tuple-element.53), channel_id=1, source_target_pairs={{0,16},{8,24},{16,0},{24,8},{32,48},{40,56},{48,32},{56,40},{1,17}... | collective-permute-start | bytes 393224 | tf_op jit(solution)/shard_map/ppermute | solution.py:193
  104.4 6.9 %collective-permute-start.9 = (f32[2,128,128]{2,1,0:T(8,128)S(1)}, f32[2,128,128]{2,1,0:T(8,128)S(1)}, u32[]{:S(2)}, u32[]{:S(2)}) collective-permute-start(f32[2,128,128]{2,1,0:T(8,128)S(1)} %get-tuple-element.51), channel_id=1, source_target_pairs={{0,48},{8,56},{16,32},{24,40},{32,16},{40,24},{48,0},{56,8},{1,49}... | collective-permute-start | bytes 393224 | tf_op jit(solution)/shard_map/ppermute | solution.py:193
  111.3 0.7 copy-start.9
  112.1 17.0 %collective-permute-start.12 = (f32[2,64,128]{2,1,0:T(8,128)S(1)}, f32[2,64,128]{2,1,0:T(8,128)S(1)}, u32[]{:S(2)}, u32[]{:S(2)}) collective-permute-start(f32[2,64,128]{2,1,0:T(8,128)S(1)} %pad_maximum_fusion.10), channel_id=1, source_target_pairs={{0,8},{8,0},{16,24},{24,16},{32,40},{40,32},{48,56},{56,48},{1,9},... | collective-permute-start | bytes 196616 | tf_op jit(solution)/shard_map/ppermute | solution.py:193
  129.1 9.9 %collective-permute-start.13 = (f32[2,64,128]{2,1,0:T(8,128)S(1)}, f32[2,64,128]{2,1,0:T(8,128)S(1)}, u32[]{:S(2)}, u32[]{:S(2)}) collective-permute-start(f32[2,64,128]{2,1,0:T(8,128)S(1)} %pad_maximum_fusion.11), channel_id=1, source_target_pairs={{0,48},{8,56},{16,32},{24,40},{32,16},{40,24},{48,0},{56,8},{1,49}... | collective-permute-start | bytes 196616 | tf_op jit(solution)/shard_map/ppermute | solution.py:193
  131.0 8.0 %collective-permute-start.14 = (f32[2,64,128]{2,1,0:T(8,128)S(1)}, f32[2,64,128]{2,1,0:T(8,128)S(1)}, u32[]{:S(2)}, u32[]{:S(2)}) collective-permute-start(f32[2,64,128]{2,1,0:T(8,128)S(1)} %pad_maximum_fusion.11), channel_id=1, source_target_pairs={{0,32},{8,40},{16,48},{24,56},{32,0},{40,8},{48,16},{56,24},{1,33}... | collective-permute-start | bytes 196616 | tf_op jit(solution)/shard_map/ppermute | solution.py:193
  136.8 6.2 %collective-permute-start.15 = (f32[2,64,128]{2,1,0:T(8,128)S(1)}, f32[2,64,128]{2,1,0:T(8,128)S(1)}, u32[]{:S(2)}, u32[]{:S(2)}) collective-permute-start(f32[2,64,128]{2,1,0:T(8,128)S(1)} %pad_maximum_fusion.11), channel_id=1, source_target_pairs={{0,16},{8,24},{16,0},{24,8},{32,48},{40,56},{48,32},{56,40},{1,17}... | collective-permute-start | bytes 196616 | tf_op jit(solution)/shard_map/ppermute | solution.py:193
  143.1 2.7 %copy-start.1 = (f32[2,256,128]{2,1,0:T(8,128)}, f32[2,256,128]{2,1,0:T(8,128)S(1)}, u32[]{:S(2)}) copy-start(f32[2,256,128]{2,1,0:T(8,128)S(1)} %pad_maximum_fusion.rows) | copy-start | bytes 786436
  144.5 0.6 copy-start.4
  145.1 0.7 copy-start.5
Sparse Core Ops, SparseCore 0:
  16.9 46.6 reduce-scatter.1
  112.1 26.4 all-gather.2

commit v9 on v6

--- a/solution.py
+++ b/solution.py
@@ -10,7 +10,7 @@
 VMEM = pl.BlockSpec(memory_space=pltpu.VMEM)
 SMEM = pl.BlockSpec(memory_space=pltpu.SMEM)
 PARAMS = pltpu.CompilerParams(vmem_limit_bytes=32 << 20)
-LARGE = pltpu.CompilerParams(vmem_limit_bytes=60 << 20)
+LARGE = pltpu.CompilerParams(vmem_limit_bytes=50 << 20)
 
 
 def position_of(table, value):
@@ -69,7 +69,7 @@
             pltpu.VMEM((2, local.shape[0], size), jnp.bfloat16),
             pltpu.SemaphoreType.DMA((2,)),
         ],
-        compiler_params=LARGE,
+        compiler_params=PARAMS,
     )(col_map, local)
 
 
@@ -79,6 +79,21 @@
 
 def column_of(col_map, n_y):
     return col_map[lax.axis_index("col") * n_y + (lax.axis_index("gz") >> 1)]
+
+
+def product_kernel(upper_inv, lower_inv, out):
+    for k in range(2):
+        out[k] = mm(upper_inv[k], lower_inv[k])
+
+
+def products(upper_inv, lower_inv):
+    return pl.pallas_call(
+        product_kernel,
+        out_shape=jax.ShapeDtypeStruct(lower_inv.shape, jnp.float32),
+        in_specs=[VMEM, VMEM],
+        out_specs=VMEM,
+        compiler_params=PARAMS,
+    )(upper_inv, lower_inv)
 
 
 def first_kernel(n_y, block_pattern, col_map, lower_inv, upper_inv, rows, up_out, term_out):
@@ -100,8 +115,8 @@
     )(block_pattern, col_map, lower_inv, upper_inv, rows)
 
 
-def last_kernel(n_y, block_pattern, row_map, col_map, lower_inv, upper_inv, rows, up0, term0,
-                merged, panels, out, high, low, buffer, sems):
+def last_kernel(n_y, block_pattern, row_map, col_map, lower_inv, upper_inv, both_inv, rows, up0,
+                term0, merged, panels, out, high, low, buffer, sems):
     slots = high.shape[1] - 1
     size, width = up0.shape
     thin = size // (2 * n_y)
@@ -128,24 +143,21 @@
     def stored(k, p):
         return high[k, p], low[k, p]
 
-    lower0, lower1 = halves(lower_inv[0]), halves(lower_inv[1])
-    upper0, upper1 = halves(upper_inv[0]), halves(upper_inv[1])
-    up0 = up0[...]
-    low_at = mask_at(block_pattern, 1, 0) * mm_halves(stored(0, slots), upper0)
-    up_at = mask_at(block_pattern, 0, 1) * mm_halves(lower0, stored(1, slots))
+    up0, term0 = up0[...], term0[...]
     mask = jnp.where(col > 1, mask_at(block_pattern, 1, col), 0.0)
-    up1 = mask * mm_halves(lower1, halves(rows[1] - mm(low_at, up0)))
-    term1 = mm_halves(upper1, halves(up1))
+    reduced = halves(rows[1] - mask_at(block_pattern, 1, 0) * mm_halves(stored(0, slots), halves(term0)))
+    term1 = mask * mm_halves(halves(both_inv[1]), reduced)
+    up1 = mask * mm_halves(halves(lower_inv[1]), reduced)
 
     def own_half(matrix):
         left, right = matrix[:, :width], matrix[:, width:]
         return jnp.where(core == 0, left, right)
 
-    term0 = jnp.where(col == 0, -own_half(upper_inv[0]), term0[...])
+    term0 = jnp.where(col == 0, -own_half(upper_inv[0]), term0)
     term1 = jnp.where(col == 1, -own_half(upper_inv[1]), term1)
-    term2 = mm_halves(upper0, halves(mm(up_at, term1)))
+    term1 = halves(term1)
+    term2 = mask_at(block_pattern, 0, 1) * mm(both_inv[0], mm_halves(stored(1, slots), term1))
     both = halves(jnp.concatenate([term0, term2], axis=1))
-    term1 = halves(term1)
     copies[1].wait()
     for p in range(slots):
         settle(p)
@@ -171,13 +183,13 @@
         out[here, :] = value.astype(jnp.bfloat16)
 
 
-def last_terms(n_y, slots, block_pattern, row_map, col_map, lower_inv, upper_inv, rows, up0, term0,
-               panels, merged):
+def last_terms(n_y, slots, block_pattern, row_map, col_map, lower_inv, upper_inv, both_inv, rows,
+               up0, term0, panels, merged):
     size = lower_inv.shape[-1]
     return pl.pallas_call(
         functools.partial(last_kernel, n_y),
         out_shape=jax.ShapeDtypeStruct(merged.shape, jnp.bfloat16),
-        in_specs=[SMEM] * 3 + [VMEM] * 6 + [pl.BlockSpec(memory_space=pltpu.HBM)],
+        in_specs=[SMEM] * 3 + [VMEM] * 7 + [pl.BlockSpec(memory_space=pltpu.HBM)],
         out_specs=VMEM,
         scratch_shapes=[
             pltpu.VMEM((2, slots + 1, size, size), jnp.bfloat16),
@@ -186,7 +198,8 @@
             pltpu.SemaphoreType.DMA((2,)),
         ],
         compiler_params=LARGE,
-    )(block_pattern, row_map, col_map, lower_inv, upper_inv, rows, up0, term0, merged, panels)
+    )(block_pattern, row_map, col_map, lower_inv, upper_inv, both_inv, rows, up0, term0, merged,
+      panels)
 
 
 def swap(x, axis, size, bit):
@@ -242,10 +255,12 @@
     other = swap(give, "gz", n_gz, 1)
     other, local = lax.optimization_barrier((other, local))
     parts = keep + other
-    panel = pick(parts, y, 0)
-    for step in (1, 3, 2):
-        chunk = pick(parts, (y + step) & (n_y - 1), 0)
-        panel = panel + lax.ppermute(chunk, "gz", around(step))
+    arrived = [
+        lax.ppermute(pick(parts, (y + step) & (n_y - 1), 0), "gz", around(step))
+        for step in (1, 3, 2)
+    ]
+    both_inv, arrived = lax.optimization_barrier((products(upper_inv, lower_inv), arrived))
+    panel = pick(parts, y, 0) + (arrived[0] + arrived[1] + arrived[2])
 
     merged = lax.psum_scatter(local.astype(jnp.float32), "gz", scatter_dimension=1, tiled=True)
 
@@ -304,8 +319,8 @@
         rows = widen(rows, swap(rows, "row", n_row, bit), row, bit)
 
     up0, term0 = first_terms(n_y, block_pattern, col_map, lower_inv, upper_inv, rows)
-    return last_terms(n_y, slots, block_pattern, row_map, col_map, lower_inv, upper_inv, rows,
-                      up0, term0, panels, merged)
+    return last_terms(n_y, slots, block_pattern, row_map, col_map, lower_inv, upper_inv, both_inv,
+                      rows, up0, term0, panels, merged)
 
 
 def solution(mesh):

time: 152 us -> 154 us (1.013)
  Pallas kernels: 10.8 us -> 7.36 us
  other arithmetic: 5.03 us -> 7.75 us
    pallas_call x1, Pallas kernels: 3.5 us -> 0.9 us  [cut_panels(): pl.pallas_call(panel_kernel, out_shape=[shape, shape], in_specs=[SMEM, pl...]
    all_gather x1, waiting for transfers between devices: 0.01 us -> 2.13 us  [shards(): panels = lax.all_gather(data, 'gz', axis=0)]
    ppermute x1, starting transfers between devices: 11.9 us -> 9.88 us  [shards(): corner_other = lax.ppermute(corner, ('row', 'col'), mirror)]
    ppermute x14, starting transfers between devices: 53.2 us -> 55.2 us  [swap(): return lax.ppermute(x, axis, [(i, i ^ bit) for i in range(size)])]
  transfers between devices with their start and end apart: 20 -> 20, of which waited for: 12 -> 12; matrix products, arithmetic and copies ran while one was open for 2% -> 4% of each run, Pallas kernels for 1% -> 1%
where the time goes in v9:
time: 154 us; the launch traced here: 151 us
  starting transfers between devices  76 us (49%)
  waiting for transfers between devices  37.7 us (24%)
  between operations  17.9 us (12%)
  other arithmetic  7.75 us (5%)
  Pallas kernels  7.36 us (5%)
  local copies, waits for them, and re-layouts  4.14 us (3%)
    ppermute x14, starting transfers between devices, swap(): return lax.ppermute(x, axis, [(i, i ^ bit) for i in range(size)])  55.2 us
    ppermute x14, waiting for transfers between devices, swap(): return lax.ppermute(x, axis, [(i, i ^ bit) for i in range(size)])  33.7 us
    ppermute x3, starting transfers between devices, shards(): lax.ppermute(pick(parts, y + step & n_y - 1, 0), 'gz', around(step))  10.9 us
    ppermute x1, starting transfers between devices, shards(): corner_other = lax.ppermute(corner, ('row', 'col'), mirror)  9.88 us
    pallas_call x1, Pallas kernels, last_terms(): pl.pallas_call(functools.partial(last_kernel, n_y), out_shape=jax.ShapeDt...  4.7 us
  transfers between devices with their start and end apart: 20, of which 12 were waited for; matrix products, arithmetic and copies ran while one was open for 4% of the time, Pallas kernels for 1%

profile of v9, /device:TPU:6, one launch (start us, length us, event | category | flops | bytes accessed | tf_op | source)
XLA Modules:
  0.0 150.9 jit_solution(10963354560477094416)
XLA Ops:
  6.5 1.6 %copy-done = bf16[1,1024,1024]{2,1,0:T(8,128)(2,1)S(1)} copy-done((bf16[1,1024,1024]{2,1,0:T(8,128)(2,1)S(1)}, bf16[1,1024,1024]{2,1,0:T(8,128)(2,1)}, u32[]{:S(2)}) %copy-start) | copy-done | bytes 2097176
  8.1 0.7 copy-done.5
  8.8 0.9 shard_map.65
  9.7 1.9 %collective-permute-start = (f32[4,2,4,32,256]{4,3,2,1,0:T(8,128)S(1)}, f32[4,2,4,32,256]{4,3,2,1,0:T(8,128)}, u32[]{:S(2)}, u32[]{:S(2)}) collective-permute-start(f32[4,2,4,32,256]{4,3,2,1,0:T(8,128)S(1)} %get-tuple-element.20), channel_id=1, source_target_pairs={{0,64},{64,0},{128,192},{192,128},{256,320},{320,256},{384,448},{4... | collective-permute-start | bytes 3145736 | tf_op jit(solution)/shard_map/ppermute | solution.py:206
  11.6 2.8 %collective-permute-done = f32[4,2,4,32,256]{4,3,2,1,0:T(8,128)} collective-permute-done((f32[4,2,4,32,256]{4,3,2,1,0:T(8,128)S(1)}, f32[4,2,4,32,256]{4,3,2,1,0:T(8,128)}, u32[]{:S(2)}, u32[]{:S(2)}) %collective-permute-start) | collective-permute-done | bytes 1048608 | tf_op jit(solution)/shard_map/ppermute | solution.py:206
  14.4 2.5 %convert_element_type.28 = f32[1024,1024]{1,0:T(8,128)} convert(bf16[1024,1024]{1,0:T(8,128)(2,1)S(1)} %bitcast.17) | non-fusion elementwise | flops 1048576 | bytes 6291456 | tf_op jit(solution)/shard_map/convert_element_type | solution.py:265
  16.8 0.0 reduce-scatter.2.cloned.1.call-update
  16.9 0.0 all-gather.3.cloned.1.call-start
  17.0 1.6 %add.23 = f32[4,2,4,32,256]{4,3,2,1,0:T(8,128)S(1)} add(f32[4,2,4,32,256]{4,3,2,1,0:T(8,128)S(1)} %get-tuple-element.19, f32[4,2,4,32,256]{4,3,2,1,0:T(8,128)} %collective-permute-done) | non-fusion elementwise | flops 262144 | bytes 3145728 | tf_op jit(solution)/shard_map/add | solution.py:257
  18.5 0.8 dynamic-slice_bitcast_fusion
  19.3 3.5 %collective-permute-start.1 = (f32[2,4,32,256]{3,2,1,0:T(8,128)}, f32[2,4,32,256]{3,2,1,0:T(8,128)S(1)}, u32[]{:S(2)}, u32[]{:S(2)}) collective-permute-start(f32[2,4,32,256]{3,2,1,0:T(8,128)} %get-tuple-element.39), channel_id=1, source_target_pairs={{0,128},{64,192},{128,256},{192,320},{256,384},{320,448},{384,0},{... | collective-permute-start | bytes 786440 | tf_op jit(solution)/shard_map/ppermute | solution.py:259
  22.8 3.6 %collective-permute-start.2 = (f32[2,4,32,256]{3,2,1,0:T(8,128)S(1)}, f32[2,4,32,256]{3,2,1,0:T(8,128)}, u32[]{:S(2)}, u32[]{:S(2)}) collective-permute-start(f32[2,4,32,256]{3,2,1,0:T(8,128)S(1)} %get-tuple-element.38), channel_id=1, source_target_pairs={{0,384},{64,448},{128,0},{192,64},{256,128},{320,192},{384,256},{4... | collective-permute-start | bytes 786440 | tf_op jit(solution)/shard_map/ppermute | solution.py:259
  26.4 3.9 %collective-permute-start.3 = (f32[2,4,32,256]{3,2,1,0:T(8,128)S(1)}, f32[2,4,32,256]{3,2,1,0:T(8,128)}, u32[]{:S(2)}, u32[]{:S(2)}) collective-permute-start(f32[2,4,32,256]{3,2,1,0:T(8,128)S(1)} %get-tuple-element.37), channel_id=1, source_target_pairs={{0,256},{64,320},{128,384},{192,448},{256,0},{320,64},{384,128},{4... | collective-permute-start | bytes 786440 | tf_op jit(solution)/shard_map/ppermute | solution.py:259
  30.3 0.7 fusion.9
  33.6 0.7 fusion.7
  35.7 0.4 shard_map.64.both_inv
  36.1 1.8 %collective-permute-done.3 = f32[2,4,32,256]{3,2,1,0:T(8,128)} collective-permute-done((f32[2,4,32,256]{3,2,1,0:T(8,128)S(1)}, f32[2,4,32,256]{3,2,1,0:T(8,128)}, u32[]{:S(2)}, u32[]{:S(2)}) %collective-permute-start.3) | collective-permute-done | bytes 262176 | tf_op jit(solution)/shard_map/ppermute | solution.py:259
  37.9 1.2 bitcast_add_fusion
  39.2 2.7 %collective-permute-start.7 = (f32[2,32,256]{2,1,0:T(8,128)S(1)}, f32[2,32,256]{2,1,0:T(8,128)S(1)}, u32[]{:S(2)}, u32[]{:S(2)}) collective-permute-start(f32[2,32,256]{2,1,0:T(8,128)S(1)} %pad_maximum_fusion.3), channel_id=1, source_target_pairs={{0,16},{8,24},{16,0},{24,8},{32,48},{40,56},{48,32},{56,40},{1,17}... | collective-permute-start | bytes 196616 | tf_op jit(solution)/shard_map/ppermute | solution.py:206
  41.9 3.8 %collective-permute-start.4 = (f32[2,64,256]{2,1,0:T(8,128)S(1)}, f32[2,64,256]{2,1,0:T(8,128)S(1)}, u32[]{:S(2)}, u32[]{:S(2)}) collective-permute-start(f32[2,64,256]{2,1,0:T(8,128)S(1)} %constant_dynamic-slice_fusion.3), channel_id=1, source_target_pairs={{0,1},{1,0},{2,3},{3,2},{4,5},{5,4},{6,7},{7,6},{8,9},{9,8},{10,11... | collective-permute-start | bytes 393224 | tf_op jit(solution)/shard_map/ppermute | solution.py:206
  45.8 8.1 %collective-permute-start.8 = (f32[2,32,256]{2,1,0:T(8,128)S(1)}, f32[2,32,256]{2,1,0:T(8,128)S(1)}, u32[]{:S(2)}, u32[]{:S(2)}) collective-permute-start(f32[2,32,256]{2,1,0:T(8,128)S(1)} %pad_maximum_fusion.4), channel_id=1, source_target_pairs={{0,32},{8,40},{16,48},{24,56},{32,0},{40,8},{48,16},{56,24},{1,33}... | collective-permute-start | bytes 196616 | tf_op jit(solution)/shard_map/ppermute | solution.py:206
  54.0 1.9 %collective-permute-start.5 = (f32[2,32,256]{2,1,0:T(8,128)S(1)}, f32[2,32,256]{2,1,0:T(8,128)S(1)}, u32[]{:S(2)}, u32[]{:S(2)}) collective-permute-start(f32[2,32,256]{2,1,0:T(8,128)S(1)} %get-tuple-element.61), channel_id=1, source_target_pairs={{0,2},{1,3},{2,0},{3,1},{4,6},{5,7},{6,4},{7,5},{8,10},{9,11},{10,... | collective-permute-start | bytes 196616 | tf_op jit(solution)/shard_map/ppermute | solution.py:206
  55.9 0.2 collective-permute-done.8
  56.2 9.9 %collective-permute-start.9 = (f32[2,32,256]{2,1,0:T(8,128)S(1)}, f32[2,32,256]{2,1,0:T(8,128)S(1)}, u32[]{:S(2)}, u32[]{:S(2)}) collective-permute-start(f32[2,32,256]{2,1,0:T(8,128)S(1)} %pad_maximum_fusion.5), channel_id=1, source_target_pairs={{0,15},{1,14},{2,13},{3,12},{4,11},{5,10},{6,9},{7,8},{8,7},{9,6},... | collective-permute-start | bytes 196616 | tf_op jit(solution)/shard_map/ppermute | solution.py:276
  66.1 7.2 %collective-permute-start.6 = (f32[2,32,256]{2,1,0:T(8,128)S(1)}, f32[2,32,256]{2,1,0:T(8,128)S(1)}, u32[]{:S(2)}, u32[]{:S(2)}) collective-permute-start(f32[2,32,256]{2,1,0:T(8,128)S(1)} %pad_maximum_fusion.2), channel_id=1, source_target_pairs={{0,4},{1,5},{2,6},{3,7},{4,0},{5,1},{6,2},{7,3},{8,12},{9,13},{10,... | collective-permute-start | bytes 196616 | tf_op jit(solution)/shard_map/ppermute | solution.py:206
  73.3 2.9 %collective-permute-start.10 = (f32[2,32,256]{2,1,0:T(8,128)S(1)}, f32[2,32,256]{2,1,0:T(8,128)S(1)}, u32[]{:S(2)}, u32[]{:S(2)}) collective-permute-start(f32[2,32,256]{2,1,0:T(8,128)S(1)} %pad_maximum_fusion.6), channel_id=1, source_target_pairs={{0,4},{1,5},{2,6},{3,7},{4,0},{5,1},{6,2},{7,3},{8,12},{9,13},{10,... | collective-permute-start | bytes 196616 | tf_op jit(solution)/shard_map/ppermute | solution.py:206
  76.3 7.9 %collective-permute-done.10 = f32[2,32,256]{2,1,0:T(8,128)S(1)} collective-permute-done((f32[2,32,256]{2,1,0:T(8,128)S(1)}, f32[2,32,256]{2,1,0:T(8,128)S(1)}, u32[]{:S(2)}, u32[]{:S(2)}) %collective-permute-start.10) | collective-permute-done | bytes 65568 | tf_op jit(solution)/shard_map/ppermute | solution.py:206
  84.2 1.9 %collective-permute-start.11 = (f32[2,64,256]{2,1,0:T(8,128)S(1)}, f32[2,64,256]{2,1,0:T(8,128)S(1)}, u32[]{:S(2)}, u32[]{:S(2)}) collective-permute-start(f32[2,64,256]{2,1,0:T(8,128)S(1)} %maximum_maximum_fusion.2), channel_id=1, source_target_pairs={{0,2},{1,3},{2,0},{3,1},{4,6},{5,7},{6,4},{7,5},{8,10},{9,11},{10,... | collective-permute-start | bytes 393224 | tf_op jit(solution)/shard_map/ppermute | solution.py:206
  86.1 0.0 reduce-scatter.2.cloned.1.call-done.merged
  86.2 1.0 constant_dynamic-slice_fusion.1
  87.2 3.0 %collective-permute-start.12 = (f32[2,128,128]{2,1,0:T(8,128)S(1)}, f32[2,128,128]{2,1,0:T(8,128)S(1)}, u32[]{:S(2)}, u32[]{:S(2)}) collective-permute-start(f32[2,128,128]{2,1,0:T(8,128)S(1)} %get-tuple-element.47), channel_id=1, source_target_pairs={{0,16},{8,24},{16,0},{24,8},{32,48},{40,56},{48,32},{56,40},{1,17}... | collective-permute-start | bytes 393224 | tf_op jit(solution)/shard_map/ppermute | solution.py:206
  90.2 2.4 %collective-permute-done.11 = f32[2,64,256]{2,1,0:T(8,128)S(1)} collective-permute-done((f32[2,64,256]{2,1,0:T(8,128)S(1)}, f32[2,64,256]{2,1,0:T(8,128)S(1)}, u32[]{:S(2)}, u32[]{:S(2)}) %collective-permute-start.11) | collective-permute-done | bytes 131104 | tf_op jit(solution)/shard_map/ppermute | solution.py:206
  92.7 1.4 collective-permute-done.12
  94.1 3.8 %collective-permute-start.14 = (f32[2,64,128]{2,1,0:T(8,128)S(1)}, f32[2,64,128]{2,1,0:T(8,128)S(1)}, u32[]{:S(2)}, u32[]{:S(2)}) collective-permute-start(f32[2,64,128]{2,1,0:T(8,128)S(1)} %constant_dynamic-slice_fusion), channel_id=1, source_target_pairs={{0,32},{8,40},{16,48},{24,56},{32,0},{40,8},{48,16},{56,24},{1,33}... | collective-permute-start | bytes 196616 | tf_op jit(solution)/shard_map/ppermute | solution.py:206
  97.9 1.9 %collective-permute-start.13 = (f32[2,96,256]{2,1,0:T(8,128)S(1)}, f32[2,96,256]{2,1,0:T(8,128)S(1)}, u32[]{:S(2)}, u32[]{:S(2)}) collective-permute-start(f32[2,96,256]{2,1,0:T(8,128)S(1)} %maximum_maximum_fusion.1), channel_id=1, source_target_pairs={{0,1},{1,0},{2,3},{3,2},{4,5},{5,4},{6,7},{7,6},{8,9},{9,8},{10,11... | collective-permute-start | bytes 589832 | tf_op jit(solution)/shard_map/ppermute | solution.py:206
  99.9 2.1 %collective-permute-done.14 = f32[2,64,128]{2,1,0:T(8,128)S(1)} collective-permute-done((f32[2,64,128]{2,1,0:T(8,128)S(1)}, f32[2,64,128]{2,1,0:T(8,128)S(1)}, u32[]{:S(2)}, u32[]{:S(2)}) %collective-permute-start.14) | collective-permute-done | bytes 65568 | tf_op jit(solution)/shard_map/ppermute | solution.py:206
  102.0 3.5 %collective-permute-done.13 = f32[2,96,256]{2,1,0:T(8,128)S(1)} collective-permute-done((f32[2,96,256]{2,1,0:T(8,128)S(1)}, f32[2,96,256]{2,1,0:T(8,128)S(1)}, u32[]{:S(2)}, u32[]{:S(2)}) %collective-permute-start.13) | collective-permute-done | bytes 196640 | tf_op jit(solution)/shard_map/ppermute | solution.py:206
  105.6 0.8 maximum_maximum_fusion
  106.3 0.0 all-gather.3.cloned.1.call-update
  106.3 9.7 %collective-permute-start.15 = (f32[2,64,128]{2,1,0:T(8,128)S(1)}, f32[2,64,128]{2,1,0:T(8,128)S(1)}, u32[]{:S(2)}, u32[]{:S(2)}) collective-permute-start(f32[2,64,128]{2,1,0:T(8,128)S(1)} %pad_maximum_fusion.7), channel_id=1, source_target_pairs={{0,8},{8,0},{16,24},{24,16},{32,40},{40,32},{48,56},{56,48},{1,9},... | collective-permute-start | bytes 196616 | tf_op jit(solution)/shard_map/ppermute | solution.py:206
  116.0 5.2 %collective-permute-done.15 = f32[2,64,128]{2,1,0:T(8,128)S(1)} collective-permute-done((f32[2,64,128]{2,1,0:T(8,128)S(1)}, f32[2,64,128]{2,1,0:T(8,128)S(1)}, u32[]{:S(2)}, u32[]{:S(2)}) %collective-permute-start.15) | collective-permute-done | bytes 65568 | tf_op jit(solution)/shard_map/ppermute | solution.py:206
  121.2 3.7 %collective-permute-start.16 = (f32[2,64,128]{2,1,0:T(8,128)S(1)}, f32[2,64,128]{2,1,0:T(8,128)S(1)}, u32[]{:S(2)}, u32[]{:S(2)}) collective-permute-start(f32[2,64,128]{2,1,0:T(8,128)S(1)} %pad_maximum_fusion.8), channel_id=1, source_target_pairs={{0,32},{8,40},{16,48},{24,56},{32,0},{40,8},{48,16},{56,24},{1,33}... | collective-permute-start | bytes 196616 | tf_op jit(solution)/shard_map/ppermute | solution.py:206
  125.0 3.9 %collective-permute-done.16 = f32[2,64,128]{2,1,0:T(8,128)S(1)} collective-permute-done((f32[2,64,128]{2,1,0:T(8,128)S(1)}, f32[2,64,128]{2,1,0:T(8,128)S(1)}, u32[]{:S(2)}, u32[]{:S(2)}) %collective-permute-start.16) | collective-permute-done | bytes 65568 | tf_op jit(solution)/shard_map/ppermute | solution.py:206
  128.9 2.6 %collective-permute-start.17 = (f32[2,128,128]{2,1,0:T(8,128)S(1)}, f32[2,128,128]{2,1,0:T(8,128)S(1)}, u32[]{:S(2)}, u32[]{:S(2)}) collective-permute-start(f32[2,128,128]{2,1,0:T(8,128)S(1)} %maximum_select_fusion.2), channel_id=1, source_target_pairs={{0,16},{8,24},{16,0},{24,8},{32,48},{40,56},{48,32},{56,40},{1,17}... | collective-permute-start | bytes 393224 | tf_op jit(solution)/shard_map/ppermute | solution.py:206
  131.5 4.3 %collective-permute-done.17 = f32[2,128,128]{2,1,0:T(8,128)S(1)} collective-permute-done((f32[2,128,128]{2,1,0:T(8,128)S(1)}, f32[2,128,128]{2,1,0:T(8,128)S(1)}, u32[]{:S(2)}, u32[]{:S(2)}) %collective-permute-start.17) | collective-permute-done | bytes 131104 | tf_op jit(solution)/shard_map/ppermute | solution.py:206
  135.8 1.4 shard_map.66
  137.2 2.1 %all-gather.3.cloned.1.call-done = f32[16,160,256]{2,1,0:T(8,128)} async-done(((f32[2,160,256]{2,1,0:T(8,128)}), f32[16,160,256]{2,1,0:T(8,128)}) %all-gather.3.cloned.1.call-update) | async-done | bytes 2621456 | tf_op jit(solution)/shard_map/all_gather | solution.py:316
  139.3 4.7 %shard_map.67 = bf16[1024,128]{1,0:T(8,128)(2,1)} custom-call(s32[32,32]{1,0:T(8,128)S(1)} %copy-done.4, s32[32]{0:T(128)S(1)} %copy-done.7, s32[32]{0:T(128)S(1)} %copy-done.6, f32[2,256,256]{2,1,0:T(8,128)S(1)} %copy-done.1, f32[2,256,256]{2,1,0:T(8,128)S(1)} %copy-done.2, f32[2,256,256]{2,1,0:T(8,128)S(1)} %shard_map.64.both_inv, ...), custom_call_target="tpu_custom_call" | custom-call | tf_op jit(solution)/shard_map/pallas_call | solution.py:189
  (56 shorter events, 0.5 us)
Async XLA Ops:
  6.5 79.6 %reduce-scatter.2.cloned.1.call-start = ((), (), s32[]{:S(2)}) async-start(), calls=%async_computation.1 | async-start | bytes 4718592 | tf_op jit(solution)/shard_map/reduce_scatter | solution.py:265
  6.5 1.6 %copy-start = (bf16[1,1024,1024]{2,1,0:T(8,128)(2,1)S(1)}, bf16[1,1024,1024]{2,1,0:T(8,128)(2,1)}, u32[]{:S(2)}) copy-start(bf16[1,1024,1024]{2,1,0:T(8,128)(2,1)} %param.6) | copy-start | bytes 6291460
  8.1 0.7 copy-start.5
  9.7 4.7 %collective-permute-start = (f32[4,2,4,32,256]{4,3,2,1,0:T(8,128)S(1)}, f32[4,2,4,32,256]{4,3,2,1,0:T(8,128)}, u32[]{:S(2)}, u32[]{:S(2)}) collective-permute-start(f32[4,2,4,32,256]{4,3,2,1,0:T(8,128)S(1)} %get-tuple-element.20), channel_id=1, source_target_pairs={{0,64},{64,0},{128,192},{192,128},{256,320},{320,256},{384,448},{4... | collective-permute-start | bytes 3145736 | tf_op jit(solution)/shard_map/ppermute | solution.py:206
  16.9 13.4 %copy-start.7 = (s32[32]{0:T(128)S(1)}, s32[32]{0:T(128)}, u32[]{:S(2)}) copy-start(s32[32]{0:T(128)} %row_map.1) | copy-start | bytes 388
  16.9 16.7 %copy-start.6 = (s32[32]{0:T(128)S(1)}, s32[32]{0:T(128)}, u32[]{:S(2)}) copy-start(s32[32]{0:T(128)} %col_map.5) | copy-start | bytes 388
  16.9 18.8 %copy-start.1 = (f32[2,256,256]{2,1,0:T(8,128)S(1)}, f32[2,256,256]{2,1,0:T(8,128)}, u32[]{:S(2)}) copy-start(f32[2,256,256]{2,1,0:T(8,128)} %lower_inv.5) | copy-start | bytes 1572868
  16.9 18.8 %copy-start.2 = (f32[2,256,256]{2,1,0:T(8,128)S(1)}, f32[2,256,256]{2,1,0:T(8,128)}, u32[]{:S(2)}) copy-start(f32[2,256,256]{2,1,0:T(8,128)} %upper_inv.5) | copy-start | bytes 1572868
  16.9 122.4 %all-gather.3.cloned.1.call-start = ((), (), s32[]{:S(2)}) async-start(), calls=%async_computation.2 | async-start | bytes 2949120 | tf_op jit(solution)/shard_map/all_gather | solution.py:316
  19.3 16.8 %collective-permute-start.1 = (f32[2,4,32,256]{3,2,1,0:T(8,128)}, f32[2,4,32,256]{3,2,1,0:T(8,128)S(1)}, u32[]{:S(2)}, u32[]{:S(2)}) collective-permute-start(f32[2,4,32,256]{3,2,1,0:T(8,128)} %get-tuple-element.39), channel_id=1, source_target_pairs={{0,128},{64,192},{128,256},{192,320},{256,384},{320,448},{384,0},{... | collective-permute-start | bytes 786440 | tf_op jit(solution)/shard_map/ppermute | solution.py:259
  22.8 13.3 %collective-permute-start.2 = (f32[2,4,32,256]{3,2,1,0:T(8,128)S(1)}, f32[2,4,32,256]{3,2,1,0:T(8,128)}, u32[]{:S(2)}, u32[]{:S(2)}) collective-permute-start(f32[2,4,32,256]{3,2,1,0:T(8,128)S(1)} %get-tuple-element.38), channel_id=1, source_target_pairs={{0,384},{64,448},{128,0},{192,64},{256,128},{320,192},{384,256},{4... | collective-permute-start | bytes 786440 | tf_op jit(solution)/shard_map/ppermute | solution.py:259
  26.4 11.6 %collective-permute-start.3 = (f32[2,4,32,256]{3,2,1,0:T(8,128)S(1)}, f32[2,4,32,256]{3,2,1,0:T(8,128)}, u32[]{:S(2)}, u32[]{:S(2)}) collective-permute-start(f32[2,4,32,256]{3,2,1,0:T(8,128)S(1)} %get-tuple-element.37), channel_id=1, source_target_pairs={{0,256},{64,320},{128,384},{192,448},{256,0},{320,64},{384,128},{4... | collective-permute-start | bytes 786440 | tf_op jit(solution)/shard_map/ppermute | solution.py:259
  39.2 6.6 %collective-permute-start.7 = (f32[2,32,256]{2,1,0:T(8,128)S(1)}, f32[2,32,256]{2,1,0:T(8,128)S(1)}, u32[]{:S(2)}, u32[]{:S(2)}) collective-permute-start(f32[2,32,256]{2,1,0:T(8,128)S(1)} %pad_maximum_fusion.3), channel_id=1, source_target_pairs={{0,16},{8,24},{16,0},{24,8},{32,48},{40,56},{48,32},{56,40},{1,17}... | collective-permute-start | bytes 196616 | tf_op jit(solution)/shard_map/ppermute | solution.py:206
  41.9 12.0 %collective-permute-start.4 = (f32[2,64,256]{2,1,0:T(8,128)S(1)}, f32[2,64,256]{2,1,0:T(8,128)S(1)}, u32[]{:S(2)}, u32[]{:S(2)}) collective-permute-start(f32[2,64,256]{2,1,0:T(8,128)S(1)} %constant_dynamic-slice_fusion.3), channel_id=1, source_target_pairs={{0,1},{1,0},{2,3},{3,2},{4,5},{5,4},{6,7},{7,6},{8,9},{9,8},{10,11... | collective-permute-start | bytes 393224 | tf_op jit(solution)/shard_map/ppermute | solution.py:206
  45.8 10.3 %collective-permute-start.8 = (f32[2,32,256]{2,1,0:T(8,128)S(1)}, f32[2,32,256]{2,1,0:T(8,128)S(1)}, u32[]{:S(2)}, u32[]{:S(2)}) collective-permute-start(f32[2,32,256]{2,1,0:T(8,128)S(1)} %pad_maximum_fusion.4), channel_id=1, source_target_pairs={{0,32},{8,40},{16,48},{24,56},{32,0},{40,8},{48,16},{56,24},{1,33}... | collective-permute-start | bytes 196616 | tf_op jit(solution)/shard_map/ppermute | solution.py:206
  54.0 12.1 %collective-permute-start.5 = (f32[2,32,256]{2,1,0:T(8,128)S(1)}, f32[2,32,256]{2,1,0:T(8,128)S(1)}, u32[]{:S(2)}, u32[]{:S(2)}) collective-permute-start(f32[2,32,256]{2,1,0:T(8,128)S(1)} %get-tuple-element.61), channel_id=1, source_target_pairs={{0,2},{1,3},{2,0},{3,1},{4,6},{5,7},{6,4},{7,5},{8,10},{9,11},{10,... | collective-permute-start | bytes 196616 | tf_op jit(solution)/shard_map/ppermute | solution.py:206
  56.2 17.1 %collective-permute-start.9 = (f32[2,32,256]{2,1,0:T(8,128)S(1)}, f32[2,32,256]{2,1,0:T(8,128)S(1)}, u32[]{:S(2)}, u32[]{:S(2)}) collective-permute-start(f32[2,32,256]{2,1,0:T(8,128)S(1)} %pad_maximum_fusion.5), channel_id=1, source_target_pairs={{0,15},{1,14},{2,13},{3,12},{4,11},{5,10},{6,9},{7,8},{8,7},{9,6},... | collective-permute-start | bytes 196616 | tf_op jit(solution)/shard_map/ppermute | solution.py:276
  66.1 10.2 %collective-permute-start.6 = (f32[2,32,256]{2,1,0:T(8,128)S(1)}, f32[2,32,256]{2,1,0:T(8,128)S(1)}, u32[]{:S(2)}, u32[]{:S(2)}) collective-permute-start(f32[2,32,256]{2,1,0:T(8,128)S(1)} %pad_maximum_fusion.2), channel_id=1, source_target_pairs={{0,4},{1,5},{2,6},{3,7},{4,0},{5,1},{6,2},{7,3},{8,12},{9,13},{10,... | collective-permute-start | bytes 196616 | tf_op jit(solution)/shard_map/ppermute | solution.py:206
  73.3 10.8 %collective-permute-start.10 = (f32[2,32,256]{2,1,0:T(8,128)S(1)}, f32[2,32,256]{2,1,0:T(8,128)S(1)}, u32[]{:S(2)}, u32[]{:S(2)}) collective-permute-start(f32[2,32,256]{2,1,0:T(8,128)S(1)} %pad_maximum_fusion.6), channel_id=1, source_target_pairs={{0,4},{1,5},{2,6},{3,7},{4,0},{5,1},{6,2},{7,3},{8,12},{9,13},{10,... | collective-permute-start | bytes 196616 | tf_op jit(solution)/shard_map/ppermute | solution.py:206
  84.2 8.5 %collective-permute-start.11 = (f32[2,64,256]{2,1,0:T(8,128)S(1)}, f32[2,64,256]{2,1,0:T(8,128)S(1)}, u32[]{:S(2)}, u32[]{:S(2)}) collective-permute-start(f32[2,64,256]{2,1,0:T(8,128)S(1)} %maximum_maximum_fusion.2), channel_id=1, source_target_pairs={{0,2},{1,3},{2,0},{3,1},{4,6},{5,7},{6,4},{7,5},{8,10},{9,11},{10,... | collective-permute-start | bytes 393224 | tf_op jit(solution)/shard_map/ppermute | solution.py:206
  87.2 48.6 %copy-start.4 = (s32[32,32]{1,0:T(8,128)S(1)}, s32[32,32]{1,0:T(8,128)}, u32[]{:S(2)}) copy-start(s32[32,32]{1,0:T(8,128)} %block_pattern.3) | copy-start | bytes 12292
  87.2 6.9 %collective-permute-start.12 = (f32[2,128,128]{2,1,0:T(8,128)S(1)}, f32[2,128,128]{2,1,0:T(8,128)S(1)}, u32[]{:S(2)}, u32[]{:S(2)}) collective-permute-start(f32[2,128,128]{2,1,0:T(8,128)S(1)} %get-tuple-element.47), channel_id=1, source_target_pairs={{0,16},{8,24},{16,0},{24,8},{32,48},{40,56},{48,32},{56,40},{1,17}... | collective-permute-start | bytes 393224 | tf_op jit(solution)/shard_map/ppermute | solution.py:206
  94.1 45.2 %copy-start.3 = (f32[1024,128]{1,0:T(8,128)S(1)}, f32[1024,128]{1,0:T(8,128)}, u32[]{:S(2)}) copy-start(f32[1024,128]{1,0:T(8,128)} %reduce-scatter.2.cloned.1.call-done.merged) | copy-start | bytes 1572868
  94.1 7.8 %collective-permute-start.14 = (f32[2,64,128]{2,1,0:T(8,128)S(1)}, f32[2,64,128]{2,1,0:T(8,128)S(1)}, u32[]{:S(2)}, u32[]{:S(2)}) collective-permute-start(f32[2,64,128]{2,1,0:T(8,128)S(1)} %constant_dynamic-slice_fusion), channel_id=1, source_target_pairs={{0,32},{8,40},{16,48},{24,56},{32,0},{40,8},{48,16},{56,24},{1,33}... | collective-permute-start | bytes 196616 | tf_op jit(solution)/shard_map/ppermute | solution.py:206
  97.9 7.6 %collective-permute-start.13 = (f32[2,96,256]{2,1,0:T(8,128)S(1)}, f32[2,96,256]{2,1,0:T(8,128)S(1)}, u32[]{:S(2)}, u32[]{:S(2)}) collective-permute-start(f32[2,96,256]{2,1,0:T(8,128)S(1)} %maximum_maximum_fusion.1), channel_id=1, source_target_pairs={{0,1},{1,0},{2,3},{3,2},{4,5},{5,4},{6,7},{7,6},{8,9},{9,8},{10,11... | collective-permute-start | bytes 589832 | tf_op jit(solution)/shard_map/ppermute | solution.py:206
  106.3 14.9 %collective-permute-start.15 = (f32[2,64,128]{2,1,0:T(8,128)S(1)}, f32[2,64,128]{2,1,0:T(8,128)S(1)}, u32[]{:S(2)}, u32[]{:S(2)}) collective-permute-start(f32[2,64,128]{2,1,0:T(8,128)S(1)} %pad_maximum_fusion.7), channel_id=1, source_target_pairs={{0,8},{8,0},{16,24},{24,16},{32,40},{40,32},{48,56},{56,48},{1,9},... | collective-permute-start | bytes 196616 | tf_op jit(solution)/shard_map/ppermute | solution.py:206
  121.2 7.7 %collective-permute-start.16 = (f32[2,64,128]{2,1,0:T(8,128)S(1)}, f32[2,64,128]{2,1,0:T(8,128)S(1)}, u32[]{:S(2)}, u32[]{:S(2)}) collective-permute-start(f32[2,64,128]{2,1,0:T(8,128)S(1)} %pad_maximum_fusion.8), channel_id=1, source_target_pairs={{0,32},{8,40},{16,48},{24,56},{32,0},{40,8},{48,16},{56,24},{1,33}... | collective-permute-start | bytes 196616 | tf_op jit(solution)/shard_map/ppermute | solution.py:206
  128.9 6.9 %collective-permute-start.17 = (f32[2,128,128]{2,1,0:T(8,128)S(1)}, f32[2,128,128]{2,1,0:T(8,128)S(1)}, u32[]{:S(2)}, u32[]{:S(2)}) collective-permute-start(f32[2,128,128]{2,1,0:T(8,128)S(1)} %maximum_select_fusion.2), channel_id=1, source_target_pairs={{0,16},{8,24},{16,0},{24,8},{32,48},{40,56},{48,32},{56,40},{1,17}... | collective-permute-start | bytes 393224 | tf_op jit(solution)/shard_map/ppermute | solution.py:206
Sparse Core Ops, SparseCore 0:
  17.0 50.0 reduce-scatter.1
  106.5 32.8 all-gather.2

commit v10 on v6

--- a/solution.py
+++ b/solution.py
@@ -10,6 +10,7 @@
 VMEM = pl.BlockSpec(memory_space=pltpu.VMEM)
 SMEM = pl.BlockSpec(memory_space=pltpu.SMEM)
 PARAMS = pltpu.CompilerParams(vmem_limit_bytes=32 << 20)
+MIDDLE = pltpu.CompilerParams(vmem_limit_bytes=50 << 20)
 LARGE = pltpu.CompilerParams(vmem_limit_bytes=60 << 20)
 
 
@@ -185,7 +186,7 @@
             pltpu.VMEM(panels.shape, jnp.float32),
             pltpu.SemaphoreType.DMA((2,)),
         ],
-        compiler_params=LARGE,
+        compiler_params=MIDDLE,
     )(block_pattern, row_map, col_map, lower_inv, upper_inv, rows, up0, term0, merged, panels)
 
 

time: 152 us -> 151 us (level)
  no operation moved by 1% of the time
where the time goes in v10:
time: 151 us; the launch traced here: 148 us
  starting transfers between devices  76.3 us (51%)
  waiting for transfers between devices  36.1 us (24%)
  between operations  18.1 us (12%)
  Pallas kernels  10 us (7%)
  other arithmetic  5.25 us (3%)
  local copies, waits for them, and re-layouts  2.31 us (2%)
    ppermute x14, starting transfers between devices, swap(): return lax.ppermute(x, axis, [(i, i ^ bit) for i in range(size)])  53.4 us
    ppermute x14, waiting for transfers between devices, swap(): return lax.ppermute(x, axis, [(i, i ^ bit) for i in range(size)])  33.6 us
    ppermute x1, starting transfers between devices, shards(): corner_other = lax.ppermute(corner, ('row', 'col'), mirror)  11.9 us
    ppermute x3, starting transfers between devices, shards(): panel = panel + lax.ppermute(chunk, 'gz', around(step))  10.9 us
    pallas_call x1, Pallas kernels, last_terms(): pl.pallas_call(functools.partial(last_kernel, n_y), out_shape=jax.ShapeDt...  5.22 us
    pallas_call x1, Pallas kernels, cut_panels(): pl.pallas_call(panel_kernel, out_shape=[shape, shape], in_specs=[SMEM, pl...  3.42 us
  transfers between devices with their start and end apart: 20, of which 12 were waited for; matrix products, arithmetic and copies ran while one was open for 2% of the time, Pallas kernels for 1%

profile of v10, /device:TPU:6, one launch (start us, length us, event | category | flops | bytes accessed | tf_op | source)
XLA Modules:
  0.0 148.1 jit_solution(9892759476940262940)
XLA Ops:
  6.5 3.4 %shard_map.64 = (f32[4,2,4,32,256]{4,3,2,1,0:T(8,128)}, f32[4,2,4,32,256]{4,3,2,1,0:T(8,128)}) custom-call(s32[32]{0:T(128)} %col_map.5, bf16[1024,1024]{1,0:T(8,128)(2,1)} %bitcast.21), custom_call_target="tpu_custom_call" | custom-call | tf_op jit(solution)/shard_map/pallas_call | solution.py:64
  10.0 1.9 %collective-permute-start = (f32[4,2,4,32,256]{4,3,2,1,0:T(8,128)}, f32[4,2,4,32,256]{4,3,2,1,0:T(8,128)S(1)}, u32[]{:S(2)}, u32[]{:S(2)}) collective-permute-start(f32[4,2,4,32,256]{4,3,2,1,0:T(8,128)} %get-tuple-element.16), channel_id=1, source_target_pairs={{0,64},{64,0},{128,192},{192,128},{256,320},{320,256},{384,448},{4... | collective-permute-start | bytes 3145736 | tf_op jit(solution)/shard_map/ppermute | solution.py:194
  11.9 2.8 %collective-permute-done = f32[4,2,4,32,256]{4,3,2,1,0:T(8,128)S(1)} collective-permute-done((f32[4,2,4,32,256]{4,3,2,1,0:T(8,128)}, f32[4,2,4,32,256]{4,3,2,1,0:T(8,128)S(1)}, u32[]{:S(2)}, u32[]{:S(2)}) %collective-permute-start) | collective-permute-done | bytes 1048608 | tf_op jit(solution)/shard_map/ppermute | solution.py:194
  14.7 2.4 %convert_element_type.28 = f32[1024,1024]{1,0:T(8,128)} convert(bf16[1024,1024]{1,0:T(8,128)(2,1)S(1)} %bitcast.22) | non-fusion elementwise | flops 1048576 | bytes 6291456 | tf_op jit(solution)/shard_map/convert_element_type | solution.py:251
  17.2 0.0 reduce-scatter.2.cloned.1.call-update
  17.2 0.0 copy-start.5
  17.2 0.0 all-gather.3.cloned.1.call-start
  17.3 1.1 copy-done.7
  18.4 0.2 add.23
  18.6 0.1 dynamic-slice_bitcast_fusion.2
  18.7 5.1 %collective-permute-start.3 = (f32[2,4,32,256]{3,2,1,0:T(8,128)S(1)}, f32[2,4,32,256]{3,2,1,0:T(8,128)S(1)}, u32[]{:S(2)}, u32[]{:S(2)}) collective-permute-start(f32[2,4,32,256]{3,2,1,0:T(8,128)S(1)} %get-tuple-element.30), channel_id=1, source_target_pairs={{0,256},{64,320},{128,384},{192,448},{256,0},{320,64},{384,128},{4... | collective-permute-start | bytes 786440 | tf_op jit(solution)/shard_map/ppermute | solution.py:249
  23.8 3.0 %collective-permute-start.2 = (f32[2,4,32,256]{3,2,1,0:T(8,128)S(1)}, f32[2,4,32,256]{3,2,1,0:T(8,128)S(1)}, u32[]{:S(2)}, u32[]{:S(2)}) collective-permute-start(f32[2,4,32,256]{3,2,1,0:T(8,128)S(1)} %get-tuple-element.31), channel_id=1, source_target_pairs={{0,384},{64,448},{128,0},{192,64},{256,128},{320,192},{384,256},{4... | collective-permute-start | bytes 786440 | tf_op jit(solution)/shard_map/ppermute | solution.py:249
  26.8 2.9 %collective-permute-start.1 = (f32[2,4,32,256]{3,2,1,0:T(8,128)S(1)}, f32[2,4,32,256]{3,2,1,0:T(8,128)S(1)}, u32[]{:S(2)}, u32[]{:S(2)}) collective-permute-start(f32[2,4,32,256]{3,2,1,0:T(8,128)S(1)} %get-tuple-element.29), channel_id=1, source_target_pairs={{0,128},{64,192},{128,256},{192,320},{256,384},{320,448},{384,0},{... | collective-permute-start | bytes 786440 | tf_op jit(solution)/shard_map/ppermute | solution.py:249
  29.7 0.7 fusion.11
  33.1 0.7 fusion.9
  35.2 1.2 collective-permute-done.2
  36.4 1.2 collective-permute-done.1
  37.7 0.1 fusion.1
  37.8 2.7 %collective-permute-start.7 = (f32[2,32,256]{2,1,0:T(8,128)S(1)}, f32[2,32,256]{2,1,0:T(8,128)S(1)}, u32[]{:S(2)}, u32[]{:S(2)}) collective-permute-start(f32[2,32,256]{2,1,0:T(8,128)S(1)} %pad_maximum_fusion.3), channel_id=1, source_target_pairs={{0,16},{8,24},{16,0},{24,8},{32,48},{40,56},{48,32},{56,40},{1,17}... | collective-permute-start | bytes 196616 | tf_op jit(solution)/shard_map/ppermute | solution.py:194
  40.6 3.8 %collective-permute-start.4 = (f32[2,64,256]{2,1,0:T(8,128)S(1)}, f32[2,64,256]{2,1,0:T(8,128)S(1)}, u32[]{:S(2)}, u32[]{:S(2)}) collective-permute-start(f32[2,64,256]{2,1,0:T(8,128)S(1)} %constant_dynamic-slice_fusion.3), channel_id=1, source_target_pairs={{0,1},{1,0},{2,3},{3,2},{4,5},{5,4},{6,7},{7,6},{8,9},{9,8},{10,11... | collective-permute-start | bytes 393224 | tf_op jit(solution)/shard_map/ppermute | solution.py:194
  44.5 5.2 %collective-permute-start.8 = (f32[2,32,256]{2,1,0:T(8,128)S(1)}, f32[2,32,256]{2,1,0:T(8,128)S(1)}, u32[]{:S(2)}, u32[]{:S(2)}) collective-permute-start(f32[2,32,256]{2,1,0:T(8,128)S(1)} %pad_maximum_fusion.4), channel_id=1, source_target_pairs={{0,32},{8,40},{16,48},{24,56},{32,0},{40,8},{48,16},{56,24},{1,33}... | collective-permute-start | bytes 196616 | tf_op jit(solution)/shard_map/ppermute | solution.py:194
  49.7 3.0 %collective-permute-start.5 = (f32[2,32,256]{2,1,0:T(8,128)S(1)}, f32[2,32,256]{2,1,0:T(8,128)S(1)}, u32[]{:S(2)}, u32[]{:S(2)}) collective-permute-start(f32[2,32,256]{2,1,0:T(8,128)S(1)} %get-tuple-element.53), channel_id=1, source_target_pairs={{0,2},{1,3},{2,0},{3,1},{4,6},{5,7},{6,4},{7,5},{8,10},{9,11},{10,... | collective-permute-start | bytes 196616 | tf_op jit(solution)/shard_map/ppermute | solution.py:194
  52.8 11.9 %collective-permute-start.9 = (f32[2,32,256]{2,1,0:T(8,128)S(1)}, f32[2,32,256]{2,1,0:T(8,128)S(1)}, u32[]{:S(2)}, u32[]{:S(2)}) collective-permute-start(f32[2,32,256]{2,1,0:T(8,128)S(1)} %pad_maximum_fusion.5), channel_id=1, source_target_pairs={{0,15},{1,14},{2,13},{3,12},{4,11},{5,10},{6,9},{7,8},{8,7},{9,6},... | collective-permute-start | bytes 196616 | tf_op jit(solution)/shard_map/ppermute | solution.py:262
  64.8 6.9 %collective-permute-start.6 = (f32[2,32,256]{2,1,0:T(8,128)S(1)}, f32[2,32,256]{2,1,0:T(8,128)S(1)}, u32[]{:S(2)}, u32[]{:S(2)}) collective-permute-start(f32[2,32,256]{2,1,0:T(8,128)S(1)} %pad_maximum_fusion.2), channel_id=1, source_target_pairs={{0,4},{1,5},{2,6},{3,7},{4,0},{5,1},{6,2},{7,3},{8,12},{9,13},{10,... | collective-permute-start | bytes 196616 | tf_op jit(solution)/shard_map/ppermute | solution.py:194
  71.8 3.1 %collective-permute-start.10 = (f32[2,32,256]{2,1,0:T(8,128)S(1)}, f32[2,32,256]{2,1,0:T(8,128)S(1)}, u32[]{:S(2)}, u32[]{:S(2)}) collective-permute-start(f32[2,32,256]{2,1,0:T(8,128)S(1)} %pad_maximum_fusion.6), channel_id=1, source_target_pairs={{0,4},{1,5},{2,6},{3,7},{4,0},{5,1},{6,2},{7,3},{8,12},{9,13},{10,... | collective-permute-start | bytes 196616 | tf_op jit(solution)/shard_map/ppermute | solution.py:194
  74.9 4.2 %collective-permute-done.6 = f32[2,32,256]{2,1,0:T(8,128)S(1)} collective-permute-done((f32[2,32,256]{2,1,0:T(8,128)S(1)}, f32[2,32,256]{2,1,0:T(8,128)S(1)}, u32[]{:S(2)}, u32[]{:S(2)}) %collective-permute-start.6) | collective-permute-done | bytes 65568 | tf_op jit(solution)/shard_map/ppermute | solution.py:194
  79.1 3.5 %collective-permute-done.10 = f32[2,32,256]{2,1,0:T(8,128)S(1)} collective-permute-done((f32[2,32,256]{2,1,0:T(8,128)S(1)}, f32[2,32,256]{2,1,0:T(8,128)S(1)}, u32[]{:S(2)}, u32[]{:S(2)}) %collective-permute-start.10) | collective-permute-done | bytes 65568 | tf_op jit(solution)/shard_map/ppermute | solution.py:194
  82.7 1.9 %collective-permute-start.11 = (f32[2,64,256]{2,1,0:T(8,128)S(1)}, f32[2,64,256]{2,1,0:T(8,128)S(1)}, u32[]{:S(2)}, u32[]{:S(2)}) collective-permute-start(f32[2,64,256]{2,1,0:T(8,128)S(1)} %maximum_maximum_fusion.2), channel_id=1, source_target_pairs={{0,2},{1,3},{2,0},{3,1},{4,6},{5,7},{6,4},{7,5},{8,10},{9,11},{10,... | collective-permute-start | bytes 393224 | tf_op jit(solution)/shard_map/ppermute | solution.py:194
  84.6 0.0 reduce-scatter.2.cloned.1.call-done.merged
  84.6 1.0 constant_dynamic-slice_fusion.1
  85.7 3.1 %collective-permute-start.12 = (f32[2,128,128]{2,1,0:T(8,128)S(1)}, f32[2,128,128]{2,1,0:T(8,128)S(1)}, u32[]{:S(2)}, u32[]{:S(2)}) collective-permute-start(f32[2,128,128]{2,1,0:T(8,128)S(1)} %get-tuple-element.39), channel_id=1, source_target_pairs={{0,16},{8,24},{16,0},{24,8},{32,48},{40,56},{48,32},{56,40},{1,17}... | collective-permute-start | bytes 393224 | tf_op jit(solution)/shard_map/ppermute | solution.py:194
  88.8 2.3 %collective-permute-done.11 = f32[2,64,256]{2,1,0:T(8,128)S(1)} collective-permute-done((f32[2,64,256]{2,1,0:T(8,128)S(1)}, f32[2,64,256]{2,1,0:T(8,128)S(1)}, u32[]{:S(2)}, u32[]{:S(2)}) %collective-permute-start.11) | collective-permute-done | bytes 131104 | tf_op jit(solution)/shard_map/ppermute | solution.py:194
  91.2 1.5 %collective-permute-done.12 = f32[2,128,128]{2,1,0:T(8,128)S(1)} collective-permute-done((f32[2,128,128]{2,1,0:T(8,128)S(1)}, f32[2,128,128]{2,1,0:T(8,128)S(1)}, u32[]{:S(2)}, u32[]{:S(2)}) %collective-permute-start.12) | collective-permute-done | bytes 131104 | tf_op jit(solution)/shard_map/ppermute | solution.py:194
  92.7 3.9 %collective-permute-start.14 = (f32[2,64,128]{2,1,0:T(8,128)S(1)}, f32[2,64,128]{2,1,0:T(8,128)S(1)}, u32[]{:S(2)}, u32[]{:S(2)}) collective-permute-start(f32[2,64,128]{2,1,0:T(8,128)S(1)} %constant_dynamic-slice_fusion), channel_id=1, source_target_pairs={{0,32},{8,40},{16,48},{24,56},{32,0},{40,8},{48,16},{56,24},{1,33}... | collective-permute-start | bytes 196616 | tf_op jit(solution)/shard_map/ppermute | solution.py:194
  96.7 1.9 %collective-permute-start.13 = (f32[2,96,256]{2,1,0:T(8,128)S(1)}, f32[2,96,256]{2,1,0:T(8,128)S(1)}, u32[]{:S(2)}, u32[]{:S(2)}) collective-permute-start(f32[2,96,256]{2,1,0:T(8,128)S(1)} %maximum_maximum_fusion.1), channel_id=1, source_target_pairs={{0,1},{1,0},{2,3},{3,2},{4,5},{5,4},{6,7},{7,6},{8,9},{9,8},{10,11... | collective-permute-start | bytes 589832 | tf_op jit(solution)/shard_map/ppermute | solution.py:194
  98.6 1.9 %collective-permute-done.14 = f32[2,64,128]{2,1,0:T(8,128)S(1)} collective-permute-done((f32[2,64,128]{2,1,0:T(8,128)S(1)}, f32[2,64,128]{2,1,0:T(8,128)S(1)}, u32[]{:S(2)}, u32[]{:S(2)}) %collective-permute-start.14) | collective-permute-done | bytes 65568 | tf_op jit(solution)/shard_map/ppermute | solution.py:194
  100.6 3.7 %collective-permute-done.13 = f32[2,96,256]{2,1,0:T(8,128)S(1)} collective-permute-done((f32[2,96,256]{2,1,0:T(8,128)S(1)}, f32[2,96,256]{2,1,0:T(8,128)S(1)}, u32[]{:S(2)}, u32[]{:S(2)}) %collective-permute-start.13) | collective-permute-done | bytes 196640 | tf_op jit(solution)/shard_map/ppermute | solution.py:194
  104.3 0.8 maximum_maximum_fusion
  105.1 0.0 all-gather.3.cloned.1.call-update
  105.1 9.5 %collective-permute-start.15 = (f32[2,64,128]{2,1,0:T(8,128)S(1)}, f32[2,64,128]{2,1,0:T(8,128)S(1)}, u32[]{:S(2)}, u32[]{:S(2)}) collective-permute-start(f32[2,64,128]{2,1,0:T(8,128)S(1)} %pad_maximum_fusion.7), channel_id=1, source_target_pairs={{0,8},{8,0},{16,24},{24,16},{32,40},{40,32},{48,56},{56,48},{1,9},... | collective-permute-start | bytes 196616 | tf_op jit(solution)/shard_map/ppermute | solution.py:194
  114.6 5.4 %collective-permute-done.15 = f32[2,64,128]{2,1,0:T(8,128)S(1)} collective-permute-done((f32[2,64,128]{2,1,0:T(8,128)S(1)}, f32[2,64,128]{2,1,0:T(8,128)S(1)}, u32[]{:S(2)}, u32[]{:S(2)}) %collective-permute-start.15) | collective-permute-done | bytes 65568 | tf_op jit(solution)/shard_map/ppermute | solution.py:194
  120.0 3.6 %collective-permute-start.16 = (f32[2,64,128]{2,1,0:T(8,128)S(1)}, f32[2,64,128]{2,1,0:T(8,128)S(1)}, u32[]{:S(2)}, u32[]{:S(2)}) collective-permute-start(f32[2,64,128]{2,1,0:T(8,128)S(1)} %pad_maximum_fusion.8), channel_id=1, source_target_pairs={{0,32},{8,40},{16,48},{24,56},{32,0},{40,8},{48,16},{56,24},{1,33}... | collective-permute-start | bytes 196616 | tf_op jit(solution)/shard_map/ppermute | solution.py:194
  123.7 4.0 %collective-permute-done.16 = f32[2,64,128]{2,1,0:T(8,128)S(1)} collective-permute-done((f32[2,64,128]{2,1,0:T(8,128)S(1)}, f32[2,64,128]{2,1,0:T(8,128)S(1)}, u32[]{:S(2)}, u32[]{:S(2)}) %collective-permute-start.16) | collective-permute-done | bytes 65568 | tf_op jit(solution)/shard_map/ppermute | solution.py:194
  127.7 2.6 %collective-permute-start.17 = (f32[2,128,128]{2,1,0:T(8,128)S(1)}, f32[2,128,128]{2,1,0:T(8,128)S(1)}, u32[]{:S(2)}, u32[]{:S(2)}) collective-permute-start(f32[2,128,128]{2,1,0:T(8,128)S(1)} %maximum_select_fusion.2), channel_id=1, source_target_pairs={{0,16},{8,24},{16,0},{24,8},{32,48},{40,56},{48,32},{56,40},{1,17}... | collective-permute-start | bytes 393224 | tf_op jit(solution)/shard_map/ppermute | solution.py:194
  130.3 4.2 %collective-permute-done.17 = f32[2,128,128]{2,1,0:T(8,128)S(1)} collective-permute-done((f32[2,128,128]{2,1,0:T(8,128)S(1)}, f32[2,128,128]{2,1,0:T(8,128)S(1)}, u32[]{:S(2)}, u32[]{:S(2)}) %collective-permute-start.17) | collective-permute-done | bytes 131104 | tf_op jit(solution)/shard_map/ppermute | solution.py:194
  134.6 1.4 shard_map.65
  136.0 0.0 all-gather.3.cloned.1.call-done
  136.0 5.2 %shard_map.66 = bf16[1024,128]{1,0:T(8,128)(2,1)} custom-call(s32[32,32]{1,0:T(8,128)S(1)} %copy-done.3, s32[32]{0:T(128)S(1)} %copy-done.5, s32[32]{0:T(128)S(1)} %copy-done.4, f32[2,256,256]{2,1,0:T(8,128)S(1)} %copy-done, f32[2,256,256]{2,1,0:T(8,128)S(1)} %copy-done.1, f32[2,256,128]{2,1,0:T(8,128)S(1)} %maximum_select_fusion.1.rows, ...), custom_call_target="tpu_custom_call" | custom-call | tf_op jit(solution)/shard_map/pallas_call | solution.py:178
  (55 shorter events, 0.5 us)
Async XLA Ops:
  6.5 8.2 %copy-start.6 = (bf16[1,1024,1024]{2,1,0:T(8,128)(2,1)S(1)}, bf16[1,1024,1024]{2,1,0:T(8,128)(2,1)}, u32[]{:S(2)}) copy-start(bf16[1,1024,1024]{2,1,0:T(8,128)(2,1)} %param.6) | copy-start | bytes 6291460
  6.5 78.1 %reduce-scatter.2.cloned.1.call-start = ((), (), s32[]{:S(2)}) async-start(), calls=%async_computation.1 | async-start | bytes 4718592 | tf_op jit(solution)/shard_map/reduce_scatter | solution.py:251
  10.0 4.8 %collective-permute-start = (f32[4,2,4,32,256]{4,3,2,1,0:T(8,128)}, f32[4,2,4,32,256]{4,3,2,1,0:T(8,128)S(1)}, u32[]{:S(2)}, u32[]{:S(2)}) collective-permute-start(f32[4,2,4,32,256]{4,3,2,1,0:T(8,128)} %get-tuple-element.16), channel_id=1, source_target_pairs={{0,64},{64,0},{128,192},{192,128},{256,320},{320,256},{384,448},{4... | collective-permute-start | bytes 3145736 | tf_op jit(solution)/shard_map/ppermute | solution.py:194
  17.2 1.2 copy-start.7
  17.2 12.5 %copy-start.5 = (s32[32]{0:T(128)S(1)}, s32[32]{0:T(128)}, u32[]{:S(2)}) copy-start(s32[32]{0:T(128)} %row_map.1) | copy-start | bytes 388
  17.2 15.8 %copy-start.4 = (s32[32]{0:T(128)S(1)}, s32[32]{0:T(128)}, u32[]{:S(2)}) copy-start(s32[32]{0:T(128)} %col_map.5) | copy-start | bytes 388
  17.2 118.8 %all-gather.3.cloned.1.call-start = ((), (), s32[]{:S(2)}) async-start(), calls=%async_computation.2 | async-start | bytes 2949120 | tf_op jit(solution)/shard_map/all_gather | solution.py:302
  18.7 16.5 %collective-permute-start.3 = (f32[2,4,32,256]{3,2,1,0:T(8,128)S(1)}, f32[2,4,32,256]{3,2,1,0:T(8,128)S(1)}, u32[]{:S(2)}, u32[]{:S(2)}) collective-permute-start(f32[2,4,32,256]{3,2,1,0:T(8,128)S(1)} %get-tuple-element.30), channel_id=1, source_target_pairs={{0,256},{64,320},{128,384},{192,448},{256,0},{320,64},{384,128},{4... | collective-permute-start | bytes 786440 | tf_op jit(solution)/shard_map/ppermute | solution.py:249
  23.8 12.6 %collective-permute-start.2 = (f32[2,4,32,256]{3,2,1,0:T(8,128)S(1)}, f32[2,4,32,256]{3,2,1,0:T(8,128)S(1)}, u32[]{:S(2)}, u32[]{:S(2)}) collective-permute-start(f32[2,4,32,256]{3,2,1,0:T(8,128)S(1)} %get-tuple-element.31), channel_id=1, source_target_pairs={{0,384},{64,448},{128,0},{192,64},{256,128},{320,192},{384,256},{4... | collective-permute-start | bytes 786440 | tf_op jit(solution)/shard_map/ppermute | solution.py:249
  26.8 10.9 %collective-permute-start.1 = (f32[2,4,32,256]{3,2,1,0:T(8,128)S(1)}, f32[2,4,32,256]{3,2,1,0:T(8,128)S(1)}, u32[]{:S(2)}, u32[]{:S(2)}) collective-permute-start(f32[2,4,32,256]{3,2,1,0:T(8,128)S(1)} %get-tuple-element.29), channel_id=1, source_target_pairs={{0,128},{64,192},{128,256},{192,320},{256,384},{320,448},{384,0},{... | collective-permute-start | bytes 786440 | tf_op jit(solution)/shard_map/ppermute | solution.py:249
  37.8 6.6 %collective-permute-start.7 = (f32[2,32,256]{2,1,0:T(8,128)S(1)}, f32[2,32,256]{2,1,0:T(8,128)S(1)}, u32[]{:S(2)}, u32[]{:S(2)}) collective-permute-start(f32[2,32,256]{2,1,0:T(8,128)S(1)} %pad_maximum_fusion.3), channel_id=1, source_target_pairs={{0,16},{8,24},{16,0},{24,8},{32,48},{40,56},{48,32},{56,40},{1,17}... | collective-permute-start | bytes 196616 | tf_op jit(solution)/shard_map/ppermute | solution.py:194
  40.6 9.1 %collective-permute-start.4 = (f32[2,64,256]{2,1,0:T(8,128)S(1)}, f32[2,64,256]{2,1,0:T(8,128)S(1)}, u32[]{:S(2)}, u32[]{:S(2)}) collective-permute-start(f32[2,64,256]{2,1,0:T(8,128)S(1)} %constant_dynamic-slice_fusion.3), channel_id=1, source_target_pairs={{0,1},{1,0},{2,3},{3,2},{4,5},{5,4},{6,7},{7,6},{8,9},{9,8},{10,11... | collective-permute-start | bytes 393224 | tf_op jit(solution)/shard_map/ppermute | solution.py:194
  44.5 8.3 %collective-permute-start.8 = (f32[2,32,256]{2,1,0:T(8,128)S(1)}, f32[2,32,256]{2,1,0:T(8,128)S(1)}, u32[]{:S(2)}, u32[]{:S(2)}) collective-permute-start(f32[2,32,256]{2,1,0:T(8,128)S(1)} %pad_maximum_fusion.4), channel_id=1, source_target_pairs={{0,32},{8,40},{16,48},{24,56},{32,0},{40,8},{48,16},{56,24},{1,33}... | collective-permute-start | bytes 196616 | tf_op jit(solution)/shard_map/ppermute | solution.py:194
  49.7 15.0 %collective-permute-start.5 = (f32[2,32,256]{2,1,0:T(8,128)S(1)}, f32[2,32,256]{2,1,0:T(8,128)S(1)}, u32[]{:S(2)}, u32[]{:S(2)}) collective-permute-start(f32[2,32,256]{2,1,0:T(8,128)S(1)} %get-tuple-element.53), channel_id=1, source_target_pairs={{0,2},{1,3},{2,0},{3,1},{4,6},{5,7},{6,4},{7,5},{8,10},{9,11},{10,... | collective-permute-start | bytes 196616 | tf_op jit(solution)/shard_map/ppermute | solution.py:194
  52.8 18.9 %collective-permute-start.9 = (f32[2,32,256]{2,1,0:T(8,128)S(1)}, f32[2,32,256]{2,1,0:T(8,128)S(1)}, u32[]{:S(2)}, u32[]{:S(2)}) collective-permute-start(f32[2,32,256]{2,1,0:T(8,128)S(1)} %pad_maximum_fusion.5), channel_id=1, source_target_pairs={{0,15},{1,14},{2,13},{3,12},{4,11},{5,10},{6,9},{7,8},{8,7},{9,6},... | collective-permute-start | bytes 196616 | tf_op jit(solution)/shard_map/ppermute | solution.py:262
  64.8 14.4 %collective-permute-start.6 = (f32[2,32,256]{2,1,0:T(8,128)S(1)}, f32[2,32,256]{2,1,0:T(8,128)S(1)}, u32[]{:S(2)}, u32[]{:S(2)}) collective-permute-start(f32[2,32,256]{2,1,0:T(8,128)S(1)} %pad_maximum_fusion.2), channel_id=1, source_target_pairs={{0,4},{1,5},{2,6},{3,7},{4,0},{5,1},{6,2},{7,3},{8,12},{9,13},{10,... | collective-permute-start | bytes 196616 | tf_op jit(solution)/shard_map/ppermute | solution.py:194
  71.8 10.9 %collective-permute-start.10 = (f32[2,32,256]{2,1,0:T(8,128)S(1)}, f32[2,32,256]{2,1,0:T(8,128)S(1)}, u32[]{:S(2)}, u32[]{:S(2)}) collective-permute-start(f32[2,32,256]{2,1,0:T(8,128)S(1)} %pad_maximum_fusion.6), channel_id=1, source_target_pairs={{0,4},{1,5},{2,6},{3,7},{4,0},{5,1},{6,2},{7,3},{8,12},{9,13},{10,... | collective-permute-start | bytes 196616 | tf_op jit(solution)/shard_map/ppermute | solution.py:194
  82.7 8.5 %collective-permute-start.11 = (f32[2,64,256]{2,1,0:T(8,128)S(1)}, f32[2,64,256]{2,1,0:T(8,128)S(1)}, u32[]{:S(2)}, u32[]{:S(2)}) collective-permute-start(f32[2,64,256]{2,1,0:T(8,128)S(1)} %maximum_maximum_fusion.2), channel_id=1, source_target_pairs={{0,2},{1,3},{2,0},{3,1},{4,6},{5,7},{6,4},{7,5},{8,10},{9,11},{10,... | collective-permute-start | bytes 393224 | tf_op jit(solution)/shard_map/ppermute | solution.py:194
  85.6 48.9 %copy-start = (f32[2,256,256]{2,1,0:T(8,128)S(1)}, f32[2,256,256]{2,1,0:T(8,128)}, u32[]{:S(2)}) copy-start(f32[2,256,256]{2,1,0:T(8,128)} %lower_inv.3) | copy-start | bytes 1572868
  85.7 48.9 %copy-start.1 = (f32[2,256,256]{2,1,0:T(8,128)S(1)}, f32[2,256,256]{2,1,0:T(8,128)}, u32[]{:S(2)}) copy-start(f32[2,256,256]{2,1,0:T(8,128)} %upper_inv.3) | copy-start | bytes 1572868
  85.7 48.9 %copy-start.3 = (s32[32,32]{1,0:T(8,128)S(1)}, s32[32,32]{1,0:T(8,128)}, u32[]{:S(2)}) copy-start(s32[32,32]{1,0:T(8,128)} %block_pattern.3) | copy-start | bytes 12292
  85.7 7.0 %collective-permute-start.12 = (f32[2,128,128]{2,1,0:T(8,128)S(1)}, f32[2,128,128]{2,1,0:T(8,128)S(1)}, u32[]{:S(2)}, u32[]{:S(2)}) collective-permute-start(f32[2,128,128]{2,1,0:T(8,128)S(1)} %get-tuple-element.39), channel_id=1, source_target_pairs={{0,16},{8,24},{16,0},{24,8},{32,48},{40,56},{48,32},{56,40},{1,17}... | collective-permute-start | bytes 393224 | tf_op jit(solution)/shard_map/ppermute | solution.py:194
  92.7 43.3 %copy-start.2 = (f32[1024,128]{1,0:T(8,128)S(1)}, f32[1024,128]{1,0:T(8,128)}, u32[]{:S(2)}) copy-start(f32[1024,128]{1,0:T(8,128)} %reduce-scatter.2.cloned.1.call-done.merged) | copy-start | bytes 1572868
  92.7 7.8 %collective-permute-start.14 = (f32[2,64,128]{2,1,0:T(8,128)S(1)}, f32[2,64,128]{2,1,0:T(8,128)S(1)}, u32[]{:S(2)}, u32[]{:S(2)}) collective-permute-start(f32[2,64,128]{2,1,0:T(8,128)S(1)} %constant_dynamic-slice_fusion), channel_id=1, source_target_pairs={{0,32},{8,40},{16,48},{24,56},{32,0},{40,8},{48,16},{56,24},{1,33}... | collective-permute-start | bytes 196616 | tf_op jit(solution)/shard_map/ppermute | solution.py:194
  96.7 7.6 %collective-permute-start.13 = (f32[2,96,256]{2,1,0:T(8,128)S(1)}, f32[2,96,256]{2,1,0:T(8,128)S(1)}, u32[]{:S(2)}, u32[]{:S(2)}) collective-permute-start(f32[2,96,256]{2,1,0:T(8,128)S(1)} %maximum_maximum_fusion.1), channel_id=1, source_target_pairs={{0,1},{1,0},{2,3},{3,2},{4,5},{5,4},{6,7},{7,6},{8,9},{9,8},{10,11... | collective-permute-start | bytes 589832 | tf_op jit(solution)/shard_map/ppermute | solution.py:194
  105.1 14.9 %collective-permute-start.15 = (f32[2,64,128]{2,1,0:T(8,128)S(1)}, f32[2,64,128]{2,1,0:T(8,128)S(1)}, u32[]{:S(2)}, u32[]{:S(2)}) collective-permute-start(f32[2,64,128]{2,1,0:T(8,128)S(1)} %pad_maximum_fusion.7), channel_id=1, source_target_pairs={{0,8},{8,0},{16,24},{24,16},{32,40},{40,32},{48,56},{56,48},{1,9},... | collective-permute-start | bytes 196616 | tf_op jit(solution)/shard_map/ppermute | solution.py:194
  120.0 7.7 %collective-permute-start.16 = (f32[2,64,128]{2,1,0:T(8,128)S(1)}, f32[2,64,128]{2,1,0:T(8,128)S(1)}, u32[]{:S(2)}, u32[]{:S(2)}) collective-permute-start(f32[2,64,128]{2,1,0:T(8,128)S(1)} %pad_maximum_fusion.8), channel_id=1, source_target_pairs={{0,32},{8,40},{16,48},{24,56},{32,0},{40,8},{48,16},{56,24},{1,33}... | collective-permute-start | bytes 196616 | tf_op jit(solution)/shard_map/ppermute | solution.py:194
  127.7 6.9 %collective-permute-start.17 = (f32[2,128,128]{2,1,0:T(8,128)S(1)}, f32[2,128,128]{2,1,0:T(8,128)S(1)}, u32[]{:S(2)}, u32[]{:S(2)}) collective-permute-start(f32[2,128,128]{2,1,0:T(8,128)S(1)} %maximum_select_fusion.2), channel_id=1, source_target_pairs={{0,16},{8,24},{16,0},{24,8},{32,48},{40,56},{48,32},{56,40},{1,17}... | collective-permute-start | bytes 393224 | tf_op jit(solution)/shard_map/ppermute | solution.py:194
Sparse Core Ops, SparseCore 0:
  17.3 49.9 reduce-scatter.1
  105.2 30.4 all-gather.2
